TPU v7x, 32 devices: a whole 2x2x4 slice. The times are simulated.
32 devices in a mesh: section: 2 (over core), dp: 4 (over y, x), tensor: 4 (over z).
Axes of the slice: x: 2, y: 2, z: 4, core: 2. Of those that a mesh axis runs over, the one named last changes fastest.
Arguments:
- layer_input_activations: bfloat16 [4, 128, 2048], P(None, ('dp', 'tensor')), may hold values from -6 to 6
- cotangent: bfloat16 [4, 128, 2048], P(None, ('dp', 'tensor')), may hold values from -0.59765625 to 0.59765625
- domain_ids: int32 [4, 4], P(None, 'dp'), may hold values from 0 to 3
- norm_gain: float32 [2, 2048], P('section'), may hold values from 0.5 to 1.5
- w_gate: bfloat16 [2, 2048, 7168], P('section', None, 'tensor'), may hold values from -0.125 to 0.125
- w_up: bfloat16 [2, 2048, 7168], P('section', None, 'tensor'), may hold values from -0.125 to 0.125
- w_down: bfloat16 [2, 7168, 2048], P('section', 'tensor'), may hold values from -0.0625 to 0.0625
Outputs:
- domain_grads: bfloat16 [2, 4, 7168, 2048], P('section', None, 'tensor', 'dp')
- level_norms: float32 [4, 3], replicated
All inputs are finite; a program needn't handle non-finite values.
Results may differ from a plain program's by a relative error of at most 0.01.
Values may be sent and summed in bfloat16 or wider, within the bound.
No kernel may reach another device: no remote copies, remote signals or barrier semaphores. Data moves between devices by JAX's collectives and lax.ppermute only.
A program may use at most 256 MiB of HBM per device.

v0:
```python
import jax
import jax.numpy as jnp
from jax import lax
from jax.sharding import PartitionSpec as P

DOMAINS = 4


def from_behind(block, axis, distance):
    devices = range(lax.axis_size(axis))
    route = [(i - distance, i) for i in devices if i - distance in devices]
    return lax.ppermute(block, axis, route)


def partner_2(value, axis, bit):
    mask = 2**bit
    pairs = [(source, source ^ mask) for source in range(lax.axis_size(axis))]
    return lax.ppermute(value, axis, pairs)


def rms_norm(values, gain):
    widened = values.astype(jnp.float32)
    scale_inv = lax.rsqrt(jnp.mean(widened * widened, axis=-1, keepdims=True) + 1e-05)
    return widened * scale_inv * gain


def record(stash, value, slot, valid):
    older = lax.dynamic_index_in_dim(stash, slot, 0, keepdims=False)
    return lax.dynamic_update_index_in_dim(stash, jnp.where(valid, value, older), slot, 0)


def squares_middle(blocks):
    return jnp.sum(jnp.square(blocks.astype(jnp.float32)), axis=(1, 2, 3))


def shards(layer_input_activations, cotangent, domain_ids, norm_gain, w_gate, w_up, w_down):
    segments = lax.axis_size("section")
    segment_idx = lax.axis_index("section")
    micro = layer_input_activations.shape[0]
    local_rows = layer_input_activations.shape[1]
    width = layer_input_activations.shape[2]
    tensor_size = lax.axis_size("tensor")
    tok_rows = local_rows * tensor_size
    gain = norm_gain[0]
    gate_up = jnp.concatenate([w_gate[0], w_up[0]], axis=1)
    down_proj = w_down[0]
    hidden_width = down_proj.shape[0]
    ticks = micro + segments - 1
    contract_last = (((1,), (1,)), ((), ()))
    x_stash = jnp.zeros((micro, local_rows, width), jnp.bfloat16)
    gate_up_memory = jnp.zeros((micro, tok_rows, 2 * hidden_width), jnp.float32)
    hidden_memory = jnp.zeros((micro, tok_rows, hidden_width), jnp.bfloat16)
    incoming = jnp.zeros((local_rows, width), jnp.bfloat16)
    for tick_index in range(ticks):
        slot = tick_index - segment_idx
        valid = (slot >= 0) & (slot < micro)
        slot = jnp.clip(slot, 0, micro - 1)
        current = jnp.where(
            segment_idx == 0, layer_input_activations[min(tick_index, micro - 1)], incoming
        )
        normed = rms_norm(current, gain).astype(jnp.bfloat16)
        gate_vals = jnp.dot(
            lax.all_gather(normed, "tensor", axis=0, tiled=True),
            gate_up,
            preferred_element_type=jnp.float32,
        )
        hidden = (jax.nn.silu(gate_vals[:, :hidden_width]) * gate_vals[:, hidden_width:]).astype(
            jnp.bfloat16
        )

        def down_terms(start, count, hidden=hidden):
            return jnp.dot(hidden, down_proj, preferred_element_type=jnp.float32)

        mixed = lax.psum_scatter(
            down_terms(jnp.int32(0), local_rows * lax.axis_size("tensor")),
            "tensor",
            scatter_dimension=0,
            tiled=True,
        )
        output = (current.astype(jnp.float32) + mixed).astype(jnp.bfloat16)
        x_stash = record(x_stash, current, slot, valid)
        gate_up_memory = record(gate_up_memory, gate_vals, slot, valid)
        hidden_memory = record(hidden_memory, hidden, slot, valid)
        if tick_index + 1 < ticks:
            incoming = from_behind(output, "section", 1)
    dy_stash = jnp.zeros((micro, tok_rows, width), jnp.bfloat16)
    arriving = jnp.zeros((local_rows, width), jnp.bfloat16)
    for tick_index in range(ticks):
        slot = tick_index - (segments - 1 - segment_idx)
        valid = (slot >= 0) & (slot < micro)
        slot = jnp.clip(slot, 0, micro - 1)
        upstream = jnp.where(
            segment_idx == segments - 1, cotangent[min(tick_index, micro - 1)], arriving
        )
        upstream_full = lax.all_gather(upstream, "tensor", axis=0, tiled=True)
        dy_stash = record(dy_stash, upstream_full, slot, valid)
        saved_gu = lax.dynamic_index_in_dim(gate_up_memory, slot, 0, keepdims=False)
        gate_part = saved_gu[:, :hidden_width]
        up_part = saved_gu[:, hidden_width:]
        d_hidden = lax.dot_general(
            upstream_full, down_proj, contract_last, preferred_element_type=jnp.float32
        )
        sig = jax.nn.sigmoid(gate_part)
        d_gate = d_hidden * up_part * (sig * (1.0 + gate_part * (1.0 - sig)))
        d_up = d_hidden * gate_part * sig
        d_both = jnp.concatenate([d_gate, d_up], axis=1).astype(jnp.bfloat16)

        def back_terms(start, count, d_both=d_both):
            return lax.dot_general(
                d_both, gate_up, contract_last, preferred_element_type=jnp.float32
            )

        d_normed = lax.psum_scatter(
            back_terms(jnp.int32(0), local_rows * lax.axis_size("tensor")),
            "tensor",
            scatter_dimension=0,
            tiled=True,
        )
        x_saved = lax.dynamic_index_in_dim(x_stash, slot, 0, keepdims=False)
        unused, pull = jax.vjp(lambda values: rms_norm(values, gain), x_saved.astype(jnp.float32))
        input_gradient = (upstream.astype(jnp.float32) + pull(d_normed)[0]).astype(jnp.bfloat16)
        if tick_index + 1 < ticks:
            arriving = from_behind(input_gradient, "section", -1)
    dp_size = lax.axis_size("dp")
    dp_bits = dp_size.bit_length() - 1
    piece_width = width // dp_size
    onehot = (domain_ids == jnp.arange(DOMAINS)[None, :]).astype(jnp.bfloat16)
    weighted = onehot[:, :, None, None] * hidden_memory[:, None, :, :]
    summed = jnp.einsum("merq,mrc->eqc", weighted, dy_stash, preferred_element_type=jnp.float32)
    blocks = summed.astype(jnp.bfloat16).reshape(DOMAINS, hidden_width, dp_size, piece_width)
    level_local = [squares_middle(blocks)]
    dp_index = lax.axis_index("dp")
    for bit in range(dp_bits):
        shape = blocks.shape
        paired = blocks.reshape(shape[0], shape[1], shape[2] // 2, 2, shape[3])
        upper = dp_index >> bit & 1
        kept = lax.dynamic_index_in_dim(paired, upper, 3, keepdims=False)
        sent = lax.dynamic_index_in_dim(paired, 1 - upper, 3, keepdims=False)
        partner = partner_2(sent, "dp", bit)
        blocks = (kept.astype(jnp.float32) + partner.astype(jnp.float32)).astype(jnp.bfloat16)
        level_local.append(squares_middle(blocks))
    result_grads = blocks.reshape(1, DOMAINS, hidden_width, piece_width)
    totals = [lax.psum(local_sum, ("section", "dp", "tensor")) for local_sum in level_local]
    entries = segments * hidden_width * tensor_size * width
    columns = [totals[level] / float((dp_size >> level) * entries) for level in range(dp_bits + 1)]
    return (result_grads, jnp.stack(columns, axis=1))


def solution(mesh):
    return jax.shard_map(
        shards,
        mesh=mesh,
        in_specs=(
            P(None, ("dp", "tensor"), None),
            P(None, ("dp", "tensor"), None),
            P(None, "dp"),
            P("section", None),
            P("section", None, "tensor"),
            P("section", None, "tensor"),
            P("section", "tensor", None),
        ),
        out_specs=(P("section", None, "tensor", "dp"), P()),
        check_vma=False,
    )
```

profile of v0, /device:TPU:0, one launch (start us, length us, event | category | flops | bytes accessed | tf_op | source)
XLA Modules:
  0.0 1124.0 jit_solution(2061266668389810875)
XLA Ops:
  9.0 15.1 %all_gather.30 = bf16[32,2048]{1,0:T(8,128)(2,1)S(1)} all-gather(bf16[8,2048]{1,0:T(8,128)(2,1)S(1)} %fusion.77), channel_id=1, replica_groups=mesh['section'=2,'dp'=4,'tensor'=4] {'tensor'}, dimensions={0}, use_global_device_ids=true | all-gather | bytes 163840 | tf_op jit(solution)/shard_map/all_gather | solution.py:63
  24.2 6.9 bitcast_dynamic-update-slice_fusion.4
  32.7 2.1 fusion.15
  37.3 18.7 %reduce-scatter.9.cloned.1.call-done = f32[8,2048]{1,0:T(8,128)} async-done(((f32[32,2048]{1,0:T(8,128)}), f32[8,2048]{1,0:T(8,128)}) %reduce-scatter.9.cloned.1.call-update) | async-done | bytes 65552 | tf_op jit(solution)/shard_map/reduce_scatter | solution.py:74
  59.4 13.5 %all_gather.31 = bf16[32,2048]{1,0:T(8,128)(2,1)S(1)} all-gather(bf16[8,2048]{1,0:T(8,128)(2,1)S(1)} %fusion.57), channel_id=1, replica_groups=mesh['section'=2,'dp'=4,'tensor'=4] {'tensor'}, dimensions={0}, use_global_device_ids=true | all-gather | bytes 163840 | tf_op jit(solution)/shard_map/all_gather | solution.py:63
  72.9 7.7 bitcast_dynamic-update-slice_fusion.3
  81.4 2.1 fusion.13
  85.1 2.0 constant_dynamic-slice_fusion.13
  87.1 14.5 %reduce-scatter.11.cloned.1.call-done = f32[8,2048]{1,0:T(8,128)} async-done(((f32[32,2048]{1,0:T(8,128)}), f32[8,2048]{1,0:T(8,128)}) %reduce-scatter.11.cloned.1.call-update) | async-done | bytes 65552 | tf_op jit(solution)/shard_map/reduce_scatter | solution.py:74
  104.8 13.5 %all_gather.32 = bf16[32,2048]{1,0:T(8,128)(2,1)S(1)} all-gather(bf16[8,2048]{1,0:T(8,128)(2,1)S(1)} %fusion.61), channel_id=1, replica_groups=mesh['section'=2,'dp'=4,'tensor'=4] {'tensor'}, dimensions={0}, use_global_device_ids=true | all-gather | bytes 163840 | tf_op jit(solution)/shard_map/all_gather | solution.py:63
  118.3 7.7 bitcast_dynamic-update-slice_fusion.2
  126.8 2.1 fusion.11
  130.5 2.0 constant_dynamic-slice_fusion.12
  132.5 14.5 %reduce-scatter.13.cloned.1.call-done = f32[8,2048]{1,0:T(8,128)} async-done(((f32[32,2048]{1,0:T(8,128)}), f32[8,2048]{1,0:T(8,128)}) %reduce-scatter.13.cloned.1.call-update) | async-done | bytes 65552 | tf_op jit(solution)/shard_map/reduce_scatter | solution.py:74
  150.2 13.5 %all_gather.33 = bf16[32,2048]{1,0:T(8,128)(2,1)S(1)} all-gather(bf16[8,2048]{1,0:T(8,128)(2,1)S(1)} %fusion.65), channel_id=1, replica_groups=mesh['section'=2,'dp'=4,'tensor'=4] {'tensor'}, dimensions={0}, use_global_device_ids=true | all-gather | bytes 163840 | tf_op jit(solution)/shard_map/all_gather | solution.py:63
  163.7 7.7 bitcast_dynamic-update-slice_fusion.1
  172.1 2.1 fusion.9
  175.7 13.8 %all-gather = bf16[1,32,2048]{2,1,0:T(8,128)(2,1)S(1)} all-gather(bf16[1,8,2048]{2,1,0:T(8,128)(2,1)} %slice_select_fusion), channel_id=2, replica_groups=mesh['section'=2,'dp'=4,'tensor'=4] {'tensor'}, dimensions={1}, use_global_device_ids=true | all-gather | bytes 163840 | tf_op jit(solution)/shard_map/all_gather | solution.py:95
  189.5 1.8 constant_dynamic-slice_fusion.11
  195.5 13.9 %all_gather.34 = bf16[32,2048]{1,0:T(8,128)(2,1)S(1)} all-gather(bf16[8,2048]{1,0:T(8,128)(2,1)S(1)} %fusion.54), channel_id=1, replica_groups=mesh['section'=2,'dp'=4,'tensor'=4] {'tensor'}, dimensions={0}, use_global_device_ids=true | all-gather | bytes 163840 | tf_op jit(solution)/shard_map/all_gather | solution.py:63
  209.4 7.8 bitcast_dynamic-update-slice_fusion
  217.2 2.6 dynamic-slice_bitcast_fusion
  219.8 2.3 fusion.29
  222.2 7.2 fusion.35
  229.5 18.2 %reduce-scatter.17.cloned.1.call-done = f32[8,2048]{1,0:T(8,128)} async-done(((f32[32,2048]{1,0:T(8,128)}), f32[8,2048]{1,0:T(8,128)}) %reduce-scatter.17.cloned.1.call-update) | async-done | bytes 65552 | tf_op jit(solution)/shard_map/reduce_scatter | solution.py:113
  252.8 13.4 %all_gather.36 = bf16[32,2048]{1,0:T(8,128)(2,1)S(1)} all-gather(bf16[8,2048]{1,0:T(8,128)(2,1)S(1)} %bitcast_select_fusion.20), channel_id=1, replica_groups=mesh['section'=2,'dp'=4,'tensor'=4] {'tensor'}, dimensions={0}, use_global_device_ids=true | all-gather | bytes 163840 | tf_op jit(solution)/shard_map/all_gather | solution.py:95
  266.2 5.4 fusion.27
  271.6 8.3 fusion.39
  281.0 17.0 %reduce-scatter.19.cloned.1.call-done = f32[8,2048]{1,0:T(8,128)} async-done(((f32[32,2048]{1,0:T(8,128)}), f32[8,2048]{1,0:T(8,128)}) %reduce-scatter.19.cloned.1.call-update) | async-done | bytes 65552 | tf_op jit(solution)/shard_map/reduce_scatter | solution.py:113
  303.1 13.4 %all_gather.37 = bf16[32,2048]{1,0:T(8,128)(2,1)S(1)} all-gather(bf16[8,2048]{1,0:T(8,128)(2,1)S(1)} %bitcast_select_fusion.15), channel_id=1, replica_groups=mesh['section'=2,'dp'=4,'tensor'=4] {'tensor'}, dimensions={0}, use_global_device_ids=true | all-gather | bytes 163840 | tf_op jit(solution)/shard_map/all_gather | solution.py:95
  316.5 5.4 fusion.25
  321.9 8.3 fusion.43
  330.3 17.8 %reduce-scatter.21.cloned.1.call-done = f32[8,2048]{1,0:T(8,128)} async-done(((f32[32,2048]{1,0:T(8,128)}), f32[8,2048]{1,0:T(8,128)}) %reduce-scatter.21.cloned.1.call-update) | async-done | bytes 65552 | tf_op jit(solution)/shard_map/reduce_scatter | solution.py:113
  353.1 13.6 %all_gather.38 = bf16[32,2048]{1,0:T(8,128)(2,1)S(1)} all-gather(bf16[8,2048]{1,0:T(8,128)(2,1)S(1)} %bitcast_select_fusion.14), channel_id=1, replica_groups=mesh['section'=2,'dp'=4,'tensor'=4] {'tensor'}, dimensions={0}, use_global_device_ids=true | all-gather | bytes 163840 | tf_op jit(solution)/shard_map/all_gather | solution.py:95
  366.8 5.4 fusion.23
  372.2 8.3 fusion.47
  380.5 18.0 %reduce-scatter.23.cloned.1.call-done = f32[8,2048]{1,0:T(8,128)} async-done(((f32[32,2048]{1,0:T(8,128)}), f32[8,2048]{1,0:T(8,128)}) %reduce-scatter.23.cloned.1.call-update) | async-done | bytes 65552 | tf_op jit(solution)/shard_map/reduce_scatter | solution.py:113
  403.6 13.4 %all_gather.39 = bf16[32,2048]{1,0:T(8,128)(2,1)S(1)} all-gather(bf16[8,2048]{1,0:T(8,128)(2,1)S(1)} %bitcast_select_fusion.13), channel_id=1, replica_groups=mesh['section'=2,'dp'=4,'tensor'=4] {'tensor'}, dimensions={0}, use_global_device_ids=true | all-gather | bytes 163840 | tf_op jit(solution)/shard_map/all_gather | solution.py:95
  417.0 14.4 %multiply_reduce_fusion = (f32[4]{0:T(128)S(1)}, bf16[4,1792,2048]{2,1,0:T(8,128)(2,1)}) fusion(bf16[4,32,2048]{2,1,0:T(8,128)(2,1)S(1)} %bitcast_dynamic-update-slice_fusion.5, bf16[4,32,1792]{2,1,0:T(8,128)(2,1)} %bitcast_dynamic-update-slice_fusion.10, bf16[4,4]{0,1:T(4,128)(2,1)S(1)} %fusion.87), kind=kOutput, calls=%fused_computation.1 | convolution fusion | flops 3817734144 | bytes 30343216 | tf_op jit(solution)/shard_map/merq,mrc->eqc/dot_general | solution.py:129
  431.4 47.7 %reshape_reshape.3 = bf16[4,1792,2,2,512]{4,3,2,1,0:T(2,128)(2,1)} reshape(bf16[4,1792,2048]{2,1,0:T(8,128)(2,1)} %get-tuple-element.65) | data formatting | bytes 58720256 | tf_op jit(solution)/shard_map/reshape;reshape | solution.py:135
  479.2 65.0 %constant_dynamic-slice_fusion.2 = (bf16[4,1792,2,1,512]{4,3,2,1,0:T(2,128)(2,1)}, bf16[4,1792,2,1,512]{4,3,2,1,0:T(2,128)(2,1)}) fusion(bf16[4,1792,2,2,512]{4,3,2,1,0:T(2,128)(2,1)} %reshape_reshape.3, s32[]{:T(128)S(6)} %select_n.307, s32[]{:T(128)S(6)} %select_n.308), kind=kLoop, calls=%fused_computation.196 | loop fusion | bytes 58720264 | tf_op jit(solution)/shard_map/jit(dynamic_index_in_dim)/dynamic_slice | solution.py:137
  544.2 19.2 %copy.19 = bf16[4,1792,2,1,512]{4,1,0,2,3:T(8,128)(2,1)} copy(bf16[4,1792,2,1,512]{4,3,2,1,0:T(2,128)(2,1)} %get-tuple-element.31) | data formatting | bytes 29360128 | tf_op jit(solution)/shard_map/jit(dynamic_index_in_dim)/dynamic_slice | solution.py:138
  564.9 313.3 %collective-permute-done.8 = bf16[4,1792,2,512]{3,1,0,2:T(8,128)(2,1)} collective-permute-done((bf16[4,1792,2,512]{3,1,0,2:T(8,128)(2,1)}, bf16[4,1792,2,512]{3,1,0,2:T(8,128)(2,1)}, u32[]{:S(2)}, u32[]{:S(2)}) %collective-permute-start.8) | collective-permute-done | bytes 14680096 | tf_op jit(solution)/shard_map/ppermute | solution.py:18
  878.1 24.7 %multiply_reduce_fusion.1 = (f32[4]{0:T(128)S(1)}, bf16[4,1792,2,512]{3,1,0,2:T(8,128)(2,1)}) fusion(bf16[4,1792,2,512]{3,1,0,2:T(8,128)(2,1)} %collective-permute-done.8, bf16[4,1792,2,1,512]{4,3,2,1,0:T(2,128)(2,1)} %get-tuple-element.30), kind=kLoop, calls=%fused_computation.4 | loop fusion | flops 51380220 | bytes 44040208 | tf_op jit(solution)/shard_map/reduce_sum | solution.py:33
  902.9 6.6 constant_dynamic-slice_fusion
  911.0 155.1 %collective-permute-done.9 = bf16[4,1792,1,512]{3,1,0,2:T(8,128)(2,1)} collective-permute-done((bf16[4,1792,1,512]{3,1,0,2:T(8,128)(2,1)}, bf16[4,1792,1,512]{3,1,0,2:T(8,128)(2,1)}, u32[]{:S(2)}, u32[]{:S(2)}) %collective-permute-start.9) | collective-permute-done | bytes 7340064 | tf_op jit(solution)/shard_map/ppermute | solution.py:18
  1066.0 11.6 %multiply_reduce_fusion.2 = (f32[4]{0:T(128)S(1)}, bf16[1,4,1792,512]{3,2,1,0:T(8,128)(2,1)}) fusion(bf16[4,1792,1,512]{3,1,0,2:T(8,128)(2,1)} %collective-permute-done.9, bf16[4,1792,2,512]{3,1,0,2:T(8,128)(2,1)} %get-tuple-element.13, s32[]{:T(128)S(6)} %select_n.309), kind=kLoop, calls=%fused_computation.8 | loop fusion | flops 25690108 | bytes 22020116 | tf_op jit(solution)/shard_map/reduce_sum | solution.py:33
  1077.6 38.4 %all-reduce = (f32[4]{0:T(128)S(1)}, f32[4]{0:T(128)S(1)}, f32[4]{0:T(128)S(1)}) all-reduce(f32[4]{0:T(128)S(1)} %get-tuple-element.32, f32[4]{0:T(128)S(1)} %get-tuple-element.12, f32[4]{0:T(128)S(1)} %get-tuple-element.64), channel_id=1, replica_groups=mesh['section'=2,'dp'=4,'tensor'=4] {'section','dp','tensor'}, use_global_device_ids=true, to_apply=%region_26.27 | all-reduce | flops 12 | bytes 96 | tf_op jit(solution)/shard_map/psum | solution.py:143
  (164 shorter events, 51.9 us)
Async XLA Ops:
  7.2 48.8 %reduce-scatter.9.cloned.1.call-start = ((), (), s32[]{:S(2)}) async-start(), calls=%async_computation.8 | async-start | bytes 327680 | tf_op jit(solution)/shard_map/reduce_scatter | solution.py:74
  24.0 8.7 slice-start
  24.2 8.5 slice-start.1
  31.1 6.2 copy-start
  31.1 3.8 copy-start.5
  31.1 28.2 %copy-start.1 = (f32[1,2048]{1,0:T(1,128)S(1)}, f32[1,2048]{1,0:T(1,128)}, u32[]{:S(2)}) copy-start(f32[1,2048]{1,0:T(1,128)} %param.10) | copy-start | bytes 24580
  34.9 66.7 %reduce-scatter.11.cloned.1.call-start = ((), (), s32[]{:S(2)}) async-start(), calls=%async_computation.9 | async-start | bytes 327680 | tf_op jit(solution)/shard_map/reduce_scatter | solution.py:74
  56.0 25.4 %slice-start.2 = ((s8[7340032]{0:T(1024)(128)(4,1)}), s8[3145728]{0:T(1024)(128)(4,1)S(1)}, s32[]{:S(2)}) async-start(s8[7340032]{0:T(1024)(128)(4,1)} %bitcast.232), calls=%async_computation.18 | async-start | bytes 6291456
  57.0 2.1 collective-permute-start
  72.9 7.7 copy-start.7
  72.9 8.4 slice-start.3
  83.5 63.5 %reduce-scatter.13.cloned.1.call-start = ((), (), s32[]{:S(2)}) async-start(), calls=%async_computation.10 | async-start | bytes 327680 | tf_op jit(solution)/shard_map/reduce_scatter | solution.py:74
  85.1 41.7 %slice-start.4 = ((s8[7340032]{0:T(1024)(128)(4,1)}), s8[3145728]{0:T(1024)(128)(4,1)S(1)}, s32[]{:S(2)}) async-start(s8[7340032]{0:T(1024)(128)(4,1)} %bitcast.234), calls=%async_computation.20 | async-start | bytes 6291456
  102.4 2.1 collective-permute-start.1
  118.3 7.7 copy-start.8
  118.3 8.4 slice-start.5
  128.9 63.3 %reduce-scatter.15.cloned.1.call-start = ((), (), s32[]{:S(2)}) async-start(), calls=%async_computation.11 | async-start | bytes 327680 | tf_op jit(solution)/shard_map/reduce_scatter | solution.py:74
  130.5 41.6 %slice-start.6 = ((s8[7340032]{0:T(1024)(128)(4,1)}), s8[3145728]{0:T(1024)(128)(4,1)S(1)}, s32[]{:S(2)}) async-start(s8[7340032]{0:T(1024)(128)(4,1)} %bitcast.236), calls=%async_computation.22 | async-start | bytes 6291456
  147.8 2.1 collective-permute-start.2
  150.0 21.4 %copy-start.6 = (bf16[8,2048]{1,0:T(8,128)(2,1)}, bf16[8,2048]{1,0:T(8,128)(2,1)S(1)}, u32[]{:S(2)}) copy-start(bf16[8,2048]{1,0:T(8,128)(2,1)S(1)} %get-tuple-element.17) | copy-start | bytes 98308
  163.7 7.7 copy-start.9
  163.7 8.4 slice-start.7
  174.3 73.5 %reduce-scatter.17.cloned.1.call-start = ((), (), s32[]{:S(2)}) async-start(), calls=%async_computation.12 | async-start | bytes 327680 | tf_op jit(solution)/shard_map/reduce_scatter | solution.py:113
  175.7 44.2 %slice-start.8 = ((s8[7340032]{0:T(1024)(128)(4,1)}), s8[3145728]{0:T(1024)(128)(4,1)S(1)}, s32[]{:S(2)}) async-start(s8[7340032]{0:T(1024)(128)(4,1)} %bitcast.238), calls=%async_computation.24 | async-start | bytes 6291456
  193.1 2.1 collective-permute-start.3
  195.4 26.7 %slice-start.10 = ((s8[7340032]{0:T(1024)(128)(4,1)}), s8[4194304]{0:T(1024)(128)(4,1)S(1)}, s32[]{:S(2)}) async-start(s8[7340032]{0:T(1024)(128)(4,1)} %bitcast.261), calls=%async_computation.26 | async-start | bytes 8388608
  209.4 10.4 slice-start.9
  209.4 12.8 %slice-start.11 = ((s8[7340032]{0:T(1024)(128)(4,1)}), s8[3145728]{0:T(1024)(128)(4,1)S(1)}, s32[]{:S(2)}) async-start(s8[7340032]{0:T(1024)(128)(4,1)} %bitcast.261), calls=%async_computation.27 | async-start | bytes 6291456
  222.2 26.6 %copy-start.11 = (bf16[4,8,2048]{2,1,0:T(8,128)(2,1)S(1)}, bf16[4,8,2048]{2,1,0:T(8,128)(2,1)}, u32[]{:S(2)}) copy-start(bf16[4,8,2048]{2,1,0:T(8,128)(2,1)} %param.8) | copy-start | bytes 393220
  222.2 44.0 %copy-start.4 = (f32[32,3584]{1,0:T(8,128)S(1)}, f32[32,3584]{1,0:T(8,128)}, u32[]{:S(2)}) copy-start(f32[32,3584]{1,0:T(8,128)} %get-tuple-element.36) | copy-start | bytes 1376260
  229.4 68.6 %reduce-scatter.19.cloned.1.call-start = ((), (), s32[]{:S(2)}) async-start(), calls=%async_computation.13 | async-start | bytes 327680 | tf_op jit(solution)/shard_map/reduce_scatter | solution.py:113
  249.7 3.1 collective-permute-start.4
  271.6 8.5 copy-start.12
  271.6 29.7 %copy-start.10 = (f32[32,3584]{1,0:T(8,128)S(1)}, f32[32,3584]{1,0:T(8,128)}, u32[]{:S(2)}) copy-start(f32[32,3584]{1,0:T(8,128)} %get-tuple-element.63) | copy-start | bytes 1376260
  271.6 44.8 %copy-start.3 = (f32[32,3584]{1,0:T(8,128)S(1)}, f32[32,3584]{1,0:T(8,128)}, u32[]{:S(2)}) copy-start(f32[32,3584]{1,0:T(8,128)} %get-tuple-element.35) | copy-start | bytes 1376260
  280.0 68.1 %reduce-scatter.21.cloned.1.call-start = ((), (), s32[]{:S(2)}) async-start(), calls=%async_computation.14 | async-start | bytes 327680 | tf_op jit(solution)/shard_map/reduce_scatter | solution.py:113
  300.0 3.1 collective-permute-start.5
  321.9 44.9 %copy-start.2 = (f32[32,3584]{1,0:T(8,128)S(1)}, f32[32,3584]{1,0:T(8,128)}, u32[]{:S(2)}) copy-start(f32[32,3584]{1,0:T(8,128)} %get-tuple-element.34) | copy-start | bytes 1376260
  330.2 68.3 %reduce-scatter.23.cloned.1.call-start = ((), (), s32[]{:S(2)}) async-start(), calls=%async_computation.15 | async-start | bytes 327680 | tf_op jit(solution)/shard_map/reduce_scatter | solution.py:113
  350.0 3.1 collective-permute-start.6
  400.5 3.1 collective-permute-start.7
  563.4 314.7 %collective-permute-start.8 = (bf16[4,1792,2,512]{3,1,0,2:T(8,128)(2,1)}, bf16[4,1792,2,512]{3,1,0,2:T(8,128)(2,1)}, u32[]{:S(2)}, u32[]{:S(2)}) collective-permute-start(bf16[4,1792,2,512]{3,1,0,2:T(8,128)(2,1)} %bitcast.229), channel_id=1, source_target_pairs={{0,4},{4,0},{8,12},{12,8},{1,5},{5,1},{9,13},{13,9},{2,6},{6,2},{1... | collective-permute-start | bytes 44040200 | tf_op jit(solution)/shard_map/ppermute | solution.py:18
  909.5 156.5 %collective-permute-start.9 = (bf16[4,1792,1,512]{3,1,0,2:T(8,128)(2,1)}, bf16[4,1792,1,512]{3,1,0,2:T(8,128)(2,1)}, u32[]{:S(2)}, u32[]{:S(2)}) collective-permute-start(bf16[4,1792,1,512]{3,1,0,2:T(8,128)(2,1)} %constant_dynamic-slice_fusion), channel_id=1, source_target_pairs={{0,8},{4,12},{8,0},{12,4},{1,9},{5,13},{9,1},{13,5},{2,10},{6,14},... | collective-permute-start | bytes 22020104 | tf_op jit(solution)/shard_map/ppermute | solution.py:18
Sparse Core Ops, SparseCore 0:
  35.0 20.9 reduce-scatter.8
  83.6 17.9 reduce-scatter.10
  129.0 17.9 reduce-scatter.12
  174.4 17.7 reduce-scatter.14
  229.6 18.0 reduce-scatter.16
  280.1 17.8 reduce-scatter.18
  330.3 17.7 reduce-scatter.20
  380.6 17.9 reduce-scatter.22
where the time goes:
time: 1130 us; the launch traced here: 1120 us
  waiting for transfers between devices  598 us (53%)
  blocking collectives  175 us (15%)
  local copies, waits for them, and re-layouts  155 us (14%)
  matrix products  111 us (10%)
  other arithmetic  55.6 us (5%)
  between operations  15.1 us (1%)
  starting transfers between devices  13.6 us (1%)
    ppermute x2, waiting for transfers between devices, partner_2(): return lax.ppermute(value, axis, pairs)  468 us
    reduce_scatter x4, waiting for transfers between devices, shards(): lax.psum_scatter(back_terms(jnp.int32(0), local_rows * lax.axis_size('ten...  71 us
    all_gather x5, blocking collectives, shards(): lax.all_gather(normed, 'tensor', axis=0, tiled=True)  69.5 us
    all_gather x5, blocking collectives, shards(): upstream_full = lax.all_gather(upstream, 'tensor', axis=0, tiled=True)  67.6 us
    dynamic_slice x1, local copies, waits for them, and re-layouts, shards(): kept = lax.dynamic_index_in_dim(paired, upper, 3, keepdims=False)  65 us
    reduce_scatter x4, waiting for transfers between devices, shards(): lax.psum_scatter(down_terms(jnp.int32(0), local_rows * lax.axis_size('ten...  48.6 us
    another operation x1, local copies, waits for them, and re-layouts, shards(): paired = blocks.reshape(shape[0], shape[1], shape[2] // 2, 2, shape[3])  47.7 us
    psum x1, blocking collectives, shards(): lax.psum(local_sum, ('section', 'dp', 'tensor'))  38.4 us
  transfers between devices with their start and end apart: 18, of which 18 were waited for; matrix products, arithmetic and copies ran while one was open for 1% of the time, Pallas kernels for 0%

commit v1 on v0

v1 whole, which is shorter than its diff:
```python
import functools

import jax
import jax.numpy as jnp
from jax import lax
from jax.experimental import pallas as pl
from jax.experimental.pallas import tpu as pltpu
from jax.sharding import PartitionSpec as P

DOMAINS = 4
EPS = 1e-05
CONTRACT_LAST = (((1,), (1,)), ((), ()))
CONTRACT_FIRST = (((0,), (0,)), ((), ()))


def swap(block, axis, offset):
    size = lax.axis_size(axis)
    return lax.ppermute(block, axis, [(i, i ^ offset) for i in range(size)])


def across(block, source, offset):
    size = lax.axis_size("tensor")
    route = [
        (source * size + i, (1 - source) * size + (i ^ offset)) for i in range(size)
    ]
    return lax.ppermute(block, ("section", "tensor"), route)


def gather_relative(block, axis):
    return [block] + [swap(block, axis, k) for k in range(1, lax.axis_size(axis))]


def gradient_kernel(ids_ref, hidden_ref, y_ref, out_ref, masked):
    piece = y_ref.shape[1]

    @pl.when(pl.program_id(0) == 0)
    def _():
        for e in range(DOMAINS):
            keep = ids_ref[...] == e
            masked[:, e * piece : (e + 1) * piece] = jnp.where(
                keep, y_ref[...].astype(jnp.float32), 0.0
            ).astype(jnp.bfloat16)

    product = lax.dot_general(
        hidden_ref[...], masked[...], CONTRACT_FIRST, preferred_element_type=jnp.float32
    )
    for e in range(DOMAINS):
        out_ref[e] = product[:, e * piece : (e + 1) * piece].astype(jnp.bfloat16)


def domain_gradients(row_ids, hidden, y):
    rows, units = hidden.shape
    piece = y.shape[1]
    tile = 256
    return pl.pallas_call(
        gradient_kernel,
        grid=(units // tile,),
        in_specs=[
            pl.BlockSpec((rows, 1), lambda i: (0, 0)),
            pl.BlockSpec((rows, tile), lambda i: (0, i)),
            pl.BlockSpec((rows, piece), lambda i: (0, 0)),
        ],
        out_specs=pl.BlockSpec((DOMAINS, tile, piece), lambda i: (0, i, 0)),
        out_shape=jax.ShapeDtypeStruct((DOMAINS, units, piece), jnp.bfloat16),
        scratch_shapes=[pltpu.VMEM((rows, DOMAINS * piece), jnp.bfloat16)],
        compiler_params=pltpu.CompilerParams(vmem_limit_bytes=32 * 2**20),
        cost_estimate=pl.CostEstimate(
            flops=2 * rows * units * DOMAINS * piece,
            bytes_accessed=2 * (rows * units + rows * piece + DOMAINS * units * piece),
            transcendentals=0,
        ),
    )(row_ids, hidden, y)


def shards(layer_input_activations, cotangent, domain_ids, norm_gain, w_gate, w_up, w_down):
    segment = lax.axis_index("section")
    dp_index = lax.axis_index("dp")
    segments = lax.axis_size("section")
    tensor_size = lax.axis_size("tensor")
    dp_size = lax.axis_size("dp")
    assert segments == 2
    micro, local_rows, width = layer_input_activations.shape
    gain = norm_gain[0][None, :]
    gate_w, up_w, down_w = w_gate[0], w_up[0], w_down[0]
    units = down_w.shape[0]
    block = micro * local_rows
    tok_rows = block * tensor_size
    first = segment == 0

    def reorder(value, offset):
        parts = value.reshape(tensor_size, block, width)
        return jnp.concatenate([parts[k ^ offset] for k in range(tensor_size)], axis=0)

    own_rows = jnp.where(first, layer_input_activations, cotangent).reshape(block, width)
    rows_in = jnp.concatenate(gather_relative(own_rows, "tensor"), axis=0)
    ids_all = gather_relative(domain_ids, "dp")
    rows_other = swap(rows_in, "section", 1)

    def layer_parts(rows):
        widened = rows.astype(jnp.float32)
        scale = lax.rsqrt(jnp.mean(widened * widened, axis=-1, keepdims=True) + EPS)
        normed = (widened * scale * gain).astype(jnp.bfloat16)
        gate = jnp.dot(normed, gate_w, preferred_element_type=jnp.float32)
        up = jnp.dot(normed, up_w, preferred_element_type=jnp.float32)
        return widened, scale, gate, up

    _, _, gate0, up0 = layer_parts(rows_in)
    hidden0 = (jax.nn.silu(gate0) * up0).astype(jnp.bfloat16)
    mixed = jnp.dot(hidden0, down_w, preferred_element_type=jnp.float32).astype(jnp.bfloat16)
    cot_rows, mixed = lax.optimization_barrier((rows_in, mixed))
    d_hidden = lax.dot_general(cot_rows, down_w, CONTRACT_LAST, preferred_element_type=jnp.float32)

    total = rows_other.astype(jnp.float32)
    for k in range(tensor_size):
        total = total + reorder(across(mixed, 0, k), k).astype(jnp.float32)
    x1 = total.astype(jnp.bfloat16)

    widened, scale, gate, up = layer_parts(x1)
    sig = jax.nn.sigmoid(gate)
    hidden1 = (gate * sig * up).astype(jnp.bfloat16)
    hidden = jnp.where(first, hidden0, hidden1)
    hidden_all = jnp.concatenate(gather_relative(hidden, "dp"), axis=0)
    d_gate = (d_hidden * up * (sig * (1.0 + gate * (1.0 - sig)))).astype(jnp.bfloat16)
    d_up = (d_hidden * gate * sig).astype(jnp.bfloat16)
    d_normed = lax.dot_general(d_gate, gate_w, CONTRACT_LAST, preferred_element_type=jnp.float32)
    d_normed = d_normed + lax.dot_general(
        d_up, up_w, CONTRACT_LAST, preferred_element_type=jnp.float32
    )
    pulled = d_normed * gain
    along = jnp.sum(pulled * widened, axis=-1, keepdims=True) / width
    term = (pulled * scale - widened * (scale * scale * scale * along)).astype(jnp.bfloat16)

    total = rows_other.astype(jnp.float32)
    for k in range(tensor_size):
        total = total + reorder(across(term, 1, k), k).astype(jnp.float32)
    dy = jnp.where(first, total.astype(jnp.bfloat16), rows_in)

    piece = width // dp_size
    columns = []
    for k in range(dp_size):
        part = lax.dynamic_slice_in_dim(dy, (dp_index ^ k) * piece, piece, axis=1)
        columns.append(part if k == 0 else swap(part, "dp", k))
    y = jnp.concatenate(columns, axis=0)

    one_row_block = [
        jnp.broadcast_to(ids[None, :, :], (tensor_size, micro, local_rows)).reshape(tok_rows, 1)
        for ids in ids_all
    ]
    row_ids = jnp.concatenate(one_row_block, axis=0)
    grads = domain_gradients(row_ids, hidden_all, y)

    gram_hidden = lax.dot_general(
        hidden_all, hidden_all, CONTRACT_LAST, preferred_element_type=jnp.float32
    )
    gram_y = lax.dot_general(y, y, CONTRACT_LAST, preferred_element_type=jnp.float32)
    pairs = jnp.where(row_ids == row_ids.T, gram_hidden * gram_y, 0.0)
    replica = jnp.arange(tok_rows * dp_size) // tok_rows
    onehot = (row_ids == jnp.arange(DOMAINS)[None, :]).astype(jnp.float32)
    levels = dp_size.bit_length()
    sums = []
    for level in range(levels):
        group = replica >> level
        of_row = jnp.sum(jnp.where(group[:, None] == group[None, :], pairs, 0.0), axis=1)
        sums.append(jnp.sum(onehot * of_row[:, None], axis=0))
    norms = jnp.stack(sums, axis=1)
    for axis in ("tensor", "dp", "section"):
        for bit in range(lax.axis_size(axis).bit_length() - 1):
            norms = norms + swap(norms, axis, 2**bit)
    entries = segments * units * tensor_size * width
    counts = [float((dp_size >> level) * entries) for level in range(levels)]
    return grads[None], norms / jnp.array(counts, jnp.float32)[None, :]


def solution(mesh):
    return jax.shard_map(
        shards,
        mesh=mesh,
        in_specs=(
            P(None, ("dp", "tensor"), None),
            P(None, ("dp", "tensor"), None),
            P(None, "dp"),
            P("section", None),
            P("section", None, "tensor"),
            P("section", None, "tensor"),
            P("section", "tensor", None),
        ),
        out_specs=(P("section", None, "tensor", "dp"), P()),
        check_vma=False,
    )
```

time: 1130 us -> 132 us (0.12)
  waiting for transfers between devices: 598 us -> 49.4 us
  blocking collectives: 175 us -> 0 us
  local copies, waits for them, and re-layouts: 155 us -> 6.52 us
  matrix products: 111 us -> 24.5 us
  other arithmetic: 55.6 us -> 3.88 us
  starting transfers between devices: 13.6 us -> 38.3 us
  between operations: 15.1 us -> 1.14 us
    ppermute x10 -> x26, waiting for transfers between devices: 478 us -> 49.4 us  [the longest x8 28.2 us: across(): return lax.ppermute(block, ('section', 'tensor'), route)]
    all_gather x10 -> x0, blocking collectives: 137 us -> none  [the longest x5 69.5 us: shards(): lax.all_gather(normed, 'tensor', axis=0, tiled=True)]
    reduce_scatter x8 -> x0, waiting for transfers between devices: 120 us -> none  [the longest x4 71 us: shards(): lax.psum_scatter(back_terms(jnp.int32(0), local_rows * lax.axis_size('ten...]
    dynamic_slice x18 -> x1, local copies, waits for them, and re-layouts: 96.5 us -> 0.05 us  [shards(): part = lax.dynamic_slice_in_dim(dy, (dp_index ^ k) * piece, piece, axis=1)]
    dot_general x18 -> x10, matrix products: 111 us -> 24.5 us  [the longest x1 6.23 us: shards(): lax.dot_general(cot_rows, down_w, CONTRACT_LAST, preferred_element_type=j...]
    another operation x1 -> x0, local copies, waits for them, and re-layouts: 47.7 us -> none  [shards(): paired = blocks.reshape(shape[0], shape[1], shape[2] // 2, 2, shape[3])]
    reduce_sum x11 -> x3, other arithmetic: 41.7 us -> 0.88 us  [the longest x2 0.73 us: layer_parts(): scale = lax.rsqrt(jnp.mean(widened * widened, axis=-1, keepdims=True) + EPS)]
    psum x1 -> x0, blocking collectives: 38.4 us -> none  [shards(): lax.psum(local_sum, ('section', 'dp', 'tensor'))]
  transfers between devices with their start and end apart: 18 -> 26, of which waited for: 18 -> 13; matrix products, arithmetic and copies ran while one was open for 1% -> 21% of each run, Pallas kernels for 0% -> 6%
where the time goes in v1:
time: 132 us; the launch traced here: 131 us
  waiting for transfers between devices  49.4 us (37%)
  starting transfers between devices  38.3 us (29%)
  matrix products  24.5 us (19%)
  Pallas kernels  7.39 us (6%)
  local copies, waits for them, and re-layouts  6.52 us (5%)
  other arithmetic  3.88 us (3%)
    ppermute x8, waiting for transfers between devices, across(): return lax.ppermute(block, ('section', 'tensor'), route)  28.2 us
    ppermute x18, starting transfers between devices, swap(): return lax.ppermute(block, axis, [(i, i ^ offset) for i in range(size)])  21.2 us
    ppermute x18, waiting for transfers between devices, swap(): return lax.ppermute(block, axis, [(i, i ^ offset) for i in range(size)])  21.2 us
    ppermute x8, starting transfers between devices, across(): return lax.ppermute(block, ('section', 'tensor'), route)  17.1 us
    pallas_call x1, Pallas kernels, domain_gradients(): pl.pallas_call(gradient_kernel, grid=(units // tile,), in_specs=[pl.Block...  7.39 us
    dot_general x1, matrix products, shards(): lax.dot_general(cot_rows, down_w, CONTRACT_LAST, preferred_element_type=j...  6.23 us
    dot_general x2, matrix products, layer_parts(): gate = jnp.dot(normed, gate_w, preferred_element_type=jnp.float32)  5.66 us
    unnamed x34, local copies, waits for them, and re-layouts  4.34 us
  transfers between devices with their start and end apart: 26, of which 13 were waited for; matrix products, arithmetic and copies ran while one was open for 21% of the time, Pallas kernels for 6%

profile of v1, /device:TPU:0, one launch (start us, length us, event | category | flops | bytes accessed | tf_op | source)
XLA Modules:
  0.0 131.1 jit_solution(8251011836941882382)
XLA Ops:
  0.6 0.9 select_bitcast_fusion
  1.6 5.1 %collective-permute-start.5 = (bf16[32,2048]{1,0:T(8,128)(2,1)S(1)}, bf16[32,2048]{1,0:T(8,128)(2,1)S(1)}, u32[]{:S(2)}, u32[]{:S(2)}) collective-permute-start(bf16[32,2048]{1,0:T(8,128)(2,1)S(1)} %select_bitcast_fusion), channel_id=1, source_target_pairs={{0,3},{1,2},{2,1},{3,0},{4,7},{5,6},{6,5},{7,4},{8,11},{9,10},{10,... | collective-permute-start | bytes 393224 | tf_op jit(solution)/shard_map/ppermute | solution.py:18
  7.3 1.6 %collective-permute-start = (s32[4,1]{0,1:T(1,128)}, s32[4,1]{0,1:T(1,128)S(1)}, u32[]{:S(2)}, u32[]{:S(2)}) collective-permute-start(s32[4,1]{0,1:T(1,128)} %param.10), channel_id=1, source_target_pairs={{0,4},{4,0},{8,12},{12,8},{1,5},{5,1},{9,13},{13,9},{2,6},{6,2},{1... | collective-permute-start | bytes 56 | tf_op jit(solution)/shard_map/ppermute | solution.py:18
  9.0 1.5 %collective-permute-start.2 = (s32[4,1]{0,1:T(1,128)}, s32[4,1]{0,1:T(1,128)S(1)}, u32[]{:S(2)}, u32[]{:S(2)}) collective-permute-start(s32[4,1]{0,1:T(1,128)} %param.10), channel_id=1, source_target_pairs={{0,12},{4,8},{8,4},{12,0},{1,13},{5,9},{9,5},{13,1},{2,14},{6,10},... | collective-permute-start | bytes 56 | tf_op jit(solution)/shard_map/ppermute | solution.py:18
  10.5 0.7 collective-permute-done.5
  11.1 6.6 %collective-permute-done.4 = bf16[32,2048]{1,0:T(8,128)(2,1)S(1)} collective-permute-done((bf16[32,2048]{1,0:T(8,128)(2,1)S(1)}, bf16[32,2048]{1,0:T(8,128)(2,1)S(1)}, u32[]{:S(2)}, u32[]{:S(2)}) %collective-permute-start.4) | collective-permute-done | bytes 131104 | tf_op jit(solution)/shard_map/ppermute | solution.py:18
  18.0 4.5 %fusion.14 = f32[128,1792]{1,0:T(8,128)S(1)} fusion(bf16[1,2048,1792]{2,1,0:T(8,128)(2,1)} %param.12, bf16[128,2048]{1,0:T(8,128)(2,1)S(1)} %get-tuple-element.5, f32[2048]{0:T(1024)} %bitcast.51, f32[128]{0:T(128)S(1)} %add_rsqrt_fusion.1), kind=kOutput, calls=%fused_computation.14 | convolution fusion | flops 940572672 | bytes 8790528 | tf_op jit(solution)/shard_map/dot_general | solution.py:103
  22.5 0.8 copy-done.8
  23.4 1.4 %fusion.25 = bf16[128,1792]{1,0:T(8,128)(2,1)S(1)} fusion(bf16[1,2048,1792]{2,1,0:T(8,128)(2,1)S(1)} %copy-done.8, f32[128,1792]{1,0:T(8,128)S(1)} %fusion.14, bf16[128,2048]{1,0:T(8,128)(2,1)S(1)} %get-tuple-element.5, f32[2048]{0:T(1024)S(1)} %bitcast.52, f32[128]{0:T(128)S(1)} %add_rsqrt_fusion.1), kind=kOutput, calls=%fused_computation.19 | convolution fusion | flops 941948928 | bytes 9249280 | tf_op jit(solution)/shard_map/dot_general | solution.py:104
  24.7 1.0 slice-done.3
  25.7 1.9 %fusion.28 = bf16[128,2048]{1,0:T(8,128)(2,1)} fusion(bf16[128,1792]{1,0:T(8,128)(2,1)S(1)} %fusion.25, bf16[1,1792,2048]{2,1,0:T(8,128)(2,1)S(1)} %bitcast.50), kind=kOutput, calls=%fused_computation.20 | convolution fusion | flops 939786240 | bytes 8323072 | tf_op jit(solution)/shard_map/dot_general | solution.py:109
  27.6 3.7 %collective-permute-start.10 = (bf16[128,2048]{1,0:T(8,128)(2,1)}, bf16[128,2048]{1,0:T(8,128)(2,1)}, u32[]{:S(2)}, u32[]{:S(2)}) collective-permute-start(bf16[128,2048]{1,0:T(8,128)(2,1)} %fusion.28), channel_id=1, source_target_pairs={{0,19},{1,18},{2,17},{3,16},{4,23},{5,22},{6,21},{7,20},{8,27},{9,... | collective-permute-start | bytes 1572872 | tf_op jit(solution)/shard_map/ppermute | solution.py:26
  31.7 1.6 %collective-permute-start.8 = (bf16[128,2048]{1,0:T(8,128)(2,1)}, bf16[128,2048]{1,0:T(8,128)(2,1)S(1)}, u32[]{:S(2)}, u32[]{:S(2)}) collective-permute-start(bf16[128,2048]{1,0:T(8,128)(2,1)} %fusion.28), channel_id=1, source_target_pairs={{0,17},{1,16},{2,19},{3,18},{4,21},{5,20},{6,23},{7,22},{8,25},{9,... | collective-permute-start | bytes 1572872 | tf_op jit(solution)/shard_map/ppermute | solution.py:26
  33.3 6.2 %fusion = f32[128,1792]{1,0:T(8,128)S(1)} fusion(bf16[128,2048]{1,0:T(8,128)(2,1)} %copy-done, bf16[1,1792,2048]{2,1,0:T(8,128)(2,1)} %param.14), kind=kOutput, calls=%fused_computation | convolution fusion | flops 939524096 | bytes 8781824 | tf_op jit(solution)/shard_map/dot_general | solution.py:111
  39.5 5.1 %collective-permute-start.9 = (bf16[128,2048]{1,0:T(8,128)(2,1)}, bf16[128,2048]{1,0:T(8,128)(2,1)S(1)}, u32[]{:S(2)}, u32[]{:S(2)}) collective-permute-start(bf16[128,2048]{1,0:T(8,128)(2,1)} %fusion.28), channel_id=1, source_target_pairs={{0,18},{1,19},{2,16},{3,17},{4,22},{5,23},{6,20},{7,21},{8,26},{9,... | collective-permute-start | bytes 1572872 | tf_op jit(solution)/shard_map/ppermute | solution.py:26
  44.6 1.1 fusion.74
  45.8 1.5 %collective-permute-start.7 = (bf16[128,2048]{1,0:T(8,128)(2,1)}, bf16[128,2048]{1,0:T(8,128)(2,1)S(1)}, u32[]{:S(2)}, u32[]{:S(2)}) collective-permute-start(bf16[128,2048]{1,0:T(8,128)(2,1)} %fusion.28), channel_id=1, source_target_pairs={{0,16},{1,17},{2,18},{3,19},{4,20},{5,21},{6,22},{7,23},{8,24},{9,... | collective-permute-start | bytes 1572872 | tf_op jit(solution)/shard_map/ppermute | solution.py:26
  47.3 4.3 %collective-permute-done.9 = bf16[128,2048]{1,0:T(8,128)(2,1)S(1)} collective-permute-done((bf16[128,2048]{1,0:T(8,128)(2,1)}, bf16[128,2048]{1,0:T(8,128)(2,1)S(1)}, u32[]{:S(2)}, u32[]{:S(2)}) %collective-permute-start.9) | collective-permute-done | bytes 524320 | tf_op jit(solution)/shard_map/ppermute | solution.py:26
  51.6 1.5 %collective-permute-start.1 = (s32[4,1]{0,1:T(1,128)S(1)}, s32[4,1]{0,1:T(1,128)S(1)}, u32[]{:S(2)}, u32[]{:S(2)}) collective-permute-start(s32[4,1]{0,1:T(1,128)S(1)} %copy-done.6), channel_id=1, source_target_pairs={{0,8},{4,12},{8,0},{12,4},{1,9},{5,13},{9,1},{13,5},{2,10},{6,14},... | collective-permute-start | bytes 56 | tf_op jit(solution)/shard_map/ppermute | solution.py:18
  53.9 1.2 fusion.12
  55.8 1.0 slice-done.5
  56.8 2.2 %fusion.52 = (bf16[128,1792]{1,0:T(8,128)(2,1)}, f32[128,1792]{1,0:T(8,128)S(1)}) fusion(bf16[128,1792]{1,0:T(8,128)(2,1)S(1)} %copy-done.3, f32[128,1792]{1,0:T(8,128)S(1)} %fusion.12, pred[]{:T(512)S(6)} %eq.34, bf16[1,2048,1792]{2,1,0:T(8,128)(2,1)S(1)} %bitcast.72, bf16[128,2048]{1,0:T(8,128)(2,1)S(1)} %get-tuple-element.21, f32[128]{0:T(128)S(1)} %add_rsqrt_fusion, ...), kind=kOutput, calls=%fused_computation.61 | convolution fusion | flops 942178304 | bytes 10625537 | tf_op jit(solution)/shard_map/dot_general | solution.py:104
  59.0 2.5 %fusion.4 = f32[128,2048]{1,0:T(8,128)S(1)} fusion(bf16[1,2048,1792]{2,1,0:T(8,128)(2,1)S(1)} %bitcast.72, f32[128,1792]{1,0:T(8,128)S(1)} %fusion, f32[128,1792]{1,0:T(8,128)S(1)} %fusion.12), kind=kOutput, calls=%fused_computation.4 | convolution fusion | flops 940900352 | bytes 10223616 | tf_op jit(solution)/shard_map/dot_general | solution.py:126
  61.6 2.7 %fusion.46 = (f32[128]{0:T(128)S(1)}, f32[128,2048]{1,0:T(8,128)S(1)}) fusion(bf16[128,2048]{1,0:T(8,128)(2,1)S(1)} %get-tuple-element.21, f32[2048]{0:T(1024)S(1)} %bitcast.55, f32[128,2048]{1,0:T(8,128)S(1)} %fusion.4, bf16[1,2048,1792]{2,1,0:T(8,128)(2,1)S(1)} %bitcast.48, f32[128,1792]{1,0:T(8,128)S(1)} %fusion.12, f32[128,1792]{1,0:T(8,128)S(1)} %fusion, ...), kind=kOutput, calls=%fused_computation.46 | convolution fusion | flops 943128448 | bytes 12722688 | tf_op jit(solution)/shard_map/dot_general | solution.py:125
  64.5 1.3 collective-permute-start.17
  66.4 1.3 collective-permute-start.15
  67.8 1.5 %collective-permute-start.13 = (bf16[128,1792]{1,0:T(8,128)(2,1)}, bf16[128,1792]{1,0:T(8,128)(2,1)S(1)}, u32[]{:S(2)}, u32[]{:S(2)}) collective-permute-start(bf16[128,1792]{1,0:T(8,128)(2,1)} %get-tuple-element.48), channel_id=1, source_target_pairs={{0,12},{4,8},{8,4},{12,0},{1,13},{5,9},{9,5},{13,1},{2,14},{6,10},... | collective-permute-start | bytes 1376264 | tf_op jit(solution)/shard_map/ppermute | solution.py:18
  69.3 1.5 %collective-permute-start.12 = (bf16[128,1792]{1,0:T(8,128)(2,1)}, bf16[128,1792]{1,0:T(8,128)(2,1)S(1)}, u32[]{:S(2)}, u32[]{:S(2)}) collective-permute-start(bf16[128,1792]{1,0:T(8,128)(2,1)} %get-tuple-element.48), channel_id=1, source_target_pairs={{0,8},{4,12},{8,0},{12,4},{1,9},{5,13},{9,1},{13,5},{2,10},{6,14},... | collective-permute-start | bytes 1376264 | tf_op jit(solution)/shard_map/ppermute | solution.py:18
  71.4 8.2 %collective-permute-done.17 = bf16[128,2048]{1,0:T(8,128)(2,1)S(1)} collective-permute-done((bf16[128,2048]{1,0:T(8,128)(2,1)S(1)}, bf16[128,2048]{1,0:T(8,128)(2,1)S(1)}, u32[]{:S(2)}, u32[]{:S(2)}) %collective-permute-start.17) | collective-permute-done | bytes 524320 | tf_op jit(solution)/shard_map/ppermute | solution.py:26
  79.6 1.3 collective-permute-start.16
  80.9 4.2 %collective-permute-done.15 = bf16[128,2048]{1,0:T(8,128)(2,1)S(1)} collective-permute-done((bf16[128,2048]{1,0:T(8,128)(2,1)S(1)}, bf16[128,2048]{1,0:T(8,128)(2,1)S(1)}, u32[]{:S(2)}, u32[]{:S(2)}) %collective-permute-start.15) | collective-permute-done | bytes 524320 | tf_op jit(solution)/shard_map/ppermute | solution.py:26
  85.1 1.3 collective-permute-start.14
  86.5 11.5 %collective-permute-done.16 = bf16[128,2048]{1,0:T(8,128)(2,1)S(1)} collective-permute-done((bf16[128,2048]{1,0:T(8,128)(2,1)S(1)}, bf16[128,2048]{1,0:T(8,128)(2,1)S(1)}, u32[]{:S(2)}, u32[]{:S(2)}) %collective-permute-start.16) | collective-permute-done | bytes 524320 | tf_op jit(solution)/shard_map/ppermute | solution.py:26
  98.0 1.6 %fusion.49 = bf16[128,2048]{1,0:T(8,128)(2,1)S(1)} fusion(bf16[128,2048]{1,0:T(8,128)(2,1)} %copy-done, bf16[128,2048]{1,0:T(8,128)(2,1)S(1)} %collective-permute-done.14, bf16[128,2048]{1,0:T(8,128)(2,1)} %copy-done.1, bf16[32,2048]{1,0:T(8,128)(2,1)S(1)} %get-tuple-element.35, bf16[32,2048]{1,0:T(8,128)(2,1)S(1)} %get-tuple-element.36, ...), kind=kLoop, calls=%fused_computation.56 | loop fusion | flops 7340032 | bytes 3670017 | tf_op jit(solution)/shard_map/jit(_where)/select_n | solution.py:136
  99.6 1.5 %collective-permute-start.20 = (bf16[128,512]{1,0:T(8,128)(2,1)S(1)}, bf16[128,512]{1,0:T(8,128)(2,1)S(1)}, u32[]{:S(2)}, u32[]{:S(2)}) collective-permute-start(bf16[128,512]{1,0:T(8,128)(2,1)S(1)} %get-tuple-element.25), channel_id=1, source_target_pairs={{0,12},{4,8},{8,4},{12,0},{1,13},{5,9},{9,5},{13,1},{2,14},{6,10},... | collective-permute-start | bytes 393224 | tf_op jit(solution)/shard_map/ppermute | solution.py:18
  101.1 1.5 %collective-permute-start.19 = (bf16[128,512]{1,0:T(8,128)(2,1)S(1)}, bf16[128,512]{1,0:T(8,128)(2,1)S(1)}, u32[]{:S(2)}, u32[]{:S(2)}) collective-permute-start(bf16[128,512]{1,0:T(8,128)(2,1)S(1)} %get-tuple-element.26), channel_id=1, source_target_pairs={{0,8},{4,12},{8,0},{12,4},{1,9},{5,13},{9,1},{13,5},{2,10},{6,14},... | collective-permute-start | bytes 393224 | tf_op jit(solution)/shard_map/ppermute | solution.py:18
  103.3 2.3 %collective-permute-done.20 = bf16[128,512]{1,0:T(8,128)(2,1)S(1)} collective-permute-done((bf16[128,512]{1,0:T(8,128)(2,1)S(1)}, bf16[128,512]{1,0:T(8,128)(2,1)S(1)}, u32[]{:S(2)}, u32[]{:S(2)}) %collective-permute-start.20) | collective-permute-done | bytes 131104 | tf_op jit(solution)/shard_map/ppermute | solution.py:18
  105.7 1.3 collective-permute-done.19
  107.0 0.7 collective-permute-done.18
  108.1 1.5 %select_reduce_fusion.2 = (f32[512]{0:T(512)S(1)}, f32[512]{0:T(512)S(1)}, f32[512]{0:T(512)S(1)}) fusion(s32[512]{0:T(512)S(1)} %fusion.61, s32[512]{0:T(512)S(1)} %get-tuple-element.52, s32[512]{0:T(512)S(1)} %get-tuple-element.53, f32[512,512]{0,1:T(8,128)S(1)} %fusion.67, bf16[128,1792]{1,0:T(8,128)(2,1)S(1)} %collective-permute-done.13, ...), kind=kOutput, calls=%fused_computation.51 | convolution fusion | flops 950008320 | bytes 2897920 | tf_op jit(solution)/shard_map/dot_general | solution.py:152
  110.0 7.4 %shard_map.95 = bf16[4,1792,512]{2,1,0:T(8,128)(2,1)} custom-call(s32[512,1]{1,0:T(8,128)S(1)} %copy.22.ids_ref, bf16[512,1792]{1,0:T(8,128)(2,1)S(1)} %pad_maximum_fusion.hidden_ref, bf16[512,512]{1,0:T(8,128)(2,1)S(1)} %pad_maximum_fusion.2.y_ref), custom_call_target="tpu_custom_call" | custom-call | flops 3758096384 | bytes 9699328 | tf_op jit(solution)/shard_map/pallas_call | solution.py:55
  117.4 2.0 %collective-permute-start.22 = (f32[4,3]{0,1:T(4,128)S(1)}, f32[4,3]{0,1:T(4,128)S(1)}, u32[]{:S(2)}, u32[]{:S(2)}) collective-permute-start(f32[4,3]{0,1:T(4,128)S(1)} %fusion.66), channel_id=1, source_target_pairs={{0,2},{1,3},{2,0},{3,1},{4,6},{5,7},{6,4},{7,5},{8,10},{9,11},{10,... | collective-permute-start | bytes 152 | tf_op jit(solution)/shard_map/ppermute | solution.py:18
  119.4 2.6 %collective-permute-done.22 = f32[4,3]{0,1:T(4,128)S(1)} collective-permute-done((f32[4,3]{0,1:T(4,128)S(1)}, f32[4,3]{0,1:T(4,128)S(1)}, u32[]{:S(2)}, u32[]{:S(2)}) %collective-permute-start.22) | collective-permute-done | bytes 80 | tf_op jit(solution)/shard_map/ppermute | solution.py:18
  122.0 0.9 collective-permute-start.23
  122.8 2.8 %collective-permute-done.23 = f32[4,3]{0,1:T(4,128)S(1)} collective-permute-done((f32[4,3]{0,1:T(4,128)S(1)}, f32[4,3]{0,1:T(4,128)S(1)}, u32[]{:S(2)}, u32[]{:S(2)}) %collective-permute-start.23) | collective-permute-done | bytes 80 | tf_op jit(solution)/shard_map/ppermute | solution.py:18
  126.2 3.0 %collective-permute-done.24 = f32[4,3]{0,1:T(4,128)S(1)} collective-permute-done((f32[4,3]{0,1:T(4,128)S(1)}, f32[4,3]{0,1:T(4,128)S(1)}, u32[]{:S(2)}, u32[]{:S(2)}) %collective-permute-start.24) | collective-permute-done | bytes 80 | tf_op jit(solution)/shard_map/ppermute | solution.py:18
  129.2 1.2 collective-permute-done.25
  130.5 0.7 copy.23
  (88 shorter events, 6.4 us)
Async XLA Ops:
  1.6 9.5 %collective-permute-start.5 = (bf16[32,2048]{1,0:T(8,128)(2,1)S(1)}, bf16[32,2048]{1,0:T(8,128)(2,1)S(1)}, u32[]{:S(2)}, u32[]{:S(2)}) collective-permute-start(bf16[32,2048]{1,0:T(8,128)(2,1)S(1)} %select_bitcast_fusion), channel_id=1, source_target_pairs={{0,3},{1,2},{2,1},{3,0},{4,7},{5,6},{6,5},{7,4},{8,11},{9,10},{10,... | collective-permute-start | bytes 393224 | tf_op jit(solution)/shard_map/ppermute | solution.py:18
  6.7 11.1 %collective-permute-start.4 = (bf16[32,2048]{1,0:T(8,128)(2,1)S(1)}, bf16[32,2048]{1,0:T(8,128)(2,1)S(1)}, u32[]{:S(2)}, u32[]{:S(2)}) collective-permute-start(bf16[32,2048]{1,0:T(8,128)(2,1)S(1)} %select_bitcast_fusion), channel_id=1, source_target_pairs={{0,2},{1,3},{2,0},{3,1},{4,6},{5,7},{6,4},{7,5},{8,10},{9,11},{10,... | collective-permute-start | bytes 393224 | tf_op jit(solution)/shard_map/ppermute | solution.py:18
  6.7 11.1 %collective-permute-start.3 = (bf16[32,2048]{1,0:T(8,128)(2,1)S(1)}, bf16[32,2048]{1,0:T(8,128)(2,1)S(1)}, u32[]{:S(2)}, u32[]{:S(2)}) collective-permute-start(bf16[32,2048]{1,0:T(8,128)(2,1)S(1)} %select_bitcast_fusion), channel_id=1, source_target_pairs={{0,1},{1,0},{2,3},{3,2},{4,5},{5,4},{6,7},{7,6},{8,9},{9,8},{10,11... | collective-permute-start | bytes 393224 | tf_op jit(solution)/shard_map/ppermute | solution.py:18
  7.3 58.5 %collective-permute-start = (s32[4,1]{0,1:T(1,128)}, s32[4,1]{0,1:T(1,128)S(1)}, u32[]{:S(2)}, u32[]{:S(2)}) collective-permute-start(s32[4,1]{0,1:T(1,128)} %param.10), channel_id=1, source_target_pairs={{0,4},{4,0},{8,12},{12,8},{1,5},{5,1},{9,13},{13,9},{2,6},{6,2},{1... | collective-permute-start | bytes 56 | tf_op jit(solution)/shard_map/ppermute | solution.py:18
  9.0 57.0 %collective-permute-start.2 = (s32[4,1]{0,1:T(1,128)}, s32[4,1]{0,1:T(1,128)S(1)}, u32[]{:S(2)}, u32[]{:S(2)}) collective-permute-start(s32[4,1]{0,1:T(1,128)} %param.10), channel_id=1, source_target_pairs={{0,12},{4,8},{8,4},{12,0},{1,13},{5,9},{9,5},{13,1},{2,14},{6,10},... | collective-permute-start | bytes 56 | tf_op jit(solution)/shard_map/ppermute | solution.py:18
  18.0 4.5 %copy-start = (bf16[128,2048]{1,0:T(8,128)(2,1)}, bf16[128,2048]{1,0:T(8,128)(2,1)S(1)}, u32[]{:S(2)}) copy-start(bf16[128,2048]{1,0:T(8,128)(2,1)S(1)} %get-tuple-element.5) | copy-start | bytes 1572868
  18.0 4.5 %copy-start.5 = (f32[1,2048]{1,0:T(1,128)S(1)}, f32[1,2048]{1,0:T(1,128)}, u32[]{:S(2)}) copy-start(f32[1,2048]{1,0:T(1,128)} %param.11) | copy-start | bytes 24580
  18.0 5.4 %copy-start.8 = (bf16[1,2048,1792]{2,1,0:T(8,128)(2,1)S(1)}, bf16[1,2048,1792]{2,1,0:T(8,128)(2,1)}, u32[]{:S(2)}) copy-start(bf16[1,2048,1792]{2,1,0:T(8,128)(2,1)} %param.13) | copy-start | bytes 22020100
  18.0 6.7 %slice-start.2 = ((s8[7340032]{0:T(1024)(128)(4,1)}), s8[4194304]{0:T(1024)(128)(4,1)S(1)}, s32[]{:S(2)}) async-start(s8[7340032]{0:T(1024)(128)(4,1)} %bitcast.49), calls=%async_computation.2 | async-start | bytes 8388608
  23.4 2.3 %slice-start.3 = ((s8[7340032]{0:T(1024)(128)(4,1)}), s8[3145728]{0:T(1024)(128)(4,1)S(1)}, s32[]{:S(2)}) async-start(s8[7340032]{0:T(1024)(128)(4,1)} %bitcast.49), calls=%async_computation.3 | async-start | bytes 6291456
  25.7 1.9 %copy-start.2 = (bf16[128,1792]{1,0:T(8,128)(2,1)}, bf16[128,1792]{1,0:T(8,128)(2,1)S(1)}, u32[]{:S(2)}) copy-start(bf16[128,1792]{1,0:T(8,128)(2,1)S(1)} %fusion.25) | copy-start | bytes 1376260
  25.7 5.7 %copy-start.6 = (s32[4,1]{0,1:T(1,128)S(1)}, s32[4,1]{0,1:T(1,128)}, u32[]{:S(2)}) copy-start(s32[4,1]{0,1:T(1,128)} %param.10) | copy-start | bytes 52
  27.6 11.9 %collective-permute-start.10 = (bf16[128,2048]{1,0:T(8,128)(2,1)}, bf16[128,2048]{1,0:T(8,128)(2,1)}, u32[]{:S(2)}, u32[]{:S(2)}) collective-permute-start(bf16[128,2048]{1,0:T(8,128)(2,1)} %fusion.28), channel_id=1, source_target_pairs={{0,19},{1,18},{2,17},{3,16},{4,23},{5,22},{6,21},{7,20},{8,27},{9,... | collective-permute-start | bytes 1572872 | tf_op jit(solution)/shard_map/ppermute | solution.py:26
  31.6 22.3 %slice-start = ((s8[7340032]{0:T(1024)(128)(4,1)}), s8[3145728]{0:T(1024)(128)(4,1)S(1)}, s32[]{:S(2)}) async-start(s8[7340032]{0:T(1024)(128)(4,1)} %bitcast.47), calls=%async_computation | async-start | bytes 6291456
  31.6 22.3 %slice-start.1 = ((s8[7340032]{0:T(1024)(128)(4,1)}), s8[4194304]{0:T(1024)(128)(4,1)S(1)}, s32[]{:S(2)}) async-start(s8[7340032]{0:T(1024)(128)(4,1)} %bitcast.47), calls=%async_computation.1 | async-start | bytes 8388608
  31.6 21.6 %collective-permute-start.6 = (bf16[128,2048]{1,0:T(8,128)(2,1)}, bf16[128,2048]{1,0:T(8,128)(2,1)S(1)}, u32[]{:S(2)}, u32[]{:S(2)}) collective-permute-start(bf16[128,2048]{1,0:T(8,128)(2,1)} %copy-done), channel_id=1, source_target_pairs={{0,16},{16,0},{1,17},{17,1},{2,18},{18,2},{3,19},{19,3},{4,20},{20... | collective-permute-start | bytes 1572872 | tf_op jit(solution)/shard_map/ppermute | solution.py:18
  31.7 14.1 %collective-permute-start.8 = (bf16[128,2048]{1,0:T(8,128)(2,1)}, bf16[128,2048]{1,0:T(8,128)(2,1)S(1)}, u32[]{:S(2)}, u32[]{:S(2)}) collective-permute-start(bf16[128,2048]{1,0:T(8,128)(2,1)} %fusion.28), channel_id=1, source_target_pairs={{0,17},{1,16},{2,19},{3,18},{4,21},{5,20},{6,23},{7,22},{8,25},{9,... | collective-permute-start | bytes 1572872 | tf_op jit(solution)/shard_map/ppermute | solution.py:26
  39.5 12.1 %collective-permute-start.9 = (bf16[128,2048]{1,0:T(8,128)(2,1)}, bf16[128,2048]{1,0:T(8,128)(2,1)S(1)}, u32[]{:S(2)}, u32[]{:S(2)}) collective-permute-start(bf16[128,2048]{1,0:T(8,128)(2,1)} %fusion.28), channel_id=1, source_target_pairs={{0,18},{1,19},{2,16},{3,17},{4,22},{5,23},{6,20},{7,21},{8,26},{9,... | collective-permute-start | bytes 1572872 | tf_op jit(solution)/shard_map/ppermute | solution.py:26
  45.8 7.5 %collective-permute-start.7 = (bf16[128,2048]{1,0:T(8,128)(2,1)}, bf16[128,2048]{1,0:T(8,128)(2,1)S(1)}, u32[]{:S(2)}, u32[]{:S(2)}) collective-permute-start(bf16[128,2048]{1,0:T(8,128)(2,1)} %fusion.28), channel_id=1, source_target_pairs={{0,16},{1,17},{2,18},{3,19},{4,20},{5,21},{6,22},{7,23},{8,24},{9,... | collective-permute-start | bytes 1572872 | tf_op jit(solution)/shard_map/ppermute | solution.py:26
  51.6 14.5 %collective-permute-start.1 = (s32[4,1]{0,1:T(1,128)S(1)}, s32[4,1]{0,1:T(1,128)S(1)}, u32[]{:S(2)}, u32[]{:S(2)}) collective-permute-start(s32[4,1]{0,1:T(1,128)S(1)} %copy-done.6), channel_id=1, source_target_pairs={{0,8},{4,12},{8,0},{12,4},{1,9},{5,13},{9,1},{13,5},{2,10},{6,14},... | collective-permute-start | bytes 56 | tf_op jit(solution)/shard_map/ppermute | solution.py:18
  53.2 1.8 %copy-start.1 = (bf16[128,2048]{1,0:T(8,128)(2,1)}, bf16[128,2048]{1,0:T(8,128)(2,1)S(1)}, u32[]{:S(2)}) copy-start(bf16[128,2048]{1,0:T(8,128)(2,1)S(1)} %collective-permute-done.6) | copy-start | bytes 1572868
  53.2 2.4 %slice-start.4 = ((s8[7340032]{0:T(1024)(128)(4,1)}), s8[4194304]{0:T(1024)(128)(4,1)S(1)}, s32[]{:S(2)}) async-start(s8[7340032]{0:T(1024)(128)(4,1)} %bitcast.71), calls=%async_computation.4 | async-start | bytes 8388608
  53.8 2.0 %copy-start.3 = (bf16[128,1792]{1,0:T(8,128)(2,1)S(1)}, bf16[128,1792]{1,0:T(8,128)(2,1)}, u32[]{:S(2)}) copy-start(bf16[128,1792]{1,0:T(8,128)(2,1)} %copy-done.2) | copy-start | bytes 1376260
  53.9 3.0 %slice-start.5 = ((s8[7340032]{0:T(1024)(128)(4,1)}), s8[3145728]{0:T(1024)(128)(4,1)S(1)}, s32[]{:S(2)}) async-start(s8[7340032]{0:T(1024)(128)(4,1)} %bitcast.71), calls=%async_computation.5 | async-start | bytes 6291456
  64.2 39.0 %copy-start.4 = (bf16[128,1792]{1,0:T(8,128)(2,1)S(1)}, bf16[128,1792]{1,0:T(8,128)(2,1)}, u32[]{:S(2)}) copy-start(bf16[128,1792]{1,0:T(8,128)(2,1)} %get-tuple-element.48) | copy-start | bytes 1376260
  64.5 15.1 %collective-permute-start.17 = (bf16[128,2048]{1,0:T(8,128)(2,1)S(1)}, bf16[128,2048]{1,0:T(8,128)(2,1)S(1)}, u32[]{:S(2)}, u32[]{:S(2)}) collective-permute-start(bf16[128,2048]{1,0:T(8,128)(2,1)S(1)} %fusion.48), channel_id=1, source_target_pairs={{16,3},{17,2},{18,1},{19,0},{20,7},{21,6},{22,5},{23,4},{24,11},{2... | collective-permute-start | bytes 1572872 | tf_op jit(solution)/shard_map/ppermute | solution.py:26
  66.4 18.8 %collective-permute-start.15 = (bf16[128,2048]{1,0:T(8,128)(2,1)S(1)}, bf16[128,2048]{1,0:T(8,128)(2,1)S(1)}, u32[]{:S(2)}, u32[]{:S(2)}) collective-permute-start(bf16[128,2048]{1,0:T(8,128)(2,1)S(1)} %fusion.48), channel_id=1, source_target_pairs={{16,1},{17,0},{18,3},{19,2},{20,5},{21,4},{22,7},{23,6},{24,9},{25... | collective-permute-start | bytes 1572872 | tf_op jit(solution)/shard_map/ppermute | solution.py:26
  67.8 34.8 %collective-permute-start.13 = (bf16[128,1792]{1,0:T(8,128)(2,1)}, bf16[128,1792]{1,0:T(8,128)(2,1)S(1)}, u32[]{:S(2)}, u32[]{:S(2)}) collective-permute-start(bf16[128,1792]{1,0:T(8,128)(2,1)} %get-tuple-element.48), channel_id=1, source_target_pairs={{0,12},{4,8},{8,4},{12,0},{1,13},{5,9},{9,5},{13,1},{2,14},{6,10},... | collective-permute-start | bytes 1376264 | tf_op jit(solution)/shard_map/ppermute | solution.py:18
  69.3 33.9 %collective-permute-start.12 = (bf16[128,1792]{1,0:T(8,128)(2,1)}, bf16[128,1792]{1,0:T(8,128)(2,1)S(1)}, u32[]{:S(2)}, u32[]{:S(2)}) collective-permute-start(bf16[128,1792]{1,0:T(8,128)(2,1)} %get-tuple-element.48), channel_id=1, source_target_pairs={{0,8},{4,12},{8,0},{12,4},{1,9},{5,13},{9,1},{13,5},{2,10},{6,14},... | collective-permute-start | bytes 1376264 | tf_op jit(solution)/shard_map/ppermute | solution.py:18
  70.8 32.4 %collective-permute-start.11 = (bf16[128,1792]{1,0:T(8,128)(2,1)}, bf16[128,1792]{1,0:T(8,128)(2,1)S(1)}, u32[]{:S(2)}, u32[]{:S(2)}) collective-permute-start(bf16[128,1792]{1,0:T(8,128)(2,1)} %get-tuple-element.48), channel_id=1, source_target_pairs={{0,4},{4,0},{8,12},{12,8},{1,5},{5,1},{9,13},{13,9},{2,6},{6,2},{1... | collective-permute-start | bytes 1376264 | tf_op jit(solution)/shard_map/ppermute | solution.py:18
  79.6 18.4 %collective-permute-start.16 = (bf16[128,2048]{1,0:T(8,128)(2,1)S(1)}, bf16[128,2048]{1,0:T(8,128)(2,1)S(1)}, u32[]{:S(2)}, u32[]{:S(2)}) collective-permute-start(bf16[128,2048]{1,0:T(8,128)(2,1)S(1)} %fusion.48), channel_id=1, source_target_pairs={{16,2},{17,3},{18,0},{19,1},{20,6},{21,7},{22,4},{23,5},{24,10},{2... | collective-permute-start | bytes 1572872 | tf_op jit(solution)/shard_map/ppermute | solution.py:26
  85.1 12.9 %collective-permute-start.14 = (bf16[128,2048]{1,0:T(8,128)(2,1)S(1)}, bf16[128,2048]{1,0:T(8,128)(2,1)S(1)}, u32[]{:S(2)}, u32[]{:S(2)}) collective-permute-start(bf16[128,2048]{1,0:T(8,128)(2,1)S(1)} %fusion.48), channel_id=1, source_target_pairs={{16,0},{17,1},{18,2},{19,3},{20,4},{21,5},{22,6},{23,7},{24,8},{25... | collective-permute-start | bytes 1572872 | tf_op jit(solution)/shard_map/ppermute | solution.py:26
  99.6 6.0 %collective-permute-start.20 = (bf16[128,512]{1,0:T(8,128)(2,1)S(1)}, bf16[128,512]{1,0:T(8,128)(2,1)S(1)}, u32[]{:S(2)}, u32[]{:S(2)}) collective-permute-start(bf16[128,512]{1,0:T(8,128)(2,1)S(1)} %get-tuple-element.25), channel_id=1, source_target_pairs={{0,12},{4,8},{8,4},{12,0},{1,13},{5,9},{9,5},{13,1},{2,14},{6,10},... | collective-permute-start | bytes 393224 | tf_op jit(solution)/shard_map/ppermute | solution.py:18
  101.1 5.8 %collective-permute-start.19 = (bf16[128,512]{1,0:T(8,128)(2,1)S(1)}, bf16[128,512]{1,0:T(8,128)(2,1)S(1)}, u32[]{:S(2)}, u32[]{:S(2)}) collective-permute-start(bf16[128,512]{1,0:T(8,128)(2,1)S(1)} %get-tuple-element.26), channel_id=1, source_target_pairs={{0,8},{4,12},{8,0},{12,4},{1,9},{5,13},{9,1},{13,5},{2,10},{6,14},... | collective-permute-start | bytes 393224 | tf_op jit(solution)/shard_map/ppermute | solution.py:18
  102.7 5.0 %collective-permute-start.18 = (bf16[128,512]{1,0:T(8,128)(2,1)S(1)}, bf16[128,512]{1,0:T(8,128)(2,1)S(1)}, u32[]{:S(2)}, u32[]{:S(2)}) collective-permute-start(bf16[128,512]{1,0:T(8,128)(2,1)S(1)} %get-tuple-element.27), channel_id=1, source_target_pairs={{0,4},{4,0},{8,12},{12,8},{1,5},{5,1},{9,13},{13,9},{2,6},{6,2},{1... | collective-permute-start | bytes 393224 | tf_op jit(solution)/shard_map/ppermute | solution.py:18
  109.7 20.7 %copy-start.7 = (f32[3]{0:T(128)S(1)}, f32[3]{0:T(128)}, u32[]{:S(2)}) copy-start(f32[3]{0:T(128)} %constant.78) | copy-start | bytes 40
  109.7 7.7 %collective-permute-start.21 = (f32[4,3]{0,1:T(4,128)S(1)}, f32[4,3]{0,1:T(4,128)S(1)}, u32[]{:S(2)}, u32[]{:S(2)}) collective-permute-start(f32[4,3]{0,1:T(4,128)S(1)} %pad_maximum_fusion.3), channel_id=1, source_target_pairs={{0,1},{1,0},{2,3},{3,2},{4,5},{5,4},{6,7},{7,6},{8,9},{9,8},{10,11... | collective-permute-start | bytes 152 | tf_op jit(solution)/shard_map/ppermute | solution.py:18
  117.4 4.5 %collective-permute-start.22 = (f32[4,3]{0,1:T(4,128)S(1)}, f32[4,3]{0,1:T(4,128)S(1)}, u32[]{:S(2)}, u32[]{:S(2)}) collective-permute-start(f32[4,3]{0,1:T(4,128)S(1)} %fusion.66), channel_id=1, source_target_pairs={{0,2},{1,3},{2,0},{3,1},{4,6},{5,7},{6,4},{7,5},{8,10},{9,11},{10,... | collective-permute-start | bytes 152 | tf_op jit(solution)/shard_map/ppermute | solution.py:18
  122.0 3.7 %collective-permute-start.23 = (f32[4,3]{0,1:T(4,128)S(1)}, f32[4,3]{0,1:T(4,128)S(1)}, u32[]{:S(2)}, u32[]{:S(2)}) collective-permute-start(f32[4,3]{0,1:T(4,128)S(1)} %fusion.77), channel_id=1, source_target_pairs={{0,4},{4,0},{8,12},{12,8},{1,5},{5,1},{9,13},{13,9},{2,6},{6,2},{1... | collective-permute-start | bytes 152 | tf_op jit(solution)/shard_map/ppermute | solution.py:18
  125.6 3.6 %collective-permute-start.24 = (f32[4,3]{0,1:T(4,128)S(1)}, f32[4,3]{0,1:T(4,128)S(1)}, u32[]{:S(2)}, u32[]{:S(2)}) collective-permute-start(f32[4,3]{0,1:T(4,128)S(1)} %add.124), channel_id=1, source_target_pairs={{0,8},{4,12},{8,0},{12,4},{1,9},{5,13},{9,1},{13,5},{2,10},{6,14},... | collective-permute-start | bytes 152 | tf_op jit(solution)/shard_map/ppermute | solution.py:18
  129.2 1.2 collective-permute-start.25

commit v2 on v1

v2 whole, which is shorter than its diff:
```python
import jax
import jax.numpy as jnp
from jax import lax
from jax.experimental import pallas as pl
from jax.experimental.pallas import tpu as pltpu
from jax.sharding import PartitionSpec as P

DOMAINS = 4
TILE = 256
EPS = 1e-05
CONTRACT_LAST = (((1,), (1,)), ((), ()))
CONTRACT_FIRST = (((0,), (0,)), ((), ()))


def swap(block, axis, offset):
    size = lax.axis_size(axis)
    return lax.ppermute(block, axis, [(i, i ^ offset) for i in range(size)])


def swap_in(block, section, axis, offset):
    size = lax.axis_size(axis)
    route = [(section * size + i, section * size + (i ^ offset)) for i in range(size)]
    return lax.ppermute(block, ("section", axis), route)


def across(block, source, offset):
    size = lax.axis_size("tensor")
    route = [
        (source * size + i, (1 - source) * size + (i ^ offset)) for i in range(size)
    ]
    return lax.ppermute(block, ("section", "tensor"), route)


def bits(axis):
    return lax.axis_size(axis).bit_length() - 1


def gather_rows(rows, section=None):
    size = lax.axis_size("tensor")
    if section is None:
        others = [swap(rows, "tensor", k) for k in range(1, size)]
    else:
        others = [swap_in(rows, section, "tensor", k) for k in range(1, size)]
    return jnp.concatenate([rows] + others, axis=0)


def scatter_sum(start, terms, source, block):
    total = start.astype(jnp.float32)
    for k in range(lax.axis_size("tensor")):
        arrived = across(terms[k * block : (k + 1) * block], source, k)
        total = total + arrived.astype(jnp.float32)
    return total.astype(jnp.bfloat16)


def load_kernel(*refs):
    count = (len(refs) - 1) // 2
    copies = [
        pltpu.make_async_copy(refs[i].at[0], refs[count + i], refs[-1].at[i])
        for i in range(count)
    ]
    for copy in copies:
        copy.start()
    for copy in copies:
        copy.wait()


def load_weights(*weights):
    total = sum(w.size * 2 for w in weights)
    return pl.pallas_call(
        load_kernel,
        in_specs=[pl.BlockSpec(memory_space=pltpu.HBM)] * len(weights),
        out_specs=[pl.BlockSpec(memory_space=pltpu.VMEM)] * len(weights),
        out_shape=[pltpu.VMEM(w.shape[1:], w.dtype) for w in weights],
        scratch_shapes=[pltpu.SemaphoreType.DMA((len(weights),))],
        compiler_params=pltpu.CompilerParams(vmem_limit_bytes=total + 2**20),
        cost_estimate=pl.CostEstimate(flops=0, bytes_accessed=total, transcendentals=0),
    )(*weights)


def gradient_kernel(ids_ref, hidden_ref, y_ref, *rest):
    out_ref, masked = rest[-2:]
    piece = y_ref.shape[1]

    @pl.when(pl.program_id(0) == 0)
    def _():
        for e in range(DOMAINS):
            keep = ids_ref[...] == e
            masked[:, e * piece : (e + 1) * piece] = jnp.where(
                keep, y_ref[...].astype(jnp.float32), 0.0
            ).astype(jnp.bfloat16)

    product = lax.dot_general(
        hidden_ref[...], masked[...], CONTRACT_FIRST, preferred_element_type=jnp.float32
    )
    for e in range(DOMAINS):
        out_ref[e] = product[:, e * piece : (e + 1) * piece].astype(jnp.bfloat16)


def domain_gradients(row_ids, hidden, y, begin, count, grads=None):
    rows, units = hidden.shape
    piece = y.shape[1]
    in_specs = [
        pl.BlockSpec((rows, 1), lambda i: (0, 0)),
        pl.BlockSpec((rows, TILE), lambda i: (0, begin + i)),
        pl.BlockSpec((rows, piece), lambda i: (0, 0)),
    ]
    operands = [row_ids, hidden, y]
    if grads is not None:
        in_specs.append(pl.BlockSpec(memory_space=pl.ANY))
        operands.append(grads)
    return pl.pallas_call(
        gradient_kernel,
        grid=(count,),
        in_specs=in_specs,
        out_specs=pl.BlockSpec((DOMAINS, TILE, piece), lambda i: (0, begin + i, 0)),
        out_shape=jax.ShapeDtypeStruct((DOMAINS, units, piece), jnp.bfloat16),
        scratch_shapes=[pltpu.VMEM((rows, DOMAINS * piece), jnp.bfloat16)],
        input_output_aliases={} if grads is None else {3: 0},
        compiler_params=pltpu.CompilerParams(vmem_limit_bytes=24 * 2**20),
        cost_estimate=pl.CostEstimate(
            flops=2 * rows * count * TILE * DOMAINS * piece,
            bytes_accessed=2 * count * TILE * (rows + DOMAINS * piece),
            transcendentals=0,
        ),
    )(*operands)


def shards(layer_input_activations, cotangent, domain_ids, norm_gain, w_gate, w_up, w_down):
    segment = lax.axis_index("section")
    dp_index = lax.axis_index("dp")
    segments = lax.axis_size("section")
    tensor_size = lax.axis_size("tensor")
    dp_size = lax.axis_size("dp")
    assert segments == 2
    micro, local_rows, width = layer_input_activations.shape
    gain = norm_gain[0][None, :]
    gate_w, up_w, down_w = load_weights(w_gate, w_up, w_down)
    units = down_w.shape[0]
    block = micro * local_rows
    tok_rows = block * tensor_size
    first = segment == 0

    x_own = layer_input_activations.reshape(block, width)
    cot_own = cotangent.reshape(block, width)
    rows_in = gather_rows(jnp.where(first, x_own, cot_own))

    def layer_parts(rows):
        widened = rows.astype(jnp.float32)
        scale = lax.rsqrt(jnp.mean(widened * widened, axis=-1, keepdims=True) + EPS)
        normed = (widened * scale * gain).astype(jnp.bfloat16)
        gate = jnp.dot(normed, gate_w, preferred_element_type=jnp.float32)
        up = jnp.dot(normed, up_w, preferred_element_type=jnp.float32)
        return widened, scale, gate, up

    id_rows = -(-micro // 16) * 16
    id_block = jnp.broadcast_to(
        jnp.pad(domain_ids.astype(jnp.bfloat16), ((0, id_rows - micro), (0, 0))), (id_rows, units)
    )

    def gather_hidden(hidden, section):
        gathered = jnp.concatenate([hidden, id_block], axis=0)[None]
        for bit in range(bits("dp")):
            other = swap_in(gathered, section, "dp", 2**bit)
            gathered = jnp.concatenate([gathered, other], axis=0)
        return gathered

    _, _, gate0, up0 = layer_parts(rows_in)
    hidden0 = (jax.nn.silu(gate0) * up0).astype(jnp.bfloat16)
    mixed = jnp.dot(hidden0, down_w, preferred_element_type=jnp.float32).astype(jnp.bfloat16)
    cot_rows, mixed = lax.optimization_barrier((rows_in, mixed))
    d_hidden = lax.dot_general(cot_rows, down_w, CONTRACT_LAST, preferred_element_type=jnp.float32)
    x1 = gather_rows(scatter_sum(x_own, mixed, 0, block), 1)
    gathered0 = gather_hidden(hidden0, 0)

    widened, scale, gate, up = layer_parts(x1)
    sig = jax.nn.sigmoid(gate)
    hidden1 = (gate * sig * up).astype(jnp.bfloat16)
    d_gate = (d_hidden * up * (sig * (1.0 + gate * (1.0 - sig)))).astype(jnp.bfloat16)
    d_up = (d_hidden * gate * sig).astype(jnp.bfloat16)
    d_normed = lax.dot_general(d_gate, gate_w, CONTRACT_LAST, preferred_element_type=jnp.float32)
    d_normed = d_normed + lax.dot_general(
        d_up, up_w, CONTRACT_LAST, preferred_element_type=jnp.float32
    )
    pulled = d_normed * gain
    along = jnp.sum(pulled * widened, axis=-1, keepdims=True) / width
    term = (pulled * scale - widened * (scale * scale * scale * along)).astype(jnp.bfloat16)
    hidden1, term = lax.optimization_barrier((hidden1, term))
    dy_own = scatter_sum(cot_own, term, 1, block)
    dy_own = jnp.where(first, dy_own, cot_own)

    piece = width // dp_size
    columns = []
    for k in range(dp_size):
        part = lax.dynamic_slice_in_dim(dy_own, (dp_index ^ k) * piece, piece, axis=1)
        columns.append(part if k == 0 else swap(part, "dp", k))
    y = gather_rows(jnp.concatenate(columns, axis=0))

    gathered = jnp.where(first, gathered0, gather_hidden(hidden1, 1))
    hidden_all = gathered[:, :tok_rows].reshape(dp_size, tensor_size, block, units)
    hidden_all = jnp.swapaxes(hidden_all, 0, 1).reshape(dp_size * tok_rows, units)
    ids_all = gathered[:, tok_rows : tok_rows + micro, 0].astype(jnp.int32)
    row_ids = jnp.broadcast_to(
        ids_all[None, :, :, None], (tensor_size, dp_size, micro, local_rows)
    ).reshape(dp_size * tok_rows, 1)
    gram_hidden = lax.dot_general(
        hidden_all, hidden_all, CONTRACT_LAST, preferred_element_type=jnp.float32
    )
    gram_y = lax.dot_general(y, y, CONTRACT_LAST, preferred_element_type=jnp.float32)
    pairs = jnp.where(row_ids == row_ids.T, gram_hidden * gram_y, 0.0)
    replica = jnp.arange(tok_rows * dp_size) // block % dp_size
    onehot = (row_ids == jnp.arange(DOMAINS)[None, :]).astype(jnp.float32)
    levels = dp_size.bit_length()
    sums = []
    for level in range(levels):
        group = replica >> level
        of_row = jnp.sum(jnp.where(group[:, None] == group[None, :], pairs, 0.0), axis=1)
        sums.append(jnp.sum(onehot * of_row[:, None], axis=0))
    norms = jnp.stack(sums, axis=1)
    rounds = [(axis, bit) for axis in ("tensor", "dp", "section") for bit in range(bits(axis))]
    tiles = units // TILE
    parts = min(len(rounds) - 1, tiles)
    grads = None
    begin = 0
    for part, (axis, bit) in enumerate(rounds):
        other = swap(norms, axis, 2**bit)
        if part < parts:
            end = tiles * (part + 1) // parts
            grads = domain_gradients(row_ids, hidden_all, y, begin, end - begin, grads)
            begin = end
        norms = norms + other
        row_ids, norms = lax.optimization_barrier((row_ids, norms))
    entries = segments * units * tensor_size * width
    counts = [float((dp_size >> level) * entries) for level in range(levels)]
    return grads[None], norms / jnp.array(counts, jnp.float32)[None, :]


def solution(mesh):
    return jax.shard_map(
        shards,
        mesh=mesh,
        in_specs=(
            P(None, ("dp", "tensor"), None),
            P(None, ("dp", "tensor"), None),
            P(None, "dp"),
            P("section", None),
            P("section", None, "tensor"),
            P("section", None, "tensor"),
            P("section", "tensor", None),
        ),
        out_specs=(P("section", None, "tensor", "dp"), P()),
        check_vma=False,
    )
```

time: 132 us -> 125 us (0.947)
  waiting for transfers between devices: 49.4 us -> 40.1 us
  Pallas kernels: 7.39 us -> 16.5 us
  matrix products: 24.5 us -> 16.1 us
  local copies, waits for them, and re-layouts: 6.52 us -> 8.36 us
    ppermute x8, waiting for transfers between devices: 28.2 us -> 12.3 us  [across(): return lax.ppermute(block, ('section', 'tensor'), route)]
    ppermute x0 -> x7, starting transfers between devices: none -> 10.4 us  [swap_in(): return lax.ppermute(block, ('section', axis), route)]
    pallas_call x1 -> x5, Pallas kernels: 7.39 us -> 16.5 us  [the longest x4 10.9 us: domain_gradients(): pl.pallas_call(gradient_kernel, grid=(count,), in_specs=in_specs, out_spe...]
    ppermute x8, starting transfers between devices: 17.1 us -> 12 us  [across(): return lax.ppermute(block, ('section', 'tensor'), route)]
    ppermute x18 -> x14, starting transfers between devices: 21.2 us -> 16.4 us  [swap(): return lax.ppermute(block, axis, [(i, i ^ offset) for i in range(size)])]
    ppermute x18 -> x14, waiting for transfers between devices: 21.2 us -> 25.7 us  [swap(): return lax.ppermute(block, axis, [(i, i ^ offset) for i in range(size)])]
    dot_general x1, matrix products: 6.23 us -> 2.58 us  [shards(): lax.dot_general(cot_rows, down_w, CONTRACT_LAST, preferred_element_type=j...]
    dot_general x2, matrix products: 5.66 us -> 2.38 us  [layer_parts(): gate = jnp.dot(normed, gate_w, preferred_element_type=jnp.float32)]
  transfers between devices with their start and end apart: 26 -> 29, of which waited for: 13 -> 16; matrix products, arithmetic and copies ran while one was open for 21% -> 3% of each run, Pallas kernels for 6% -> 13%
where the time goes in v2:
time: 125 us; the launch traced here: 124 us
  waiting for transfers between devices  40.1 us (32%)
  starting transfers between devices  38.9 us (31%)
  Pallas kernels  16.5 us (13%)
  matrix products  16.1 us (13%)
  local copies, waits for them, and re-layouts  8.36 us (7%)
  other arithmetic  3.13 us (3%)
    ppermute x14, waiting for transfers between devices, swap(): return lax.ppermute(block, axis, [(i, i ^ offset) for i in range(size)])  25.7 us
    ppermute x14, starting transfers between devices, swap(): return lax.ppermute(block, axis, [(i, i ^ offset) for i in range(size)])  16.4 us
    ppermute x8, waiting for transfers between devices, across(): return lax.ppermute(block, ('section', 'tensor'), route)  12.3 us
    ppermute x8, starting transfers between devices, across(): return lax.ppermute(block, ('section', 'tensor'), route)  12 us
    pallas_call x4, Pallas kernels, domain_gradients(): pl.pallas_call(gradient_kernel, grid=(count,), in_specs=in_specs, out_spe...  10.9 us
    ppermute x7, starting transfers between devices, swap_in(): return lax.ppermute(block, ('section', axis), route)  10.4 us
    pallas_call x1, Pallas kernels, load_weights(): pl.pallas_call(load_kernel, in_specs=[pl.BlockSpec(memory_space=pltpu.HBM...  5.68 us
    unnamed x22, local copies, waits for them, and re-layouts  4.39 us
  transfers between devices with their start and end apart: 29, of which 16 were waited for; matrix products, arithmetic and copies ran while one was open for 3% of the time, Pallas kernels for 13%

profile of v2, /device:TPU:0, one launch (start us, length us, event | category | flops | bytes accessed | tf_op | source)
XLA Modules:
  0.0 124.3 jit_solution(4334671365466669207)
XLA Ops:
  1.6 5.1 %collective-permute-start.2 = (bf16[32,2048]{1,0:T(8,128)(2,1)S(1)}, bf16[32,2048]{1,0:T(8,128)(2,1)S(1)}, u32[]{:S(2)}, u32[]{:S(2)}) collective-permute-start(bf16[32,2048]{1,0:T(8,128)(2,1)S(1)} %bitcast_select_fusion), channel_id=1, source_target_pairs={{0,3},{1,2},{2,1},{3,0},{4,7},{5,6},{6,5},{7,4},{8,11},{9,10},{10,... | collective-permute-start | bytes 393224 | tf_op jit(solution)/shard_map/ppermute | solution.py:17
  7.4 3.1 %copy-done = bf16[1,2048,1792]{2,1,0:T(8,128)(2,1)S(1)} copy-done((bf16[1,2048,1792]{2,1,0:T(8,128)(2,1)S(1)}, bf16[1,2048,1792]{2,1,0:T(8,128)(2,1)}, u32[]{:S(2)}) %copy-start) | copy-done | bytes 7340056
  10.5 5.7 %shard_map.95 = (bf16[2048,1792]{1,0:T(8,128)(2,1)S(1)}, bf16[2048,1792]{1,0:T(8,128)(2,1)S(1)}, bf16[1792,2048]{1,0:T(8,128)(2,1)S(1)}) custom-call(bf16[1,2048,1792]{2,1,0:T(8,128)(2,1)S(1)} %copy-done, bf16[1,2048,1792]{2,1,0:T(8,128)(2,1)} %refs_1_.1, bf16[1,1792,2048]{2,1,0:T(8,128)(2,1)} %refs_2_.1), custom_call_target="tpu_custom_call" | custom-call | bytes 22020096 | tf_op jit(solution)/shard_map/pallas_call | solution.py:69
  16.2 1.6 %collective-permute-done.1 = bf16[32,2048]{1,0:T(8,128)(2,1)S(1)} collective-permute-done((bf16[32,2048]{1,0:T(8,128)(2,1)S(1)}, bf16[32,2048]{1,0:T(8,128)(2,1)S(1)}, u32[]{:S(2)}, u32[]{:S(2)}) %collective-permute-start.1) | collective-permute-done | bytes 131104 | tf_op jit(solution)/shard_map/ppermute | solution.py:17
  18.0 1.2 fusion.21
  19.2 1.4 %fusion.1 = bf16[128,1792]{1,0:T(8,128)(2,1)S(1)} fusion(bf16[2048,1792]{1,0:T(8,128)(2,1)S(1)} %get-tuple-element.17, f32[128,1792]{1,0:T(8,128)S(1)} %fusion.21, bf16[128,2048]{1,0:T(8,128)(2,1)S(1)} %get-tuple-element.20, f32[2048]{0:T(1024)S(1)} %bitcast.43, f32[128]{0:T(128)S(1)} %add_rsqrt_fusion.1), kind=kOutput, calls=%fused_computation.3 | convolution fusion | flops 941948928 | bytes 9249280 | tf_op jit(solution)/shard_map/dot_general | solution.py:152
  20.6 1.1 convolution_convert_fusion
  21.8 1.3 %collective-permute-start.5 = (bf16[32,2048]{1,0:T(8,128)(2,1)S(1)}, bf16[32,2048]{1,0:T(8,128)(2,1)S(1)}, u32[]{:S(2)}, u32[]{:S(2)}) collective-permute-start(bf16[32,2048]{1,0:T(8,128)(2,1)S(1)} %get-tuple-element.50), channel_id=1, source_target_pairs={{0,16},{1,17},{2,18},{3,19},{4,20},{5,21},{6,22},{7,23},{8,24},{9,... | collective-permute-start | bytes 393224 | tf_op jit(solution)/shard_map/ppermute | solution.py:31
  23.1 3.0 %collective-permute-start.8 = (bf16[32,2048]{1,0:T(8,128)(2,1)S(1)}, bf16[32,2048]{1,0:T(8,128)(2,1)S(1)}, u32[]{:S(2)}, u32[]{:S(2)}) collective-permute-start(bf16[32,2048]{1,0:T(8,128)(2,1)S(1)} %get-tuple-element.51), channel_id=1, source_target_pairs={{0,19},{1,18},{2,17},{3,16},{4,23},{5,22},{6,21},{7,20},{8,27},{9,... | collective-permute-start | bytes 393224 | tf_op jit(solution)/shard_map/ppermute | solution.py:31
  26.1 1.3 %collective-permute-start.7 = (bf16[32,2048]{1,0:T(8,128)(2,1)S(1)}, bf16[32,2048]{1,0:T(8,128)(2,1)S(1)}, u32[]{:S(2)}, u32[]{:S(2)}) collective-permute-start(bf16[32,2048]{1,0:T(8,128)(2,1)S(1)} %get-tuple-element.52), channel_id=1, source_target_pairs={{0,18},{1,19},{2,16},{3,17},{4,22},{5,23},{6,20},{7,21},{8,26},{9,... | collective-permute-start | bytes 393224 | tf_op jit(solution)/shard_map/ppermute | solution.py:31
  27.4 1.3 %collective-permute-start.6 = (bf16[32,2048]{1,0:T(8,128)(2,1)S(1)}, bf16[32,2048]{1,0:T(8,128)(2,1)S(1)}, u32[]{:S(2)}, u32[]{:S(2)}) collective-permute-start(bf16[32,2048]{1,0:T(8,128)(2,1)S(1)} %get-tuple-element.53), channel_id=1, source_target_pairs={{0,17},{1,16},{2,19},{3,18},{4,21},{5,20},{6,23},{7,22},{8,25},{9,... | collective-permute-start | bytes 393224 | tf_op jit(solution)/shard_map/ppermute | solution.py:31
  28.8 1.2 collective-permute-done.7
  30.0 1.4 %collective-permute-done.6 = bf16[32,2048]{1,0:T(8,128)(2,1)S(1)} collective-permute-done((bf16[32,2048]{1,0:T(8,128)(2,1)S(1)}, bf16[32,2048]{1,0:T(8,128)(2,1)S(1)}, u32[]{:S(2)}, u32[]{:S(2)}) %collective-permute-start.6) | collective-permute-done | bytes 131104 | tf_op jit(solution)/shard_map/ppermute | solution.py:31
  33.5 2.6 %fusion.33 = f32[128,1792]{1,0:T(8,128)S(1)} fusion(bf16[128,2048]{1,0:T(8,128)(2,1)S(1)} %get-tuple-element.20, bf16[1792,2048]{1,0:T(8,128)(2,1)S(1)} %get-tuple-element.18), kind=kOutput, calls=%fused_computation.89 | convolution fusion | flops 939524096 | bytes 8781824 | tf_op jit(solution)/shard_map/dot_general | solution.py:171
  36.4 1.2 fusion.18
  37.6 1.4 %multiply_convert_fusion.2 = (bf16[128,1792]{1,0:T(8,128)(2,1)S(1)}, f32[128,1792]{1,0:T(8,128)S(1)}) fusion(f32[128,1792]{1,0:T(8,128)S(1)} %fusion.18, bf16[2048,1792]{1,0:T(8,128)(2,1)S(1)} %get-tuple-element.17, f32[128]{0:T(128)S(1)} %add_rsqrt_fusion, f32[2048]{0:T(1024)S(1)} %bitcast.45, bf16[32,2048]{1,0:T(8,128)(2,1)S(1)} %collective-permute-done.11, ...), kind=kOutput, calls=%fused_computation.30 | convolution fusion | flops 943783936 | bytes 10166784 | tf_op jit(solution)/shard_map/dot_general | solution.py:152
  39.0 2.5 %fusion.12 = f32[128,2048]{1,0:T(8,128)S(1)} fusion(bf16[2048,1792]{1,0:T(8,128)(2,1)S(1)} %get-tuple-element.16, f32[128,1792]{1,0:T(8,128)S(1)} %fusion.18, f32[128,1792]{1,0:T(8,128)S(1)} %fusion.33, f32[128,1792]{1,0:T(8,128)S(1)} %get-tuple-element.62), kind=kOutput, calls=%fused_computation.36 | convolution fusion | flops 941817856 | bytes 11141120 | tf_op jit(solution)/shard_map/dot_general | solution.py:180
  42.0 2.6 %fusion.9 = (f32[128]{0:T(128)S(1)}, f32[128,2048]{1,0:T(8,128)S(1)}) fusion(bf16[32,2048]{1,0:T(8,128)(2,1)S(1)} %collective-permute-done.11, bf16[32,2048]{1,0:T(8,128)(2,1)S(1)} %collective-permute-done.10, bf16[32,2048]{1,0:T(8,128)(2,1)S(1)} %collective-permute-done.9, bf16[32,2048]{1,0:T(8,128)(2,1)S(1)} %add_convert_fusion.1, f32[2048]{0:T(1024)S(1)} %bitcast.46, ...), kind=kOutput, calls=%fused_computation.20 | convolution fusion | flops 944045952 | bytes 11805184 | tf_op jit(solution)/shard_map/dot_general | solution.py:181
  45.9 3.6 %collective-permute-start.3 = (bf16[1,144,1792]{2,1,0:T(8,128)(2,1)S(1)}, bf16[1,144,1792]{2,1,0:T(8,128)(2,1)S(1)}, u32[]{:S(2)}, u32[]{:S(2)}) collective-permute-start(bf16[1,144,1792]{2,1,0:T(8,128)(2,1)S(1)} %get-tuple-element.60), channel_id=1, source_target_pairs={{0,4},{4,0},{8,12},{12,8},{1,5},{5,1},{9,13},{13,9},{2,6},{6,2},{1... | collective-permute-start | bytes 1548296 | tf_op jit(solution)/shard_map/ppermute | solution.py:23
  49.6 1.3 %collective-permute-start.14 = (bf16[32,2048]{1,0:T(8,128)(2,1)S(1)}, bf16[32,2048]{1,0:T(8,128)(2,1)S(1)}, u32[]{:S(2)}, u32[]{:S(2)}) collective-permute-start(bf16[32,2048]{1,0:T(8,128)(2,1)S(1)} %get-tuple-element.46), channel_id=1, source_target_pairs={{16,0},{17,1},{18,2},{19,3},{20,4},{21,5},{22,6},{23,7},{24,8},{25... | collective-permute-start | bytes 393224 | tf_op jit(solution)/shard_map/ppermute | solution.py:31
  50.9 1.3 %collective-permute-start.17 = (bf16[32,2048]{1,0:T(8,128)(2,1)S(1)}, bf16[32,2048]{1,0:T(8,128)(2,1)S(1)}, u32[]{:S(2)}, u32[]{:S(2)}) collective-permute-start(bf16[32,2048]{1,0:T(8,128)(2,1)S(1)} %get-tuple-element.47), channel_id=1, source_target_pairs={{16,3},{17,2},{18,1},{19,0},{20,7},{21,6},{22,5},{23,4},{24,11},{2... | collective-permute-start | bytes 393224 | tf_op jit(solution)/shard_map/ppermute | solution.py:31
  52.2 1.3 %collective-permute-start.16 = (bf16[32,2048]{1,0:T(8,128)(2,1)S(1)}, bf16[32,2048]{1,0:T(8,128)(2,1)S(1)}, u32[]{:S(2)}, u32[]{:S(2)}) collective-permute-start(bf16[32,2048]{1,0:T(8,128)(2,1)S(1)} %get-tuple-element.48), channel_id=1, source_target_pairs={{16,2},{17,3},{18,0},{19,1},{20,6},{21,7},{22,4},{23,5},{24,10},{2... | collective-permute-start | bytes 393224 | tf_op jit(solution)/shard_map/ppermute | solution.py:31
  53.5 1.3 %collective-permute-start.15 = (bf16[32,2048]{1,0:T(8,128)(2,1)S(1)}, bf16[32,2048]{1,0:T(8,128)(2,1)S(1)}, u32[]{:S(2)}, u32[]{:S(2)}) collective-permute-start(bf16[32,2048]{1,0:T(8,128)(2,1)S(1)} %get-tuple-element.49), channel_id=1, source_target_pairs={{16,1},{17,0},{18,3},{19,2},{20,5},{21,4},{22,7},{23,6},{24,9},{25... | collective-permute-start | bytes 393224 | tf_op jit(solution)/shard_map/ppermute | solution.py:31
  54.9 2.0 %collective-permute-done.3 = bf16[1,144,1792]{2,1,0:T(8,128)(2,1)S(1)} collective-permute-done((bf16[1,144,1792]{2,1,0:T(8,128)(2,1)S(1)}, bf16[1,144,1792]{2,1,0:T(8,128)(2,1)S(1)}, u32[]{:S(2)}, u32[]{:S(2)}) %collective-permute-start.3) | collective-permute-done | bytes 516128 | tf_op jit(solution)/shard_map/ppermute | solution.py:23
  57.7 3.2 %collective-permute-done.14 = bf16[32,2048]{1,0:T(8,128)(2,1)S(1)} collective-permute-done((bf16[32,2048]{1,0:T(8,128)(2,1)S(1)}, bf16[32,2048]{1,0:T(8,128)(2,1)S(1)}, u32[]{:S(2)}, u32[]{:S(2)}) %collective-permute-start.14) | collective-permute-done | bytes 131104 | tf_op jit(solution)/shard_map/ppermute | solution.py:31
  60.9 3.4 %collective-permute-start.4 = (bf16[2,144,1792]{2,1,0:T(8,128)(2,1)S(1)}, bf16[2,144,1792]{2,1,0:T(8,128)(2,1)S(1)}, u32[]{:S(2)}, u32[]{:S(2)}) collective-permute-start(bf16[2,144,1792]{2,1,0:T(8,128)(2,1)S(1)} %pad_maximum_fusion), channel_id=1, source_target_pairs={{0,8},{4,12},{8,0},{12,4},{1,9},{5,13},{9,1},{13,5},{2,10},{6,14},... | collective-permute-start | bytes 3096584 | tf_op jit(solution)/shard_map/ppermute | solution.py:23
  64.3 1.5 %collective-permute-done.17 = bf16[32,2048]{1,0:T(8,128)(2,1)S(1)} collective-permute-done((bf16[32,2048]{1,0:T(8,128)(2,1)S(1)}, bf16[32,2048]{1,0:T(8,128)(2,1)S(1)}, u32[]{:S(2)}, u32[]{:S(2)}) %collective-permute-start.17) | collective-permute-done | bytes 131104 | tf_op jit(solution)/shard_map/ppermute | solution.py:31
  65.9 3.9 %collective-permute-done.16 = bf16[32,2048]{1,0:T(8,128)(2,1)S(1)} collective-permute-done((bf16[32,2048]{1,0:T(8,128)(2,1)S(1)}, bf16[32,2048]{1,0:T(8,128)(2,1)S(1)}, u32[]{:S(2)}, u32[]{:S(2)}) %collective-permute-start.16) | collective-permute-done | bytes 131104 | tf_op jit(solution)/shard_map/ppermute | solution.py:31
  69.8 1.1 collective-permute-done.15
  71.0 1.7 %collective-permute-start.20 = (bf16[32,512]{1,0:T(8,128)(2,1)S(1)}, bf16[32,512]{1,0:T(8,128)(2,1)S(1)}, u32[]{:S(2)}, u32[]{:S(2)}) collective-permute-start(bf16[32,512]{1,0:T(8,128)(2,1)S(1)} %get-tuple-element.54), channel_id=1, source_target_pairs={{0,12},{4,8},{8,4},{12,0},{1,13},{5,9},{9,5},{13,1},{2,14},{6,10},... | collective-permute-start | bytes 98312 | tf_op jit(solution)/shard_map/ppermute | solution.py:17
  73.3 1.3 %collective-permute-start.18 = (bf16[32,512]{1,0:T(8,128)(2,1)S(1)}, bf16[32,512]{1,0:T(8,128)(2,1)S(1)}, u32[]{:S(2)}, u32[]{:S(2)}) collective-permute-start(bf16[32,512]{1,0:T(8,128)(2,1)S(1)} %get-tuple-element.56), channel_id=1, source_target_pairs={{0,4},{4,0},{8,12},{12,8},{1,5},{5,1},{9,13},{13,9},{2,6},{6,2},{1... | collective-permute-start | bytes 98312 | tf_op jit(solution)/shard_map/ppermute | solution.py:17
  74.6 1.7 %collective-permute-done.20 = bf16[32,512]{1,0:T(8,128)(2,1)S(1)} collective-permute-done((bf16[32,512]{1,0:T(8,128)(2,1)S(1)}, bf16[32,512]{1,0:T(8,128)(2,1)S(1)}, u32[]{:S(2)}, u32[]{:S(2)}) %collective-permute-start.20) | collective-permute-done | bytes 32800 | tf_op jit(solution)/shard_map/ppermute | solution.py:17
  76.2 9.2 %collective-permute-done.19 = bf16[32,512]{1,0:T(8,128)(2,1)S(1)} collective-permute-done((bf16[32,512]{1,0:T(8,128)(2,1)S(1)}, bf16[32,512]{1,0:T(8,128)(2,1)S(1)}, u32[]{:S(2)}, u32[]{:S(2)}) %collective-permute-start.19) | collective-permute-done | bytes 32800 | tf_op jit(solution)/shard_map/ppermute | solution.py:17
  85.4 2.2 %collective-permute-start.23 = (bf16[128,512]{1,0:T(8,128)(2,1)S(1)}, bf16[128,512]{1,0:T(8,128)(2,1)S(1)}, u32[]{:S(2)}, u32[]{:S(2)}) collective-permute-start(bf16[128,512]{1,0:T(8,128)(2,1)S(1)} %pad_maximum_fusion.4), channel_id=1, source_target_pairs={{0,3},{1,2},{2,1},{3,0},{4,7},{5,6},{6,5},{7,4},{8,11},{9,10},{10,... | collective-permute-start | bytes 393224 | tf_op jit(solution)/shard_map/ppermute | solution.py:17
  88.1 1.8 %collective-permute-start.21 = (bf16[128,512]{1,0:T(8,128)(2,1)S(1)}, bf16[128,512]{1,0:T(8,128)(2,1)S(1)}, u32[]{:S(2)}, u32[]{:S(2)}) collective-permute-start(bf16[128,512]{1,0:T(8,128)(2,1)S(1)} %pad_maximum_fusion.4), channel_id=1, source_target_pairs={{0,1},{1,0},{2,3},{3,2},{4,5},{5,4},{6,7},{7,6},{8,9},{9,8},{10,11... | collective-permute-start | bytes 393224 | tf_op jit(solution)/shard_map/ppermute | solution.py:17
  89.9 4.0 %collective-permute-done.21 = bf16[128,512]{1,0:T(8,128)(2,1)S(1)} collective-permute-done((bf16[128,512]{1,0:T(8,128)(2,1)S(1)}, bf16[128,512]{1,0:T(8,128)(2,1)S(1)}, u32[]{:S(2)}, u32[]{:S(2)}) %collective-permute-start.21) | collective-permute-done | bytes 131104 | tf_op jit(solution)/shard_map/ppermute | solution.py:17
  93.9 5.6 %collective-permute-done.22 = bf16[128,512]{1,0:T(8,128)(2,1)S(1)} collective-permute-done((bf16[128,512]{1,0:T(8,128)(2,1)S(1)}, bf16[128,512]{1,0:T(8,128)(2,1)S(1)}, u32[]{:S(2)}, u32[]{:S(2)}) %collective-permute-start.22) | collective-permute-done | bytes 131104 | tf_op jit(solution)/shard_map/ppermute | solution.py:17
  100.1 1.4 %slice.41 = bf16[4,128,1792]{2,1,0:T(8,128)(2,1)} slice(bf16[4,144,1792]{2,1,0:T(8,128)(2,1)S(1)} %maximum_select_fusion), slice={[0:4], [0:128], [0:1792]} | slice | bytes 3670016 | tf_op jit(solution)/shard_map/slice | solution.py:199
  101.7 1.6 %copy.21 = bf16[4,4,32,1792]{3,2,0,1:T(8,128)(2,1)S(1)} copy(bf16[4,4,32,1792]{3,2,1,0:T(8,128)(2,1)} %bitcast.41) | data formatting | bytes 3670016 | tf_op jit(solution)/shard_map/reshape | solution.py:199
  103.5 1.1 fusion.34
  106.0 1.8 %shard_map.96.rest_0_ = bf16[4,1792,512]{2,1,0:T(8,128)(2,1)} custom-call(s32[512,1]{1,0:T(8,128)S(1)} %copy.22.ids_ref, bf16[512,1792]{1,0:T(8,128)(2,1)S(1)} %bitcast.36, bf16[512,512]{1,0:T(8,128)(2,1)S(1)} %constant_dynamic-update-slice_fusion.y_ref), custom_call_target="tpu_custom_call" | custom-call | flops 536870912 | bytes 1310720 | tf_op jit(solution)/shard_map/pallas_call | solution.py:111
  107.8 1.7 %collective-permute-done.24 = f32[4,3]{0,1:T(4,128)S(1)} collective-permute-done((f32[4,3]{0,1:T(4,128)S(1)}, f32[4,3]{0,1:T(4,128)S(1)}, u32[]{:S(2)}, u32[]{:S(2)}) %collective-permute-start.24) | collective-permute-done | bytes 80 | tf_op jit(solution)/shard_map/ppermute | solution.py:17
  109.5 1.1 collective-permute-start.25
  110.8 3.0 %shard_map.97.rest_0_ = bf16[4,1792,512]{2,1,0:T(8,128)(2,1)} custom-call(s32[512,1]{1,0:T(8,128)S(1)} %copy.23.ids_ref, bf16[512,1792]{1,0:T(8,128)(2,1)S(1)} %bitcast.37, bf16[512,512]{1,0:T(8,128)(2,1)S(1)} %constant_dynamic-update-slice_fusion.y_ref, bf16[4,1792,512]{2,1,0:T(8,128)(2,1)} %shard_map.96.rest_0_), custom_call_target="tpu_custom_call", output_to_operand_aliasing={{}: (3, {})} | custom-call | flops 1073741824 | bytes 2621440 | tf_op jit(solution)/shard_map/pallas_call | solution.py:111
  114.2 3.0 %shard_map.98.rest_0_ = bf16[4,1792,512]{2,1,0:T(8,128)(2,1)} custom-call(s32[512,1]{1,0:T(8,128)S(1)} %copy.24.ids_ref, bf16[512,1792]{1,0:T(8,128)(2,1)S(1)} %bitcast.38, bf16[512,512]{1,0:T(8,128)(2,1)S(1)} %constant_dynamic-update-slice_fusion.y_ref, bf16[4,1792,512]{2,1,0:T(8,128)(2,1)} %shard_map.97.rest_0_), custom_call_target="tpu_custom_call", output_to_operand_aliasing={{}: (3, {})} | custom-call | flops 1073741824 | bytes 2621440 | tf_op jit(solution)/shard_map/pallas_call | solution.py:111
  117.7 1.5 %collective-permute-start.27 = (f32[4,3]{0,1:T(4,128)S(1)}, f32[4,3]{0,1:T(4,128)S(1)}, u32[]{:S(2)}, u32[]{:S(2)}) collective-permute-start(f32[4,3]{0,1:T(4,128)S(1)} %add.157), channel_id=1, source_target_pairs={{0,8},{4,12},{8,0},{12,4},{1,9},{5,13},{9,1},{13,5},{2,10},{6,14},... | collective-permute-start | bytes 152 | tf_op jit(solution)/shard_map/ppermute | solution.py:17
  119.4 3.0 %shard_map.99 = bf16[4,1792,512]{2,1,0:T(8,128)(2,1)} custom-call(s32[512,1]{1,0:T(8,128)S(1)} %copy.25.ids_ref, bf16[512,1792]{1,0:T(8,128)(2,1)S(1)} %bitcast.39, bf16[512,512]{1,0:T(8,128)(2,1)S(1)} %constant_dynamic-update-slice_fusion.y_ref, bf16[4,1792,512]{2,1,0:T(8,128)(2,1)} %shard_map.98.rest_0_), custom_call_target="tpu_custom_call", output_to_operand_aliasing={{}: (3, {})} | custom-call | flops 1073741824 | bytes 2621440 | tf_op jit(solution)/shard_map/pallas_call | solution.py:111
  122.4 1.1 collective-permute-done.28
  (88 shorter events, 12.3 us)
Async XLA Ops:
  0.6 17.4 %copy-start.5 = (f32[1,2048]{1,0:T(1,128)S(1)}, f32[1,2048]{1,0:T(1,128)}, u32[]{:S(2)}) copy-start(f32[1,2048]{1,0:T(1,128)} %param.11) | copy-start | bytes 24580
  1.6 14.5 %collective-permute-start.2 = (bf16[32,2048]{1,0:T(8,128)(2,1)S(1)}, bf16[32,2048]{1,0:T(8,128)(2,1)S(1)}, u32[]{:S(2)}, u32[]{:S(2)}) collective-permute-start(bf16[32,2048]{1,0:T(8,128)(2,1)S(1)} %bitcast_select_fusion), channel_id=1, source_target_pairs={{0,3},{1,2},{2,1},{3,0},{4,7},{5,6},{6,5},{7,4},{8,11},{9,10},{10,... | collective-permute-start | bytes 393224 | tf_op jit(solution)/shard_map/ppermute | solution.py:17
  6.8 11.1 %collective-permute-start.1 = (bf16[32,2048]{1,0:T(8,128)(2,1)S(1)}, bf16[32,2048]{1,0:T(8,128)(2,1)S(1)}, u32[]{:S(2)}, u32[]{:S(2)}) collective-permute-start(bf16[32,2048]{1,0:T(8,128)(2,1)S(1)} %bitcast_select_fusion), channel_id=1, source_target_pairs={{0,2},{1,3},{2,0},{3,1},{4,6},{5,7},{6,4},{7,5},{8,10},{9,11},{10,... | collective-permute-start | bytes 393224 | tf_op jit(solution)/shard_map/ppermute | solution.py:17
  6.8 11.1 %collective-permute-start = (bf16[32,2048]{1,0:T(8,128)(2,1)S(1)}, bf16[32,2048]{1,0:T(8,128)(2,1)S(1)}, u32[]{:S(2)}, u32[]{:S(2)}) collective-permute-start(bf16[32,2048]{1,0:T(8,128)(2,1)S(1)} %bitcast_select_fusion), channel_id=1, source_target_pairs={{0,1},{1,0},{2,3},{3,2},{4,5},{5,4},{6,7},{7,6},{8,9},{9,8},{10,11... | collective-permute-start | bytes 393224 | tf_op jit(solution)/shard_map/ppermute | solution.py:17
  7.4 3.1 %copy-start = (bf16[1,2048,1792]{2,1,0:T(8,128)(2,1)S(1)}, bf16[1,2048,1792]{2,1,0:T(8,128)(2,1)}, u32[]{:S(2)}) copy-start(bf16[1,2048,1792]{2,1,0:T(8,128)(2,1)} %refs_0_.1) | copy-start | bytes 22020100
  16.2 21.4 %copy-start.1 = (bf16[2048,1792]{1,0:T(8,128)(2,1)}, bf16[2048,1792]{1,0:T(8,128)(2,1)S(1)}, u32[]{:S(2)}) copy-start(bf16[2048,1792]{1,0:T(8,128)(2,1)S(1)} %get-tuple-element.17) | copy-start | bytes 22020100
  20.6 8.1 %copy-start.7 = (s32[4,1]{0,1:T(1,128)S(1)}, s32[4,1]{0,1:T(1,128)}, u32[]{:S(2)}) copy-start(s32[4,1]{0,1:T(1,128)} %param.10) | copy-start | bytes 52
  20.6 10.8 %copy-start.3 = (bf16[4,8,2048]{2,1,0:T(8,128)(2,1)S(1)}, bf16[4,8,2048]{2,1,0:T(8,128)(2,1)}, u32[]{:S(2)}) copy-start(bf16[4,8,2048]{2,1,0:T(8,128)(2,1)} %param.8) | copy-start | bytes 393220
  21.8 6.9 %collective-permute-start.5 = (bf16[32,2048]{1,0:T(8,128)(2,1)S(1)}, bf16[32,2048]{1,0:T(8,128)(2,1)S(1)}, u32[]{:S(2)}, u32[]{:S(2)}) collective-permute-start(bf16[32,2048]{1,0:T(8,128)(2,1)S(1)} %get-tuple-element.50), channel_id=1, source_target_pairs={{0,16},{1,17},{2,18},{3,19},{4,20},{5,21},{6,22},{7,23},{8,24},{9,... | collective-permute-start | bytes 393224 | tf_op jit(solution)/shard_map/ppermute | solution.py:31
  23.1 5.6 %collective-permute-start.8 = (bf16[32,2048]{1,0:T(8,128)(2,1)S(1)}, bf16[32,2048]{1,0:T(8,128)(2,1)S(1)}, u32[]{:S(2)}, u32[]{:S(2)}) collective-permute-start(bf16[32,2048]{1,0:T(8,128)(2,1)S(1)} %get-tuple-element.51), channel_id=1, source_target_pairs={{0,19},{1,18},{2,17},{3,16},{4,23},{5,22},{6,21},{7,20},{8,27},{9,... | collective-permute-start | bytes 393224 | tf_op jit(solution)/shard_map/ppermute | solution.py:31
  26.1 3.9 %collective-permute-start.7 = (bf16[32,2048]{1,0:T(8,128)(2,1)S(1)}, bf16[32,2048]{1,0:T(8,128)(2,1)S(1)}, u32[]{:S(2)}, u32[]{:S(2)}) collective-permute-start(bf16[32,2048]{1,0:T(8,128)(2,1)S(1)} %get-tuple-element.52), channel_id=1, source_target_pairs={{0,18},{1,19},{2,16},{3,17},{4,22},{5,23},{6,20},{7,21},{8,26},{9,... | collective-permute-start | bytes 393224 | tf_op jit(solution)/shard_map/ppermute | solution.py:31
  27.4 4.0 %collective-permute-start.6 = (bf16[32,2048]{1,0:T(8,128)(2,1)S(1)}, bf16[32,2048]{1,0:T(8,128)(2,1)S(1)}, u32[]{:S(2)}, u32[]{:S(2)}) collective-permute-start(bf16[32,2048]{1,0:T(8,128)(2,1)S(1)} %get-tuple-element.53), channel_id=1, source_target_pairs={{0,17},{1,16},{2,19},{3,18},{4,21},{5,20},{6,23},{7,22},{8,25},{9,... | collective-permute-start | bytes 393224 | tf_op jit(solution)/shard_map/ppermute | solution.py:31
  31.5 4.6 %collective-permute-start.11 = (bf16[32,2048]{1,0:T(8,128)(2,1)S(1)}, bf16[32,2048]{1,0:T(8,128)(2,1)S(1)}, u32[]{:S(2)}, u32[]{:S(2)}) collective-permute-start(bf16[32,2048]{1,0:T(8,128)(2,1)S(1)} %add_convert_fusion.1), channel_id=1, source_target_pairs={{16,19},{17,18},{18,17},{19,16},{20,23},{21,22},{22,21},{23,20},{2... | collective-permute-start | bytes 393224 | tf_op jit(solution)/shard_map/ppermute | solution.py:23
  32.2 4.0 %collective-permute-start.10 = (bf16[32,2048]{1,0:T(8,128)(2,1)S(1)}, bf16[32,2048]{1,0:T(8,128)(2,1)S(1)}, u32[]{:S(2)}, u32[]{:S(2)}) collective-permute-start(bf16[32,2048]{1,0:T(8,128)(2,1)S(1)} %add_convert_fusion.1), channel_id=1, source_target_pairs={{16,18},{17,19},{18,16},{19,17},{20,22},{21,23},{22,20},{23,21},{2... | collective-permute-start | bytes 393224 | tf_op jit(solution)/shard_map/ppermute | solution.py:23
  32.9 3.3 %collective-permute-start.9 = (bf16[32,2048]{1,0:T(8,128)(2,1)S(1)}, bf16[32,2048]{1,0:T(8,128)(2,1)S(1)}, u32[]{:S(2)}, u32[]{:S(2)}) collective-permute-start(bf16[32,2048]{1,0:T(8,128)(2,1)S(1)} %add_convert_fusion.1), channel_id=1, source_target_pairs={{16,17},{17,16},{18,19},{19,18},{20,21},{21,20},{22,23},{23,22},{2... | collective-permute-start | bytes 393224 | tf_op jit(solution)/shard_map/ppermute | solution.py:23
  38.9 3.1 %copy-start.2 = (bf16[2048,1792]{1,0:T(8,128)(2,1)S(1)}, bf16[2048,1792]{1,0:T(8,128)(2,1)}, u32[]{:S(2)}) copy-start(bf16[2048,1792]{1,0:T(8,128)(2,1)} %copy-done.1) | copy-start | bytes 22020100
  44.6 26.2 %copy-start.4 = (bf16[4,8,2048]{2,1,0:T(8,128)(2,1)S(1)}, bf16[4,8,2048]{2,1,0:T(8,128)(2,1)}, u32[]{:S(2)}) copy-start(bf16[4,8,2048]{2,1,0:T(8,128)(2,1)} %param.9) | copy-start | bytes 393220
  45.2 8.3 %collective-permute-start.12 = (bf16[1,144,1792]{2,1,0:T(8,128)(2,1)S(1)}, bf16[1,144,1792]{2,1,0:T(8,128)(2,1)S(1)}, u32[]{:S(2)}, u32[]{:S(2)}) collective-permute-start(bf16[1,144,1792]{2,1,0:T(8,128)(2,1)S(1)} %get-tuple-element.59), channel_id=1, source_target_pairs={{16,20},{20,16},{24,28},{28,24},{17,21},{21,17},{25,29},{29,25},{1... | collective-permute-start | bytes 1548296 | tf_op jit(solution)/shard_map/ppermute | solution.py:23
  45.9 11.0 %collective-permute-start.3 = (bf16[1,144,1792]{2,1,0:T(8,128)(2,1)S(1)}, bf16[1,144,1792]{2,1,0:T(8,128)(2,1)S(1)}, u32[]{:S(2)}, u32[]{:S(2)}) collective-permute-start(bf16[1,144,1792]{2,1,0:T(8,128)(2,1)S(1)} %get-tuple-element.60), channel_id=1, source_target_pairs={{0,4},{4,0},{8,12},{12,8},{1,5},{5,1},{9,13},{13,9},{2,6},{6,2},{1... | collective-permute-start | bytes 1548296 | tf_op jit(solution)/shard_map/ppermute | solution.py:23
  49.6 11.3 %collective-permute-start.14 = (bf16[32,2048]{1,0:T(8,128)(2,1)S(1)}, bf16[32,2048]{1,0:T(8,128)(2,1)S(1)}, u32[]{:S(2)}, u32[]{:S(2)}) collective-permute-start(bf16[32,2048]{1,0:T(8,128)(2,1)S(1)} %get-tuple-element.46), channel_id=1, source_target_pairs={{16,0},{17,1},{18,2},{19,3},{20,4},{21,5},{22,6},{23,7},{24,8},{25... | collective-permute-start | bytes 393224 | tf_op jit(solution)/shard_map/ppermute | solution.py:31
  50.9 15.0 %collective-permute-start.17 = (bf16[32,2048]{1,0:T(8,128)(2,1)S(1)}, bf16[32,2048]{1,0:T(8,128)(2,1)S(1)}, u32[]{:S(2)}, u32[]{:S(2)}) collective-permute-start(bf16[32,2048]{1,0:T(8,128)(2,1)S(1)} %get-tuple-element.47), channel_id=1, source_target_pairs={{16,3},{17,2},{18,1},{19,0},{20,7},{21,6},{22,5},{23,4},{24,11},{2... | collective-permute-start | bytes 393224 | tf_op jit(solution)/shard_map/ppermute | solution.py:31
  52.2 17.6 %collective-permute-start.16 = (bf16[32,2048]{1,0:T(8,128)(2,1)S(1)}, bf16[32,2048]{1,0:T(8,128)(2,1)S(1)}, u32[]{:S(2)}, u32[]{:S(2)}) collective-permute-start(bf16[32,2048]{1,0:T(8,128)(2,1)S(1)} %get-tuple-element.48), channel_id=1, source_target_pairs={{16,2},{17,3},{18,0},{19,1},{20,6},{21,7},{22,4},{23,5},{24,10},{2... | collective-permute-start | bytes 393224 | tf_op jit(solution)/shard_map/ppermute | solution.py:31
  53.5 17.4 %collective-permute-start.15 = (bf16[32,2048]{1,0:T(8,128)(2,1)S(1)}, bf16[32,2048]{1,0:T(8,128)(2,1)S(1)}, u32[]{:S(2)}, u32[]{:S(2)}) collective-permute-start(bf16[32,2048]{1,0:T(8,128)(2,1)S(1)} %get-tuple-element.49), channel_id=1, source_target_pairs={{16,1},{17,0},{18,3},{19,2},{20,5},{21,4},{22,7},{23,6},{24,9},{25... | collective-permute-start | bytes 393224 | tf_op jit(solution)/shard_map/ppermute | solution.py:31
  56.9 42.6 %collective-permute-start.13 = (bf16[2,144,1792]{2,1,0:T(8,128)(2,1)S(1)}, bf16[2,144,1792]{2,1,0:T(8,128)(2,1)S(1)}, u32[]{:S(2)}, u32[]{:S(2)}) collective-permute-start(bf16[2,144,1792]{2,1,0:T(8,128)(2,1)S(1)} %pad_maximum_fusion.1), channel_id=1, source_target_pairs={{16,24},{20,28},{24,16},{28,20},{17,25},{21,29},{25,17},{29,21},{1... | collective-permute-start | bytes 3096584 | tf_op jit(solution)/shard_map/ppermute | solution.py:23
  60.9 38.6 %collective-permute-start.4 = (bf16[2,144,1792]{2,1,0:T(8,128)(2,1)S(1)}, bf16[2,144,1792]{2,1,0:T(8,128)(2,1)S(1)}, u32[]{:S(2)}, u32[]{:S(2)}) collective-permute-start(bf16[2,144,1792]{2,1,0:T(8,128)(2,1)S(1)} %pad_maximum_fusion), channel_id=1, source_target_pairs={{0,8},{4,12},{8,0},{12,4},{1,9},{5,13},{9,1},{13,5},{2,10},{6,14},... | collective-permute-start | bytes 3096584 | tf_op jit(solution)/shard_map/ppermute | solution.py:23
  71.0 5.2 %collective-permute-start.20 = (bf16[32,512]{1,0:T(8,128)(2,1)S(1)}, bf16[32,512]{1,0:T(8,128)(2,1)S(1)}, u32[]{:S(2)}, u32[]{:S(2)}) collective-permute-start(bf16[32,512]{1,0:T(8,128)(2,1)S(1)} %get-tuple-element.54), channel_id=1, source_target_pairs={{0,12},{4,8},{8,4},{12,0},{1,13},{5,9},{9,5},{13,1},{2,14},{6,10},... | collective-permute-start | bytes 98312 | tf_op jit(solution)/shard_map/ppermute | solution.py:17
  72.7 12.7 %collective-permute-start.19 = (bf16[32,512]{1,0:T(8,128)(2,1)S(1)}, bf16[32,512]{1,0:T(8,128)(2,1)S(1)}, u32[]{:S(2)}, u32[]{:S(2)}) collective-permute-start(bf16[32,512]{1,0:T(8,128)(2,1)S(1)} %get-tuple-element.55), channel_id=1, source_target_pairs={{0,8},{4,12},{8,0},{12,4},{1,9},{5,13},{9,1},{13,5},{2,10},{6,14},... | collective-permute-start | bytes 98312 | tf_op jit(solution)/shard_map/ppermute | solution.py:17
  73.3 12.2 %collective-permute-start.18 = (bf16[32,512]{1,0:T(8,128)(2,1)S(1)}, bf16[32,512]{1,0:T(8,128)(2,1)S(1)}, u32[]{:S(2)}, u32[]{:S(2)}) collective-permute-start(bf16[32,512]{1,0:T(8,128)(2,1)S(1)} %get-tuple-element.56), channel_id=1, source_target_pairs={{0,4},{4,0},{8,12},{12,8},{1,5},{5,1},{9,13},{13,9},{2,6},{6,2},{1... | collective-permute-start | bytes 98312 | tf_op jit(solution)/shard_map/ppermute | solution.py:17
  85.4 14.0 %collective-permute-start.23 = (bf16[128,512]{1,0:T(8,128)(2,1)S(1)}, bf16[128,512]{1,0:T(8,128)(2,1)S(1)}, u32[]{:S(2)}, u32[]{:S(2)}) collective-permute-start(bf16[128,512]{1,0:T(8,128)(2,1)S(1)} %pad_maximum_fusion.4), channel_id=1, source_target_pairs={{0,3},{1,2},{2,1},{3,0},{4,7},{5,6},{6,5},{7,4},{8,11},{9,10},{10,... | collective-permute-start | bytes 393224 | tf_op jit(solution)/shard_map/ppermute | solution.py:17
  87.7 11.8 %collective-permute-start.22 = (bf16[128,512]{1,0:T(8,128)(2,1)S(1)}, bf16[128,512]{1,0:T(8,128)(2,1)S(1)}, u32[]{:S(2)}, u32[]{:S(2)}) collective-permute-start(bf16[128,512]{1,0:T(8,128)(2,1)S(1)} %pad_maximum_fusion.4), channel_id=1, source_target_pairs={{0,2},{1,3},{2,0},{3,1},{4,6},{5,7},{6,4},{7,5},{8,10},{9,11},{10,... | collective-permute-start | bytes 393224 | tf_op jit(solution)/shard_map/ppermute | solution.py:17
  88.1 5.8 %collective-permute-start.21 = (bf16[128,512]{1,0:T(8,128)(2,1)S(1)}, bf16[128,512]{1,0:T(8,128)(2,1)S(1)}, u32[]{:S(2)}, u32[]{:S(2)}) collective-permute-start(bf16[128,512]{1,0:T(8,128)(2,1)S(1)} %pad_maximum_fusion.4), channel_id=1, source_target_pairs={{0,1},{1,0},{2,3},{3,2},{4,5},{5,4},{6,7},{7,6},{8,9},{9,8},{10,11... | collective-permute-start | bytes 393224 | tf_op jit(solution)/shard_map/ppermute | solution.py:17
  105.9 3.6 %collective-permute-start.24 = (f32[4,3]{0,1:T(4,128)S(1)}, f32[4,3]{0,1:T(4,128)S(1)}, u32[]{:S(2)}, u32[]{:S(2)}) collective-permute-start(f32[4,3]{0,1:T(4,128)S(1)} %pad_maximum_fusion.5), channel_id=1, source_target_pairs={{0,1},{1,0},{2,3},{3,2},{4,5},{5,4},{6,7},{7,6},{8,9},{9,8},{10,11... | collective-permute-start | bytes 152 | tf_op jit(solution)/shard_map/ppermute | solution.py:17
  109.5 4.5 %collective-permute-start.25 = (f32[4,3]{0,1:T(4,128)S(1)}, f32[4,3]{0,1:T(4,128)S(1)}, u32[]{:S(2)}, u32[]{:S(2)}) collective-permute-start(f32[4,3]{0,1:T(4,128)S(1)} %fusion.30), channel_id=1, source_target_pairs={{0,2},{1,3},{2,0},{3,1},{4,6},{5,7},{6,4},{7,5},{8,10},{9,11},{10,... | collective-permute-start | bytes 152 | tf_op jit(solution)/shard_map/ppermute | solution.py:17
  114.1 3.6 %collective-permute-start.26 = (f32[4,3]{0,1:T(4,128)S(1)}, f32[4,3]{0,1:T(4,128)S(1)}, u32[]{:S(2)}, u32[]{:S(2)}) collective-permute-start(f32[4,3]{0,1:T(4,128)S(1)} %add.156), channel_id=1, source_target_pairs={{0,4},{4,0},{8,12},{12,8},{1,5},{5,1},{9,13},{13,9},{2,6},{6,2},{1... | collective-permute-start | bytes 152 | tf_op jit(solution)/shard_map/ppermute | solution.py:17
  117.7 4.7 %collective-permute-start.27 = (f32[4,3]{0,1:T(4,128)S(1)}, f32[4,3]{0,1:T(4,128)S(1)}, u32[]{:S(2)}, u32[]{:S(2)}) collective-permute-start(f32[4,3]{0,1:T(4,128)S(1)} %add.157), channel_id=1, source_target_pairs={{0,8},{4,12},{8,0},{12,4},{1,9},{5,13},{9,1},{13,5},{2,10},{6,14},... | collective-permute-start | bytes 152 | tf_op jit(solution)/shard_map/ppermute | solution.py:17
  119.4 4.2 %copy-start.6 = (f32[3]{0:T(128)S(1)}, f32[3]{0:T(128)}, u32[]{:S(2)}) copy-start(f32[3]{0:T(128)} %constant.97) | copy-start | bytes 40
  122.4 1.2 collective-permute-start.28

commit v3 on v2

--- a/solution.py
+++ b/solution.py
@@ -66,6 +66,7 @@
 
 def load_weights(*weights):
     total = sum(w.size * 2 for w in weights)
+    weights = [pltpu.with_memory_space_constraint(w, pltpu.HBM) for w in weights]
     return pl.pallas_call(
         load_kernel,
         in_specs=[pl.BlockSpec(memory_space=pltpu.HBM)] * len(weights),
@@ -152,14 +153,8 @@
         up = jnp.dot(normed, up_w, preferred_element_type=jnp.float32)
         return widened, scale, gate, up
 
-    id_rows = -(-micro // 16) * 16
-    id_block = jnp.broadcast_to(
-        jnp.pad(domain_ids.astype(jnp.bfloat16), ((0, id_rows - micro), (0, 0))), (id_rows, units)
-    )
-
-    def gather_hidden(hidden, section):
-        gathered = jnp.concatenate([hidden, id_block], axis=0)[None]
-        for bit in range(bits("dp")):
+    def gather_hidden(gathered, section, begin, end):
+        for bit in range(begin, end):
             other = swap_in(gathered, section, "dp", 2**bit)
             gathered = jnp.concatenate([gathered, other], axis=0)
         return gathered
@@ -167,10 +162,13 @@
     _, _, gate0, up0 = layer_parts(rows_in)
     hidden0 = (jax.nn.silu(gate0) * up0).astype(jnp.bfloat16)
     mixed = jnp.dot(hidden0, down_w, preferred_element_type=jnp.float32).astype(jnp.bfloat16)
-    cot_rows, mixed = lax.optimization_barrier((rows_in, mixed))
+    cot_rows, hidden0, mixed = lax.optimization_barrier((rows_in, hidden0, mixed))
     d_hidden = lax.dot_general(cot_rows, down_w, CONTRACT_LAST, preferred_element_type=jnp.float32)
-    x1 = gather_rows(scatter_sum(x_own, mixed, 0, block), 1)
-    gathered0 = gather_hidden(hidden0, 0)
+    some0 = gather_hidden(hidden0, 0, 0, 1)
+    x1_own = scatter_sum(x_own, mixed, 0, block)
+    x1_own, d_hidden, some0 = lax.optimization_barrier((x1_own, d_hidden, some0))
+    x1 = gather_rows(x1_own, 1)
+    all0 = gather_hidden(some0, 0, 1, bits("dp"))
 
     widened, scale, gate, up = layer_parts(x1)
     sig = jax.nn.sigmoid(gate)
@@ -184,30 +182,40 @@
     pulled = d_normed * gain
     along = jnp.sum(pulled * widened, axis=-1, keepdims=True) / width
     term = (pulled * scale - widened * (scale * scale * scale * along)).astype(jnp.bfloat16)
-    hidden1, term = lax.optimization_barrier((hidden1, term))
+    term, all0 = lax.optimization_barrier((term, all0))
     dy_own = scatter_sum(cot_own, term, 1, block)
     dy_own = jnp.where(first, dy_own, cot_own)
+    dy_own, hidden1 = lax.optimization_barrier((dy_own, hidden1))
 
     piece = width // dp_size
-    columns = []
+    id_rows = -(-micro // 16) * 16
+    id_block = jnp.broadcast_to(
+        jnp.pad(domain_ids.astype(jnp.bfloat16), ((0, id_rows - micro), (0, 0))), (id_rows, piece)
+    )
+    messages = []
     for k in range(dp_size):
         part = lax.dynamic_slice_in_dim(dy_own, (dp_index ^ k) * piece, piece, axis=1)
-        columns.append(part if k == 0 else swap(part, "dp", k))
-    y = gather_rows(jnp.concatenate(columns, axis=0))
-
-    gathered = jnp.where(first, gathered0, gather_hidden(hidden1, 1))
-    hidden_all = gathered[:, :tok_rows].reshape(dp_size, tensor_size, block, units)
-    hidden_all = jnp.swapaxes(hidden_all, 0, 1).reshape(dp_size * tok_rows, units)
-    ids_all = gathered[:, tok_rows : tok_rows + micro, 0].astype(jnp.int32)
-    row_ids = jnp.broadcast_to(
-        ids_all[None, :, :, None], (tensor_size, dp_size, micro, local_rows)
-    ).reshape(dp_size * tok_rows, 1)
+        part = jnp.concatenate([part, id_block], axis=0)
+        messages.append(part if k == 0 else swap(part, "dp", k))
+    all1 = gather_hidden(hidden1, 1, 0, bits("dp"))
+    hidden_all = jnp.where(first, all0, all1)
     gram_hidden = lax.dot_general(
         hidden_all, hidden_all, CONTRACT_LAST, preferred_element_type=jnp.float32
     )
+    columns = jnp.concatenate([message[:block] for message in messages], axis=0)
+    columns, hidden_all, gram_hidden = lax.optimization_barrier(
+        (columns, hidden_all, gram_hidden)
+    )
+    y = gather_rows(columns).reshape(tensor_size, dp_size, block, piece)
+    y = jnp.swapaxes(y, 0, 1).reshape(dp_size * tok_rows, piece)
+    ids_all = jnp.stack([message[block : block + micro, 0] for message in messages])
+    row_ids = jnp.broadcast_to(
+        ids_all.astype(jnp.int32)[:, None, :, None], (dp_size, tensor_size, micro, local_rows)
+    ).reshape(dp_size * tok_rows, 1)
+
     gram_y = lax.dot_general(y, y, CONTRACT_LAST, preferred_element_type=jnp.float32)
     pairs = jnp.where(row_ids == row_ids.T, gram_hidden * gram_y, 0.0)
-    replica = jnp.arange(tok_rows * dp_size) // block % dp_size
+    replica = jnp.arange(tok_rows * dp_size) // tok_rows
     onehot = (row_ids == jnp.arange(DOMAINS)[None, :]).astype(jnp.float32)
     levels = dp_size.bit_length()
     sums = []
@@ -218,7 +226,7 @@
     norms = jnp.stack(sums, axis=1)
     rounds = [(axis, bit) for axis in ("tensor", "dp", "section") for bit in range(bits(axis))]
     tiles = units // TILE
-    parts = min(len(rounds) - 1, tiles)
+    parts = min(3, tiles)
     grads = None
     begin = 0
     for part, (axis, bit) in enumerate(rounds):

time: 125 us -> 129 us (1.032)
  starting transfers between devices: 38.9 us -> 53 us
  waiting for transfers between devices: 40.1 us -> 30.7 us
  local copies, waits for them, and re-layouts: 8.36 us -> 1.98 us
  other arithmetic: 3.13 us -> 7.75 us
    ppermute x14, starting transfers between devices: 16.4 us -> 29.7 us  [swap(): return lax.ppermute(block, axis, [(i, i ^ offset) for i in range(size)])]
    ppermute x14, waiting for transfers between devices: 25.7 us -> 14.7 us  [swap(): return lax.ppermute(block, axis, [(i, i ^ offset) for i in range(size)])]
    ppermute x7, waiting for transfers between devices: 2.05 us -> 10.5 us  [swap_in(): return lax.ppermute(block, ('section', axis), route)]
    ppermute x8, waiting for transfers between devices: 12.3 us -> 5.53 us  [across(): return lax.ppermute(block, ('section', 'tensor'), route)]
    unnamed x22 -> x11, local copies, waits for them, and re-layouts: 4.39 us -> 0.7 us
    reduce_sum x0 -> x1, other arithmetic: none -> 1.89 us  [shards(): jnp.sum(jnp.where(group[:, None] == group[None, :], pairs, 0.0), axis=1)]
    select_n x1, other arithmetic: 0.42 us -> 2.16 us  [shards(): hidden_all = jnp.where(first, all0, all1)]
    pallas_call x1, Pallas kernels: 5.68 us -> 7.28 us  [load_weights(): pl.pallas_call(load_kernel, in_specs=[pl.BlockSpec(memory_space=pltpu.HBM...]
  transfers between devices with their start and end apart: 29 -> 29, of which waited for: 16 -> 13; matrix products, arithmetic and copies ran while one was open for 3% -> 9% of each run, Pallas kernels for 13% -> 13%
where the time goes in v3:
time: 129 us; the launch traced here: 128 us
  starting transfers between devices  53 us (41%)
  waiting for transfers between devices  30.7 us (24%)
  Pallas kernels  17.2 us (13%)
  matrix products  16.6 us (13%)
  other arithmetic  7.75 us (6%)
  local copies, waits for them, and re-layouts  1.98 us (2%)
    ppermute x14, starting transfers between devices, swap(): return lax.ppermute(block, axis, [(i, i ^ offset) for i in range(size)])  29.7 us
    ppermute x14, waiting for transfers between devices, swap(): return lax.ppermute(block, axis, [(i, i ^ offset) for i in range(size)])  14.7 us
    ppermute x8, starting transfers between devices, across(): return lax.ppermute(block, ('section', 'tensor'), route)  12.2 us
    ppermute x7, starting transfers between devices, swap_in(): return lax.ppermute(block, ('section', axis), route)  11.1 us
    ppermute x7, waiting for transfers between devices, swap_in(): return lax.ppermute(block, ('section', axis), route)  10.5 us
    pallas_call x3, Pallas kernels, domain_gradients(): pl.pallas_call(gradient_kernel, grid=(count,), in_specs=in_specs, out_spe...  9.93 us
    pallas_call x1, Pallas kernels, load_weights(): pl.pallas_call(load_kernel, in_specs=[pl.BlockSpec(memory_space=pltpu.HBM...  7.28 us
    ppermute x8, waiting for transfers between devices, across(): return lax.ppermute(block, ('section', 'tensor'), route)  5.53 us
  transfers between devices with their start and end apart: 29, of which 13 were waited for; matrix products, arithmetic and copies ran while one was open for 9% of the time, Pallas kernels for 13%

profile of v3, /device:TPU:0, one launch (start us, length us, event | category | flops | bytes accessed | tf_op | source)
XLA Modules:
  0.0 128.4 jit_solution(1955302807075542354)
XLA Ops:
  0.6 1.0 bitcast_select_fusion
  1.6 5.1 %collective-permute-start.2 = (bf16[32,2048]{1,0:T(8,128)(2,1)S(1)}, bf16[32,2048]{1,0:T(8,128)(2,1)S(1)}, u32[]{:S(2)}, u32[]{:S(2)}) collective-permute-start(bf16[32,2048]{1,0:T(8,128)(2,1)S(1)} %bitcast_select_fusion), channel_id=1, source_target_pairs={{0,3},{1,2},{2,1},{3,0},{4,7},{5,6},{6,5},{7,4},{8,11},{9,10},{10,... | collective-permute-start | bytes 393224 | tf_op jit(solution)/shard_map/ppermute | solution.py:17
  7.4 7.3 %shard_map.95 = (bf16[2048,1792]{1,0:T(8,128)(2,1)S(1)}, bf16[2048,1792]{1,0:T(8,128)(2,1)S(1)}, bf16[1792,2048]{1,0:T(8,128)(2,1)S(1)}) custom-call(bf16[1,2048,1792]{2,1,0:T(8,128)(2,1)} %refs_0_.1, bf16[1,2048,1792]{2,1,0:T(8,128)(2,1)} %refs_1_.1, bf16[1,1792,2048]{2,1,0:T(8,128)(2,1)} %refs_2_.1), custom_call_target="tpu_custom_call" | custom-call | bytes 22020096 | tf_op jit(solution)/shard_map/pallas_call | solution.py:70
  14.7 3.1 %collective-permute-done.1 = bf16[32,2048]{1,0:T(8,128)(2,1)S(1)} collective-permute-done((bf16[32,2048]{1,0:T(8,128)(2,1)S(1)}, bf16[32,2048]{1,0:T(8,128)(2,1)S(1)}, u32[]{:S(2)}, u32[]{:S(2)}) %collective-permute-start.1) | collective-permute-done | bytes 131104 | tf_op jit(solution)/shard_map/ppermute | solution.py:17
  18.0 1.2 fusion.20
  19.2 1.4 %fusion.1 = bf16[128,1792]{1,0:T(8,128)(2,1)S(1)} fusion(bf16[2048,1792]{1,0:T(8,128)(2,1)S(1)} %get-tuple-element.24, f32[128,1792]{1,0:T(8,128)S(1)} %fusion.20, bf16[128,2048]{1,0:T(8,128)(2,1)S(1)} %get-tuple-element.27, f32[2048]{0:T(1024)S(1)} %bitcast.43, f32[128]{0:T(128)S(1)} %add_rsqrt_fusion.1), kind=kOutput, calls=%fused_computation.3 | convolution fusion | flops 941948928 | bytes 9249280 | tf_op jit(solution)/shard_map/dot_general | solution.py:153
  20.6 1.2 convolution_convert_fusion
  21.9 3.0 %collective-permute-start.6 = (bf16[32,2048]{1,0:T(8,128)(2,1)S(1)}, bf16[32,2048]{1,0:T(8,128)(2,1)S(1)}, u32[]{:S(2)}, u32[]{:S(2)}) collective-permute-start(bf16[32,2048]{1,0:T(8,128)(2,1)S(1)} %get-tuple-element.63), channel_id=1, source_target_pairs={{0,19},{1,18},{2,17},{3,16},{4,23},{5,22},{6,21},{7,20},{8,27},{9,... | collective-permute-start | bytes 393224 | tf_op jit(solution)/shard_map/ppermute | solution.py:31
  24.8 1.3 %collective-permute-start.5 = (bf16[32,2048]{1,0:T(8,128)(2,1)S(1)}, bf16[32,2048]{1,0:T(8,128)(2,1)S(1)}, u32[]{:S(2)}, u32[]{:S(2)}) collective-permute-start(bf16[32,2048]{1,0:T(8,128)(2,1)S(1)} %get-tuple-element.64), channel_id=1, source_target_pairs={{0,18},{1,19},{2,16},{3,17},{4,22},{5,23},{6,20},{7,21},{8,26},{9,... | collective-permute-start | bytes 393224 | tf_op jit(solution)/shard_map/ppermute | solution.py:31
  26.1 1.3 %collective-permute-start.4 = (bf16[32,2048]{1,0:T(8,128)(2,1)S(1)}, bf16[32,2048]{1,0:T(8,128)(2,1)S(1)}, u32[]{:S(2)}, u32[]{:S(2)}) collective-permute-start(bf16[32,2048]{1,0:T(8,128)(2,1)S(1)} %get-tuple-element.65), channel_id=1, source_target_pairs={{0,17},{1,16},{2,19},{3,18},{4,21},{5,20},{6,23},{7,22},{8,25},{9,... | collective-permute-start | bytes 393224 | tf_op jit(solution)/shard_map/ppermute | solution.py:31
  27.4 1.3 %collective-permute-start.3 = (bf16[32,2048]{1,0:T(8,128)(2,1)S(1)}, bf16[32,2048]{1,0:T(8,128)(2,1)S(1)}, u32[]{:S(2)}, u32[]{:S(2)}) collective-permute-start(bf16[32,2048]{1,0:T(8,128)(2,1)S(1)} %get-tuple-element.62), channel_id=1, source_target_pairs={{0,16},{1,17},{2,18},{3,19},{4,20},{5,21},{6,22},{7,23},{8,24},{9,... | collective-permute-start | bytes 393224 | tf_op jit(solution)/shard_map/ppermute | solution.py:31
  28.8 2.6 %fusion.34 = f32[128,1792]{1,0:T(8,128)S(1)} fusion(bf16[128,2048]{1,0:T(8,128)(2,1)S(1)} %get-tuple-element.27, bf16[1792,2048]{1,0:T(8,128)(2,1)S(1)} %get-tuple-element.25), kind=kOutput, calls=%fused_computation.84 | convolution fusion | flops 939524096 | bytes 8781824 | tf_op jit(solution)/shard_map/dot_general | solution.py:166
  31.3 3.4 %collective-permute-start.7 = (bf16[128,1792]{1,0:T(8,128)(2,1)S(1)}, bf16[128,1792]{1,0:T(8,128)(2,1)S(1)}, u32[]{:S(2)}, u32[]{:S(2)}) collective-permute-start(bf16[128,1792]{1,0:T(8,128)(2,1)S(1)} %fusion.1), channel_id=1, source_target_pairs={{0,4},{4,0},{8,12},{12,8},{1,5},{5,1},{9,13},{13,9},{2,6},{6,2},{1... | collective-permute-start | bytes 1376264 | tf_op jit(solution)/shard_map/ppermute | solution.py:23
  34.9 6.8 %collective-permute-done.7 = bf16[128,1792]{1,0:T(8,128)(2,1)S(1)} collective-permute-done((bf16[128,1792]{1,0:T(8,128)(2,1)S(1)}, bf16[128,1792]{1,0:T(8,128)(2,1)S(1)}, u32[]{:S(2)}, u32[]{:S(2)}) %collective-permute-start.7) | collective-permute-done | bytes 458784 | tf_op jit(solution)/shard_map/ppermute | solution.py:23
  43.8 3.4 %collective-permute-start.11 = (bf16[256,1792]{1,0:T(8,128)(2,1)S(1)}, bf16[256,1792]{1,0:T(8,128)(2,1)S(1)}, u32[]{:S(2)}, u32[]{:S(2)}) collective-permute-start(bf16[256,1792]{1,0:T(8,128)(2,1)S(1)} %pad_maximum_fusion.1), channel_id=1, source_target_pairs={{0,8},{4,12},{8,0},{12,4},{1,9},{5,13},{9,1},{13,5},{2,10},{6,14},... | collective-permute-start | bytes 2752520 | tf_op jit(solution)/shard_map/ppermute | solution.py:23
  47.5 1.2 fusion.15
  48.7 1.4 %multiply_convert_fusion = (bf16[128,1792]{1,0:T(8,128)(2,1)S(1)}, f32[128,1792]{1,0:T(8,128)S(1)}) fusion(f32[128,1792]{1,0:T(8,128)S(1)} %fusion.15, bf16[2048,1792]{1,0:T(8,128)(2,1)S(1)} %get-tuple-element.24, f32[128]{0:T(128)S(1)} %add_rsqrt_fusion, f32[2048]{0:T(1024)S(1)} %bitcast.45, bf16[32,2048]{1,0:T(8,128)(2,1)S(1)} %collective-permute-done.10, ...), kind=kOutput, calls=%fused_computation.28 | convolution fusion | flops 943783936 | bytes 10166784 | tf_op jit(solution)/shard_map/dot_general | solution.py:153
  50.1 2.5 %fusion.11 = f32[128,2048]{1,0:T(8,128)S(1)} fusion(bf16[2048,1792]{1,0:T(8,128)(2,1)S(1)} %get-tuple-element.23, f32[128,1792]{1,0:T(8,128)S(1)} %fusion.15, f32[128,1792]{1,0:T(8,128)S(1)} %fusion.34, f32[128,1792]{1,0:T(8,128)S(1)} %get-tuple-element.78), kind=kOutput, calls=%fused_computation.35 | convolution fusion | flops 941817856 | bytes 11141120 | tf_op jit(solution)/shard_map/dot_general | solution.py:178
  52.6 2.6 %fusion.8 = (f32[128]{0:T(128)S(1)}, f32[128,2048]{1,0:T(8,128)S(1)}) fusion(bf16[32,2048]{1,0:T(8,128)(2,1)S(1)} %collective-permute-done.10, bf16[32,2048]{1,0:T(8,128)(2,1)S(1)} %collective-permute-done.9, bf16[32,2048]{1,0:T(8,128)(2,1)S(1)} %collective-permute-done.8, bf16[32,2048]{1,0:T(8,128)(2,1)S(1)} %add_convert_fusion.1, f32[2048]{0:T(1024)S(1)} %bitcast.46, ...), kind=kOutput, calls=%fused_computation.19 | convolution fusion | flops 944045952 | bytes 11805184 | tf_op jit(solution)/shard_map/dot_general | solution.py:179
  55.4 3.7 %collective-permute-done.11 = bf16[256,1792]{1,0:T(8,128)(2,1)S(1)} collective-permute-done((bf16[256,1792]{1,0:T(8,128)(2,1)S(1)}, bf16[256,1792]{1,0:T(8,128)(2,1)S(1)}, u32[]{:S(2)}, u32[]{:S(2)}) %collective-permute-start.11) | collective-permute-done | bytes 917536 | tf_op jit(solution)/shard_map/ppermute | solution.py:23
  59.1 1.3 %pad_maximum_fusion = bf16[512,1792]{1,0:T(8,128)(2,1)} fusion(bf16[256,1792]{1,0:T(8,128)(2,1)S(1)} %collective-permute-done.11, bf16[256,1792]{1,0:T(8,128)(2,1)S(1)} %pad_maximum_fusion.1), kind=kLoop, calls=%fused_computation.5 | loop fusion | flops 3670016 | bytes 3670016 | tf_op jit(solution)/shard_map/concatenate | solution.py:159
  60.5 1.5 %collective-permute-start.15 = (bf16[32,2048]{1,0:T(8,128)(2,1)S(1)}, bf16[32,2048]{1,0:T(8,128)(2,1)S(1)}, u32[]{:S(2)}, u32[]{:S(2)}) collective-permute-start(bf16[32,2048]{1,0:T(8,128)(2,1)S(1)} %get-tuple-element.59), channel_id=1, source_target_pairs={{16,3},{17,2},{18,1},{19,0},{20,7},{21,6},{22,5},{23,4},{24,11},{2... | collective-permute-start | bytes 393224 | tf_op jit(solution)/shard_map/ppermute | solution.py:31
  62.0 1.3 %collective-permute-start.14 = (bf16[32,2048]{1,0:T(8,128)(2,1)S(1)}, bf16[32,2048]{1,0:T(8,128)(2,1)S(1)}, u32[]{:S(2)}, u32[]{:S(2)}) collective-permute-start(bf16[32,2048]{1,0:T(8,128)(2,1)S(1)} %get-tuple-element.60), channel_id=1, source_target_pairs={{16,2},{17,3},{18,0},{19,1},{20,6},{21,7},{22,4},{23,5},{24,10},{2... | collective-permute-start | bytes 393224 | tf_op jit(solution)/shard_map/ppermute | solution.py:31
  63.3 1.3 %collective-permute-start.13 = (bf16[32,2048]{1,0:T(8,128)(2,1)S(1)}, bf16[32,2048]{1,0:T(8,128)(2,1)S(1)}, u32[]{:S(2)}, u32[]{:S(2)}) collective-permute-start(bf16[32,2048]{1,0:T(8,128)(2,1)S(1)} %get-tuple-element.61), channel_id=1, source_target_pairs={{16,1},{17,0},{18,3},{19,2},{20,5},{21,4},{22,7},{23,6},{24,9},{25... | collective-permute-start | bytes 393224 | tf_op jit(solution)/shard_map/ppermute | solution.py:31
  64.6 1.3 %collective-permute-start.12 = (bf16[32,2048]{1,0:T(8,128)(2,1)S(1)}, bf16[32,2048]{1,0:T(8,128)(2,1)S(1)}, u32[]{:S(2)}, u32[]{:S(2)}) collective-permute-start(bf16[32,2048]{1,0:T(8,128)(2,1)S(1)} %get-tuple-element.58), channel_id=1, source_target_pairs={{16,0},{17,1},{18,2},{19,3},{20,4},{21,5},{22,6},{23,7},{24,8},{25... | collective-permute-start | bytes 393224 | tf_op jit(solution)/shard_map/ppermute | solution.py:31
  65.9 2.8 %collective-permute-done.15 = bf16[32,2048]{1,0:T(8,128)(2,1)S(1)} collective-permute-done((bf16[32,2048]{1,0:T(8,128)(2,1)S(1)}, bf16[32,2048]{1,0:T(8,128)(2,1)S(1)}, u32[]{:S(2)}, u32[]{:S(2)}) %collective-permute-start.15) | collective-permute-done | bytes 131104 | tf_op jit(solution)/shard_map/ppermute | solution.py:31
  68.7 2.7 %collective-permute-done.14 = bf16[32,2048]{1,0:T(8,128)(2,1)S(1)} collective-permute-done((bf16[32,2048]{1,0:T(8,128)(2,1)S(1)}, bf16[32,2048]{1,0:T(8,128)(2,1)S(1)}, u32[]{:S(2)}, u32[]{:S(2)}) %collective-permute-start.14) | collective-permute-done | bytes 131104 | tf_op jit(solution)/shard_map/ppermute | solution.py:31
  71.5 0.7 collective-permute-start.19
  72.3 1.6 %collective-permute-start.20 = (bf16[256,1792]{1,0:T(8,128)(2,1)S(1)}, bf16[256,1792]{1,0:T(8,128)(2,1)}, u32[]{:S(2)}, u32[]{:S(2)}) collective-permute-start(bf16[256,1792]{1,0:T(8,128)(2,1)S(1)} %pad_maximum_fusion.2), channel_id=1, source_target_pairs={{16,24},{20,28},{24,16},{28,20},{17,25},{21,29},{25,17},{29,21},{1... | collective-permute-start | bytes 2752520 | tf_op jit(solution)/shard_map/ppermute | solution.py:23
  74.1 2.5 %collective-permute-start.18 = (bf16[48,512]{1,0:T(8,128)(2,1)S(1)}, bf16[48,512]{1,0:T(8,128)(2,1)S(1)}, u32[]{:S(2)}, u32[]{:S(2)}) collective-permute-start(bf16[48,512]{1,0:T(8,128)(2,1)S(1)} %get-tuple-element.74), channel_id=1, source_target_pairs={{0,12},{4,8},{8,4},{12,0},{1,13},{5,9},{9,5},{13,1},{2,14},{6,10},... | collective-permute-start | bytes 147464 | tf_op jit(solution)/shard_map/ppermute | solution.py:17
  77.7 2.1 %collective-permute-done.18 = bf16[48,512]{1,0:T(8,128)(2,1)S(1)} collective-permute-done((bf16[48,512]{1,0:T(8,128)(2,1)S(1)}, bf16[48,512]{1,0:T(8,128)(2,1)S(1)}, u32[]{:S(2)}, u32[]{:S(2)}) %collective-permute-start.18) | collective-permute-done | bytes 49184 | tf_op jit(solution)/shard_map/ppermute | solution.py:17
  79.7 1.0 collective-permute-done.17
  81.5 2.2 %maximum_select_fusion.hidden_ref = bf16[512,1792]{1,0:T(8,128)(2,1)S(1)} fusion(bf16[512,1792]{1,0:T(8,128)(2,1)} %pad_maximum_fusion, bf16[256,1792]{1,0:T(8,128)(2,1)} %collective-permute-done.20, bf16[128,1792]{1,0:T(8,128)(2,1)S(1)} %collective-permute-done.19, bf16[128,1792]{1,0:T(8,128)(2,1)S(1)} %get-tuple-element.35, pred[]{:T(512)S(6)} %eq.34), kind=kLoop, calls=%fused_computation.6 | loop fusion | flops 6422528 | bytes 5505025 | tf_op jit(solution)/shard_map/jit(_where)/select_n | solution.py:201
  83.6 2.1 %fusion.35 = f32[512,512]{1,0:T(8,128)} fusion(bf16[512,1792]{1,0:T(8,128)(2,1)S(1)} %maximum_select_fusion.hidden_ref), kind=kOutput, calls=%fused_computation.85 | convolution fusion | flops 939524096 | bytes 2883584 | tf_op jit(solution)/shard_map/dot_general | solution.py:202
  85.8 1.8 %collective-permute-start.23 = (bf16[128,512]{1,0:T(8,128)(2,1)S(1)}, bf16[128,512]{1,0:T(8,128)(2,1)S(1)}, u32[]{:S(2)}, u32[]{:S(2)}) collective-permute-start(bf16[128,512]{1,0:T(8,128)(2,1)S(1)} %pad_maximum_fusion.6), channel_id=1, source_target_pairs={{0,3},{1,2},{2,1},{3,0},{4,7},{5,6},{6,5},{7,4},{8,11},{9,10},{10,... | collective-permute-start | bytes 393224 | tf_op jit(solution)/shard_map/ppermute | solution.py:17
  87.6 2.5 %collective-permute-start.21 = (bf16[128,512]{1,0:T(8,128)(2,1)S(1)}, bf16[128,512]{1,0:T(8,128)(2,1)S(1)}, u32[]{:S(2)}, u32[]{:S(2)}) collective-permute-start(bf16[128,512]{1,0:T(8,128)(2,1)S(1)} %pad_maximum_fusion.6), channel_id=1, source_target_pairs={{0,1},{1,0},{2,3},{3,2},{4,5},{5,4},{6,7},{7,6},{8,9},{9,8},{10,11... | collective-permute-start | bytes 393224 | tf_op jit(solution)/shard_map/ppermute | solution.py:17
  90.7 2.0 %collective-permute-done.23 = bf16[128,512]{1,0:T(8,128)(2,1)S(1)} collective-permute-done((bf16[128,512]{1,0:T(8,128)(2,1)S(1)}, bf16[128,512]{1,0:T(8,128)(2,1)S(1)}, u32[]{:S(2)}, u32[]{:S(2)}) %collective-permute-start.23) | collective-permute-done | bytes 131104 | tf_op jit(solution)/shard_map/ppermute | solution.py:17
  92.7 2.7 %collective-permute-done.22 = bf16[128,512]{1,0:T(8,128)(2,1)S(1)} collective-permute-done((bf16[128,512]{1,0:T(8,128)(2,1)S(1)}, bf16[128,512]{1,0:T(8,128)(2,1)S(1)}, u32[]{:S(2)}, u32[]{:S(2)}) %collective-permute-start.22) | collective-permute-done | bytes 131104 | tf_op jit(solution)/shard_map/ppermute | solution.py:17
  95.9 1.9 %select_reduce_fusion.2 = (f32[512]{0:T(512)S(1)}, f32[512]{0:T(512)S(1)}, f32[512]{0:T(512)S(1)}) fusion(s32[512]{0:T(512)S(1)} %fusion.26, s32[512]{0:T(512)S(1)} %get-tuple-element.79, s32[512]{0:T(512)S(1)} %get-tuple-element.80, f32[512,512]{1,0:T(8,128)} %fusion.35, f32[512,512]{1,0:T(8,128)S(1)} %fusion.36, s32[512]{0:T(512)S(1)} %eq.35), kind=kLoop, calls=%fused_computation.24 | loop fusion | flops 3144192 | bytes 2111488 | tf_op jit(solution)/shard_map/reduce_sum | solution.py:224
  98.1 3.0 %shard_map.96.rest_0_ = bf16[4,1792,512]{2,1,0:T(8,128)(2,1)} custom-call(s32[512,1]{1,0:T(8,128)S(1)} %copy.23.ids_ref, bf16[512,1792]{1,0:T(8,128)(2,1)S(1)} %maximum_select_fusion.hidden_ref, bf16[512,512]{1,0:T(8,128)(2,1)S(1)} %bitcast.37), custom_call_target="tpu_custom_call" | custom-call | flops 1073741824 | bytes 2621440 | tf_op jit(solution)/shard_map/pallas_call | solution.py:112
  101.6 1.9 %collective-permute-start.25 = (f32[4,3]{0,1:T(4,128)S(1)}, f32[4,3]{0,1:T(4,128)S(1)}, u32[]{:S(2)}, u32[]{:S(2)}) collective-permute-start(f32[4,3]{0,1:T(4,128)S(1)} %fusion.31), channel_id=1, source_target_pairs={{0,2},{1,3},{2,0},{3,1},{4,6},{5,7},{6,4},{7,5},{8,10},{9,11},{10,... | collective-permute-start | bytes 152 | tf_op jit(solution)/shard_map/ppermute | solution.py:17
  103.6 3.0 %shard_map.97.rest_0_ = bf16[4,1792,512]{2,1,0:T(8,128)(2,1)} custom-call(s32[512,1]{1,0:T(8,128)S(1)} %copy.24.ids_ref, bf16[512,1792]{1,0:T(8,128)(2,1)S(1)} %maximum_select_fusion.hidden_ref, bf16[512,512]{1,0:T(8,128)(2,1)S(1)} %bitcast.38, bf16[4,1792,512]{2,1,0:T(8,128)(2,1)} %shard_map.96.rest_0_), custom_call_target="tpu_custom_call", output_to_operand_aliasing={{}: (3, {})} | custom-call | flops 1073741824 | bytes 2621440 | tf_op jit(solution)/shard_map/pallas_call | solution.py:112
  106.8 0.8 collective-permute-start.26
  107.6 3.9 %shard_map.98 = bf16[4,1792,512]{2,1,0:T(8,128)(2,1)} custom-call(s32[512,1]{1,0:T(8,128)S(1)} %copy.25.ids_ref, bf16[512,1792]{1,0:T(8,128)(2,1)S(1)} %maximum_select_fusion.hidden_ref, bf16[512,512]{1,0:T(8,128)(2,1)S(1)} %bitcast.39, bf16[4,1792,512]{2,1,0:T(8,128)(2,1)} %shard_map.97.rest_0_), custom_call_target="tpu_custom_call", output_to_operand_aliasing={{}: (3, {})} | custom-call | flops 1610612736 | bytes 3932160 | tf_op jit(solution)/shard_map/pallas_call | solution.py:112
  111.5 1.6 %collective-permute-start.27 = (f32[4,3]{0,1:T(4,128)S(1)}, f32[4,3]{0,1:T(4,128)S(1)}, u32[]{:S(2)}, u32[]{:S(2)}) collective-permute-start(f32[4,3]{0,1:T(4,128)S(1)} %add.126), channel_id=1, source_target_pairs={{0,8},{4,12},{8,0},{12,4},{1,9},{5,13},{9,1},{13,5},{2,10},{6,14},... | collective-permute-start | bytes 152 | tf_op jit(solution)/shard_map/ppermute | solution.py:17
  113.1 2.0 %collective-permute-done.27 = f32[4,3]{0,1:T(4,128)S(1)} collective-permute-done((f32[4,3]{0,1:T(4,128)S(1)}, f32[4,3]{0,1:T(4,128)S(1)}, u32[]{:S(2)}, u32[]{:S(2)}) %collective-permute-start.27) | collective-permute-done | bytes 80 | tf_op jit(solution)/shard_map/ppermute | solution.py:17
  115.1 11.7 %collective-permute-start.28 = (f32[4,3]{0,1:T(4,128)S(1)}, f32[4,3]{0,1:T(4,128)S(1)}, u32[]{:S(2)}, u32[]{:S(2)}) collective-permute-start(f32[4,3]{0,1:T(4,128)S(1)} %add.127), channel_id=1, source_target_pairs={{0,16},{16,0},{1,17},{17,1},{2,18},{18,2},{3,19},{19,3},{4,20},{20... | collective-permute-start | bytes 152 | tf_op jit(solution)/shard_map/ppermute | solution.py:17
  126.8 0.8 collective-permute-done.28
  (82 shorter events, 8.7 us)
Async XLA Ops:
  1.6 16.4 %copy-start.2 = (f32[1,2048]{1,0:T(1,128)S(1)}, f32[1,2048]{1,0:T(1,128)}, u32[]{:S(2)}) copy-start(f32[1,2048]{1,0:T(1,128)} %param.11) | copy-start | bytes 24580
  1.6 13.1 %collective-permute-start.2 = (bf16[32,2048]{1,0:T(8,128)(2,1)S(1)}, bf16[32,2048]{1,0:T(8,128)(2,1)S(1)}, u32[]{:S(2)}, u32[]{:S(2)}) collective-permute-start(bf16[32,2048]{1,0:T(8,128)(2,1)S(1)} %bitcast_select_fusion), channel_id=1, source_target_pairs={{0,3},{1,2},{2,1},{3,0},{4,7},{5,6},{6,5},{7,4},{8,11},{9,10},{10,... | collective-permute-start | bytes 393224 | tf_op jit(solution)/shard_map/ppermute | solution.py:17
  6.8 11.1 %collective-permute-start.1 = (bf16[32,2048]{1,0:T(8,128)(2,1)S(1)}, bf16[32,2048]{1,0:T(8,128)(2,1)S(1)}, u32[]{:S(2)}, u32[]{:S(2)}) collective-permute-start(bf16[32,2048]{1,0:T(8,128)(2,1)S(1)} %bitcast_select_fusion), channel_id=1, source_target_pairs={{0,2},{1,3},{2,0},{3,1},{4,6},{5,7},{6,4},{7,5},{8,10},{9,11},{10,... | collective-permute-start | bytes 393224 | tf_op jit(solution)/shard_map/ppermute | solution.py:17
  6.8 11.1 %collective-permute-start = (bf16[32,2048]{1,0:T(8,128)(2,1)S(1)}, bf16[32,2048]{1,0:T(8,128)(2,1)S(1)}, u32[]{:S(2)}, u32[]{:S(2)}) collective-permute-start(bf16[32,2048]{1,0:T(8,128)(2,1)S(1)} %bitcast_select_fusion), channel_id=1, source_target_pairs={{0,1},{1,0},{2,3},{3,2},{4,5},{5,4},{6,7},{7,6},{8,9},{9,8},{10,11... | collective-permute-start | bytes 393224 | tf_op jit(solution)/shard_map/ppermute | solution.py:17
  21.8 13.0 %copy-start = (bf16[4,8,2048]{2,1,0:T(8,128)(2,1)S(1)}, bf16[4,8,2048]{2,1,0:T(8,128)(2,1)}, u32[]{:S(2)}) copy-start(bf16[4,8,2048]{2,1,0:T(8,128)(2,1)} %param.8) | copy-start | bytes 393220
  21.9 12.9 %collective-permute-start.6 = (bf16[32,2048]{1,0:T(8,128)(2,1)S(1)}, bf16[32,2048]{1,0:T(8,128)(2,1)S(1)}, u32[]{:S(2)}, u32[]{:S(2)}) collective-permute-start(bf16[32,2048]{1,0:T(8,128)(2,1)S(1)} %get-tuple-element.63), channel_id=1, source_target_pairs={{0,19},{1,18},{2,17},{3,16},{4,23},{5,22},{6,21},{7,20},{8,27},{9,... | collective-permute-start | bytes 393224 | tf_op jit(solution)/shard_map/ppermute | solution.py:31
  24.8 9.9 %collective-permute-start.5 = (bf16[32,2048]{1,0:T(8,128)(2,1)S(1)}, bf16[32,2048]{1,0:T(8,128)(2,1)S(1)}, u32[]{:S(2)}, u32[]{:S(2)}) collective-permute-start(bf16[32,2048]{1,0:T(8,128)(2,1)S(1)} %get-tuple-element.64), channel_id=1, source_target_pairs={{0,18},{1,19},{2,16},{3,17},{4,22},{5,23},{6,20},{7,21},{8,26},{9,... | collective-permute-start | bytes 393224 | tf_op jit(solution)/shard_map/ppermute | solution.py:31
  26.1 8.6 %collective-permute-start.4 = (bf16[32,2048]{1,0:T(8,128)(2,1)S(1)}, bf16[32,2048]{1,0:T(8,128)(2,1)S(1)}, u32[]{:S(2)}, u32[]{:S(2)}) collective-permute-start(bf16[32,2048]{1,0:T(8,128)(2,1)S(1)} %get-tuple-element.65), channel_id=1, source_target_pairs={{0,17},{1,16},{2,19},{3,18},{4,21},{5,20},{6,23},{7,22},{8,25},{9,... | collective-permute-start | bytes 393224 | tf_op jit(solution)/shard_map/ppermute | solution.py:31
  27.4 7.3 %collective-permute-start.3 = (bf16[32,2048]{1,0:T(8,128)(2,1)S(1)}, bf16[32,2048]{1,0:T(8,128)(2,1)S(1)}, u32[]{:S(2)}, u32[]{:S(2)}) collective-permute-start(bf16[32,2048]{1,0:T(8,128)(2,1)S(1)} %get-tuple-element.62), channel_id=1, source_target_pairs={{0,16},{1,17},{2,18},{3,19},{4,20},{5,21},{6,22},{7,23},{8,24},{9,... | collective-permute-start | bytes 393224 | tf_op jit(solution)/shard_map/ppermute | solution.py:31
  31.3 10.4 %collective-permute-start.7 = (bf16[128,1792]{1,0:T(8,128)(2,1)S(1)}, bf16[128,1792]{1,0:T(8,128)(2,1)S(1)}, u32[]{:S(2)}, u32[]{:S(2)}) collective-permute-start(bf16[128,1792]{1,0:T(8,128)(2,1)S(1)} %fusion.1), channel_id=1, source_target_pairs={{0,4},{4,0},{8,12},{12,8},{1,5},{5,1},{9,13},{13,9},{2,6},{6,2},{1... | collective-permute-start | bytes 1376264 | tf_op jit(solution)/shard_map/ppermute | solution.py:23
  41.8 5.5 %collective-permute-start.10 = (bf16[32,2048]{1,0:T(8,128)(2,1)S(1)}, bf16[32,2048]{1,0:T(8,128)(2,1)S(1)}, u32[]{:S(2)}, u32[]{:S(2)}) collective-permute-start(bf16[32,2048]{1,0:T(8,128)(2,1)S(1)} %add_convert_fusion.1), channel_id=1, source_target_pairs={{16,19},{17,18},{18,17},{19,16},{20,23},{21,22},{22,21},{23,20},{2... | collective-permute-start | bytes 393224 | tf_op jit(solution)/shard_map/ppermute | solution.py:23
  42.5 4.8 %collective-permute-start.9 = (bf16[32,2048]{1,0:T(8,128)(2,1)S(1)}, bf16[32,2048]{1,0:T(8,128)(2,1)S(1)}, u32[]{:S(2)}, u32[]{:S(2)}) collective-permute-start(bf16[32,2048]{1,0:T(8,128)(2,1)S(1)} %add_convert_fusion.1), channel_id=1, source_target_pairs={{16,18},{17,19},{18,16},{19,17},{20,22},{21,23},{22,20},{23,21},{2... | collective-permute-start | bytes 393224 | tf_op jit(solution)/shard_map/ppermute | solution.py:23
  43.1 4.1 %collective-permute-start.8 = (bf16[32,2048]{1,0:T(8,128)(2,1)S(1)}, bf16[32,2048]{1,0:T(8,128)(2,1)S(1)}, u32[]{:S(2)}, u32[]{:S(2)}) collective-permute-start(bf16[32,2048]{1,0:T(8,128)(2,1)S(1)} %add_convert_fusion.1), channel_id=1, source_target_pairs={{16,17},{17,16},{18,19},{19,18},{20,21},{21,20},{22,23},{23,22},{2... | collective-permute-start | bytes 393224 | tf_op jit(solution)/shard_map/ppermute | solution.py:23
  43.8 15.3 %collective-permute-start.11 = (bf16[256,1792]{1,0:T(8,128)(2,1)S(1)}, bf16[256,1792]{1,0:T(8,128)(2,1)S(1)}, u32[]{:S(2)}, u32[]{:S(2)}) collective-permute-start(bf16[256,1792]{1,0:T(8,128)(2,1)S(1)} %pad_maximum_fusion.1), channel_id=1, source_target_pairs={{0,8},{4,12},{8,0},{12,4},{1,9},{5,13},{9,1},{13,5},{2,10},{6,14},... | collective-permute-start | bytes 2752520 | tf_op jit(solution)/shard_map/ppermute | solution.py:23
  52.6 18.8 %copy-start.1 = (bf16[4,8,2048]{2,1,0:T(8,128)(2,1)S(1)}, bf16[4,8,2048]{2,1,0:T(8,128)(2,1)}, u32[]{:S(2)}) copy-start(bf16[4,8,2048]{2,1,0:T(8,128)(2,1)} %param.9) | copy-start | bytes 393220
  52.6 19.6 %copy-start.4 = (s32[4,1]{0,1:T(1,128)S(1)}, s32[4,1]{0,1:T(1,128)}, u32[]{:S(2)}) copy-start(s32[4,1]{0,1:T(1,128)} %param.10) | copy-start | bytes 52
  60.5 8.2 %collective-permute-start.15 = (bf16[32,2048]{1,0:T(8,128)(2,1)S(1)}, bf16[32,2048]{1,0:T(8,128)(2,1)S(1)}, u32[]{:S(2)}, u32[]{:S(2)}) collective-permute-start(bf16[32,2048]{1,0:T(8,128)(2,1)S(1)} %get-tuple-element.59), channel_id=1, source_target_pairs={{16,3},{17,2},{18,1},{19,0},{20,7},{21,6},{22,5},{23,4},{24,11},{2... | collective-permute-start | bytes 393224 | tf_op jit(solution)/shard_map/ppermute | solution.py:31
  62.0 9.4 %collective-permute-start.14 = (bf16[32,2048]{1,0:T(8,128)(2,1)S(1)}, bf16[32,2048]{1,0:T(8,128)(2,1)S(1)}, u32[]{:S(2)}, u32[]{:S(2)}) collective-permute-start(bf16[32,2048]{1,0:T(8,128)(2,1)S(1)} %get-tuple-element.60), channel_id=1, source_target_pairs={{16,2},{17,3},{18,0},{19,1},{20,6},{21,7},{22,4},{23,5},{24,10},{2... | collective-permute-start | bytes 393224 | tf_op jit(solution)/shard_map/ppermute | solution.py:31
  63.3 8.1 %collective-permute-start.13 = (bf16[32,2048]{1,0:T(8,128)(2,1)S(1)}, bf16[32,2048]{1,0:T(8,128)(2,1)S(1)}, u32[]{:S(2)}, u32[]{:S(2)}) collective-permute-start(bf16[32,2048]{1,0:T(8,128)(2,1)S(1)} %get-tuple-element.61), channel_id=1, source_target_pairs={{16,1},{17,0},{18,3},{19,2},{20,5},{21,4},{22,7},{23,6},{24,9},{25... | collective-permute-start | bytes 393224 | tf_op jit(solution)/shard_map/ppermute | solution.py:31
  64.6 6.8 %collective-permute-start.12 = (bf16[32,2048]{1,0:T(8,128)(2,1)S(1)}, bf16[32,2048]{1,0:T(8,128)(2,1)S(1)}, u32[]{:S(2)}, u32[]{:S(2)}) collective-permute-start(bf16[32,2048]{1,0:T(8,128)(2,1)S(1)} %get-tuple-element.58), channel_id=1, source_target_pairs={{16,0},{17,1},{18,2},{19,3},{20,4},{21,5},{22,6},{23,7},{24,8},{25... | collective-permute-start | bytes 393224 | tf_op jit(solution)/shard_map/ppermute | solution.py:31
  71.5 0.7 collective-permute-start.19
  72.3 9.2 %collective-permute-start.20 = (bf16[256,1792]{1,0:T(8,128)(2,1)S(1)}, bf16[256,1792]{1,0:T(8,128)(2,1)}, u32[]{:S(2)}, u32[]{:S(2)}) collective-permute-start(bf16[256,1792]{1,0:T(8,128)(2,1)S(1)} %pad_maximum_fusion.2), channel_id=1, source_target_pairs={{16,24},{20,28},{24,16},{28,20},{17,25},{21,29},{25,17},{29,21},{1... | collective-permute-start | bytes 2752520 | tf_op jit(solution)/shard_map/ppermute | solution.py:23
  74.1 5.6 %collective-permute-start.18 = (bf16[48,512]{1,0:T(8,128)(2,1)S(1)}, bf16[48,512]{1,0:T(8,128)(2,1)S(1)}, u32[]{:S(2)}, u32[]{:S(2)}) collective-permute-start(bf16[48,512]{1,0:T(8,128)(2,1)S(1)} %get-tuple-element.74), channel_id=1, source_target_pairs={{0,12},{4,8},{8,4},{12,0},{1,13},{5,9},{9,5},{13,1},{2,14},{6,10},... | collective-permute-start | bytes 147464 | tf_op jit(solution)/shard_map/ppermute | solution.py:17
  76.6 4.1 %collective-permute-start.17 = (bf16[48,512]{1,0:T(8,128)(2,1)S(1)}, bf16[48,512]{1,0:T(8,128)(2,1)S(1)}, u32[]{:S(2)}, u32[]{:S(2)}) collective-permute-start(bf16[48,512]{1,0:T(8,128)(2,1)S(1)} %get-tuple-element.73), channel_id=1, source_target_pairs={{0,8},{4,12},{8,0},{12,4},{1,9},{5,13},{9,1},{13,5},{2,10},{6,14},... | collective-permute-start | bytes 147464 | tf_op jit(solution)/shard_map/ppermute | solution.py:17
  77.1 4.1 %collective-permute-start.16 = (bf16[48,512]{1,0:T(8,128)(2,1)S(1)}, bf16[48,512]{1,0:T(8,128)(2,1)S(1)}, u32[]{:S(2)}, u32[]{:S(2)}) collective-permute-start(bf16[48,512]{1,0:T(8,128)(2,1)S(1)} %get-tuple-element.72), channel_id=1, source_target_pairs={{0,4},{4,0},{8,12},{12,8},{1,5},{5,1},{9,13},{13,9},{2,6},{6,2},{1... | collective-permute-start | bytes 147464 | tf_op jit(solution)/shard_map/ppermute | solution.py:17
  85.8 6.9 %collective-permute-start.23 = (bf16[128,512]{1,0:T(8,128)(2,1)S(1)}, bf16[128,512]{1,0:T(8,128)(2,1)S(1)}, u32[]{:S(2)}, u32[]{:S(2)}) collective-permute-start(bf16[128,512]{1,0:T(8,128)(2,1)S(1)} %pad_maximum_fusion.6), channel_id=1, source_target_pairs={{0,3},{1,2},{2,1},{3,0},{4,7},{5,6},{6,5},{7,4},{8,11},{9,10},{10,... | collective-permute-start | bytes 393224 | tf_op jit(solution)/shard_map/ppermute | solution.py:17
  87.6 7.7 %collective-permute-start.22 = (bf16[128,512]{1,0:T(8,128)(2,1)S(1)}, bf16[128,512]{1,0:T(8,128)(2,1)S(1)}, u32[]{:S(2)}, u32[]{:S(2)}) collective-permute-start(bf16[128,512]{1,0:T(8,128)(2,1)S(1)} %pad_maximum_fusion.6), channel_id=1, source_target_pairs={{0,2},{1,3},{2,0},{3,1},{4,6},{5,7},{6,4},{7,5},{8,10},{9,11},{10,... | collective-permute-start | bytes 393224 | tf_op jit(solution)/shard_map/ppermute | solution.py:17
  87.6 7.7 %collective-permute-start.21 = (bf16[128,512]{1,0:T(8,128)(2,1)S(1)}, bf16[128,512]{1,0:T(8,128)(2,1)S(1)}, u32[]{:S(2)}, u32[]{:S(2)}) collective-permute-start(bf16[128,512]{1,0:T(8,128)(2,1)S(1)} %pad_maximum_fusion.6), channel_id=1, source_target_pairs={{0,1},{1,0},{2,3},{3,2},{4,5},{5,4},{6,7},{7,6},{8,9},{9,8},{10,11... | collective-permute-start | bytes 393224 | tf_op jit(solution)/shard_map/ppermute | solution.py:17
  98.0 3.6 %collective-permute-start.24 = (f32[4,3]{0,1:T(4,128)S(1)}, f32[4,3]{0,1:T(4,128)S(1)}, u32[]{:S(2)}, u32[]{:S(2)}) collective-permute-start(f32[4,3]{0,1:T(4,128)S(1)} %pad_maximum_fusion.10), channel_id=1, source_target_pairs={{0,1},{1,0},{2,3},{3,2},{4,5},{5,4},{6,7},{7,6},{8,9},{9,8},{10,11... | collective-permute-start | bytes 152 | tf_op jit(solution)/shard_map/ppermute | solution.py:17
  101.6 5.0 %collective-permute-start.25 = (f32[4,3]{0,1:T(4,128)S(1)}, f32[4,3]{0,1:T(4,128)S(1)}, u32[]{:S(2)}, u32[]{:S(2)}) collective-permute-start(f32[4,3]{0,1:T(4,128)S(1)} %fusion.31), channel_id=1, source_target_pairs={{0,2},{1,3},{2,0},{3,1},{4,6},{5,7},{6,4},{7,5},{8,10},{9,11},{10,... | collective-permute-start | bytes 152 | tf_op jit(solution)/shard_map/ppermute | solution.py:17
  106.8 20.8 %copy-start.3 = (f32[3]{0:T(128)S(1)}, f32[3]{0:T(128)}, u32[]{:S(2)}) copy-start(f32[3]{0:T(128)} %constant.82) | copy-start | bytes 40
  106.8 4.7 %collective-permute-start.26 = (f32[4,3]{0,1:T(4,128)S(1)}, f32[4,3]{0,1:T(4,128)S(1)}, u32[]{:S(2)}, u32[]{:S(2)}) collective-permute-start(f32[4,3]{0,1:T(4,128)S(1)} %add.125), channel_id=1, source_target_pairs={{0,4},{4,0},{8,12},{12,8},{1,5},{5,1},{9,13},{13,9},{2,6},{6,2},{1... | collective-permute-start | bytes 152 | tf_op jit(solution)/shard_map/ppermute | solution.py:17
  111.5 3.6 %collective-permute-start.27 = (f32[4,3]{0,1:T(4,128)S(1)}, f32[4,3]{0,1:T(4,128)S(1)}, u32[]{:S(2)}, u32[]{:S(2)}) collective-permute-start(f32[4,3]{0,1:T(4,128)S(1)} %add.126), channel_id=1, source_target_pairs={{0,8},{4,12},{8,0},{12,4},{1,9},{5,13},{9,1},{13,5},{2,10},{6,14},... | collective-permute-start | bytes 152 | tf_op jit(solution)/shard_map/ppermute | solution.py:17
  115.1 12.5 %collective-permute-start.28 = (f32[4,3]{0,1:T(4,128)S(1)}, f32[4,3]{0,1:T(4,128)S(1)}, u32[]{:S(2)}, u32[]{:S(2)}) collective-permute-start(f32[4,3]{0,1:T(4,128)S(1)} %add.127), channel_id=1, source_target_pairs={{0,16},{16,0},{1,17},{17,1},{2,18},{18,2},{3,19},{19,3},{4,20},{20... | collective-permute-start | bytes 152 | tf_op jit(solution)/shard_map/ppermute | solution.py:17

commit v4 on v3

--- a/solution.py
+++ b/solution.py
@@ -1,3 +1,5 @@
+import functools
+
 import jax
 import jax.numpy as jnp
 from jax import lax
@@ -35,13 +37,9 @@
     return lax.axis_size(axis).bit_length() - 1
 
 
-def gather_rows(rows, section=None):
-    size = lax.axis_size("tensor")
-    if section is None:
-        others = [swap(rows, "tensor", k) for k in range(1, size)]
-    else:
-        others = [swap_in(rows, section, "tensor", k) for k in range(1, size)]
-    return jnp.concatenate([rows] + others, axis=0)
+def gather_in(rows, section, axis):
+    size = lax.axis_size(axis)
+    return [rows] + [swap_in(rows, section, axis, k) for k in range(1, size)]
 
 
 def scatter_sum(start, terms, source, block):
@@ -126,6 +124,116 @@
     )(*operands)
 
 
+def assemble_kernel(count, flag_ref, *refs):
+    pieces = refs[: 2 * count]
+    hidden_ref, gram_ref, sems = refs[2 * count :]
+    rows = pieces[0].shape[0]
+    for section in range(2):
+
+        @pl.when(flag_ref[0] == section)
+        def _(section=section):
+            copies = [
+                pltpu.make_async_copy(
+                    pieces[section * count + k],
+                    hidden_ref.at[pl.ds(k * rows, rows)],
+                    sems.at[k],
+                )
+                for k in range(count)
+            ]
+            for copy in copies:
+                copy.start()
+            for copy in copies:
+                copy.wait()
+
+    total = rows * count
+    step = min(total, 512)
+    for begin in range(0, total, step):
+        gram_ref[begin : begin + step, :] = lax.dot_general(
+            hidden_ref[begin : begin + step, :],
+            hidden_ref[...],
+            CONTRACT_LAST,
+            preferred_element_type=jnp.float32,
+        )
+
+
+def assemble(segment, pieces0, pieces1):
+    count = len(pieces0)
+    rows, units = pieces0[0].shape
+    total = rows * count
+    pieces = [pltpu.with_memory_space_constraint(p, pltpu.HBM) for p in pieces0 + pieces1]
+    return pl.pallas_call(
+        functools.partial(assemble_kernel, count),
+        in_specs=[pl.BlockSpec(memory_space=pltpu.SMEM)]
+        + [pl.BlockSpec(memory_space=pl.ANY)] * (2 * count),
+        out_specs=[pl.BlockSpec(memory_space=pltpu.VMEM)] * 2,
+        out_shape=[
+            jax.ShapeDtypeStruct((total, units), jnp.bfloat16),
+            jax.ShapeDtypeStruct((total, total), jnp.float32),
+        ],
+        scratch_shapes=[pltpu.SemaphoreType.DMA((count,))],
+        compiler_params=pltpu.CompilerParams(
+            vmem_limit_bytes=2 * total * units + 4 * total * total + 4 * 2**20
+        ),
+        cost_estimate=pl.CostEstimate(
+            flops=2 * total * total * units,
+            bytes_accessed=4 * total * units + 4 * total * total,
+            transcendentals=0,
+        ),
+    )(segment.reshape(1), *pieces)
+
+
+def norms_kernel(replicas, levels, ids_ref, ids_row_ref, gram_ref, *refs):
+    *parts, y_ref, norms_ref, acc = refs
+    block = parts[0].shape[0] // replicas
+    tok_rows = block * len(parts)
+    for t, part in enumerate(parts):
+        for k in range(replicas):
+            y_ref[k * tok_rows + t * block : k * tok_rows + (t + 1) * block, :] = part[
+                k * block : (k + 1) * block, :
+            ]
+    acc[...] = jnp.zeros_like(acc)
+    lane = lax.broadcasted_iota(jnp.int32, (1, acc.shape[1]), 1)
+    for k in range(replicas):
+        columns = slice(k * tok_rows, (k + 1) * tok_rows)
+        gram_y = lax.dot_general(
+            y_ref[...], y_ref[columns, :], CONTRACT_LAST, preferred_element_type=jnp.float32
+        )
+        pairs = jnp.where(ids_ref[...] == ids_row_ref[:, columns], gram_ref[:, columns] * gram_y, 0.0)
+        of_row = jnp.sum(pairs, axis=1, keepdims=True)
+        for level in range(levels):
+            begin = (k >> level << level) * tok_rows
+            end = begin + (tok_rows << level)
+            acc[begin:end, :] += jnp.where(lane == level, of_row[begin:end], 0.0)
+    for e in range(DOMAINS):
+        norms_ref[e : e + 1, :] = jnp.sum(
+            jnp.where(ids_ref[...] == e, acc[...], 0.0), axis=0, keepdims=True
+        )
+    norms_ref[DOMAINS:, :] = jnp.zeros_like(norms_ref[DOMAINS:, :])
+
+
+def norm_sums(row_ids, gram_hidden, parts, replicas, levels):
+    total = gram_hidden.shape[0]
+    piece = parts[0].shape[1]
+    return pl.pallas_call(
+        functools.partial(norms_kernel, replicas, levels),
+        in_specs=[pl.BlockSpec(memory_space=pltpu.VMEM)] * (3 + len(parts)),
+        out_specs=[pl.BlockSpec(memory_space=pltpu.VMEM)] * 2,
+        out_shape=[
+            jax.ShapeDtypeStruct((total, piece), jnp.bfloat16),
+            jax.ShapeDtypeStruct((8, 128), jnp.float32),
+        ],
+        scratch_shapes=[pltpu.VMEM((total, 128), jnp.float32)],
+        compiler_params=pltpu.CompilerParams(
+            vmem_limit_bytes=8 * total * piece + 4 * total * total + 1024 * total * 4 + 8 * 2**20
+        ),
+        cost_estimate=pl.CostEstimate(
+            flops=2 * total * total * piece + 4 * total * total,
+            bytes_accessed=4 * total * piece + 4 * total * total,
+            transcendentals=0,
+        ),
+    )(row_ids, row_ids.reshape(1, total), gram_hidden, *parts)
+
+
 def shards(layer_input_activations, cotangent, domain_ids, norm_gain, w_gate, w_up, w_down):
     segment = lax.axis_index("section")
     dp_index = lax.axis_index("dp")
@@ -135,7 +243,8 @@
     assert segments == 2
     micro, local_rows, width = layer_input_activations.shape
     gain = norm_gain[0][None, :]
-    gate_w, up_w, down_w = load_weights(w_gate, w_up, w_down)
+    gate_w, up_w = load_weights(w_gate, w_up)
+    down_w = w_down[0]
     units = down_w.shape[0]
     block = micro * local_rows
     tok_rows = block * tensor_size
@@ -143,7 +252,9 @@
 
     x_own = layer_input_activations.reshape(block, width)
     cot_own = cotangent.reshape(block, width)
-    rows_in = gather_rows(jnp.where(first, x_own, cot_own))
+    x0 = jnp.concatenate(gather_in(x_own, 0, "tensor"), axis=0)
+    cot_late, gate_w, up_w = lax.optimization_barrier((cot_own, gate_w, up_w))
+    cot_rows = jnp.concatenate(gather_in(cot_late, 1, "tensor"), axis=0)
 
     def layer_parts(rows):
         widened = rows.astype(jnp.float32)
@@ -153,28 +264,23 @@
         up = jnp.dot(normed, up_w, preferred_element_type=jnp.float32)
         return widened, scale, gate, up
 
-    def gather_hidden(gathered, section, begin, end):
-        for bit in range(begin, end):
-            other = swap_in(gathered, section, "dp", 2**bit)
-            gathered = jnp.concatenate([gathered, other], axis=0)
-        return gathered
-
-    _, _, gate0, up0 = layer_parts(rows_in)
+    _, _, gate0, up0 = layer_parts(x0)
     hidden0 = (jax.nn.silu(gate0) * up0).astype(jnp.bfloat16)
     mixed = jnp.dot(hidden0, down_w, preferred_element_type=jnp.float32).astype(jnp.bfloat16)
-    cot_rows, hidden0, mixed = lax.optimization_barrier((rows_in, hidden0, mixed))
+    cot_rows, hidden0, mixed = lax.optimization_barrier((cot_rows, hidden0, mixed))
     d_hidden = lax.dot_general(cot_rows, down_w, CONTRACT_LAST, preferred_element_type=jnp.float32)
-    some0 = gather_hidden(hidden0, 0, 0, 1)
     x1_own = scatter_sum(x_own, mixed, 0, block)
-    x1_own, d_hidden, some0 = lax.optimization_barrier((x1_own, d_hidden, some0))
-    x1 = gather_rows(x1_own, 1)
-    all0 = gather_hidden(some0, 0, 1, bits("dp"))
+    x1_own, d_hidden = lax.optimization_barrier((x1_own, d_hidden))
+    x1 = jnp.concatenate(gather_in(x1_own, 1, "tensor"), axis=0)
+    x1, hidden0 = lax.optimization_barrier((x1, hidden0))
+    pieces0 = gather_in(hidden0, 0, "dp")
 
     widened, scale, gate, up = layer_parts(x1)
     sig = jax.nn.sigmoid(gate)
     hidden1 = (gate * sig * up).astype(jnp.bfloat16)
     d_gate = (d_hidden * up * (sig * (1.0 + gate * (1.0 - sig)))).astype(jnp.bfloat16)
     d_up = (d_hidden * gate * sig).astype(jnp.bfloat16)
+    d_gate, d_up = lax.optimization_barrier((d_gate, d_up))
     d_normed = lax.dot_general(d_gate, gate_w, CONTRACT_LAST, preferred_element_type=jnp.float32)
     d_normed = d_normed + lax.dot_general(
         d_up, up_w, CONTRACT_LAST, preferred_element_type=jnp.float32
@@ -182,7 +288,7 @@
     pulled = d_normed * gain
     along = jnp.sum(pulled * widened, axis=-1, keepdims=True) / width
     term = (pulled * scale - widened * (scale * scale * scale * along)).astype(jnp.bfloat16)
-    term, all0 = lax.optimization_barrier((term, all0))
+    term, pieces0 = lax.optimization_barrier((term, pieces0))
     dy_own = scatter_sum(cot_own, term, 1, block)
     dy_own = jnp.where(first, dy_own, cot_own)
     dy_own, hidden1 = lax.optimization_barrier((dy_own, hidden1))
@@ -197,33 +303,17 @@
         part = lax.dynamic_slice_in_dim(dy_own, (dp_index ^ k) * piece, piece, axis=1)
         part = jnp.concatenate([part, id_block], axis=0)
         messages.append(part if k == 0 else swap(part, "dp", k))
-    all1 = gather_hidden(hidden1, 1, 0, bits("dp"))
-    hidden_all = jnp.where(first, all0, all1)
-    gram_hidden = lax.dot_general(
-        hidden_all, hidden_all, CONTRACT_LAST, preferred_element_type=jnp.float32
-    )
+    pieces1 = gather_in(hidden1, 1, "dp")
     columns = jnp.concatenate([message[:block] for message in messages], axis=0)
-    columns, hidden_all, gram_hidden = lax.optimization_barrier(
-        (columns, hidden_all, gram_hidden)
-    )
-    y = gather_rows(columns).reshape(tensor_size, dp_size, block, piece)
-    y = jnp.swapaxes(y, 0, 1).reshape(dp_size * tok_rows, piece)
+    columns, pieces1 = lax.optimization_barrier((columns, pieces1))
+    parts_y = [columns] + [swap(columns, "tensor", k) for k in range(1, tensor_size)]
+    hidden_all, gram_hidden = assemble(segment, pieces0, pieces1)
     ids_all = jnp.stack([message[block : block + micro, 0] for message in messages])
     row_ids = jnp.broadcast_to(
         ids_all.astype(jnp.int32)[:, None, :, None], (dp_size, tensor_size, micro, local_rows)
     ).reshape(dp_size * tok_rows, 1)
-
-    gram_y = lax.dot_general(y, y, CONTRACT_LAST, preferred_element_type=jnp.float32)
-    pairs = jnp.where(row_ids == row_ids.T, gram_hidden * gram_y, 0.0)
-    replica = jnp.arange(tok_rows * dp_size) // tok_rows
-    onehot = (row_ids == jnp.arange(DOMAINS)[None, :]).astype(jnp.float32)
     levels = dp_size.bit_length()
-    sums = []
-    for level in range(levels):
-        group = replica >> level
-        of_row = jnp.sum(jnp.where(group[:, None] == group[None, :], pairs, 0.0), axis=1)
-        sums.append(jnp.sum(onehot * of_row[:, None], axis=0))
-    norms = jnp.stack(sums, axis=1)
+    y, norms = norm_sums(row_ids, gram_hidden, parts_y, dp_size, levels)
     rounds = [(axis, bit) for axis in ("tensor", "dp", "section") for bit in range(bits(axis))]
     tiles = units // TILE
     parts = min(3, tiles)
@@ -239,7 +329,7 @@
         row_ids, norms = lax.optimization_barrier((row_ids, norms))
     entries = segments * units * tensor_size * width
     counts = [float((dp_size >> level) * entries) for level in range(levels)]
-    return grads[None], norms / jnp.array(counts, jnp.float32)[None, :]
+    return grads[None], norms[:DOMAINS, :levels] / jnp.array(counts, jnp.float32)[None, :]
 
 
 def solution(mesh):

time: 129 us -> 122 us (0.946)
  waiting for transfers between devices: 30.7 us -> 24 us
  other arithmetic: 7.75 us -> 1.61 us
  starting transfers between devices: 53 us -> 58.9 us
  matrix products: 16.6 us -> 14.1 us
  Pallas kernels: 17.2 us -> 18.8 us
    ppermute x7 -> x15, starting transfers between devices: 11.1 us -> 26.8 us  [swap_in(): return lax.ppermute(block, ('section', axis), route)]
    ppermute x14 -> x11, starting transfers between devices: 29.7 us -> 19.7 us  [swap(): return lax.ppermute(block, axis, [(i, i ^ offset) for i in range(size)])]
    ppermute x7 -> x15, waiting for transfers between devices: 10.5 us -> 2.31 us  [swap_in(): return lax.ppermute(block, ('section', axis), route)]
    ppermute x8, waiting for transfers between devices: 5.53 us -> 11.1 us  [across(): return lax.ppermute(block, ('section', 'tensor'), route)]
    ppermute x14 -> x11, waiting for transfers between devices: 14.7 us -> 10.6 us  [swap(): return lax.ppermute(block, axis, [(i, i ^ offset) for i in range(size)])]
    pallas_call x0 -> x2, Pallas kernels: none -> 3.7 us  [the longest x1 2.62 us: assemble(): pl.pallas_call(functools.partial(assemble_kernel, count), in_specs=[pl.Bl...]
    select_n x2 -> x0, other arithmetic: 3.15 us -> none  [the longest x1 2.16 us: shards(): hidden_all = jnp.where(first, all0, all1)]
    dot_general x2 -> x0, matrix products: 2.59 us -> none  [the longest x1 2.12 us: shards(): lax.dot_general(hidden_all, hidden_all, CONTRACT_LAST, preferred_element_...]
  transfers between devices with their start and end apart: 29 -> 34, of which waited for: 13 -> 10; matrix products, arithmetic and copies ran while one was open for 9% -> 13% of each run, Pallas kernels for 13% -> 15%
where the time goes in v4:
time: 122 us; the launch traced here: 121 us
  starting transfers between devices  58.9 us (48%)
  waiting for transfers between devices  24 us (20%)
  Pallas kernels  18.8 us (15%)
  matrix products  14.1 us (12%)
  local copies, waits for them, and re-layouts  2.07 us (2%)
  other arithmetic  1.61 us (1%)
  between operations  1.4 us (1%)
    ppermute x15, starting transfers between devices, swap_in(): return lax.ppermute(block, ('section', axis), route)  26.8 us
    ppermute x11, starting transfers between devices, swap(): return lax.ppermute(block, axis, [(i, i ^ offset) for i in range(size)])  19.7 us
    ppermute x8, starting transfers between devices, across(): return lax.ppermute(block, ('section', 'tensor'), route)  12.4 us
    ppermute x8, waiting for transfers between devices, across(): return lax.ppermute(block, ('section', 'tensor'), route)  11.1 us
    ppermute x11, waiting for transfers between devices, swap(): return lax.ppermute(block, axis, [(i, i ^ offset) for i in range(size)])  10.6 us
    pallas_call x3, Pallas kernels, domain_gradients(): pl.pallas_call(gradient_kernel, grid=(count,), in_specs=in_specs, out_spe...  9.91 us
    pallas_call x1, Pallas kernels, load_weights(): pl.pallas_call(load_kernel, in_specs=[pl.BlockSpec(memory_space=pltpu.HBM...  5.19 us
    dot_general x2, matrix products, layer_parts(): up = jnp.dot(normed, up_w, preferred_element_type=jnp.float32)  2.92 us
  transfers between devices with their start and end apart: 34, of which 10 were waited for; matrix products, arithmetic and copies ran while one was open for 13% of the time, Pallas kernels for 15%

profile of v4, /device:TPU:0, one launch (start us, length us, event | category | flops | bytes accessed | tf_op | source)
XLA Modules:
  0.0 120.9 jit_solution(11107154171838005887)
XLA Ops:
  0.7 5.1 %collective-permute-start.3 = (bf16[32,2048]{1,0:T(8,128)(2,1)}, bf16[32,2048]{1,0:T(8,128)(2,1)S(1)}, u32[]{:S(2)}, u32[]{:S(2)}) collective-permute-start(bf16[32,2048]{1,0:T(8,128)(2,1)} %bitcast.34), channel_id=1, source_target_pairs={{0,1},{1,0},{2,3},{3,2},{4,5},{5,4},{6,7},{7,6},{8,9},{9,8},{10,11... | collective-permute-start | bytes 393224 | tf_op jit(solution)/shard_map/ppermute | solution.py:25
  5.7 4.5 %collective-permute-start.4 = (bf16[32,2048]{1,0:T(8,128)(2,1)}, bf16[32,2048]{1,0:T(8,128)(2,1)S(1)}, u32[]{:S(2)}, u32[]{:S(2)}) collective-permute-start(bf16[32,2048]{1,0:T(8,128)(2,1)} %bitcast.35), channel_id=1, source_target_pairs={{0,2},{1,3},{2,0},{3,1},{4,6},{5,7},{6,4},{7,5},{8,10},{9,11},{10,... | collective-permute-start | bytes 393224 | tf_op jit(solution)/shard_map/ppermute | solution.py:25
  10.2 1.9 %collective-permute-start.5 = (bf16[32,2048]{1,0:T(8,128)(2,1)}, bf16[32,2048]{1,0:T(8,128)(2,1)S(1)}, u32[]{:S(2)}, u32[]{:S(2)}) collective-permute-start(bf16[32,2048]{1,0:T(8,128)(2,1)} %bitcast.36), channel_id=1, source_target_pairs={{0,3},{1,2},{2,1},{3,0},{4,7},{5,6},{6,5},{7,4},{8,11},{9,10},{10,... | collective-permute-start | bytes 393224 | tf_op jit(solution)/shard_map/ppermute | solution.py:25
  12.2 5.2 %shard_map.95 = (bf16[2048,1792]{1,0:T(8,128)(2,1)S(1)}, bf16[2048,1792]{1,0:T(8,128)(2,1)S(1)}) custom-call(bf16[1,2048,1792]{2,1,0:T(8,128)(2,1)} %refs_0_.1, bf16[1,2048,1792]{2,1,0:T(8,128)(2,1)} %refs_1_.1), custom_call_target="tpu_custom_call" | custom-call | bytes 14680064 | tf_op jit(solution)/shard_map/pallas_call | solution.py:68
  19.4 1.1 collective-permute-done.5
  20.8 1.2 fusion.24
  22.0 1.4 %fusion.5.refs_0_ = bf16[128,1792]{1,0:T(8,128)(2,1)S(1)} fusion(bf16[2048,1792]{1,0:T(8,128)(2,1)S(1)} %get-tuple-element.41, f32[128,1792]{1,0:T(8,128)S(1)} %fusion.24, f32[2048]{0:T(1024)S(1)} %bitcast.45, f32[128]{0:T(128)S(1)} %add_rsqrt_fusion.1, bf16[32,2048]{1,0:T(8,128)(2,1)S(1)} %collective-permute-done.5, ...), kind=kOutput, calls=%fused_computation.7 | convolution fusion | flops 943783936 | bytes 9249280 | tf_op jit(solution)/shard_map/dot_general | solution.py:264
  23.4 0.8 slice-done.1
  24.2 1.2 %fusion.6 = bf16[128,2048]{1,0:T(8,128)(2,1)S(1)} fusion(bf16[128,1792]{1,0:T(8,128)(2,1)S(1)} %fusion.5.refs_0_, bf16[1,1792,2048]{2,1,0:T(8,128)(2,1)S(1)} %bitcast.33), kind=kOutput, calls=%fused_computation.8 | convolution fusion | flops 939786240 | bytes 8323072 | tf_op jit(solution)/shard_map/dot_general | solution.py:269
  25.5 1.3 %collective-permute-start.6 = (bf16[32,2048]{1,0:T(8,128)(2,1)S(1)}, bf16[32,2048]{1,0:T(8,128)(2,1)S(1)}, u32[]{:S(2)}, u32[]{:S(2)}) collective-permute-start(bf16[32,2048]{1,0:T(8,128)(2,1)S(1)} %get-tuple-element.79), channel_id=1, source_target_pairs={{0,16},{1,17},{2,18},{3,19},{4,20},{5,21},{6,22},{7,23},{8,24},{9,... | collective-permute-start | bytes 393224 | tf_op jit(solution)/shard_map/ppermute | solution.py:33
  26.8 1.3 %collective-permute-start.7 = (bf16[32,2048]{1,0:T(8,128)(2,1)S(1)}, bf16[32,2048]{1,0:T(8,128)(2,1)S(1)}, u32[]{:S(2)}, u32[]{:S(2)}) collective-permute-start(bf16[32,2048]{1,0:T(8,128)(2,1)S(1)} %get-tuple-element.82), channel_id=1, source_target_pairs={{0,17},{1,16},{2,19},{3,18},{4,21},{5,20},{6,23},{7,22},{8,25},{9,... | collective-permute-start | bytes 393224 | tf_op jit(solution)/shard_map/ppermute | solution.py:33
  28.1 1.3 %collective-permute-start.8 = (bf16[32,2048]{1,0:T(8,128)(2,1)S(1)}, bf16[32,2048]{1,0:T(8,128)(2,1)S(1)}, u32[]{:S(2)}, u32[]{:S(2)}) collective-permute-start(bf16[32,2048]{1,0:T(8,128)(2,1)S(1)} %get-tuple-element.81), channel_id=1, source_target_pairs={{0,18},{1,19},{2,16},{3,17},{4,22},{5,23},{6,20},{7,21},{8,26},{9,... | collective-permute-start | bytes 393224 | tf_op jit(solution)/shard_map/ppermute | solution.py:33
  29.4 3.2 %collective-permute-start.9 = (bf16[32,2048]{1,0:T(8,128)(2,1)S(1)}, bf16[32,2048]{1,0:T(8,128)(2,1)S(1)}, u32[]{:S(2)}, u32[]{:S(2)}) collective-permute-start(bf16[32,2048]{1,0:T(8,128)(2,1)S(1)} %get-tuple-element.80), channel_id=1, source_target_pairs={{0,19},{1,18},{2,17},{3,16},{4,23},{5,22},{6,21},{7,20},{8,27},{9,... | collective-permute-start | bytes 393224 | tf_op jit(solution)/shard_map/ppermute | solution.py:33
  32.7 2.5 %fusion = f32[128,1792]{1,0:T(8,128)S(1)} fusion(bf16[128,2048]{1,0:T(8,128)(2,1)S(1)} %pad_maximum_fusion, bf16[1,1792,2048]{2,1,0:T(8,128)(2,1)S(1)} %bitcast.33), kind=kOutput, calls=%fused_computation | convolution fusion | flops 939524096 | bytes 8781824 | tf_op jit(solution)/shard_map/dot_general | solution.py:271
  37.5 3.4 %collective-permute-start.13 = (bf16[128,1792]{1,0:T(8,128)(2,1)S(1)}, bf16[128,1792]{1,0:T(8,128)(2,1)S(1)}, u32[]{:S(2)}, u32[]{:S(2)}) collective-permute-start(bf16[128,1792]{1,0:T(8,128)(2,1)S(1)} %fusion.5.refs_0_), channel_id=1, source_target_pairs={{0,4},{4,0},{8,12},{12,8},{1,5},{5,1},{9,13},{13,9},{2,6},{6,2},{1... | collective-permute-start | bytes 1376264 | tf_op jit(solution)/shard_map/ppermute | solution.py:25
  40.8 3.4 %collective-permute-start.14 = (bf16[128,1792]{1,0:T(8,128)(2,1)S(1)}, bf16[128,1792]{1,0:T(8,128)(2,1)S(1)}, u32[]{:S(2)}, u32[]{:S(2)}) collective-permute-start(bf16[128,1792]{1,0:T(8,128)(2,1)S(1)} %fusion.5.refs_0_), channel_id=1, source_target_pairs={{0,8},{4,12},{8,0},{12,4},{1,9},{5,13},{9,1},{13,5},{2,10},{6,14},... | collective-permute-start | bytes 1376264 | tf_op jit(solution)/shard_map/ppermute | solution.py:25
  44.3 2.4 %collective-permute-start.15 = (bf16[128,1792]{1,0:T(8,128)(2,1)S(1)}, bf16[128,1792]{1,0:T(8,128)(2,1)S(1)}, u32[]{:S(2)}, u32[]{:S(2)}) collective-permute-start(bf16[128,1792]{1,0:T(8,128)(2,1)S(1)} %fusion.5.refs_0_), channel_id=1, source_target_pairs={{0,12},{4,8},{8,4},{12,0},{1,13},{5,9},{9,5},{13,1},{2,14},{6,10},... | collective-permute-start | bytes 1376264 | tf_op jit(solution)/shard_map/ppermute | solution.py:25
  46.9 1.2 %fusion.19 = f32[128,1792]{1,0:T(8,128)S(1)} fusion(bf16[2048,1792]{1,0:T(8,128)(2,1)S(1)} %get-tuple-element.40, bf16[128,2048]{1,0:T(8,128)(2,1)S(1)} %pad_maximum_fusion.2, f32[128]{0:T(128)S(1)} %add_rsqrt_fusion, f32[2048]{0:T(1024)S(1)} %bitcast.46), kind=kOutput, calls=%fused_computation.34 | convolution fusion | flops 940572672 | bytes 8790528 | tf_op jit(solution)/shard_map/dot_general | solution.py:263
  48.1 1.6 %multiply_convert_fusion = (bf16[128,1792]{1,0:T(8,128)(2,1)S(1)}, bf16[128,1792]{1,0:T(8,128)(2,1)S(1)}, bf16[128,1792]{1,0:T(8,128)(2,1)S(1)}) fusion(f32[128,1792]{1,0:T(8,128)S(1)} %fusion.19, f32[128,1792]{1,0:T(8,128)S(1)} %fusion, bf16[2048,1792]{1,0:T(8,128)(2,1)S(1)} %get-tuple-element.41, bf16[128,2048]{1,0:T(8,128)(2,1)S(1)} %pad_maximum_fusion.2, ...), kind=kOutput, calls=%fused_computation.24 | convolution fusion | flops 944242688 | bytes 11084288 | tf_op jit(solution)/shard_map/dot_general | solution.py:264
  49.7 2.4 %fusion.29 = f32[128,2048]{1,0:T(8,128)S(1)} fusion(bf16[128,1792]{1,0:T(8,128)(2,1)S(1)} %get-tuple-element.48, bf16[2048,1792]{1,0:T(8,128)(2,1)S(1)} %get-tuple-element.40), kind=kOutput, calls=%fused_computation.58 | convolution fusion | flops 939524096 | bytes 8847360 | tf_op jit(solution)/shard_map/dot_general | solution.py:284
  52.1 2.6 %fusion.15 = (f32[128]{0:T(128)S(1)}, f32[128,2048]{1,0:T(8,128)S(1)}) fusion(bf16[128,2048]{1,0:T(8,128)(2,1)S(1)} %pad_maximum_fusion.2, f32[2048]{0:T(1024)S(1)} %bitcast.48, f32[128,2048]{1,0:T(8,128)S(1)} %fusion.29, bf16[128,1792]{1,0:T(8,128)(2,1)S(1)} %get-tuple-element.49, bf16[2048,1792]{1,0:T(8,128)(2,1)S(1)} %get-tuple-element.41), kind=kOutput, calls=%fused_computation.21 | convolution fusion | flops 940834688 | bytes 10428928 | tf_op jit(solution)/shard_map/dot_general | solution.py:285
  55.0 1.1 collective-permute-done.14.refs_2_
  56.2 1.3 %collective-permute-start.16 = (bf16[32,2048]{1,0:T(8,128)(2,1)S(1)}, bf16[32,2048]{1,0:T(8,128)(2,1)S(1)}, u32[]{:S(2)}, u32[]{:S(2)}) collective-permute-start(bf16[32,2048]{1,0:T(8,128)(2,1)S(1)} %get-tuple-element.75), channel_id=1, source_target_pairs={{16,0},{17,1},{18,2},{19,3},{20,4},{21,5},{22,6},{23,7},{24,8},{25... | collective-permute-start | bytes 393224 | tf_op jit(solution)/shard_map/ppermute | solution.py:33
  57.5 1.5 %collective-permute-start.17 = (bf16[32,2048]{1,0:T(8,128)(2,1)S(1)}, bf16[32,2048]{1,0:T(8,128)(2,1)S(1)}, u32[]{:S(2)}, u32[]{:S(2)}) collective-permute-start(bf16[32,2048]{1,0:T(8,128)(2,1)S(1)} %get-tuple-element.78), channel_id=1, source_target_pairs={{16,1},{17,0},{18,3},{19,2},{20,5},{21,4},{22,7},{23,6},{24,9},{25... | collective-permute-start | bytes 393224 | tf_op jit(solution)/shard_map/ppermute | solution.py:33
  59.0 1.3 %collective-permute-start.18 = (bf16[32,2048]{1,0:T(8,128)(2,1)S(1)}, bf16[32,2048]{1,0:T(8,128)(2,1)S(1)}, u32[]{:S(2)}, u32[]{:S(2)}) collective-permute-start(bf16[32,2048]{1,0:T(8,128)(2,1)S(1)} %get-tuple-element.77), channel_id=1, source_target_pairs={{16,2},{17,3},{18,0},{19,1},{20,6},{21,7},{22,4},{23,5},{24,10},{2... | collective-permute-start | bytes 393224 | tf_op jit(solution)/shard_map/ppermute | solution.py:33
  60.3 1.3 %collective-permute-start.19 = (bf16[32,2048]{1,0:T(8,128)(2,1)S(1)}, bf16[32,2048]{1,0:T(8,128)(2,1)S(1)}, u32[]{:S(2)}, u32[]{:S(2)}) collective-permute-start(bf16[32,2048]{1,0:T(8,128)(2,1)S(1)} %get-tuple-element.76), channel_id=1, source_target_pairs={{16,3},{17,2},{18,1},{19,0},{20,7},{21,6},{22,5},{23,4},{24,11},{2... | collective-permute-start | bytes 393224 | tf_op jit(solution)/shard_map/ppermute | solution.py:33
  61.7 1.8 %collective-permute-done.16 = bf16[32,2048]{1,0:T(8,128)(2,1)S(1)} collective-permute-done((bf16[32,2048]{1,0:T(8,128)(2,1)S(1)}, bf16[32,2048]{1,0:T(8,128)(2,1)S(1)}, u32[]{:S(2)}, u32[]{:S(2)}) %collective-permute-start.16) | collective-permute-done | bytes 131104 | tf_op jit(solution)/shard_map/ppermute | solution.py:33
  63.5 4.6 %collective-permute-done.17 = bf16[32,2048]{1,0:T(8,128)(2,1)S(1)} collective-permute-done((bf16[32,2048]{1,0:T(8,128)(2,1)S(1)}, bf16[32,2048]{1,0:T(8,128)(2,1)S(1)}, u32[]{:S(2)}, u32[]{:S(2)}) %collective-permute-start.17) | collective-permute-done | bytes 131104 | tf_op jit(solution)/shard_map/ppermute | solution.py:33
  68.1 4.7 %collective-permute-done.18 = bf16[32,2048]{1,0:T(8,128)(2,1)S(1)} collective-permute-done((bf16[32,2048]{1,0:T(8,128)(2,1)S(1)}, bf16[32,2048]{1,0:T(8,128)(2,1)S(1)}, u32[]{:S(2)}, u32[]{:S(2)}) %collective-permute-start.18) | collective-permute-done | bytes 131104 | tf_op jit(solution)/shard_map/ppermute | solution.py:33
  73.0 1.5 %collective-permute-start.20 = (bf16[48,512]{1,0:T(8,128)(2,1)S(1)}, bf16[48,512]{1,0:T(8,128)(2,1)S(1)}, u32[]{:S(2)}, u32[]{:S(2)}) collective-permute-start(bf16[48,512]{1,0:T(8,128)(2,1)S(1)} %get-tuple-element.89), channel_id=1, source_target_pairs={{0,4},{4,0},{8,12},{12,8},{1,5},{5,1},{9,13},{13,9},{2,6},{6,2},{1... | collective-permute-start | bytes 147464 | tf_op jit(solution)/shard_map/ppermute | solution.py:19
  74.5 1.5 %collective-permute-start.21 = (bf16[48,512]{1,0:T(8,128)(2,1)S(1)}, bf16[48,512]{1,0:T(8,128)(2,1)S(1)}, u32[]{:S(2)}, u32[]{:S(2)}) collective-permute-start(bf16[48,512]{1,0:T(8,128)(2,1)S(1)} %get-tuple-element.90), channel_id=1, source_target_pairs={{0,8},{4,12},{8,0},{12,4},{1,9},{5,13},{9,1},{13,5},{2,10},{6,14},... | collective-permute-start | bytes 147464 | tf_op jit(solution)/shard_map/ppermute | solution.py:19
  77.3 0.7 collective-permute-start.24
  78.0 0.7 collective-permute-start.25
  78.7 2.9 %collective-permute-done.22 = bf16[48,512]{1,0:T(8,128)(2,1)S(1)} collective-permute-done((bf16[48,512]{1,0:T(8,128)(2,1)S(1)}, bf16[48,512]{1,0:T(8,128)(2,1)S(1)}, u32[]{:S(2)}, u32[]{:S(2)}) %collective-permute-start.22) | collective-permute-done | bytes 49184 | tf_op jit(solution)/shard_map/ppermute | solution.py:19
  82.1 2.0 %collective-permute-start.26 = (bf16[128,512]{1,0:T(8,128)(2,1)S(1)}, bf16[128,512]{1,0:T(8,128)(2,1)S(1)}, u32[]{:S(2)}, u32[]{:S(2)}) collective-permute-start(bf16[128,512]{1,0:T(8,128)(2,1)S(1)} %pad_maximum_fusion.3.refs_0_), channel_id=1, source_target_pairs={{0,1},{1,0},{2,3},{3,2},{4,5},{5,4},{6,7},{7,6},{8,9},{9,8},{10,11... | collective-permute-start | bytes 393224 | tf_op jit(solution)/shard_map/ppermute | solution.py:19
  84.0 0.8 collective-permute-start.27
  84.9 2.2 %collective-permute-start.28 = (bf16[128,512]{1,0:T(8,128)(2,1)S(1)}, bf16[128,512]{1,0:T(8,128)(2,1)S(1)}, u32[]{:S(2)}, u32[]{:S(2)}) collective-permute-start(bf16[128,512]{1,0:T(8,128)(2,1)S(1)} %pad_maximum_fusion.3.refs_0_), channel_id=1, source_target_pairs={{0,3},{1,2},{2,1},{3,0},{4,7},{5,6},{6,5},{7,4},{8,11},{9,10},{10,... | collective-permute-start | bytes 393224 | tf_op jit(solution)/shard_map/ppermute | solution.py:19
  87.6 2.6 %shard_map.96 = (bf16[512,1792]{1,0:T(8,128)(2,1)S(1)}, f32[512,512]{1,0:T(8,128)S(1)}) custom-call(s32[1]{0:T(128)} %bitcast.6.flag_ref, bf16[128,1792]{1,0:T(8,128)(2,1)} %copy-done, bf16[128,1792]{1,0:T(8,128)(2,1)} %copy-done.3, bf16[128,1792]{1,0:T(8,128)(2,1)} %copy-done.4, bf16[128,1792]{1,0:T(8,128)(2,1)} %copy-done.5, bf16[128,1792]{1,0:T(8,128)(2,1)} %copy-done.6, ...), custom_call_target="tpu_custom_call" | custom-call | flops 939524096 | bytes 4718592 | tf_op jit(solution)/shard_map/pallas_call | solution.py:164
  90.2 2.5 %collective-permute-done.27.refs_2_ = bf16[128,512]{1,0:T(8,128)(2,1)S(1)} collective-permute-done((bf16[128,512]{1,0:T(8,128)(2,1)S(1)}, bf16[128,512]{1,0:T(8,128)(2,1)S(1)}, u32[]{:S(2)}, u32[]{:S(2)}) %collective-permute-start.27) | collective-permute-done | bytes 131104 | tf_op jit(solution)/shard_map/ppermute | solution.py:19
  92.7 1.1 shard_map.97
  93.8 2.0 %collective-permute-start.29 = (f32[8,128]{1,0:T(8,128)S(1)}, f32[8,128]{1,0:T(8,128)S(1)}, u32[]{:S(2)}, u32[]{:S(2)}) collective-permute-start(f32[8,128]{1,0:T(8,128)S(1)} %get-tuple-element.64), channel_id=1, source_target_pairs={{0,1},{1,0},{2,3},{3,2},{4,5},{5,4},{6,7},{7,6},{8,9},{9,8},{10,11... | collective-permute-start | bytes 12296 | tf_op jit(solution)/shard_map/ppermute | solution.py:19
  95.8 2.0 %collective-permute-done.29 = f32[8,128]{1,0:T(8,128)S(1)} collective-permute-done((f32[8,128]{1,0:T(8,128)S(1)}, f32[8,128]{1,0:T(8,128)S(1)}, u32[]{:S(2)}, u32[]{:S(2)}) %collective-permute-start.29) | collective-permute-done | bytes 4128 | tf_op jit(solution)/shard_map/ppermute | solution.py:19
  97.9 1.8 %collective-permute-start.30 = (f32[8,128]{1,0:T(8,128)S(1)}, f32[8,128]{1,0:T(8,128)S(1)}, u32[]{:S(2)}, u32[]{:S(2)}) collective-permute-start(f32[8,128]{1,0:T(8,128)S(1)} %add.103), channel_id=1, source_target_pairs={{0,2},{1,3},{2,0},{3,1},{4,6},{5,7},{6,4},{7,5},{8,10},{9,11},{10,... | collective-permute-start | bytes 12296 | tf_op jit(solution)/shard_map/ppermute | solution.py:19
  99.7 2.8 %collective-permute-done.30 = f32[8,128]{1,0:T(8,128)S(1)} collective-permute-done((f32[8,128]{1,0:T(8,128)S(1)}, f32[8,128]{1,0:T(8,128)S(1)}, u32[]{:S(2)}, u32[]{:S(2)}) %collective-permute-start.30) | collective-permute-done | bytes 4128 | tf_op jit(solution)/shard_map/ppermute | solution.py:19
  103.0 3.0 %shard_map.98.rest_0_ = bf16[4,1792,512]{2,1,0:T(8,128)(2,1)} custom-call(s32[512,1]{1,0:T(8,128)S(1)} %copy.12.ids_ref, bf16[512,1792]{1,0:T(8,128)(2,1)S(1)} %get-tuple-element.68.hidden_ref, bf16[512,512]{1,0:T(8,128)(2,1)S(1)} %get-tuple-element.69.y_ref), custom_call_target="tpu_custom_call" | custom-call | flops 1073741824 | bytes 2621440 | tf_op jit(solution)/shard_map/pallas_call | solution.py:110
  106.4 3.0 %shard_map.99.rest_0_ = bf16[4,1792,512]{2,1,0:T(8,128)(2,1)} custom-call(s32[512,1]{1,0:T(8,128)S(1)} %copy.14.ids_ref, bf16[512,1792]{1,0:T(8,128)(2,1)S(1)} %get-tuple-element.68.hidden_ref, bf16[512,512]{1,0:T(8,128)(2,1)S(1)} %get-tuple-element.69.y_ref, bf16[4,1792,512]{2,1,0:T(8,128)(2,1)} %shard_map.98.rest_0_), custom_call_target="tpu_custom_call", output_to_operand_aliasing={{}: (3, {})} | custom-call | flops 1073741824 | bytes 2621440 | tf_op jit(solution)/shard_map/pallas_call | solution.py:110
  109.9 6.5 %collective-permute-start.33 = (f32[8,128]{1,0:T(8,128)S(1)}, f32[8,128]{1,0:T(8,128)S(1)}, u32[]{:S(2)}, u32[]{:S(2)}) collective-permute-start(f32[8,128]{1,0:T(8,128)S(1)} %add.106), channel_id=1, source_target_pairs={{0,16},{16,0},{1,17},{17,1},{2,18},{18,2},{3,19},{19,3},{4,20},{20... | collective-permute-start | bytes 12296 | tf_op jit(solution)/shard_map/ppermute | solution.py:19
  116.4 3.9 %shard_map.100 = bf16[4,1792,512]{2,1,0:T(8,128)(2,1)} custom-call(s32[512,1]{1,0:T(8,128)S(1)} %copy.15.ids_ref, bf16[512,1792]{1,0:T(8,128)(2,1)S(1)} %get-tuple-element.68.hidden_ref, bf16[512,512]{1,0:T(8,128)(2,1)S(1)} %get-tuple-element.69.y_ref, bf16[4,1792,512]{2,1,0:T(8,128)(2,1)} %shard_map.99.rest_0_), custom_call_target="tpu_custom_call", output_to_operand_aliasing={{}: (3, {})} | custom-call | flops 1610612736 | bytes 3932160 | tf_op jit(solution)/shard_map/pallas_call | solution.py:110
  (102 shorter events, 9.3 us)
Async XLA Ops:
  0.6 16.7 %copy-start.2 = (bf16[4,8,2048]{2,1,0:T(8,128)(2,1)S(1)}, bf16[4,8,2048]{2,1,0:T(8,128)(2,1)}, u32[]{:S(2)}) copy-start(bf16[4,8,2048]{2,1,0:T(8,128)(2,1)} %param.9) | copy-start | bytes 393220
  0.6 19.9 %copy-start.1 = (bf16[4,8,2048]{2,1,0:T(8,128)(2,1)S(1)}, bf16[4,8,2048]{2,1,0:T(8,128)(2,1)}, u32[]{:S(2)}) copy-start(bf16[4,8,2048]{2,1,0:T(8,128)(2,1)} %param.8) | copy-start | bytes 393220
  0.7 20.1 %copy-start.10 = (f32[1,2048]{1,0:T(1,128)S(1)}, f32[1,2048]{1,0:T(1,128)}, u32[]{:S(2)}) copy-start(f32[1,2048]{1,0:T(1,128)} %param.11) | copy-start | bytes 24580
  0.7 18.1 %collective-permute-start.3 = (bf16[32,2048]{1,0:T(8,128)(2,1)}, bf16[32,2048]{1,0:T(8,128)(2,1)S(1)}, u32[]{:S(2)}, u32[]{:S(2)}) collective-permute-start(bf16[32,2048]{1,0:T(8,128)(2,1)} %bitcast.34), channel_id=1, source_target_pairs={{0,1},{1,0},{2,3},{3,2},{4,5},{5,4},{6,7},{7,6},{8,9},{9,8},{10,11... | collective-permute-start | bytes 393224 | tf_op jit(solution)/shard_map/ppermute | solution.py:25
  5.7 13.7 %collective-permute-start.4 = (bf16[32,2048]{1,0:T(8,128)(2,1)}, bf16[32,2048]{1,0:T(8,128)(2,1)S(1)}, u32[]{:S(2)}, u32[]{:S(2)}) collective-permute-start(bf16[32,2048]{1,0:T(8,128)(2,1)} %bitcast.35), channel_id=1, source_target_pairs={{0,2},{1,3},{2,0},{3,1},{4,6},{5,7},{6,4},{7,5},{8,10},{9,11},{10,... | collective-permute-start | bytes 393224 | tf_op jit(solution)/shard_map/ppermute | solution.py:25
  10.2 10.3 %collective-permute-start.5 = (bf16[32,2048]{1,0:T(8,128)(2,1)}, bf16[32,2048]{1,0:T(8,128)(2,1)S(1)}, u32[]{:S(2)}, u32[]{:S(2)}) collective-permute-start(bf16[32,2048]{1,0:T(8,128)(2,1)} %bitcast.36), channel_id=1, source_target_pairs={{0,3},{1,2},{2,1},{3,0},{4,7},{5,6},{6,5},{7,4},{8,11},{9,10},{10,... | collective-permute-start | bytes 393224 | tf_op jit(solution)/shard_map/ppermute | solution.py:25
  17.4 8.0 %collective-permute-start = (bf16[32,2048]{1,0:T(8,128)(2,1)S(1)}, bf16[32,2048]{1,0:T(8,128)(2,1)S(1)}, u32[]{:S(2)}, u32[]{:S(2)}) collective-permute-start(bf16[32,2048]{1,0:T(8,128)(2,1)S(1)} %bitcast.40), channel_id=1, source_target_pairs={{16,17},{17,16},{18,19},{19,18},{20,21},{21,20},{22,23},{23,22},{2... | collective-permute-start | bytes 393224 | tf_op jit(solution)/shard_map/ppermute | solution.py:25
  18.0 7.4 %collective-permute-start.1 = (bf16[32,2048]{1,0:T(8,128)(2,1)S(1)}, bf16[32,2048]{1,0:T(8,128)(2,1)S(1)}, u32[]{:S(2)}, u32[]{:S(2)}) collective-permute-start(bf16[32,2048]{1,0:T(8,128)(2,1)S(1)} %bitcast.41), channel_id=1, source_target_pairs={{16,18},{17,19},{18,16},{19,17},{20,22},{21,23},{22,20},{23,21},{2... | collective-permute-start | bytes 393224 | tf_op jit(solution)/shard_map/ppermute | solution.py:25
  18.7 6.7 %collective-permute-start.2 = (bf16[32,2048]{1,0:T(8,128)(2,1)S(1)}, bf16[32,2048]{1,0:T(8,128)(2,1)S(1)}, u32[]{:S(2)}, u32[]{:S(2)}) collective-permute-start(bf16[32,2048]{1,0:T(8,128)(2,1)S(1)} %bitcast.42), channel_id=1, source_target_pairs={{16,19},{17,18},{18,17},{19,16},{20,23},{21,22},{22,21},{23,20},{2... | collective-permute-start | bytes 393224 | tf_op jit(solution)/shard_map/ppermute | solution.py:25
  20.8 2.6 %slice-start = ((s8[7340032]{0:T(1024)(128)(4,1)}), s8[4194304]{0:T(1024)(128)(4,1)S(1)}, s32[]{:S(2)}) async-start(s8[7340032]{0:T(1024)(128)(4,1)} %bitcast.32), calls=%async_computation | async-start | bytes 8388608
  22.0 2.2 %slice-start.1 = ((s8[7340032]{0:T(1024)(128)(4,1)}), s8[3145728]{0:T(1024)(128)(4,1)S(1)}, s32[]{:S(2)}) async-start(s8[7340032]{0:T(1024)(128)(4,1)} %bitcast.32), calls=%async_computation.1 | async-start | bytes 6291456
  24.2 20.1 %copy-start = (bf16[128,1792]{1,0:T(8,128)(2,1)}, bf16[128,1792]{1,0:T(8,128)(2,1)S(1)}, u32[]{:S(2)}) copy-start(bf16[128,1792]{1,0:T(8,128)(2,1)S(1)} %fusion.5.refs_0_) | copy-start | bytes 1376260
  25.5 9.7 %collective-permute-start.6 = (bf16[32,2048]{1,0:T(8,128)(2,1)S(1)}, bf16[32,2048]{1,0:T(8,128)(2,1)S(1)}, u32[]{:S(2)}, u32[]{:S(2)}) collective-permute-start(bf16[32,2048]{1,0:T(8,128)(2,1)S(1)} %get-tuple-element.79), channel_id=1, source_target_pairs={{0,16},{1,17},{2,18},{3,19},{4,20},{5,21},{6,22},{7,23},{8,24},{9,... | collective-permute-start | bytes 393224 | tf_op jit(solution)/shard_map/ppermute | solution.py:33
  26.8 8.4 %collective-permute-start.7 = (bf16[32,2048]{1,0:T(8,128)(2,1)S(1)}, bf16[32,2048]{1,0:T(8,128)(2,1)S(1)}, u32[]{:S(2)}, u32[]{:S(2)}) collective-permute-start(bf16[32,2048]{1,0:T(8,128)(2,1)S(1)} %get-tuple-element.82), channel_id=1, source_target_pairs={{0,17},{1,16},{2,19},{3,18},{4,21},{5,20},{6,23},{7,22},{8,25},{9,... | collective-permute-start | bytes 393224 | tf_op jit(solution)/shard_map/ppermute | solution.py:33
  28.1 7.1 %collective-permute-start.8 = (bf16[32,2048]{1,0:T(8,128)(2,1)S(1)}, bf16[32,2048]{1,0:T(8,128)(2,1)S(1)}, u32[]{:S(2)}, u32[]{:S(2)}) collective-permute-start(bf16[32,2048]{1,0:T(8,128)(2,1)S(1)} %get-tuple-element.81), channel_id=1, source_target_pairs={{0,18},{1,19},{2,16},{3,17},{4,22},{5,23},{6,20},{7,21},{8,26},{9,... | collective-permute-start | bytes 393224 | tf_op jit(solution)/shard_map/ppermute | solution.py:33
  29.4 5.8 %collective-permute-start.9 = (bf16[32,2048]{1,0:T(8,128)(2,1)S(1)}, bf16[32,2048]{1,0:T(8,128)(2,1)S(1)}, u32[]{:S(2)}, u32[]{:S(2)}) collective-permute-start(bf16[32,2048]{1,0:T(8,128)(2,1)S(1)} %get-tuple-element.80), channel_id=1, source_target_pairs={{0,19},{1,18},{2,17},{3,16},{4,23},{5,22},{6,21},{7,20},{8,27},{9,... | collective-permute-start | bytes 393224 | tf_op jit(solution)/shard_map/ppermute | solution.py:33
  35.3 2.0 %collective-permute-start.10 = (bf16[32,2048]{1,0:T(8,128)(2,1)S(1)}, bf16[32,2048]{1,0:T(8,128)(2,1)S(1)}, u32[]{:S(2)}, u32[]{:S(2)}) collective-permute-start(bf16[32,2048]{1,0:T(8,128)(2,1)S(1)} %add_convert_fusion.1), channel_id=1, source_target_pairs={{16,17},{17,16},{18,19},{19,18},{20,21},{21,20},{22,23},{23,22},{2... | collective-permute-start | bytes 393224 | tf_op jit(solution)/shard_map/ppermute | solution.py:25
  36.0 1.4 %collective-permute-start.11 = (bf16[32,2048]{1,0:T(8,128)(2,1)S(1)}, bf16[32,2048]{1,0:T(8,128)(2,1)S(1)}, u32[]{:S(2)}, u32[]{:S(2)}) collective-permute-start(bf16[32,2048]{1,0:T(8,128)(2,1)S(1)} %add_convert_fusion.1), channel_id=1, source_target_pairs={{16,18},{17,19},{18,16},{19,17},{20,22},{21,23},{22,20},{23,21},{2... | collective-permute-start | bytes 393224 | tf_op jit(solution)/shard_map/ppermute | solution.py:25
  36.7 0.7 collective-permute-start.12
  37.5 17.5 %collective-permute-start.13 = (bf16[128,1792]{1,0:T(8,128)(2,1)S(1)}, bf16[128,1792]{1,0:T(8,128)(2,1)S(1)}, u32[]{:S(2)}, u32[]{:S(2)}) collective-permute-start(bf16[128,1792]{1,0:T(8,128)(2,1)S(1)} %fusion.5.refs_0_), channel_id=1, source_target_pairs={{0,4},{4,0},{8,12},{12,8},{1,5},{5,1},{9,13},{13,9},{2,6},{6,2},{1... | collective-permute-start | bytes 1376264 | tf_op jit(solution)/shard_map/ppermute | solution.py:25
  40.8 15.3 %collective-permute-start.14 = (bf16[128,1792]{1,0:T(8,128)(2,1)S(1)}, bf16[128,1792]{1,0:T(8,128)(2,1)S(1)}, u32[]{:S(2)}, u32[]{:S(2)}) collective-permute-start(bf16[128,1792]{1,0:T(8,128)(2,1)S(1)} %fusion.5.refs_0_), channel_id=1, source_target_pairs={{0,8},{4,12},{8,0},{12,4},{1,9},{5,13},{9,1},{13,5},{2,10},{6,14},... | collective-permute-start | bytes 1376264 | tf_op jit(solution)/shard_map/ppermute | solution.py:25
  44.3 11.8 %collective-permute-start.15 = (bf16[128,1792]{1,0:T(8,128)(2,1)S(1)}, bf16[128,1792]{1,0:T(8,128)(2,1)S(1)}, u32[]{:S(2)}, u32[]{:S(2)}) collective-permute-start(bf16[128,1792]{1,0:T(8,128)(2,1)S(1)} %fusion.5.refs_0_), channel_id=1, source_target_pairs={{0,12},{4,8},{8,4},{12,0},{1,13},{5,9},{9,5},{13,1},{2,14},{6,10},... | collective-permute-start | bytes 1376264 | tf_op jit(solution)/shard_map/ppermute | solution.py:25
  49.7 28.3 %copy-start.6 = (bf16[128,1792]{1,0:T(8,128)(2,1)}, bf16[128,1792]{1,0:T(8,128)(2,1)S(1)}, u32[]{:S(2)}) copy-start(bf16[128,1792]{1,0:T(8,128)(2,1)S(1)} %get-tuple-element.58.refs_4_) | copy-start | bytes 1376260
  52.1 9.4 %copy-start.12 = (s32[4,1]{0,1:T(1,128)S(1)}, s32[4,1]{0,1:T(1,128)}, u32[]{:S(2)}) copy-start(s32[4,1]{0,1:T(1,128)} %param.10) | copy-start | bytes 52
  55.0 32.6 %copy-start.3 = (bf16[128,1792]{1,0:T(8,128)(2,1)}, bf16[128,1792]{1,0:T(8,128)(2,1)S(1)}, u32[]{:S(2)}) copy-start(bf16[128,1792]{1,0:T(8,128)(2,1)S(1)} %collective-permute-done.13.refs_1_) | copy-start | bytes 1376260
  56.1 31.4 %copy-start.4 = (bf16[128,1792]{1,0:T(8,128)(2,1)}, bf16[128,1792]{1,0:T(8,128)(2,1)S(1)}, u32[]{:S(2)}) copy-start(bf16[128,1792]{1,0:T(8,128)(2,1)S(1)} %collective-permute-done.14.refs_2_) | copy-start | bytes 1376260
  56.1 31.5 %copy-start.5 = (bf16[128,1792]{1,0:T(8,128)(2,1)}, bf16[128,1792]{1,0:T(8,128)(2,1)S(1)}, u32[]{:S(2)}) copy-start(bf16[128,1792]{1,0:T(8,128)(2,1)S(1)} %collective-permute-done.15.refs_3_) | copy-start | bytes 1376260
  56.2 7.3 %collective-permute-start.16 = (bf16[32,2048]{1,0:T(8,128)(2,1)S(1)}, bf16[32,2048]{1,0:T(8,128)(2,1)S(1)}, u32[]{:S(2)}, u32[]{:S(2)}) collective-permute-start(bf16[32,2048]{1,0:T(8,128)(2,1)S(1)} %get-tuple-element.75), channel_id=1, source_target_pairs={{16,0},{17,1},{18,2},{19,3},{20,4},{21,5},{22,6},{23,7},{24,8},{25... | collective-permute-start | bytes 393224 | tf_op jit(solution)/shard_map/ppermute | solution.py:33
  57.5 10.6 %collective-permute-start.17 = (bf16[32,2048]{1,0:T(8,128)(2,1)S(1)}, bf16[32,2048]{1,0:T(8,128)(2,1)S(1)}, u32[]{:S(2)}, u32[]{:S(2)}) collective-permute-start(bf16[32,2048]{1,0:T(8,128)(2,1)S(1)} %get-tuple-element.78), channel_id=1, source_target_pairs={{16,1},{17,0},{18,3},{19,2},{20,5},{21,4},{22,7},{23,6},{24,9},{25... | collective-permute-start | bytes 393224 | tf_op jit(solution)/shard_map/ppermute | solution.py:33
  59.0 13.8 %collective-permute-start.18 = (bf16[32,2048]{1,0:T(8,128)(2,1)S(1)}, bf16[32,2048]{1,0:T(8,128)(2,1)S(1)}, u32[]{:S(2)}, u32[]{:S(2)}) collective-permute-start(bf16[32,2048]{1,0:T(8,128)(2,1)S(1)} %get-tuple-element.77), channel_id=1, source_target_pairs={{16,2},{17,3},{18,0},{19,1},{20,6},{21,7},{22,4},{23,5},{24,10},{2... | collective-permute-start | bytes 393224 | tf_op jit(solution)/shard_map/ppermute | solution.py:33
  60.3 12.6 %collective-permute-start.19 = (bf16[32,2048]{1,0:T(8,128)(2,1)S(1)}, bf16[32,2048]{1,0:T(8,128)(2,1)S(1)}, u32[]{:S(2)}, u32[]{:S(2)}) collective-permute-start(bf16[32,2048]{1,0:T(8,128)(2,1)S(1)} %get-tuple-element.76), channel_id=1, source_target_pairs={{16,3},{17,2},{18,1},{19,0},{20,7},{21,6},{22,5},{23,4},{24,11},{2... | collective-permute-start | bytes 393224 | tf_op jit(solution)/shard_map/ppermute | solution.py:33
  73.0 4.9 %collective-permute-start.20 = (bf16[48,512]{1,0:T(8,128)(2,1)S(1)}, bf16[48,512]{1,0:T(8,128)(2,1)S(1)}, u32[]{:S(2)}, u32[]{:S(2)}) collective-permute-start(bf16[48,512]{1,0:T(8,128)(2,1)S(1)} %get-tuple-element.89), channel_id=1, source_target_pairs={{0,4},{4,0},{8,12},{12,8},{1,5},{5,1},{9,13},{13,9},{2,6},{6,2},{1... | collective-permute-start | bytes 147464 | tf_op jit(solution)/shard_map/ppermute | solution.py:19
  74.5 4.2 %collective-permute-start.21 = (bf16[48,512]{1,0:T(8,128)(2,1)S(1)}, bf16[48,512]{1,0:T(8,128)(2,1)S(1)}, u32[]{:S(2)}, u32[]{:S(2)}) collective-permute-start(bf16[48,512]{1,0:T(8,128)(2,1)S(1)} %get-tuple-element.90), channel_id=1, source_target_pairs={{0,8},{4,12},{8,0},{12,4},{1,9},{5,13},{9,1},{13,5},{2,10},{6,14},... | collective-permute-start | bytes 147464 | tf_op jit(solution)/shard_map/ppermute | solution.py:19
  76.1 5.6 %collective-permute-start.22 = (bf16[48,512]{1,0:T(8,128)(2,1)S(1)}, bf16[48,512]{1,0:T(8,128)(2,1)S(1)}, u32[]{:S(2)}, u32[]{:S(2)}) collective-permute-start(bf16[48,512]{1,0:T(8,128)(2,1)S(1)} %get-tuple-element.91), channel_id=1, source_target_pairs={{0,12},{4,8},{8,4},{12,0},{1,13},{5,9},{9,5},{13,1},{2,14},{6,10},... | collective-permute-start | bytes 147464 | tf_op jit(solution)/shard_map/ppermute | solution.py:19
  76.6 5.4 %collective-permute-start.23 = (bf16[128,1792]{1,0:T(8,128)(2,1)S(1)}, bf16[128,1792]{1,0:T(8,128)(2,1)S(1)}, u32[]{:S(2)}, u32[]{:S(2)}) collective-permute-start(bf16[128,1792]{1,0:T(8,128)(2,1)S(1)} %get-tuple-element.58.refs_4_), channel_id=1, source_target_pairs={{16,20},{20,16},{24,28},{28,24},{17,21},{21,17},{25,29},{29,25},{1... | collective-permute-start | bytes 1376264 | tf_op jit(solution)/shard_map/ppermute | solution.py:25
  77.3 4.8 %collective-permute-start.24 = (bf16[128,1792]{1,0:T(8,128)(2,1)S(1)}, bf16[128,1792]{1,0:T(8,128)(2,1)S(1)}, u32[]{:S(2)}, u32[]{:S(2)}) collective-permute-start(bf16[128,1792]{1,0:T(8,128)(2,1)S(1)} %get-tuple-element.58.refs_4_), channel_id=1, source_target_pairs={{16,24},{20,28},{24,16},{28,20},{17,25},{21,29},{25,17},{29,21},{1... | collective-permute-start | bytes 1376264 | tf_op jit(solution)/shard_map/ppermute | solution.py:25
  78.0 4.1 %collective-permute-start.25 = (bf16[128,1792]{1,0:T(8,128)(2,1)S(1)}, bf16[128,1792]{1,0:T(8,128)(2,1)S(1)}, u32[]{:S(2)}, u32[]{:S(2)}) collective-permute-start(bf16[128,1792]{1,0:T(8,128)(2,1)S(1)} %get-tuple-element.58.refs_4_), channel_id=1, source_target_pairs={{16,28},{20,24},{24,20},{28,16},{17,29},{21,25},{25,21},{29,17},{1... | collective-permute-start | bytes 1376264 | tf_op jit(solution)/shard_map/ppermute | solution.py:25
  82.0 5.6 %copy-start.7 = (bf16[128,1792]{1,0:T(8,128)(2,1)}, bf16[128,1792]{1,0:T(8,128)(2,1)S(1)}, u32[]{:S(2)}) copy-start(bf16[128,1792]{1,0:T(8,128)(2,1)S(1)} %collective-permute-done.23.refs_5_) | copy-start | bytes 1376260
  82.1 2.8 %copy-start.9 = (bf16[128,1792]{1,0:T(8,128)(2,1)}, bf16[128,1792]{1,0:T(8,128)(2,1)S(1)}, u32[]{:S(2)}) copy-start(bf16[128,1792]{1,0:T(8,128)(2,1)S(1)} %collective-permute-done.25.refs_7_) | copy-start | bytes 1376260
  82.1 8.2 %collective-permute-start.26 = (bf16[128,512]{1,0:T(8,128)(2,1)S(1)}, bf16[128,512]{1,0:T(8,128)(2,1)S(1)}, u32[]{:S(2)}, u32[]{:S(2)}) collective-permute-start(bf16[128,512]{1,0:T(8,128)(2,1)S(1)} %pad_maximum_fusion.3.refs_0_), channel_id=1, source_target_pairs={{0,1},{1,0},{2,3},{3,2},{4,5},{5,4},{6,7},{7,6},{8,9},{9,8},{10,11... | collective-permute-start | bytes 393224 | tf_op jit(solution)/shard_map/ppermute | solution.py:19
  84.0 8.7 %collective-permute-start.27 = (bf16[128,512]{1,0:T(8,128)(2,1)S(1)}, bf16[128,512]{1,0:T(8,128)(2,1)S(1)}, u32[]{:S(2)}, u32[]{:S(2)}) collective-permute-start(bf16[128,512]{1,0:T(8,128)(2,1)S(1)} %pad_maximum_fusion.3.refs_0_), channel_id=1, source_target_pairs={{0,2},{1,3},{2,0},{3,1},{4,6},{5,7},{6,4},{7,5},{8,10},{9,11},{10,... | collective-permute-start | bytes 393224 | tf_op jit(solution)/shard_map/ppermute | solution.py:19
  84.9 7.8 %collective-permute-start.28 = (bf16[128,512]{1,0:T(8,128)(2,1)S(1)}, bf16[128,512]{1,0:T(8,128)(2,1)S(1)}, u32[]{:S(2)}, u32[]{:S(2)}) collective-permute-start(bf16[128,512]{1,0:T(8,128)(2,1)S(1)} %pad_maximum_fusion.3.refs_0_), channel_id=1, source_target_pairs={{0,3},{1,2},{2,1},{3,0},{4,7},{5,6},{6,5},{7,4},{8,11},{9,10},{10,... | collective-permute-start | bytes 393224 | tf_op jit(solution)/shard_map/ppermute | solution.py:19
  93.8 4.1 %collective-permute-start.29 = (f32[8,128]{1,0:T(8,128)S(1)}, f32[8,128]{1,0:T(8,128)S(1)}, u32[]{:S(2)}, u32[]{:S(2)}) collective-permute-start(f32[8,128]{1,0:T(8,128)S(1)} %get-tuple-element.64), channel_id=1, source_target_pairs={{0,1},{1,0},{2,3},{3,2},{4,5},{5,4},{6,7},{7,6},{8,9},{9,8},{10,11... | collective-permute-start | bytes 12296 | tf_op jit(solution)/shard_map/ppermute | solution.py:19
  97.9 4.6 %collective-permute-start.30 = (f32[8,128]{1,0:T(8,128)S(1)}, f32[8,128]{1,0:T(8,128)S(1)}, u32[]{:S(2)}, u32[]{:S(2)}) collective-permute-start(f32[8,128]{1,0:T(8,128)S(1)} %add.103), channel_id=1, source_target_pairs={{0,2},{1,3},{2,0},{3,1},{4,6},{5,7},{6,4},{7,5},{8,10},{9,11},{10,... | collective-permute-start | bytes 12296 | tf_op jit(solution)/shard_map/ppermute | solution.py:19
  102.5 3.7 %collective-permute-start.31 = (f32[8,128]{1,0:T(8,128)S(1)}, f32[8,128]{1,0:T(8,128)S(1)}, u32[]{:S(2)}, u32[]{:S(2)}) collective-permute-start(f32[8,128]{1,0:T(8,128)S(1)} %add.104), channel_id=1, source_target_pairs={{0,4},{4,0},{8,12},{12,8},{1,5},{5,1},{9,13},{13,9},{2,6},{6,2},{1... | collective-permute-start | bytes 12296 | tf_op jit(solution)/shard_map/ppermute | solution.py:19
  106.2 3.7 %collective-permute-start.32 = (f32[8,128]{1,0:T(8,128)S(1)}, f32[8,128]{1,0:T(8,128)S(1)}, u32[]{:S(2)}, u32[]{:S(2)}) collective-permute-start(f32[8,128]{1,0:T(8,128)S(1)} %add.105), channel_id=1, source_target_pairs={{0,8},{4,12},{8,0},{12,4},{1,9},{5,13},{9,1},{13,5},{2,10},{6,14},... | collective-permute-start | bytes 12296 | tf_op jit(solution)/shard_map/ppermute | solution.py:19
  109.9 10.5 %copy-start.11 = (f32[3]{0:T(128)S(1)}, f32[3]{0:T(128)}, u32[]{:S(2)}) copy-start(f32[3]{0:T(128)} %constant.50) | copy-start | bytes 40
  109.9 10.5 %collective-permute-start.33 = (f32[8,128]{1,0:T(8,128)S(1)}, f32[8,128]{1,0:T(8,128)S(1)}, u32[]{:S(2)}, u32[]{:S(2)}) collective-permute-start(f32[8,128]{1,0:T(8,128)S(1)} %add.106), channel_id=1, source_target_pairs={{0,16},{16,0},{1,17},{17,1},{2,18},{18,2},{3,19},{19,3},{4,20},{20... | collective-permute-start | bytes 12296 | tf_op jit(solution)/shard_map/ppermute | solution.py:19
  (1 other events, 2.0 us)

commit v5 on v4

--- a/solution.py
+++ b/solution.py
@@ -40,6 +40,10 @@
 def gather_in(rows, section, axis):
     size = lax.axis_size(axis)
     return [rows] + [swap_in(rows, section, axis, k) for k in range(1, size)]
+
+
+def gather(rows, axis):
+    return [rows] + [swap(rows, axis, k) for k in range(1, lax.axis_size(axis))]
 
 
 def scatter_sum(start, terms, source, block):
@@ -243,8 +247,7 @@
     assert segments == 2
     micro, local_rows, width = layer_input_activations.shape
     gain = norm_gain[0][None, :]
-    gate_w, up_w = load_weights(w_gate, w_up)
-    down_w = w_down[0]
+    gate_w, up_w, down_w = load_weights(w_gate, w_up, w_down)
     units = down_w.shape[0]
     block = micro * local_rows
     tok_rows = block * tensor_size
@@ -252,9 +255,7 @@
 
     x_own = layer_input_activations.reshape(block, width)
     cot_own = cotangent.reshape(block, width)
-    x0 = jnp.concatenate(gather_in(x_own, 0, "tensor"), axis=0)
-    cot_late, gate_w, up_w = lax.optimization_barrier((cot_own, gate_w, up_w))
-    cot_rows = jnp.concatenate(gather_in(cot_late, 1, "tensor"), axis=0)
+    rows_in = jnp.concatenate(gather(jnp.where(first, x_own, cot_own), "tensor"), axis=0)
 
     def layer_parts(rows):
         widened = rows.astype(jnp.float32)
@@ -264,10 +265,10 @@
         up = jnp.dot(normed, up_w, preferred_element_type=jnp.float32)
         return widened, scale, gate, up
 
-    _, _, gate0, up0 = layer_parts(x0)
+    _, _, gate0, up0 = layer_parts(rows_in)
     hidden0 = (jax.nn.silu(gate0) * up0).astype(jnp.bfloat16)
     mixed = jnp.dot(hidden0, down_w, preferred_element_type=jnp.float32).astype(jnp.bfloat16)
-    cot_rows, hidden0, mixed = lax.optimization_barrier((cot_rows, hidden0, mixed))
+    cot_rows, hidden0, mixed = lax.optimization_barrier((rows_in, hidden0, mixed))
     d_hidden = lax.dot_general(cot_rows, down_w, CONTRACT_LAST, preferred_element_type=jnp.float32)
     x1_own = scatter_sum(x_own, mixed, 0, block)
     x1_own, d_hidden = lax.optimization_barrier((x1_own, d_hidden))
@@ -306,7 +307,7 @@
     pieces1 = gather_in(hidden1, 1, "dp")
     columns = jnp.concatenate([message[:block] for message in messages], axis=0)
     columns, pieces1 = lax.optimization_barrier((columns, pieces1))
-    parts_y = [columns] + [swap(columns, "tensor", k) for k in range(1, tensor_size)]
+    parts_y = gather(columns, "tensor")
     hidden_all, gram_hidden = assemble(segment, pieces0, pieces1)
     ids_all = jnp.stack([message[block : block + micro, 0] for message in messages])
     row_ids = jnp.broadcast_to(
@@ -314,18 +315,24 @@
     ).reshape(dp_size * tok_rows, 1)
     levels = dp_size.bit_length()
     y, norms = norm_sums(row_ids, gram_hidden, parts_y, dp_size, levels)
-    rounds = [(axis, bit) for axis in ("tensor", "dp", "section") for bit in range(bits(axis))]
+    rounds = [
+        (axis, bit, min(2, bits(axis) - bit))
+        for axis in ("tensor", "dp", "section")
+        for bit in range(0, bits(axis), 2)
+    ]
     tiles = units // TILE
-    parts = min(3, tiles)
+    parts = min(len(rounds), tiles)
     grads = None
     begin = 0
-    for part, (axis, bit) in enumerate(rounds):
-        other = swap(norms, axis, 2**bit)
+    for part, (axis, bit, count) in enumerate(rounds):
+        others = [swap(norms, axis, k << bit) for k in range(1, 1 << count)]
         if part < parts:
             end = tiles * (part + 1) // parts
             grads = domain_gradients(row_ids, hidden_all, y, begin, end - begin, grads)
             begin = end
-        norms = norms + other
+        norms = norms + others[0]
+        if count == 2:
+            norms = norms + (others[1] + others[2])
         row_ids, norms = lax.optimization_barrier((row_ids, norms))
     entries = segments * units * tensor_size * width
     counts = [float((dp_size >> level) * entries) for level in range(levels)]

time: 122 us -> 111 us (0.910)
  waiting for transfers between devices: 24 us -> 16.2 us
  starting transfers between devices: 58.9 us -> 53.4 us
  Pallas kernels: 18.8 us -> 20.9 us
    ppermute x15 -> x9, starting transfers between devices: 26.8 us -> 13.3 us  [swap_in(): return lax.ppermute(block, ('section', axis), route)]
    ppermute x11 -> x16, starting transfers between devices: 19.7 us -> 27.9 us  [swap(): return lax.ppermute(block, axis, [(i, i ^ offset) for i in range(size)])]
    ppermute x8, waiting for transfers between devices: 11.1 us -> 6.99 us  [across(): return lax.ppermute(block, ('section', 'tensor'), route)]
    ppermute x11 -> x16, waiting for transfers between devices: 10.6 us -> 7.97 us  [swap(): return lax.ppermute(block, axis, [(i, i ^ offset) for i in range(size)])]
    pallas_call x1, Pallas kernels: 5.19 us -> 7.28 us  [load_weights(): pl.pallas_call(load_kernel, in_specs=[pl.BlockSpec(memory_space=pltpu.HBM...]
  transfers between devices with their start and end apart: 34 -> 33, of which waited for: 10 -> 10; matrix products, arithmetic and copies ran while one was open for 13% -> 11% of each run, Pallas kernels for 15% -> 18%
where the time goes in v5:
time: 111 us; the launch traced here: 110 us
  starting transfers between devices  53.4 us (48%)
  Pallas kernels  20.9 us (19%)
  waiting for transfers between devices  16.2 us (15%)
  matrix products  14 us (13%)
  other arithmetic  2.56 us (2%)
  local copies, waits for them, and re-layouts  2.05 us (2%)
  between operations  1.29 us (1%)
    ppermute x16, starting transfers between devices, swap(): return lax.ppermute(block, axis, [(i, i ^ offset) for i in range(size)])  27.9 us
    ppermute x9, starting transfers between devices, swap_in(): return lax.ppermute(block, ('section', axis), route)  13.3 us
    ppermute x8, starting transfers between devices, across(): return lax.ppermute(block, ('section', 'tensor'), route)  12.2 us
    pallas_call x3, Pallas kernels, domain_gradients(): pl.pallas_call(gradient_kernel, grid=(count,), in_specs=in_specs, out_spe...  9.93 us
    ppermute x16, waiting for transfers between devices, swap(): return lax.ppermute(block, axis, [(i, i ^ offset) for i in range(size)])  7.97 us
    pallas_call x1, Pallas kernels, load_weights(): pl.pallas_call(load_kernel, in_specs=[pl.BlockSpec(memory_space=pltpu.HBM...  7.28 us
    ppermute x8, waiting for transfers between devices, across(): return lax.ppermute(block, ('section', 'tensor'), route)  6.99 us
    dot_general x2, matrix products, layer_parts(): up = jnp.dot(normed, up_w, preferred_element_type=jnp.float32)  2.87 us
  transfers between devices with their start and end apart: 33, of which 10 were waited for; matrix products, arithmetic and copies ran while one was open for 11% of the time, Pallas kernels for 18%

profile of v5, /device:TPU:0, one launch (start us, length us, event | category | flops | bytes accessed | tf_op | source)
XLA Modules:
  0.0 110.3 jit_solution(2401576655793779100)
XLA Ops:
  0.6 1.0 bitcast_select_fusion
  1.6 5.1 %collective-permute-start.2 = (bf16[32,2048]{1,0:T(8,128)(2,1)S(1)}, bf16[32,2048]{1,0:T(8,128)(2,1)S(1)}, u32[]{:S(2)}, u32[]{:S(2)}) collective-permute-start(bf16[32,2048]{1,0:T(8,128)(2,1)S(1)} %bitcast_select_fusion), channel_id=1, source_target_pairs={{0,3},{1,2},{2,1},{3,0},{4,7},{5,6},{6,5},{7,4},{8,11},{9,10},{10,... | collective-permute-start | bytes 393224 | tf_op jit(solution)/shard_map/ppermute | solution.py:19
  7.4 7.3 %shard_map.95 = (bf16[2048,1792]{1,0:T(8,128)(2,1)S(1)}, bf16[2048,1792]{1,0:T(8,128)(2,1)S(1)}, bf16[1792,2048]{1,0:T(8,128)(2,1)S(1)}) custom-call(bf16[1,2048,1792]{2,1,0:T(8,128)(2,1)} %refs_0_.1, bf16[1,2048,1792]{2,1,0:T(8,128)(2,1)} %refs_1_.1, bf16[1,1792,2048]{2,1,0:T(8,128)(2,1)} %refs_2_.1), custom_call_target="tpu_custom_call" | custom-call | bytes 22020096 | tf_op jit(solution)/shard_map/pallas_call | solution.py:72
  14.7 3.1 %collective-permute-done.1 = bf16[32,2048]{1,0:T(8,128)(2,1)S(1)} collective-permute-done((bf16[32,2048]{1,0:T(8,128)(2,1)S(1)}, bf16[32,2048]{1,0:T(8,128)(2,1)S(1)}, u32[]{:S(2)}, u32[]{:S(2)}) %collective-permute-start.1) | collective-permute-done | bytes 131104 | tf_op jit(solution)/shard_map/ppermute | solution.py:19
  18.0 1.2 %fusion.17 = f32[128,1792]{1,0:T(8,128)S(1)} fusion(bf16[2048,1792]{1,0:T(8,128)(2,1)S(1)} %get-tuple-element.35, bf16[128,2048]{1,0:T(8,128)(2,1)S(1)} %get-tuple-element.39, f32[2048]{0:T(1024)S(1)} %bitcast.29, f32[128]{0:T(128)S(1)} %add_rsqrt_fusion.1), kind=kOutput, calls=%fused_computation.31 | convolution fusion | flops 940572672 | bytes 8790528 | tf_op jit(solution)/shard_map/dot_general | solution.py:264
  19.2 1.4 %fusion.1.refs_0_ = bf16[128,1792]{1,0:T(8,128)(2,1)S(1)} fusion(bf16[2048,1792]{1,0:T(8,128)(2,1)S(1)} %get-tuple-element.36, f32[128,1792]{1,0:T(8,128)S(1)} %fusion.17, bf16[128,2048]{1,0:T(8,128)(2,1)S(1)} %get-tuple-element.39, f32[2048]{0:T(1024)S(1)} %bitcast.30, f32[128]{0:T(128)S(1)} %add_rsqrt_fusion.1), kind=kOutput, calls=%fused_computation.3 | convolution fusion | flops 941948928 | bytes 9249280 | tf_op jit(solution)/shard_map/dot_general | solution.py:265
  20.6 1.1 %convolution_convert_fusion = bf16[128,2048]{1,0:T(8,128)(2,1)S(1)} fusion(bf16[128,1792]{1,0:T(8,128)(2,1)S(1)} %fusion.1.refs_0_, bf16[1792,2048]{1,0:T(8,128)(2,1)S(1)} %get-tuple-element.37), kind=kOutput, calls=%fused_computation.4 | convolution fusion | flops 939786240 | bytes 8323072 | tf_op jit(solution)/shard_map/dot_general | solution.py:270
  21.8 3.0 %collective-permute-start.6 = (bf16[32,2048]{1,0:T(8,128)(2,1)S(1)}, bf16[32,2048]{1,0:T(8,128)(2,1)S(1)}, u32[]{:S(2)}, u32[]{:S(2)}) collective-permute-start(bf16[32,2048]{1,0:T(8,128)(2,1)S(1)} %get-tuple-element.78), channel_id=1, source_target_pairs={{0,19},{1,18},{2,17},{3,16},{4,23},{5,22},{6,21},{7,20},{8,27},{9,... | collective-permute-start | bytes 393224 | tf_op jit(solution)/shard_map/ppermute | solution.py:33
  24.8 1.3 %collective-permute-start.5 = (bf16[32,2048]{1,0:T(8,128)(2,1)S(1)}, bf16[32,2048]{1,0:T(8,128)(2,1)S(1)}, u32[]{:S(2)}, u32[]{:S(2)}) collective-permute-start(bf16[32,2048]{1,0:T(8,128)(2,1)S(1)} %get-tuple-element.79), channel_id=1, source_target_pairs={{0,18},{1,19},{2,16},{3,17},{4,22},{5,23},{6,20},{7,21},{8,26},{9,... | collective-permute-start | bytes 393224 | tf_op jit(solution)/shard_map/ppermute | solution.py:33
  26.1 1.3 %collective-permute-start.4 = (bf16[32,2048]{1,0:T(8,128)(2,1)S(1)}, bf16[32,2048]{1,0:T(8,128)(2,1)S(1)}, u32[]{:S(2)}, u32[]{:S(2)}) collective-permute-start(bf16[32,2048]{1,0:T(8,128)(2,1)S(1)} %get-tuple-element.80), channel_id=1, source_target_pairs={{0,17},{1,16},{2,19},{3,18},{4,21},{5,20},{6,23},{7,22},{8,25},{9,... | collective-permute-start | bytes 393224 | tf_op jit(solution)/shard_map/ppermute | solution.py:33
  27.4 1.3 %collective-permute-start.3 = (bf16[32,2048]{1,0:T(8,128)(2,1)S(1)}, bf16[32,2048]{1,0:T(8,128)(2,1)S(1)}, u32[]{:S(2)}, u32[]{:S(2)}) collective-permute-start(bf16[32,2048]{1,0:T(8,128)(2,1)S(1)} %get-tuple-element.77), channel_id=1, source_target_pairs={{0,16},{1,17},{2,18},{3,19},{4,20},{5,21},{6,22},{7,23},{8,24},{9,... | collective-permute-start | bytes 393224 | tf_op jit(solution)/shard_map/ppermute | solution.py:33
  28.7 2.5 %fusion.22 = f32[128,1792]{1,0:T(8,128)S(1)} fusion(bf16[128,2048]{1,0:T(8,128)(2,1)S(1)} %get-tuple-element.39, bf16[1792,2048]{1,0:T(8,128)(2,1)S(1)} %get-tuple-element.37), kind=kOutput, calls=%fused_computation.56 | convolution fusion | flops 939524096 | bytes 8781824 | tf_op jit(solution)/shard_map/dot_general | solution.py:272
  31.4 0.7 collective-permute-start.9
  32.0 0.7 collective-permute-start.8
  32.7 0.7 collective-permute-start.7
  33.5 3.4 %collective-permute-start.10 = (bf16[128,1792]{1,0:T(8,128)(2,1)S(1)}, bf16[128,1792]{1,0:T(8,128)(2,1)S(1)}, u32[]{:S(2)}, u32[]{:S(2)}) collective-permute-start(bf16[128,1792]{1,0:T(8,128)(2,1)S(1)} %fusion.1.refs_0_), channel_id=1, source_target_pairs={{0,4},{4,0},{8,12},{12,8},{1,5},{5,1},{9,13},{13,9},{2,6},{6,2},{1... | collective-permute-start | bytes 1376264 | tf_op jit(solution)/shard_map/ppermute | solution.py:25
  36.9 3.4 %collective-permute-start.11 = (bf16[128,1792]{1,0:T(8,128)(2,1)S(1)}, bf16[128,1792]{1,0:T(8,128)(2,1)S(1)}, u32[]{:S(2)}, u32[]{:S(2)}) collective-permute-start(bf16[128,1792]{1,0:T(8,128)(2,1)S(1)} %fusion.1.refs_0_), channel_id=1, source_target_pairs={{0,8},{4,12},{8,0},{12,4},{1,9},{5,13},{9,1},{13,5},{2,10},{6,14},... | collective-permute-start | bytes 1376264 | tf_op jit(solution)/shard_map/ppermute | solution.py:25
  40.3 2.4 %collective-permute-start.12 = (bf16[128,1792]{1,0:T(8,128)(2,1)S(1)}, bf16[128,1792]{1,0:T(8,128)(2,1)S(1)}, u32[]{:S(2)}, u32[]{:S(2)}) collective-permute-start(bf16[128,1792]{1,0:T(8,128)(2,1)S(1)} %fusion.1.refs_0_), channel_id=1, source_target_pairs={{0,12},{4,8},{8,4},{12,0},{1,13},{5,9},{9,5},{13,1},{2,14},{6,10},... | collective-permute-start | bytes 1376264 | tf_op jit(solution)/shard_map/ppermute | solution.py:25
  42.9 1.2 %fusion.12 = f32[128,1792]{1,0:T(8,128)S(1)} fusion(bf16[2048,1792]{1,0:T(8,128)(2,1)S(1)} %get-tuple-element.35, bf16[128,2048]{1,0:T(8,128)(2,1)S(1)} %pad_maximum_fusion.1, f32[128]{0:T(128)S(1)} %add_rsqrt_fusion, f32[2048]{0:T(1024)S(1)} %bitcast.31), kind=kOutput, calls=%fused_computation.29 | convolution fusion | flops 940572672 | bytes 8790528 | tf_op jit(solution)/shard_map/dot_general | solution.py:264
  44.1 1.5 %multiply_convert_fusion = (bf16[128,1792]{1,0:T(8,128)(2,1)S(1)}, bf16[128,1792]{1,0:T(8,128)(2,1)S(1)}, bf16[128,1792]{1,0:T(8,128)(2,1)S(1)}) fusion(f32[128,1792]{1,0:T(8,128)S(1)} %fusion.12, f32[128,1792]{1,0:T(8,128)S(1)} %fusion.22, bf16[2048,1792]{1,0:T(8,128)(2,1)S(1)} %get-tuple-element.36, bf16[128,2048]{1,0:T(8,128)(2,1)S(1)} %pad_maximum_fusion.1, ...), kind=kOutput, calls=%fused_computation.20 | convolution fusion | flops 944242688 | bytes 11084288 | tf_op jit(solution)/shard_map/dot_general | solution.py:265
  45.6 2.5 %fusion.23 = f32[128,2048]{1,0:T(8,128)S(1)} fusion(bf16[128,1792]{1,0:T(8,128)(2,1)S(1)} %get-tuple-element.44, bf16[2048,1792]{1,0:T(8,128)(2,1)S(1)} %get-tuple-element.35), kind=kOutput, calls=%fused_computation.57 | convolution fusion | flops 939524096 | bytes 8847360 | tf_op jit(solution)/shard_map/dot_general | solution.py:285
  48.1 2.6 %fusion.8 = (f32[128]{0:T(128)S(1)}, f32[128,2048]{1,0:T(8,128)S(1)}) fusion(bf16[128,2048]{1,0:T(8,128)(2,1)S(1)} %pad_maximum_fusion.1, f32[2048]{0:T(1024)S(1)} %bitcast.33, f32[128,2048]{1,0:T(8,128)S(1)} %fusion.23, bf16[128,1792]{1,0:T(8,128)(2,1)S(1)} %get-tuple-element.45, bf16[2048,1792]{1,0:T(8,128)(2,1)S(1)} %get-tuple-element.36), kind=kOutput, calls=%fused_computation.17 | convolution fusion | flops 940834688 | bytes 10428928 | tf_op jit(solution)/shard_map/dot_general | solution.py:286
  51.0 1.2 %collective-permute-done.11.refs_2_ = bf16[128,1792]{1,0:T(8,128)(2,1)S(1)} collective-permute-done((bf16[128,1792]{1,0:T(8,128)(2,1)S(1)}, bf16[128,1792]{1,0:T(8,128)(2,1)S(1)}, u32[]{:S(2)}, u32[]{:S(2)}) %collective-permute-start.11) | collective-permute-done | bytes 458784 | tf_op jit(solution)/shard_map/ppermute | solution.py:25
  52.2 1.3 %collective-permute-start.16 = (bf16[32,2048]{1,0:T(8,128)(2,1)S(1)}, bf16[32,2048]{1,0:T(8,128)(2,1)S(1)}, u32[]{:S(2)}, u32[]{:S(2)}) collective-permute-start(bf16[32,2048]{1,0:T(8,128)(2,1)S(1)} %get-tuple-element.74), channel_id=1, source_target_pairs={{16,3},{17,2},{18,1},{19,0},{20,7},{21,6},{22,5},{23,4},{24,11},{2... | collective-permute-start | bytes 393224 | tf_op jit(solution)/shard_map/ppermute | solution.py:33
  53.5 1.3 %collective-permute-start.15 = (bf16[32,2048]{1,0:T(8,128)(2,1)S(1)}, bf16[32,2048]{1,0:T(8,128)(2,1)S(1)}, u32[]{:S(2)}, u32[]{:S(2)}) collective-permute-start(bf16[32,2048]{1,0:T(8,128)(2,1)S(1)} %get-tuple-element.75), channel_id=1, source_target_pairs={{16,2},{17,3},{18,0},{19,1},{20,6},{21,7},{22,4},{23,5},{24,10},{2... | collective-permute-start | bytes 393224 | tf_op jit(solution)/shard_map/ppermute | solution.py:33
  54.8 1.3 %collective-permute-start.14 = (bf16[32,2048]{1,0:T(8,128)(2,1)S(1)}, bf16[32,2048]{1,0:T(8,128)(2,1)S(1)}, u32[]{:S(2)}, u32[]{:S(2)}) collective-permute-start(bf16[32,2048]{1,0:T(8,128)(2,1)S(1)} %get-tuple-element.76), channel_id=1, source_target_pairs={{16,1},{17,0},{18,3},{19,2},{20,5},{21,4},{22,7},{23,6},{24,9},{25... | collective-permute-start | bytes 393224 | tf_op jit(solution)/shard_map/ppermute | solution.py:33
  56.1 1.5 %collective-permute-start.13 = (bf16[32,2048]{1,0:T(8,128)(2,1)S(1)}, bf16[32,2048]{1,0:T(8,128)(2,1)S(1)}, u32[]{:S(2)}, u32[]{:S(2)}) collective-permute-start(bf16[32,2048]{1,0:T(8,128)(2,1)S(1)} %get-tuple-element.73), channel_id=1, source_target_pairs={{16,0},{17,1},{18,2},{19,3},{20,4},{21,5},{22,6},{23,7},{24,8},{25... | collective-permute-start | bytes 393224 | tf_op jit(solution)/shard_map/ppermute | solution.py:33
  57.7 3.2 %collective-permute-done.16 = bf16[32,2048]{1,0:T(8,128)(2,1)S(1)} collective-permute-done((bf16[32,2048]{1,0:T(8,128)(2,1)S(1)}, bf16[32,2048]{1,0:T(8,128)(2,1)S(1)}, u32[]{:S(2)}, u32[]{:S(2)}) %collective-permute-start.16) | collective-permute-done | bytes 131104 | tf_op jit(solution)/shard_map/ppermute | solution.py:33
  60.9 3.8 %collective-permute-done.15 = bf16[32,2048]{1,0:T(8,128)(2,1)S(1)} collective-permute-done((bf16[32,2048]{1,0:T(8,128)(2,1)S(1)}, bf16[32,2048]{1,0:T(8,128)(2,1)S(1)}, u32[]{:S(2)}, u32[]{:S(2)}) %collective-permute-start.15) | collective-permute-done | bytes 131104 | tf_op jit(solution)/shard_map/ppermute | solution.py:33
  65.0 2.5 %collective-permute-start.19 = (bf16[48,512]{1,0:T(8,128)(2,1)S(1)}, bf16[48,512]{1,0:T(8,128)(2,1)S(1)}, u32[]{:S(2)}, u32[]{:S(2)}) collective-permute-start(bf16[48,512]{1,0:T(8,128)(2,1)S(1)} %get-tuple-element.89), channel_id=1, source_target_pairs={{0,12},{4,8},{8,4},{12,0},{1,13},{5,9},{9,5},{13,1},{2,14},{6,10},... | collective-permute-start | bytes 147464 | tf_op jit(solution)/shard_map/ppermute | solution.py:19
  68.5 0.7 collective-permute-start.20
  69.2 0.7 collective-permute-start.21
  70.3 0.7 collective-permute-start.22
  71.6 1.1 collective-permute-done.17
  73.2 0.7 copy-done.8
  73.9 1.5 %collective-permute-start.24 = (bf16[128,512]{1,0:T(8,128)(2,1)S(1)}, bf16[128,512]{1,0:T(8,128)(2,1)S(1)}, u32[]{:S(2)}, u32[]{:S(2)}) collective-permute-start(bf16[128,512]{1,0:T(8,128)(2,1)S(1)} %pad_maximum_fusion.2.refs_0_), channel_id=1, source_target_pairs={{0,2},{1,3},{2,0},{3,1},{4,6},{5,7},{6,4},{7,5},{8,10},{9,11},{10,... | collective-permute-start | bytes 393224 | tf_op jit(solution)/shard_map/ppermute | solution.py:19
  75.4 2.2 %collective-permute-start.25 = (bf16[128,512]{1,0:T(8,128)(2,1)S(1)}, bf16[128,512]{1,0:T(8,128)(2,1)S(1)}, u32[]{:S(2)}, u32[]{:S(2)}) collective-permute-start(bf16[128,512]{1,0:T(8,128)(2,1)S(1)} %pad_maximum_fusion.2.refs_0_), channel_id=1, source_target_pairs={{0,3},{1,2},{2,1},{3,0},{4,7},{5,6},{6,5},{7,4},{8,11},{9,10},{10,... | collective-permute-start | bytes 393224 | tf_op jit(solution)/shard_map/ppermute | solution.py:19
  78.0 2.6 %shard_map.96 = (bf16[512,1792]{1,0:T(8,128)(2,1)S(1)}, f32[512,512]{1,0:T(8,128)S(1)}) custom-call(s32[1]{0:T(128)} %bitcast.5.flag_ref, bf16[128,1792]{1,0:T(8,128)(2,1)} %copy-done, bf16[128,1792]{1,0:T(8,128)(2,1)} %copy-done.3, bf16[128,1792]{1,0:T(8,128)(2,1)} %copy-done.4, bf16[128,1792]{1,0:T(8,128)(2,1)} %copy-done.5, bf16[128,1792]{1,0:T(8,128)(2,1)} %copy-done.6, ...), custom_call_target="tpu_custom_call" | custom-call | flops 939524096 | bytes 4718592 | tf_op jit(solution)/shard_map/pallas_call | solution.py:168
  80.7 1.9 %collective-permute-done.24.refs_2_ = bf16[128,512]{1,0:T(8,128)(2,1)S(1)} collective-permute-done((bf16[128,512]{1,0:T(8,128)(2,1)S(1)}, bf16[128,512]{1,0:T(8,128)(2,1)S(1)}, u32[]{:S(2)}, u32[]{:S(2)}) %collective-permute-start.24) | collective-permute-done | bytes 131104 | tf_op jit(solution)/shard_map/ppermute | solution.py:19
  82.6 1.1 shard_map.97
  83.7 2.2 %collective-permute-start.27 = (f32[8,128]{1,0:T(8,128)S(1)}, f32[8,128]{1,0:T(8,128)S(1)}, u32[]{:S(2)}, u32[]{:S(2)}) collective-permute-start(f32[8,128]{1,0:T(8,128)S(1)} %get-tuple-element.60), channel_id=1, source_target_pairs={{0,2},{1,3},{2,0},{3,1},{4,6},{5,7},{6,4},{7,5},{8,10},{9,11},{10,... | collective-permute-start | bytes 12296 | tf_op jit(solution)/shard_map/ppermute | solution.py:19
  85.9 2.2 %collective-permute-start.28 = (f32[8,128]{1,0:T(8,128)S(1)}, f32[8,128]{1,0:T(8,128)S(1)}, u32[]{:S(2)}, u32[]{:S(2)}) collective-permute-start(f32[8,128]{1,0:T(8,128)S(1)} %get-tuple-element.60), channel_id=1, source_target_pairs={{0,3},{1,2},{2,1},{3,0},{4,7},{5,6},{6,5},{7,4},{8,11},{9,10},{10,... | collective-permute-start | bytes 12296 | tf_op jit(solution)/shard_map/ppermute | solution.py:19
  88.1 3.0 %shard_map.98.rest_0_ = bf16[4,1792,512]{2,1,0:T(8,128)(2,1)} custom-call(s32[512,1]{1,0:T(8,128)S(1)} %copy.12.ids_ref, bf16[512,1792]{1,0:T(8,128)(2,1)S(1)} %get-tuple-element.64.hidden_ref, bf16[512,512]{1,0:T(8,128)(2,1)S(1)} %get-tuple-element.65.y_ref), custom_call_target="tpu_custom_call" | custom-call | flops 1073741824 | bytes 2621440 | tf_op jit(solution)/shard_map/pallas_call | solution.py:114
  91.9 1.5 %collective-permute-start.30 = (f32[8,128]{1,0:T(8,128)S(1)}, f32[8,128]{1,0:T(8,128)S(1)}, u32[]{:S(2)}, u32[]{:S(2)}) collective-permute-start(f32[8,128]{1,0:T(8,128)S(1)} %add_add_fusion.1), channel_id=1, source_target_pairs={{0,8},{4,12},{8,0},{12,4},{1,9},{5,13},{9,1},{13,5},{2,10},{6,14},... | collective-permute-start | bytes 12296 | tf_op jit(solution)/shard_map/ppermute | solution.py:19
  93.9 1.5 %collective-permute-start.29 = (f32[8,128]{1,0:T(8,128)S(1)}, f32[8,128]{1,0:T(8,128)S(1)}, u32[]{:S(2)}, u32[]{:S(2)}) collective-permute-start(f32[8,128]{1,0:T(8,128)S(1)} %add_add_fusion.1), channel_id=1, source_target_pairs={{0,4},{4,0},{8,12},{12,8},{1,5},{5,1},{9,13},{13,9},{2,6},{6,2},{1... | collective-permute-start | bytes 12296 | tf_op jit(solution)/shard_map/ppermute | solution.py:19
  95.6 3.0 %shard_map.99.rest_0_ = bf16[4,1792,512]{2,1,0:T(8,128)(2,1)} custom-call(s32[512,1]{1,0:T(8,128)S(1)} %copy.14.ids_ref, bf16[512,1792]{1,0:T(8,128)(2,1)S(1)} %get-tuple-element.64.hidden_ref, bf16[512,512]{1,0:T(8,128)(2,1)S(1)} %get-tuple-element.65.y_ref, bf16[4,1792,512]{2,1,0:T(8,128)(2,1)} %shard_map.98.rest_0_), custom_call_target="tpu_custom_call", output_to_operand_aliasing={{}: (3, {})} | custom-call | flops 1073741824 | bytes 2621440 | tf_op jit(solution)/shard_map/pallas_call | solution.py:114
  98.8 7.0 %collective-permute-start.32 = (f32[8,128]{1,0:T(8,128)S(1)}, f32[8,128]{1,0:T(8,128)S(1)}, u32[]{:S(2)}, u32[]{:S(2)}) collective-permute-start(f32[8,128]{1,0:T(8,128)S(1)} %add_add_fusion), channel_id=1, source_target_pairs={{0,16},{16,0},{1,17},{17,1},{2,18},{18,2},{3,19},{19,3},{4,20},{20... | collective-permute-start | bytes 12296 | tf_op jit(solution)/shard_map/ppermute | solution.py:19
  105.7 3.9 %shard_map.100 = bf16[4,1792,512]{2,1,0:T(8,128)(2,1)} custom-call(s32[512,1]{1,0:T(8,128)S(1)} %copy.15.ids_ref, bf16[512,1792]{1,0:T(8,128)(2,1)S(1)} %get-tuple-element.64.hidden_ref, bf16[512,512]{1,0:T(8,128)(2,1)S(1)} %get-tuple-element.65.y_ref, bf16[4,1792,512]{2,1,0:T(8,128)(2,1)} %shard_map.99.rest_0_), custom_call_target="tpu_custom_call", output_to_operand_aliasing={{}: (3, {})} | custom-call | flops 1610612736 | bytes 3932160 | tf_op jit(solution)/shard_map/pallas_call | solution.py:114
  (93 shorter events, 7.0 us)
Async XLA Ops:
  1.6 16.4 %copy-start.10 = (f32[1,2048]{1,0:T(1,128)S(1)}, f32[1,2048]{1,0:T(1,128)}, u32[]{:S(2)}) copy-start(f32[1,2048]{1,0:T(1,128)} %param.11) | copy-start | bytes 24580
  1.6 13.1 %collective-permute-start.2 = (bf16[32,2048]{1,0:T(8,128)(2,1)S(1)}, bf16[32,2048]{1,0:T(8,128)(2,1)S(1)}, u32[]{:S(2)}, u32[]{:S(2)}) collective-permute-start(bf16[32,2048]{1,0:T(8,128)(2,1)S(1)} %bitcast_select_fusion), channel_id=1, source_target_pairs={{0,3},{1,2},{2,1},{3,0},{4,7},{5,6},{6,5},{7,4},{8,11},{9,10},{10,... | collective-permute-start | bytes 393224 | tf_op jit(solution)/shard_map/ppermute | solution.py:19
  6.8 11.1 %collective-permute-start.1 = (bf16[32,2048]{1,0:T(8,128)(2,1)S(1)}, bf16[32,2048]{1,0:T(8,128)(2,1)S(1)}, u32[]{:S(2)}, u32[]{:S(2)}) collective-permute-start(bf16[32,2048]{1,0:T(8,128)(2,1)S(1)} %bitcast_select_fusion), channel_id=1, source_target_pairs={{0,2},{1,3},{2,0},{3,1},{4,6},{5,7},{6,4},{7,5},{8,10},{9,11},{10,... | collective-permute-start | bytes 393224 | tf_op jit(solution)/shard_map/ppermute | solution.py:19
  6.8 11.1 %collective-permute-start = (bf16[32,2048]{1,0:T(8,128)(2,1)S(1)}, bf16[32,2048]{1,0:T(8,128)(2,1)S(1)}, u32[]{:S(2)}, u32[]{:S(2)}) collective-permute-start(bf16[32,2048]{1,0:T(8,128)(2,1)S(1)} %bitcast_select_fusion), channel_id=1, source_target_pairs={{0,1},{1,0},{2,3},{3,2},{4,5},{5,4},{6,7},{7,6},{8,9},{9,8},{10,11... | collective-permute-start | bytes 393224 | tf_op jit(solution)/shard_map/ppermute | solution.py:19
  20.6 19.7 %copy-start = (bf16[128,1792]{1,0:T(8,128)(2,1)}, bf16[128,1792]{1,0:T(8,128)(2,1)S(1)}, u32[]{:S(2)}) copy-start(bf16[128,1792]{1,0:T(8,128)(2,1)S(1)} %fusion.1.refs_0_) | copy-start | bytes 1376260
  21.7 9.5 %copy-start.1 = (bf16[4,8,2048]{2,1,0:T(8,128)(2,1)S(1)}, bf16[4,8,2048]{2,1,0:T(8,128)(2,1)}, u32[]{:S(2)}) copy-start(bf16[4,8,2048]{2,1,0:T(8,128)(2,1)} %param.8) | copy-start | bytes 393220
  21.8 9.4 %collective-permute-start.6 = (bf16[32,2048]{1,0:T(8,128)(2,1)S(1)}, bf16[32,2048]{1,0:T(8,128)(2,1)S(1)}, u32[]{:S(2)}, u32[]{:S(2)}) collective-permute-start(bf16[32,2048]{1,0:T(8,128)(2,1)S(1)} %get-tuple-element.78), channel_id=1, source_target_pairs={{0,19},{1,18},{2,17},{3,16},{4,23},{5,22},{6,21},{7,20},{8,27},{9,... | collective-permute-start | bytes 393224 | tf_op jit(solution)/shard_map/ppermute | solution.py:33
  24.8 6.5 %collective-permute-start.5 = (bf16[32,2048]{1,0:T(8,128)(2,1)S(1)}, bf16[32,2048]{1,0:T(8,128)(2,1)S(1)}, u32[]{:S(2)}, u32[]{:S(2)}) collective-permute-start(bf16[32,2048]{1,0:T(8,128)(2,1)S(1)} %get-tuple-element.79), channel_id=1, source_target_pairs={{0,18},{1,19},{2,16},{3,17},{4,22},{5,23},{6,20},{7,21},{8,26},{9,... | collective-permute-start | bytes 393224 | tf_op jit(solution)/shard_map/ppermute | solution.py:33
  26.1 5.2 %collective-permute-start.4 = (bf16[32,2048]{1,0:T(8,128)(2,1)S(1)}, bf16[32,2048]{1,0:T(8,128)(2,1)S(1)}, u32[]{:S(2)}, u32[]{:S(2)}) collective-permute-start(bf16[32,2048]{1,0:T(8,128)(2,1)S(1)} %get-tuple-element.80), channel_id=1, source_target_pairs={{0,17},{1,16},{2,19},{3,18},{4,21},{5,20},{6,23},{7,22},{8,25},{9,... | collective-permute-start | bytes 393224 | tf_op jit(solution)/shard_map/ppermute | solution.py:33
  27.4 3.9 %collective-permute-start.3 = (bf16[32,2048]{1,0:T(8,128)(2,1)S(1)}, bf16[32,2048]{1,0:T(8,128)(2,1)S(1)}, u32[]{:S(2)}, u32[]{:S(2)}) collective-permute-start(bf16[32,2048]{1,0:T(8,128)(2,1)S(1)} %get-tuple-element.77), channel_id=1, source_target_pairs={{0,16},{1,17},{2,18},{3,19},{4,20},{5,21},{6,22},{7,23},{8,24},{9,... | collective-permute-start | bytes 393224 | tf_op jit(solution)/shard_map/ppermute | solution.py:33
  31.4 2.0 %collective-permute-start.9 = (bf16[32,2048]{1,0:T(8,128)(2,1)S(1)}, bf16[32,2048]{1,0:T(8,128)(2,1)S(1)}, u32[]{:S(2)}, u32[]{:S(2)}) collective-permute-start(bf16[32,2048]{1,0:T(8,128)(2,1)S(1)} %add_convert_fusion.1), channel_id=1, source_target_pairs={{16,19},{17,18},{18,17},{19,16},{20,23},{21,22},{22,21},{23,20},{2... | collective-permute-start | bytes 393224 | tf_op jit(solution)/shard_map/ppermute | solution.py:25
  32.0 1.4 %collective-permute-start.8 = (bf16[32,2048]{1,0:T(8,128)(2,1)S(1)}, bf16[32,2048]{1,0:T(8,128)(2,1)S(1)}, u32[]{:S(2)}, u32[]{:S(2)}) collective-permute-start(bf16[32,2048]{1,0:T(8,128)(2,1)S(1)} %add_convert_fusion.1), channel_id=1, source_target_pairs={{16,18},{17,19},{18,16},{19,17},{20,22},{21,23},{22,20},{23,21},{2... | collective-permute-start | bytes 393224 | tf_op jit(solution)/shard_map/ppermute | solution.py:25
  32.7 0.7 collective-permute-start.7
  33.5 17.5 %collective-permute-start.10 = (bf16[128,1792]{1,0:T(8,128)(2,1)S(1)}, bf16[128,1792]{1,0:T(8,128)(2,1)S(1)}, u32[]{:S(2)}, u32[]{:S(2)}) collective-permute-start(bf16[128,1792]{1,0:T(8,128)(2,1)S(1)} %fusion.1.refs_0_), channel_id=1, source_target_pairs={{0,4},{4,0},{8,12},{12,8},{1,5},{5,1},{9,13},{13,9},{2,6},{6,2},{1... | collective-permute-start | bytes 1376264 | tf_op jit(solution)/shard_map/ppermute | solution.py:25
  36.9 15.3 %collective-permute-start.11 = (bf16[128,1792]{1,0:T(8,128)(2,1)S(1)}, bf16[128,1792]{1,0:T(8,128)(2,1)S(1)}, u32[]{:S(2)}, u32[]{:S(2)}) collective-permute-start(bf16[128,1792]{1,0:T(8,128)(2,1)S(1)} %fusion.1.refs_0_), channel_id=1, source_target_pairs={{0,8},{4,12},{8,0},{12,4},{1,9},{5,13},{9,1},{13,5},{2,10},{6,14},... | collective-permute-start | bytes 1376264 | tf_op jit(solution)/shard_map/ppermute | solution.py:25
  40.3 11.8 %collective-permute-start.12 = (bf16[128,1792]{1,0:T(8,128)(2,1)S(1)}, bf16[128,1792]{1,0:T(8,128)(2,1)S(1)}, u32[]{:S(2)}, u32[]{:S(2)}) collective-permute-start(bf16[128,1792]{1,0:T(8,128)(2,1)S(1)} %fusion.1.refs_0_), channel_id=1, source_target_pairs={{0,12},{4,8},{8,4},{12,0},{1,13},{5,9},{9,5},{13,1},{2,14},{6,10},... | collective-permute-start | bytes 1376264 | tf_op jit(solution)/shard_map/ppermute | solution.py:25
  45.6 24.7 %copy-start.6 = (bf16[128,1792]{1,0:T(8,128)(2,1)}, bf16[128,1792]{1,0:T(8,128)(2,1)S(1)}, u32[]{:S(2)}) copy-start(bf16[128,1792]{1,0:T(8,128)(2,1)S(1)} %get-tuple-element.54.refs_4_) | copy-start | bytes 1376260
  48.1 9.5 %copy-start.12 = (s32[4,1]{0,1:T(1,128)S(1)}, s32[4,1]{0,1:T(1,128)}, u32[]{:S(2)}) copy-start(s32[4,1]{0,1:T(1,128)} %param.10) | copy-start | bytes 52
  48.1 16.6 %copy-start.2 = (bf16[4,8,2048]{2,1,0:T(8,128)(2,1)S(1)}, bf16[4,8,2048]{2,1,0:T(8,128)(2,1)}, u32[]{:S(2)}) copy-start(bf16[4,8,2048]{2,1,0:T(8,128)(2,1)} %param.9) | copy-start | bytes 393220
  51.0 27.0 %copy-start.3 = (bf16[128,1792]{1,0:T(8,128)(2,1)}, bf16[128,1792]{1,0:T(8,128)(2,1)S(1)}, u32[]{:S(2)}) copy-start(bf16[128,1792]{1,0:T(8,128)(2,1)S(1)} %collective-permute-done.10.refs_1_) | copy-start | bytes 1376260
  52.2 25.8 %copy-start.4 = (bf16[128,1792]{1,0:T(8,128)(2,1)}, bf16[128,1792]{1,0:T(8,128)(2,1)S(1)}, u32[]{:S(2)}) copy-start(bf16[128,1792]{1,0:T(8,128)(2,1)S(1)} %collective-permute-done.11.refs_2_) | copy-start | bytes 1376260
  52.2 25.8 %copy-start.5 = (bf16[128,1792]{1,0:T(8,128)(2,1)}, bf16[128,1792]{1,0:T(8,128)(2,1)S(1)}, u32[]{:S(2)}) copy-start(bf16[128,1792]{1,0:T(8,128)(2,1)S(1)} %collective-permute-done.12.refs_3_) | copy-start | bytes 1376260
  52.2 8.7 %collective-permute-start.16 = (bf16[32,2048]{1,0:T(8,128)(2,1)S(1)}, bf16[32,2048]{1,0:T(8,128)(2,1)S(1)}, u32[]{:S(2)}, u32[]{:S(2)}) collective-permute-start(bf16[32,2048]{1,0:T(8,128)(2,1)S(1)} %get-tuple-element.74), channel_id=1, source_target_pairs={{16,3},{17,2},{18,1},{19,0},{20,7},{21,6},{22,5},{23,4},{24,11},{2... | collective-permute-start | bytes 393224 | tf_op jit(solution)/shard_map/ppermute | solution.py:33
  53.5 11.2 %collective-permute-start.15 = (bf16[32,2048]{1,0:T(8,128)(2,1)S(1)}, bf16[32,2048]{1,0:T(8,128)(2,1)S(1)}, u32[]{:S(2)}, u32[]{:S(2)}) collective-permute-start(bf16[32,2048]{1,0:T(8,128)(2,1)S(1)} %get-tuple-element.75), channel_id=1, source_target_pairs={{16,2},{17,3},{18,0},{19,1},{20,6},{21,7},{22,4},{23,5},{24,10},{2... | collective-permute-start | bytes 393224 | tf_op jit(solution)/shard_map/ppermute | solution.py:33
  54.8 9.9 %collective-permute-start.14 = (bf16[32,2048]{1,0:T(8,128)(2,1)S(1)}, bf16[32,2048]{1,0:T(8,128)(2,1)S(1)}, u32[]{:S(2)}, u32[]{:S(2)}) collective-permute-start(bf16[32,2048]{1,0:T(8,128)(2,1)S(1)} %get-tuple-element.76), channel_id=1, source_target_pairs={{16,1},{17,0},{18,3},{19,2},{20,5},{21,4},{22,7},{23,6},{24,9},{25... | collective-permute-start | bytes 393224 | tf_op jit(solution)/shard_map/ppermute | solution.py:33
  56.1 8.6 %collective-permute-start.13 = (bf16[32,2048]{1,0:T(8,128)(2,1)S(1)}, bf16[32,2048]{1,0:T(8,128)(2,1)S(1)}, u32[]{:S(2)}, u32[]{:S(2)}) collective-permute-start(bf16[32,2048]{1,0:T(8,128)(2,1)S(1)} %get-tuple-element.73), channel_id=1, source_target_pairs={{16,0},{17,1},{18,2},{19,3},{20,4},{21,5},{22,6},{23,7},{24,8},{25... | collective-permute-start | bytes 393224 | tf_op jit(solution)/shard_map/ppermute | solution.py:33
  65.0 5.4 %collective-permute-start.19 = (bf16[48,512]{1,0:T(8,128)(2,1)S(1)}, bf16[48,512]{1,0:T(8,128)(2,1)S(1)}, u32[]{:S(2)}, u32[]{:S(2)}) collective-permute-start(bf16[48,512]{1,0:T(8,128)(2,1)S(1)} %get-tuple-element.89), channel_id=1, source_target_pairs={{0,12},{4,8},{8,4},{12,0},{1,13},{5,9},{9,5},{13,1},{2,14},{6,10},... | collective-permute-start | bytes 147464 | tf_op jit(solution)/shard_map/ppermute | solution.py:19
  67.5 4.1 %collective-permute-start.18 = (bf16[48,512]{1,0:T(8,128)(2,1)S(1)}, bf16[48,512]{1,0:T(8,128)(2,1)S(1)}, u32[]{:S(2)}, u32[]{:S(2)}) collective-permute-start(bf16[48,512]{1,0:T(8,128)(2,1)S(1)} %get-tuple-element.88), channel_id=1, source_target_pairs={{0,8},{4,12},{8,0},{12,4},{1,9},{5,13},{9,1},{13,5},{2,10},{6,14},... | collective-permute-start | bytes 147464 | tf_op jit(solution)/shard_map/ppermute | solution.py:19
  68.0 4.7 %collective-permute-start.17 = (bf16[48,512]{1,0:T(8,128)(2,1)S(1)}, bf16[48,512]{1,0:T(8,128)(2,1)S(1)}, u32[]{:S(2)}, u32[]{:S(2)}) collective-permute-start(bf16[48,512]{1,0:T(8,128)(2,1)S(1)} %get-tuple-element.87), channel_id=1, source_target_pairs={{0,4},{4,0},{8,12},{12,8},{1,5},{5,1},{9,13},{13,9},{2,6},{6,2},{1... | collective-permute-start | bytes 147464 | tf_op jit(solution)/shard_map/ppermute | solution.py:19
  68.5 4.5 %collective-permute-start.20 = (bf16[128,1792]{1,0:T(8,128)(2,1)S(1)}, bf16[128,1792]{1,0:T(8,128)(2,1)S(1)}, u32[]{:S(2)}, u32[]{:S(2)}) collective-permute-start(bf16[128,1792]{1,0:T(8,128)(2,1)S(1)} %get-tuple-element.54.refs_4_), channel_id=1, source_target_pairs={{16,20},{20,16},{24,28},{28,24},{17,21},{21,17},{25,29},{29,25},{1... | collective-permute-start | bytes 1376264 | tf_op jit(solution)/shard_map/ppermute | solution.py:25
  69.2 3.9 %collective-permute-start.21 = (bf16[128,1792]{1,0:T(8,128)(2,1)S(1)}, bf16[128,1792]{1,0:T(8,128)(2,1)S(1)}, u32[]{:S(2)}, u32[]{:S(2)}) collective-permute-start(bf16[128,1792]{1,0:T(8,128)(2,1)S(1)} %get-tuple-element.54.refs_4_), channel_id=1, source_target_pairs={{16,24},{20,28},{24,16},{28,20},{17,25},{21,29},{25,17},{29,21},{1... | collective-permute-start | bytes 1376264 | tf_op jit(solution)/shard_map/ppermute | solution.py:25
  70.3 2.7 %collective-permute-start.22 = (bf16[128,1792]{1,0:T(8,128)(2,1)S(1)}, bf16[128,1792]{1,0:T(8,128)(2,1)S(1)}, u32[]{:S(2)}, u32[]{:S(2)}) collective-permute-start(bf16[128,1792]{1,0:T(8,128)(2,1)S(1)} %get-tuple-element.54.refs_4_), channel_id=1, source_target_pairs={{16,28},{20,24},{24,20},{28,16},{17,29},{21,25},{25,21},{29,17},{1... | collective-permute-start | bytes 1376264 | tf_op jit(solution)/shard_map/ppermute | solution.py:25
  73.0 5.0 %copy-start.7 = (bf16[128,1792]{1,0:T(8,128)(2,1)}, bf16[128,1792]{1,0:T(8,128)(2,1)S(1)}, u32[]{:S(2)}) copy-start(bf16[128,1792]{1,0:T(8,128)(2,1)S(1)} %collective-permute-done.20.refs_5_) | copy-start | bytes 1376260
  73.1 0.8 copy-start.8
  73.1 2.3 %copy-start.9 = (bf16[128,1792]{1,0:T(8,128)(2,1)}, bf16[128,1792]{1,0:T(8,128)(2,1)S(1)}, u32[]{:S(2)}) copy-start(bf16[128,1792]{1,0:T(8,128)(2,1)S(1)} %collective-permute-done.22.refs_7_) | copy-start | bytes 1376260
  73.1 7.6 %collective-permute-start.23 = (bf16[128,512]{1,0:T(8,128)(2,1)S(1)}, bf16[128,512]{1,0:T(8,128)(2,1)S(1)}, u32[]{:S(2)}, u32[]{:S(2)}) collective-permute-start(bf16[128,512]{1,0:T(8,128)(2,1)S(1)} %pad_maximum_fusion.2.refs_0_), channel_id=1, source_target_pairs={{0,1},{1,0},{2,3},{3,2},{4,5},{5,4},{6,7},{7,6},{8,9},{9,8},{10,11... | collective-permute-start | bytes 393224 | tf_op jit(solution)/shard_map/ppermute | solution.py:19
  73.9 8.7 %collective-permute-start.24 = (bf16[128,512]{1,0:T(8,128)(2,1)S(1)}, bf16[128,512]{1,0:T(8,128)(2,1)S(1)}, u32[]{:S(2)}, u32[]{:S(2)}) collective-permute-start(bf16[128,512]{1,0:T(8,128)(2,1)S(1)} %pad_maximum_fusion.2.refs_0_), channel_id=1, source_target_pairs={{0,2},{1,3},{2,0},{3,1},{4,6},{5,7},{6,4},{7,5},{8,10},{9,11},{10,... | collective-permute-start | bytes 393224 | tf_op jit(solution)/shard_map/ppermute | solution.py:19
  75.4 7.2 %collective-permute-start.25 = (bf16[128,512]{1,0:T(8,128)(2,1)S(1)}, bf16[128,512]{1,0:T(8,128)(2,1)S(1)}, u32[]{:S(2)}, u32[]{:S(2)}) collective-permute-start(bf16[128,512]{1,0:T(8,128)(2,1)S(1)} %pad_maximum_fusion.2.refs_0_), channel_id=1, source_target_pairs={{0,3},{1,2},{2,1},{3,0},{4,7},{5,6},{6,5},{7,4},{8,11},{9,10},{10,... | collective-permute-start | bytes 393224 | tf_op jit(solution)/shard_map/ppermute | solution.py:19
  83.7 7.4 %collective-permute-start.27 = (f32[8,128]{1,0:T(8,128)S(1)}, f32[8,128]{1,0:T(8,128)S(1)}, u32[]{:S(2)}, u32[]{:S(2)}) collective-permute-start(f32[8,128]{1,0:T(8,128)S(1)} %get-tuple-element.60), channel_id=1, source_target_pairs={{0,2},{1,3},{2,0},{3,1},{4,6},{5,7},{6,4},{7,5},{8,10},{9,11},{10,... | collective-permute-start | bytes 12296 | tf_op jit(solution)/shard_map/ppermute | solution.py:19
  85.9 5.5 %collective-permute-start.28 = (f32[8,128]{1,0:T(8,128)S(1)}, f32[8,128]{1,0:T(8,128)S(1)}, u32[]{:S(2)}, u32[]{:S(2)}) collective-permute-start(f32[8,128]{1,0:T(8,128)S(1)} %get-tuple-element.60), channel_id=1, source_target_pairs={{0,3},{1,2},{2,1},{3,0},{4,7},{5,6},{6,5},{7,4},{8,11},{9,10},{10,... | collective-permute-start | bytes 12296 | tf_op jit(solution)/shard_map/ppermute | solution.py:19
  88.1 3.8 %collective-permute-start.26 = (f32[8,128]{1,0:T(8,128)S(1)}, f32[8,128]{1,0:T(8,128)S(1)}, u32[]{:S(2)}, u32[]{:S(2)}) collective-permute-start(f32[8,128]{1,0:T(8,128)S(1)} %get-tuple-element.60), channel_id=1, source_target_pairs={{0,1},{1,0},{2,3},{3,2},{4,5},{5,4},{6,7},{7,6},{8,9},{9,8},{10,11... | collective-permute-start | bytes 12296 | tf_op jit(solution)/shard_map/ppermute | solution.py:19
  91.9 6.7 %collective-permute-start.30 = (f32[8,128]{1,0:T(8,128)S(1)}, f32[8,128]{1,0:T(8,128)S(1)}, u32[]{:S(2)}, u32[]{:S(2)}) collective-permute-start(f32[8,128]{1,0:T(8,128)S(1)} %add_add_fusion.1), channel_id=1, source_target_pairs={{0,8},{4,12},{8,0},{12,4},{1,9},{5,13},{9,1},{13,5},{2,10},{6,14},... | collective-permute-start | bytes 12296 | tf_op jit(solution)/shard_map/ppermute | solution.py:19
  93.4 5.1 %collective-permute-start.31 = (f32[8,128]{1,0:T(8,128)S(1)}, f32[8,128]{1,0:T(8,128)S(1)}, u32[]{:S(2)}, u32[]{:S(2)}) collective-permute-start(f32[8,128]{1,0:T(8,128)S(1)} %add_add_fusion.1), channel_id=1, source_target_pairs={{0,12},{4,8},{8,4},{12,0},{1,13},{5,9},{9,5},{13,1},{2,14},{6,10},... | collective-permute-start | bytes 12296 | tf_op jit(solution)/shard_map/ppermute | solution.py:19
  93.9 4.7 %collective-permute-start.29 = (f32[8,128]{1,0:T(8,128)S(1)}, f32[8,128]{1,0:T(8,128)S(1)}, u32[]{:S(2)}, u32[]{:S(2)}) collective-permute-start(f32[8,128]{1,0:T(8,128)S(1)} %add_add_fusion.1), channel_id=1, source_target_pairs={{0,4},{4,0},{8,12},{12,8},{1,5},{5,1},{9,13},{13,9},{2,6},{6,2},{1... | collective-permute-start | bytes 12296 | tf_op jit(solution)/shard_map/ppermute | solution.py:19
  98.7 11.0 %copy-start.11 = (f32[3]{0:T(128)S(1)}, f32[3]{0:T(128)}, u32[]{:S(2)}) copy-start(f32[3]{0:T(128)} %constant.50) | copy-start | bytes 40
  98.8 10.9 %collective-permute-start.32 = (f32[8,128]{1,0:T(8,128)S(1)}, f32[8,128]{1,0:T(8,128)S(1)}, u32[]{:S(2)}, u32[]{:S(2)}) collective-permute-start(f32[8,128]{1,0:T(8,128)S(1)} %add_add_fusion), channel_id=1, source_target_pairs={{0,16},{16,0},{1,17},{17,1},{2,18},{18,2},{3,19},{19,3},{4,20},{20... | collective-permute-start | bytes 12296 | tf_op jit(solution)/shard_map/ppermute | solution.py:19

commit v6 on v5

--- a/solution.py
+++ b/solution.py
@@ -46,12 +46,28 @@
     return [rows] + [swap(rows, axis, k) for k in range(1, lax.axis_size(axis))]
 
 
-def scatter_sum(start, terms, source, block):
+def scatter_sum(start, terms, source, block, rows):
+    arrived = [
+        across(terms[k * block : (k + 1) * block], source, k)
+        for k in range(lax.axis_size("tensor"))
+    ]
+    others = []
+    for k in range(1, lax.axis_size("dp")):
+        near = 1 if k == 1 and source == 0 else 0
+        if k == 1 and source == 1:
+            late = None
+            others.append(late)
+            continue
+        late, arrived[near] = lax.optimization_barrier((rows, arrived[near]))
+        others.append(swap_in(late, source, "dp", k))
     total = start.astype(jnp.float32)
-    for k in range(lax.axis_size("tensor")):
-        arrived = across(terms[k * block : (k + 1) * block], source, k)
-        total = total + arrived.astype(jnp.float32)
-    return total.astype(jnp.bfloat16)
+    for value in arrived:
+        total = total + value.astype(jnp.float32)
+    total = total.astype(jnp.bfloat16)
+    if others[0] is None:
+        late, total = lax.optimization_barrier((rows, total))
+        others[0] = swap_in(late, source, "dp", 1)
+    return total, [rows] + others
 
 
 def load_kernel(*refs):
@@ -270,11 +286,9 @@
     mixed = jnp.dot(hidden0, down_w, preferred_element_type=jnp.float32).astype(jnp.bfloat16)
     cot_rows, hidden0, mixed = lax.optimization_barrier((rows_in, hidden0, mixed))
     d_hidden = lax.dot_general(cot_rows, down_w, CONTRACT_LAST, preferred_element_type=jnp.float32)
-    x1_own = scatter_sum(x_own, mixed, 0, block)
+    x1_own, pieces0 = scatter_sum(x_own, mixed, 0, block, hidden0)
     x1_own, d_hidden = lax.optimization_barrier((x1_own, d_hidden))
     x1 = jnp.concatenate(gather_in(x1_own, 1, "tensor"), axis=0)
-    x1, hidden0 = lax.optimization_barrier((x1, hidden0))
-    pieces0 = gather_in(hidden0, 0, "dp")
 
     widened, scale, gate, up = layer_parts(x1)
     sig = jax.nn.sigmoid(gate)
@@ -290,9 +304,8 @@
     along = jnp.sum(pulled * widened, axis=-1, keepdims=True) / width
     term = (pulled * scale - widened * (scale * scale * scale * along)).astype(jnp.bfloat16)
     term, pieces0 = lax.optimization_barrier((term, pieces0))
-    dy_own = scatter_sum(cot_own, term, 1, block)
+    dy_own, pieces1 = scatter_sum(cot_own, term, 1, block, hidden1)
     dy_own = jnp.where(first, dy_own, cot_own)
-    dy_own, hidden1 = lax.optimization_barrier((dy_own, hidden1))
 
     piece = width // dp_size
     id_rows = -(-micro // 16) * 16
@@ -304,9 +317,8 @@
         part = lax.dynamic_slice_in_dim(dy_own, (dp_index ^ k) * piece, piece, axis=1)
         part = jnp.concatenate([part, id_block], axis=0)
         messages.append(part if k == 0 else swap(part, "dp", k))
-    pieces1 = gather_in(hidden1, 1, "dp")
     columns = jnp.concatenate([message[:block] for message in messages], axis=0)
-    columns, pieces1 = lax.optimization_barrier((columns, pieces1))
+    columns, pieces1[1] = lax.optimization_barrier((columns, pieces1[1]))
     parts_y = gather(columns, "tensor")
     hidden_all, gram_hidden = assemble(segment, pieces0, pieces1)
     ids_all = jnp.stack([message[block : block + micro, 0] for message in messages])

time: 111 us -> 107 us (0.964)
  starting transfers between devices: 53.4 us -> 48.9 us
  local copies, waits for them, and re-layouts: 2.05 us -> 3.61 us
    ppermute x16, starting transfers between devices: 27.9 us -> 23.5 us  [swap(): return lax.ppermute(block, axis, [(i, i ^ offset) for i in range(size)])]
    unnamed x26, local copies, waits for them, and re-layouts: 0.8 us -> 2.37 us
    ppermute x8, waiting for transfers between devices: 6.99 us -> 5.56 us  [across(): return lax.ppermute(block, ('section', 'tensor'), route)]
  transfers between devices with their start and end apart: 33 -> 33, of which waited for: 10 -> 9; matrix products, arithmetic and copies ran while one was open for 11% -> 11% of each run, Pallas kernels for 18% -> 19%
where the time goes in v6:
time: 107 us
  starting transfers between devices  48.9 us (46%)
  Pallas kernels  20.9 us (20%)
  waiting for transfers between devices  15.3 us (14%)
  matrix products  13.6 us (13%)
  local copies, waits for them, and re-layouts  3.61 us (3%)
  other arithmetic  3.18 us (3%)
  between operations  1.28 us (1%)
    ppermute x16, starting transfers between devices, swap(): return lax.ppermute(block, axis, [(i, i ^ offset) for i in range(size)])  23.5 us
    ppermute x9, starting transfers between devices, swap_in(): return lax.ppermute(block, ('section', axis), route)  13.3 us
    ppermute x8, starting transfers between devices, across(): return lax.ppermute(block, ('section', 'tensor'), route)  12.2 us
    pallas_call x3, Pallas kernels, domain_gradients(): pl.pallas_call(gradient_kernel, grid=(count,), in_specs=in_specs, out_spe...  9.95 us
    ppermute x16, waiting for transfers between devices, swap(): return lax.ppermute(block, axis, [(i, i ^ offset) for i in range(size)])  8.87 us
    pallas_call x1, Pallas kernels, load_weights(): pl.pallas_call(load_kernel, in_specs=[pl.BlockSpec(memory_space=pltpu.HBM...  7.28 us
    ppermute x8, waiting for transfers between devices, across(): return lax.ppermute(block, ('section', 'tensor'), route)  5.56 us
    pallas_call x1, Pallas kernels, assemble(): pl.pallas_call(functools.partial(assemble_kernel, count), in_specs=[pl.Bl...  2.61 us
  transfers between devices with their start and end apart: 33, of which 9 were waited for; matrix products, arithmetic and copies ran while one was open for 11% of the time, Pallas kernels for 19%

profile of v6, /device:TPU:0, one launch (start us, length us, event | category | flops | bytes accessed | tf_op | source)
XLA Modules:
  0.0 106.8 jit_solution(6135913382751984860)
XLA Ops:
  0.6 1.0 bitcast_select_fusion.1
  1.6 5.1 %collective-permute-start.2 = (bf16[32,2048]{1,0:T(8,128)(2,1)S(1)}, bf16[32,2048]{1,0:T(8,128)(2,1)S(1)}, u32[]{:S(2)}, u32[]{:S(2)}) collective-permute-start(bf16[32,2048]{1,0:T(8,128)(2,1)S(1)} %bitcast_select_fusion.1), channel_id=1, source_target_pairs={{0,3},{1,2},{2,1},{3,0},{4,7},{5,6},{6,5},{7,4},{8,11},{9,10},{10,... | collective-permute-start | bytes 393224 | tf_op jit(solution)/shard_map/ppermute | solution.py:19
  7.4 7.3 %shard_map.95 = (bf16[2048,1792]{1,0:T(8,128)(2,1)S(1)}, bf16[2048,1792]{1,0:T(8,128)(2,1)S(1)}, bf16[1792,2048]{1,0:T(8,128)(2,1)S(1)}) custom-call(bf16[1,2048,1792]{2,1,0:T(8,128)(2,1)} %refs_0_.1, bf16[1,2048,1792]{2,1,0:T(8,128)(2,1)} %refs_1_.1, bf16[1,1792,2048]{2,1,0:T(8,128)(2,1)} %refs_2_.1), custom_call_target="tpu_custom_call" | custom-call | bytes 22020096 | tf_op jit(solution)/shard_map/pallas_call | solution.py:88
  14.7 3.1 %collective-permute-done.1 = bf16[32,2048]{1,0:T(8,128)(2,1)S(1)} collective-permute-done((bf16[32,2048]{1,0:T(8,128)(2,1)S(1)}, bf16[32,2048]{1,0:T(8,128)(2,1)S(1)}, u32[]{:S(2)}, u32[]{:S(2)}) %collective-permute-start.1) | collective-permute-done | bytes 131104 | tf_op jit(solution)/shard_map/ppermute | solution.py:19
  18.0 1.2 %fusion.16 = f32[128,1792]{1,0:T(8,128)S(1)} fusion(bf16[2048,1792]{1,0:T(8,128)(2,1)S(1)} %get-tuple-element.40, bf16[128,2048]{1,0:T(8,128)(2,1)S(1)} %get-tuple-element.48, f32[2048]{0:T(1024)S(1)} %bitcast.30, f32[128]{0:T(128)S(1)} %add_rsqrt_fusion.1), kind=kOutput, calls=%fused_computation.30 | convolution fusion | flops 940572672 | bytes 8790528 | tf_op jit(solution)/shard_map/dot_general | solution.py:280
  19.2 1.3 %fusion.1.refs_0_ = bf16[128,1792]{1,0:T(8,128)(2,1)S(1)} fusion(bf16[2048,1792]{1,0:T(8,128)(2,1)S(1)} %get-tuple-element.41, f32[128,1792]{1,0:T(8,128)S(1)} %fusion.16, bf16[128,2048]{1,0:T(8,128)(2,1)S(1)} %get-tuple-element.48, f32[2048]{0:T(1024)S(1)} %bitcast.31, f32[128]{0:T(128)S(1)} %add_rsqrt_fusion.1), kind=kOutput, calls=%fused_computation.3 | convolution fusion | flops 941948928 | bytes 9249280 | tf_op jit(solution)/shard_map/dot_general | solution.py:281
  20.6 1.1 %convolution_convert_fusion = bf16[128,2048]{1,0:T(8,128)(2,1)S(1)} fusion(bf16[128,1792]{1,0:T(8,128)(2,1)S(1)} %fusion.1.refs_0_, bf16[1792,2048]{1,0:T(8,128)(2,1)S(1)} %get-tuple-element.42), kind=kOutput, calls=%fused_computation.4 | convolution fusion | flops 939786240 | bytes 8323072 | tf_op jit(solution)/shard_map/dot_general | solution.py:286
  21.8 3.0 %collective-permute-start.6 = (bf16[32,2048]{1,0:T(8,128)(2,1)S(1)}, bf16[32,2048]{1,0:T(8,128)(2,1)S(1)}, u32[]{:S(2)}, u32[]{:S(2)}) collective-permute-start(bf16[32,2048]{1,0:T(8,128)(2,1)S(1)} %get-tuple-element.88), channel_id=1, source_target_pairs={{0,19},{1,18},{2,17},{3,16},{4,23},{5,22},{6,21},{7,20},{8,27},{9,... | collective-permute-start | bytes 393224 | tf_op jit(solution)/shard_map/ppermute | solution.py:33
  24.8 1.3 %collective-permute-start.5 = (bf16[32,2048]{1,0:T(8,128)(2,1)S(1)}, bf16[32,2048]{1,0:T(8,128)(2,1)S(1)}, u32[]{:S(2)}, u32[]{:S(2)}) collective-permute-start(bf16[32,2048]{1,0:T(8,128)(2,1)S(1)} %get-tuple-element.89), channel_id=1, source_target_pairs={{0,18},{1,19},{2,16},{3,17},{4,22},{5,23},{6,20},{7,21},{8,26},{9,... | collective-permute-start | bytes 393224 | tf_op jit(solution)/shard_map/ppermute | solution.py:33
  26.1 1.3 %collective-permute-start.4 = (bf16[32,2048]{1,0:T(8,128)(2,1)S(1)}, bf16[32,2048]{1,0:T(8,128)(2,1)S(1)}, u32[]{:S(2)}, u32[]{:S(2)}) collective-permute-start(bf16[32,2048]{1,0:T(8,128)(2,1)S(1)} %get-tuple-element.90), channel_id=1, source_target_pairs={{0,17},{1,16},{2,19},{3,18},{4,21},{5,20},{6,23},{7,22},{8,25},{9,... | collective-permute-start | bytes 393224 | tf_op jit(solution)/shard_map/ppermute | solution.py:33
  27.4 1.3 %collective-permute-start.3 = (bf16[32,2048]{1,0:T(8,128)(2,1)S(1)}, bf16[32,2048]{1,0:T(8,128)(2,1)S(1)}, u32[]{:S(2)}, u32[]{:S(2)}) collective-permute-start(bf16[32,2048]{1,0:T(8,128)(2,1)S(1)} %get-tuple-element.87), channel_id=1, source_target_pairs={{0,16},{1,17},{2,18},{3,19},{4,20},{5,21},{6,22},{7,23},{8,24},{9,... | collective-permute-start | bytes 393224 | tf_op jit(solution)/shard_map/ppermute | solution.py:33
  28.7 2.5 %fusion.21 = f32[128,1792]{1,0:T(8,128)S(1)} fusion(bf16[128,2048]{1,0:T(8,128)(2,1)S(1)} %get-tuple-element.48, bf16[1792,2048]{1,0:T(8,128)(2,1)S(1)} %get-tuple-element.42), kind=kOutput, calls=%fused_computation.56 | convolution fusion | flops 939524096 | bytes 8781824 | tf_op jit(solution)/shard_map/dot_general | solution.py:288
  31.4 0.7 collective-permute-start.9
  33.4 3.4 %collective-permute-start.10 = (bf16[128,1792]{1,0:T(8,128)(2,1)S(1)}, bf16[128,1792]{1,0:T(8,128)(2,1)S(1)}, u32[]{:S(2)}, u32[]{:S(2)}) collective-permute-start(bf16[128,1792]{1,0:T(8,128)(2,1)S(1)} %fusion.1.refs_0_), channel_id=1, source_target_pairs={{0,4},{4,0},{8,12},{12,8},{1,5},{5,1},{9,13},{13,9},{2,6},{6,2},{1... | collective-permute-start | bytes 1376264 | tf_op jit(solution)/shard_map/ppermute | solution.py:25
  36.8 3.5 %collective-permute-start.11 = (bf16[128,1792]{1,0:T(8,128)(2,1)S(1)}, bf16[128,1792]{1,0:T(8,128)(2,1)S(1)}, u32[]{:S(2)}, u32[]{:S(2)}) collective-permute-start(bf16[128,1792]{1,0:T(8,128)(2,1)S(1)} %fusion.1.refs_0_), channel_id=1, source_target_pairs={{0,8},{4,12},{8,0},{12,4},{1,9},{5,13},{9,1},{13,5},{2,10},{6,14},... | collective-permute-start | bytes 1376264 | tf_op jit(solution)/shard_map/ppermute | solution.py:25
  40.3 2.4 %collective-permute-start.12 = (bf16[128,1792]{1,0:T(8,128)(2,1)S(1)}, bf16[128,1792]{1,0:T(8,128)(2,1)S(1)}, u32[]{:S(2)}, u32[]{:S(2)}) collective-permute-start(bf16[128,1792]{1,0:T(8,128)(2,1)S(1)} %fusion.1.refs_0_), channel_id=1, source_target_pairs={{0,12},{4,8},{8,4},{12,0},{1,13},{5,9},{9,5},{13,1},{2,14},{6,10},... | collective-permute-start | bytes 1376264 | tf_op jit(solution)/shard_map/ppermute | solution.py:25
  42.9 1.2 %fusion.13 = f32[128,1792]{1,0:T(8,128)S(1)} fusion(bf16[2048,1792]{1,0:T(8,128)(2,1)S(1)} %get-tuple-element.40, f32[128]{0:T(128)S(1)} %add_rsqrt_fusion, f32[2048]{0:T(1024)S(1)} %bitcast.32, bf16[32,2048]{1,0:T(8,128)(2,1)S(1)} %collective-permute-done.9, bf16[32,2048]{1,0:T(8,128)(2,1)S(1)} %collective-permute-done.8, ...), kind=kOutput, calls=%fused_computation.29 | convolution fusion | flops 942407680 | bytes 8790528 | tf_op jit(solution)/shard_map/dot_general | solution.py:280
  44.1 1.2 %fusion.11 = f32[128,1792]{1,0:T(8,128)S(1)} fusion(bf16[2048,1792]{1,0:T(8,128)(2,1)S(1)} %get-tuple-element.41, f32[128]{0:T(128)S(1)} %add_rsqrt_fusion, f32[2048]{0:T(1024)S(1)} %bitcast.33, bf16[32,2048]{1,0:T(8,128)(2,1)S(1)} %collective-permute-done.9, bf16[32,2048]{1,0:T(8,128)(2,1)S(1)} %collective-permute-done.8, ...), kind=kOutput, calls=%fused_computation.28 | convolution fusion | flops 942407680 | bytes 8790528 | tf_op jit(solution)/shard_map/dot_general | solution.py:281
  45.9 2.5 %fusion.22 = f32[128,2048]{1,0:T(8,128)S(1)} fusion(bf16[128,1792]{1,0:T(8,128)(2,1)S(1)} %get-tuple-element.51, bf16[2048,1792]{1,0:T(8,128)(2,1)S(1)} %get-tuple-element.40), kind=kOutput, calls=%fused_computation.57 | convolution fusion | flops 939524096 | bytes 8847360 | tf_op jit(solution)/shard_map/dot_general | solution.py:299
  48.4 2.6 %fusion.8 = (f32[128]{0:T(128)S(1)}, f32[128,2048]{1,0:T(8,128)S(1)}) fusion(bf16[32,2048]{1,0:T(8,128)(2,1)S(1)} %collective-permute-done.9, bf16[32,2048]{1,0:T(8,128)(2,1)S(1)} %collective-permute-done.8, bf16[32,2048]{1,0:T(8,128)(2,1)S(1)} %collective-permute-done.7, bf16[32,2048]{1,0:T(8,128)(2,1)S(1)} %add_convert_fusion.1, f32[2048]{0:T(1024)S(1)} %bitcast.34, ...), kind=kOutput, calls=%fused_computation.17 | convolution fusion | flops 942669696 | bytes 10428928 | tf_op jit(solution)/shard_map/dot_general | solution.py:300
  51.2 0.8 collective-permute-done.11.refs_2_
  52.1 0.7 copy-done.5
  52.9 1.5 %collective-permute-start.16 = (bf16[32,2048]{1,0:T(8,128)(2,1)S(1)}, bf16[32,2048]{1,0:T(8,128)(2,1)S(1)}, u32[]{:S(2)}, u32[]{:S(2)}) collective-permute-start(bf16[32,2048]{1,0:T(8,128)(2,1)S(1)} %get-tuple-element.84), channel_id=1, source_target_pairs={{16,3},{17,2},{18,1},{19,0},{20,7},{21,6},{22,5},{23,4},{24,11},{2... | collective-permute-start | bytes 393224 | tf_op jit(solution)/shard_map/ppermute | solution.py:33
  54.4 1.3 %collective-permute-start.15 = (bf16[32,2048]{1,0:T(8,128)(2,1)S(1)}, bf16[32,2048]{1,0:T(8,128)(2,1)S(1)}, u32[]{:S(2)}, u32[]{:S(2)}) collective-permute-start(bf16[32,2048]{1,0:T(8,128)(2,1)S(1)} %get-tuple-element.85), channel_id=1, source_target_pairs={{16,2},{17,3},{18,0},{19,1},{20,6},{21,7},{22,4},{23,5},{24,10},{2... | collective-permute-start | bytes 393224 | tf_op jit(solution)/shard_map/ppermute | solution.py:33
  55.7 1.3 %collective-permute-start.14 = (bf16[32,2048]{1,0:T(8,128)(2,1)S(1)}, bf16[32,2048]{1,0:T(8,128)(2,1)S(1)}, u32[]{:S(2)}, u32[]{:S(2)}) collective-permute-start(bf16[32,2048]{1,0:T(8,128)(2,1)S(1)} %get-tuple-element.86), channel_id=1, source_target_pairs={{16,1},{17,0},{18,3},{19,2},{20,5},{21,4},{22,7},{23,6},{24,9},{25... | collective-permute-start | bytes 393224 | tf_op jit(solution)/shard_map/ppermute | solution.py:33
  57.0 1.3 %collective-permute-start.13 = (bf16[32,2048]{1,0:T(8,128)(2,1)S(1)}, bf16[32,2048]{1,0:T(8,128)(2,1)S(1)}, u32[]{:S(2)}, u32[]{:S(2)}) collective-permute-start(bf16[32,2048]{1,0:T(8,128)(2,1)S(1)} %get-tuple-element.83), channel_id=1, source_target_pairs={{16,0},{17,1},{18,2},{19,3},{20,4},{21,5},{22,6},{23,7},{24,8},{25... | collective-permute-start | bytes 393224 | tf_op jit(solution)/shard_map/ppermute | solution.py:33
  58.4 3.0 %collective-permute-done.13 = bf16[32,2048]{1,0:T(8,128)(2,1)S(1)} collective-permute-done((bf16[32,2048]{1,0:T(8,128)(2,1)S(1)}, bf16[32,2048]{1,0:T(8,128)(2,1)S(1)}, u32[]{:S(2)}, u32[]{:S(2)}) %collective-permute-start.13) | collective-permute-done | bytes 131104 | tf_op jit(solution)/shard_map/ppermute | solution.py:33
  61.4 2.6 %collective-permute-done.15 = bf16[32,2048]{1,0:T(8,128)(2,1)S(1)} collective-permute-done((bf16[32,2048]{1,0:T(8,128)(2,1)S(1)}, bf16[32,2048]{1,0:T(8,128)(2,1)S(1)}, u32[]{:S(2)}, u32[]{:S(2)}) %collective-permute-start.15) | collective-permute-done | bytes 131104 | tf_op jit(solution)/shard_map/ppermute | solution.py:33
  64.2 2.4 %collective-permute-start.19 = (bf16[48,512]{1,0:T(8,128)(2,1)S(1)}, bf16[48,512]{1,0:T(8,128)(2,1)S(1)}, u32[]{:S(2)}, u32[]{:S(2)}) collective-permute-start(bf16[48,512]{1,0:T(8,128)(2,1)S(1)} %get-tuple-element.99), channel_id=1, source_target_pairs={{0,12},{4,8},{8,4},{12,0},{1,13},{5,9},{9,5},{13,1},{2,14},{6,10},... | collective-permute-start | bytes 147464 | tf_op jit(solution)/shard_map/ppermute | solution.py:19
  66.6 0.7 collective-permute-start.20
  68.5 0.7 collective-permute-start.21
  69.8 0.7 collective-permute-start.22
  70.6 1.0 collective-permute-done.18
  71.6 1.0 collective-permute-done.17
  72.9 2.2 %collective-permute-start.24 = (bf16[128,512]{1,0:T(8,128)(2,1)S(1)}, bf16[128,512]{1,0:T(8,128)(2,1)S(1)}, u32[]{:S(2)}, u32[]{:S(2)}) collective-permute-start(bf16[128,512]{1,0:T(8,128)(2,1)S(1)} %pad_maximum_fusion.2.refs_0_), channel_id=1, source_target_pairs={{0,2},{1,3},{2,0},{3,1},{4,6},{5,7},{6,4},{7,5},{8,10},{9,11},{10,... | collective-permute-start | bytes 393224 | tf_op jit(solution)/shard_map/ppermute | solution.py:19
  75.1 2.1 %collective-permute-start.25 = (bf16[128,512]{1,0:T(8,128)(2,1)S(1)}, bf16[128,512]{1,0:T(8,128)(2,1)S(1)}, u32[]{:S(2)}, u32[]{:S(2)}) collective-permute-start(bf16[128,512]{1,0:T(8,128)(2,1)S(1)} %pad_maximum_fusion.2.refs_0_), channel_id=1, source_target_pairs={{0,3},{1,2},{2,1},{3,0},{4,7},{5,6},{6,5},{7,4},{8,11},{9,10},{10,... | collective-permute-start | bytes 393224 | tf_op jit(solution)/shard_map/ppermute | solution.py:19
  77.8 0.8 copy-done.8
  78.5 0.8 copy-done.9
  79.3 2.6 %shard_map.96 = (bf16[512,1792]{1,0:T(8,128)(2,1)S(1)}, f32[512,512]{1,0:T(8,128)S(1)}) custom-call(s32[1]{0:T(128)} %bitcast.5.flag_ref, bf16[128,1792]{1,0:T(8,128)(2,1)} %copy-done, bf16[128,1792]{1,0:T(8,128)(2,1)} %copy-done.4, bf16[128,1792]{1,0:T(8,128)(2,1)} %copy-done.5, bf16[128,1792]{1,0:T(8,128)(2,1)} %copy-done.6, bf16[128,1792]{1,0:T(8,128)(2,1)} %copy-done.1, ...), custom_call_target="tpu_custom_call" | custom-call | flops 939524096 | bytes 4718592 | tf_op jit(solution)/shard_map/pallas_call | solution.py:184
  82.0 2.6 %collective-permute-done.25.refs_3_ = bf16[128,512]{1,0:T(8,128)(2,1)S(1)} collective-permute-done((bf16[128,512]{1,0:T(8,128)(2,1)S(1)}, bf16[128,512]{1,0:T(8,128)(2,1)S(1)}, u32[]{:S(2)}, u32[]{:S(2)}) %collective-permute-start.25) | collective-permute-done | bytes 131104 | tf_op jit(solution)/shard_map/ppermute | solution.py:19
  84.5 1.1 %shard_map.97 = (bf16[512,512]{1,0:T(8,128)(2,1)S(1)}, f32[8,128]{1,0:T(8,128)S(1)}) custom-call(s32[512,1]{1,0:T(8,128)S(1)} %copy.12.ids_ref, s32[1,512]{1,0:T(1,128)S(1)} %reshape_reshape.3.ids_row_ref, f32[512,512]{1,0:T(8,128)S(1)} %get-tuple-element.68.gram_ref, bf16[128,512]{1,0:T(8,128)(2,1)S(1)} %pad_maximum_fusion.2.refs_0_, ...), custom_call_target="tpu_custom_call" | custom-call | flops 269484032 | bytes 2097152 | tf_op jit(solution)/shard_map/pallas_call | solution.py:237
  85.6 3.2 %collective-permute-start.27 = (f32[8,128]{1,0:T(8,128)S(1)}, f32[8,128]{1,0:T(8,128)S(1)}, u32[]{:S(2)}, u32[]{:S(2)}) collective-permute-start(f32[8,128]{1,0:T(8,128)S(1)} %get-tuple-element.70), channel_id=1, source_target_pairs={{0,2},{1,3},{2,0},{3,1},{4,6},{5,7},{6,4},{7,5},{8,10},{9,11},{10,... | collective-permute-start | bytes 12296 | tf_op jit(solution)/shard_map/ppermute | solution.py:19
  88.8 2.4 %collective-permute-start.28 = (f32[8,128]{1,0:T(8,128)S(1)}, f32[8,128]{1,0:T(8,128)S(1)}, u32[]{:S(2)}, u32[]{:S(2)}) collective-permute-start(f32[8,128]{1,0:T(8,128)S(1)} %get-tuple-element.70), channel_id=1, source_target_pairs={{0,3},{1,2},{2,1},{3,0},{4,7},{5,6},{6,5},{7,4},{8,11},{9,10},{10,... | collective-permute-start | bytes 12296 | tf_op jit(solution)/shard_map/ppermute | solution.py:19
  91.2 3.0 %shard_map.98.rest_0_ = bf16[4,1792,512]{2,1,0:T(8,128)(2,1)} custom-call(s32[512,1]{1,0:T(8,128)S(1)} %copy.12.ids_ref, bf16[512,1792]{1,0:T(8,128)(2,1)S(1)} %get-tuple-element.74.hidden_ref, bf16[512,512]{1,0:T(8,128)(2,1)S(1)} %get-tuple-element.75.y_ref), custom_call_target="tpu_custom_call" | custom-call | flops 1073741824 | bytes 2621440 | tf_op jit(solution)/shard_map/pallas_call | solution.py:130
  94.8 2.5 %collective-permute-start.30 = (f32[8,128]{1,0:T(8,128)S(1)}, f32[8,128]{1,0:T(8,128)S(1)}, u32[]{:S(2)}, u32[]{:S(2)}) collective-permute-start(f32[8,128]{1,0:T(8,128)S(1)} %add_add_fusion.1), channel_id=1, source_target_pairs={{0,8},{4,12},{8,0},{12,4},{1,9},{5,13},{9,1},{13,5},{2,10},{6,14},... | collective-permute-start | bytes 12296 | tf_op jit(solution)/shard_map/ppermute | solution.py:19
  97.3 1.5 %collective-permute-start.29 = (f32[8,128]{1,0:T(8,128)S(1)}, f32[8,128]{1,0:T(8,128)S(1)}, u32[]{:S(2)}, u32[]{:S(2)}) collective-permute-start(f32[8,128]{1,0:T(8,128)S(1)} %add_add_fusion.1), channel_id=1, source_target_pairs={{0,4},{4,0},{8,12},{12,8},{1,5},{5,1},{9,13},{13,9},{2,6},{6,2},{1... | collective-permute-start | bytes 12296 | tf_op jit(solution)/shard_map/ppermute | solution.py:19
  99.0 3.0 %shard_map.99.rest_0_ = bf16[4,1792,512]{2,1,0:T(8,128)(2,1)} custom-call(s32[512,1]{1,0:T(8,128)S(1)} %copy.14.ids_ref, bf16[512,1792]{1,0:T(8,128)(2,1)S(1)} %get-tuple-element.74.hidden_ref, bf16[512,512]{1,0:T(8,128)(2,1)S(1)} %get-tuple-element.75.y_ref, bf16[4,1792,512]{2,1,0:T(8,128)(2,1)} %shard_map.98.rest_0_), custom_call_target="tpu_custom_call", output_to_operand_aliasing={{}: (3, {})} | custom-call | flops 1073741824 | bytes 2621440 | tf_op jit(solution)/shard_map/pallas_call | solution.py:130
  102.3 4.0 %shard_map.100 = bf16[4,1792,512]{2,1,0:T(8,128)(2,1)} custom-call(s32[512,1]{1,0:T(8,128)S(1)} %copy.15.ids_ref, bf16[512,1792]{1,0:T(8,128)(2,1)S(1)} %get-tuple-element.74.hidden_ref, bf16[512,512]{1,0:T(8,128)(2,1)S(1)} %get-tuple-element.75.y_ref, bf16[4,1792,512]{2,1,0:T(8,128)(2,1)} %shard_map.99.rest_0_), custom_call_target="tpu_custom_call", output_to_operand_aliasing={{}: (3, {})} | custom-call | flops 1610612736 | bytes 3932160 | tf_op jit(solution)/shard_map/pallas_call | solution.py:130
  (94 shorter events, 8.1 us)
Async XLA Ops:
  1.6 16.4 %copy-start.10 = (f32[1,2048]{1,0:T(1,128)S(1)}, f32[1,2048]{1,0:T(1,128)}, u32[]{:S(2)}) copy-start(f32[1,2048]{1,0:T(1,128)} %param.11) | copy-start | bytes 24580
  1.6 13.1 %collective-permute-start.2 = (bf16[32,2048]{1,0:T(8,128)(2,1)S(1)}, bf16[32,2048]{1,0:T(8,128)(2,1)S(1)}, u32[]{:S(2)}, u32[]{:S(2)}) collective-permute-start(bf16[32,2048]{1,0:T(8,128)(2,1)S(1)} %bitcast_select_fusion.1), channel_id=1, source_target_pairs={{0,3},{1,2},{2,1},{3,0},{4,7},{5,6},{6,5},{7,4},{8,11},{9,10},{10,... | collective-permute-start | bytes 393224 | tf_op jit(solution)/shard_map/ppermute | solution.py:19
  6.8 11.1 %collective-permute-start.1 = (bf16[32,2048]{1,0:T(8,128)(2,1)S(1)}, bf16[32,2048]{1,0:T(8,128)(2,1)S(1)}, u32[]{:S(2)}, u32[]{:S(2)}) collective-permute-start(bf16[32,2048]{1,0:T(8,128)(2,1)S(1)} %bitcast_select_fusion.1), channel_id=1, source_target_pairs={{0,2},{1,3},{2,0},{3,1},{4,6},{5,7},{6,4},{7,5},{8,10},{9,11},{10,... | collective-permute-start | bytes 393224 | tf_op jit(solution)/shard_map/ppermute | solution.py:19
  6.8 11.1 %collective-permute-start = (bf16[32,2048]{1,0:T(8,128)(2,1)S(1)}, bf16[32,2048]{1,0:T(8,128)(2,1)S(1)}, u32[]{:S(2)}, u32[]{:S(2)}) collective-permute-start(bf16[32,2048]{1,0:T(8,128)(2,1)S(1)} %bitcast_select_fusion.1), channel_id=1, source_target_pairs={{0,1},{1,0},{2,3},{3,2},{4,5},{5,4},{6,7},{7,6},{8,9},{9,8},{10,11... | collective-permute-start | bytes 393224 | tf_op jit(solution)/shard_map/ppermute | solution.py:19
  20.6 19.7 %copy-start = (bf16[128,1792]{1,0:T(8,128)(2,1)}, bf16[128,1792]{1,0:T(8,128)(2,1)S(1)}, u32[]{:S(2)}) copy-start(bf16[128,1792]{1,0:T(8,128)(2,1)S(1)} %fusion.1.refs_0_) | copy-start | bytes 1376260
  21.7 9.5 %copy-start.3 = (bf16[4,8,2048]{2,1,0:T(8,128)(2,1)S(1)}, bf16[4,8,2048]{2,1,0:T(8,128)(2,1)}, u32[]{:S(2)}) copy-start(bf16[4,8,2048]{2,1,0:T(8,128)(2,1)} %param.8) | copy-start | bytes 393220
  21.8 9.4 %collective-permute-start.6 = (bf16[32,2048]{1,0:T(8,128)(2,1)S(1)}, bf16[32,2048]{1,0:T(8,128)(2,1)S(1)}, u32[]{:S(2)}, u32[]{:S(2)}) collective-permute-start(bf16[32,2048]{1,0:T(8,128)(2,1)S(1)} %get-tuple-element.88), channel_id=1, source_target_pairs={{0,19},{1,18},{2,17},{3,16},{4,23},{5,22},{6,21},{7,20},{8,27},{9,... | collective-permute-start | bytes 393224 | tf_op jit(solution)/shard_map/ppermute | solution.py:33
  24.8 6.5 %collective-permute-start.5 = (bf16[32,2048]{1,0:T(8,128)(2,1)S(1)}, bf16[32,2048]{1,0:T(8,128)(2,1)S(1)}, u32[]{:S(2)}, u32[]{:S(2)}) collective-permute-start(bf16[32,2048]{1,0:T(8,128)(2,1)S(1)} %get-tuple-element.89), channel_id=1, source_target_pairs={{0,18},{1,19},{2,16},{3,17},{4,22},{5,23},{6,20},{7,21},{8,26},{9,... | collective-permute-start | bytes 393224 | tf_op jit(solution)/shard_map/ppermute | solution.py:33
  26.1 5.2 %collective-permute-start.4 = (bf16[32,2048]{1,0:T(8,128)(2,1)S(1)}, bf16[32,2048]{1,0:T(8,128)(2,1)S(1)}, u32[]{:S(2)}, u32[]{:S(2)}) collective-permute-start(bf16[32,2048]{1,0:T(8,128)(2,1)S(1)} %get-tuple-element.90), channel_id=1, source_target_pairs={{0,17},{1,16},{2,19},{3,18},{4,21},{5,20},{6,23},{7,22},{8,25},{9,... | collective-permute-start | bytes 393224 | tf_op jit(solution)/shard_map/ppermute | solution.py:33
  27.4 3.9 %collective-permute-start.3 = (bf16[32,2048]{1,0:T(8,128)(2,1)S(1)}, bf16[32,2048]{1,0:T(8,128)(2,1)S(1)}, u32[]{:S(2)}, u32[]{:S(2)}) collective-permute-start(bf16[32,2048]{1,0:T(8,128)(2,1)S(1)} %get-tuple-element.87), channel_id=1, source_target_pairs={{0,16},{1,17},{2,18},{3,19},{4,20},{5,21},{6,22},{7,23},{8,24},{9,... | collective-permute-start | bytes 393224 | tf_op jit(solution)/shard_map/ppermute | solution.py:33
  31.4 8.9 %collective-permute-start.9 = (bf16[32,2048]{1,0:T(8,128)(2,1)S(1)}, bf16[32,2048]{1,0:T(8,128)(2,1)S(1)}, u32[]{:S(2)}, u32[]{:S(2)}) collective-permute-start(bf16[32,2048]{1,0:T(8,128)(2,1)S(1)} %add_convert_fusion.1), channel_id=1, source_target_pairs={{16,19},{17,18},{18,17},{19,16},{20,23},{21,22},{22,21},{23,20},{2... | collective-permute-start | bytes 393224 | tf_op jit(solution)/shard_map/ppermute | solution.py:25
  32.0 10.6 %collective-permute-start.8 = (bf16[32,2048]{1,0:T(8,128)(2,1)S(1)}, bf16[32,2048]{1,0:T(8,128)(2,1)S(1)}, u32[]{:S(2)}, u32[]{:S(2)}) collective-permute-start(bf16[32,2048]{1,0:T(8,128)(2,1)S(1)} %add_convert_fusion.1), channel_id=1, source_target_pairs={{16,18},{17,19},{18,16},{19,17},{20,22},{21,23},{22,20},{23,21},{2... | collective-permute-start | bytes 393224 | tf_op jit(solution)/shard_map/ppermute | solution.py:25
  32.7 9.9 %collective-permute-start.7 = (bf16[32,2048]{1,0:T(8,128)(2,1)S(1)}, bf16[32,2048]{1,0:T(8,128)(2,1)S(1)}, u32[]{:S(2)}, u32[]{:S(2)}) collective-permute-start(bf16[32,2048]{1,0:T(8,128)(2,1)S(1)} %add_convert_fusion.1), channel_id=1, source_target_pairs={{16,17},{17,16},{18,19},{19,18},{20,21},{21,20},{22,23},{23,22},{2... | collective-permute-start | bytes 393224 | tf_op jit(solution)/shard_map/ppermute | solution.py:25
  33.4 17.8 %collective-permute-start.10 = (bf16[128,1792]{1,0:T(8,128)(2,1)S(1)}, bf16[128,1792]{1,0:T(8,128)(2,1)S(1)}, u32[]{:S(2)}, u32[]{:S(2)}) collective-permute-start(bf16[128,1792]{1,0:T(8,128)(2,1)S(1)} %fusion.1.refs_0_), channel_id=1, source_target_pairs={{0,4},{4,0},{8,12},{12,8},{1,5},{5,1},{9,13},{13,9},{2,6},{6,2},{1... | collective-permute-start | bytes 1376264 | tf_op jit(solution)/shard_map/ppermute | solution.py:25
  36.8 15.3 %collective-permute-start.11 = (bf16[128,1792]{1,0:T(8,128)(2,1)S(1)}, bf16[128,1792]{1,0:T(8,128)(2,1)S(1)}, u32[]{:S(2)}, u32[]{:S(2)}) collective-permute-start(bf16[128,1792]{1,0:T(8,128)(2,1)S(1)} %fusion.1.refs_0_), channel_id=1, source_target_pairs={{0,8},{4,12},{8,0},{12,4},{1,9},{5,13},{9,1},{13,5},{2,10},{6,14},... | collective-permute-start | bytes 1376264 | tf_op jit(solution)/shard_map/ppermute | solution.py:25
  40.3 11.8 %collective-permute-start.12 = (bf16[128,1792]{1,0:T(8,128)(2,1)S(1)}, bf16[128,1792]{1,0:T(8,128)(2,1)S(1)}, u32[]{:S(2)}, u32[]{:S(2)}) collective-permute-start(bf16[128,1792]{1,0:T(8,128)(2,1)S(1)} %fusion.1.refs_0_), channel_id=1, source_target_pairs={{0,12},{4,8},{8,4},{12,0},{1,13},{5,9},{9,5},{13,1},{2,14},{6,10},... | collective-permute-start | bytes 1376264 | tf_op jit(solution)/shard_map/ppermute | solution.py:25
  45.9 23.9 %copy-start.1 = (bf16[128,1792]{1,0:T(8,128)(2,1)}, bf16[128,1792]{1,0:T(8,128)(2,1)S(1)}, u32[]{:S(2)}) copy-start(bf16[128,1792]{1,0:T(8,128)(2,1)S(1)} %get-tuple-element.67.refs_4_) | copy-start | bytes 1376260
  48.4 9.9 %copy-start.12 = (s32[4,1]{0,1:T(1,128)S(1)}, s32[4,1]{0,1:T(1,128)}, u32[]{:S(2)}) copy-start(s32[4,1]{0,1:T(1,128)} %param.10) | copy-start | bytes 52
  48.4 15.6 %copy-start.2 = (bf16[4,8,2048]{2,1,0:T(8,128)(2,1)S(1)}, bf16[4,8,2048]{2,1,0:T(8,128)(2,1)}, u32[]{:S(2)}) copy-start(bf16[4,8,2048]{2,1,0:T(8,128)(2,1)} %param.9) | copy-start | bytes 393220
  51.2 0.9 copy-start.4
  52.1 0.8 copy-start.5
  52.1 2.3 %copy-start.6 = (bf16[128,1792]{1,0:T(8,128)(2,1)}, bf16[128,1792]{1,0:T(8,128)(2,1)S(1)}, u32[]{:S(2)}) copy-start(bf16[128,1792]{1,0:T(8,128)(2,1)S(1)} %collective-permute-done.12.refs_3_) | copy-start | bytes 1376260
  52.9 8.5 %collective-permute-start.16 = (bf16[32,2048]{1,0:T(8,128)(2,1)S(1)}, bf16[32,2048]{1,0:T(8,128)(2,1)S(1)}, u32[]{:S(2)}, u32[]{:S(2)}) collective-permute-start(bf16[32,2048]{1,0:T(8,128)(2,1)S(1)} %get-tuple-element.84), channel_id=1, source_target_pairs={{16,3},{17,2},{18,1},{19,0},{20,7},{21,6},{22,5},{23,4},{24,11},{2... | collective-permute-start | bytes 393224 | tf_op jit(solution)/shard_map/ppermute | solution.py:33
  54.4 9.6 %collective-permute-start.15 = (bf16[32,2048]{1,0:T(8,128)(2,1)S(1)}, bf16[32,2048]{1,0:T(8,128)(2,1)S(1)}, u32[]{:S(2)}, u32[]{:S(2)}) collective-permute-start(bf16[32,2048]{1,0:T(8,128)(2,1)S(1)} %get-tuple-element.85), channel_id=1, source_target_pairs={{16,2},{17,3},{18,0},{19,1},{20,6},{21,7},{22,4},{23,5},{24,10},{2... | collective-permute-start | bytes 393224 | tf_op jit(solution)/shard_map/ppermute | solution.py:33
  55.7 8.3 %collective-permute-start.14 = (bf16[32,2048]{1,0:T(8,128)(2,1)S(1)}, bf16[32,2048]{1,0:T(8,128)(2,1)S(1)}, u32[]{:S(2)}, u32[]{:S(2)}) collective-permute-start(bf16[32,2048]{1,0:T(8,128)(2,1)S(1)} %get-tuple-element.86), channel_id=1, source_target_pairs={{16,1},{17,0},{18,3},{19,2},{20,5},{21,4},{22,7},{23,6},{24,9},{25... | collective-permute-start | bytes 393224 | tf_op jit(solution)/shard_map/ppermute | solution.py:33
  57.0 4.4 %collective-permute-start.13 = (bf16[32,2048]{1,0:T(8,128)(2,1)S(1)}, bf16[32,2048]{1,0:T(8,128)(2,1)S(1)}, u32[]{:S(2)}, u32[]{:S(2)}) collective-permute-start(bf16[32,2048]{1,0:T(8,128)(2,1)S(1)} %get-tuple-element.83), channel_id=1, source_target_pairs={{16,0},{17,1},{18,2},{19,3},{20,4},{21,5},{22,6},{23,7},{24,8},{25... | collective-permute-start | bytes 393224 | tf_op jit(solution)/shard_map/ppermute | solution.py:33
  64.2 5.6 %collective-permute-start.19 = (bf16[48,512]{1,0:T(8,128)(2,1)S(1)}, bf16[48,512]{1,0:T(8,128)(2,1)S(1)}, u32[]{:S(2)}, u32[]{:S(2)}) collective-permute-start(bf16[48,512]{1,0:T(8,128)(2,1)S(1)} %get-tuple-element.99), channel_id=1, source_target_pairs={{0,12},{4,8},{8,4},{12,0},{1,13},{5,9},{9,5},{13,1},{2,14},{6,10},... | collective-permute-start | bytes 147464 | tf_op jit(solution)/shard_map/ppermute | solution.py:19
  66.6 6.2 %collective-permute-start.20 = (bf16[128,1792]{1,0:T(8,128)(2,1)S(1)}, bf16[128,1792]{1,0:T(8,128)(2,1)S(1)}, u32[]{:S(2)}, u32[]{:S(2)}) collective-permute-start(bf16[128,1792]{1,0:T(8,128)(2,1)S(1)} %get-tuple-element.67.refs_4_), channel_id=1, source_target_pairs={{16,20},{20,16},{24,28},{28,24},{17,21},{21,17},{25,29},{29,25},{1... | collective-permute-start | bytes 1376264 | tf_op jit(solution)/shard_map/ppermute | solution.py:25
  67.3 4.3 %collective-permute-start.18 = (bf16[48,512]{1,0:T(8,128)(2,1)S(1)}, bf16[48,512]{1,0:T(8,128)(2,1)S(1)}, u32[]{:S(2)}, u32[]{:S(2)}) collective-permute-start(bf16[48,512]{1,0:T(8,128)(2,1)S(1)} %get-tuple-element.98), channel_id=1, source_target_pairs={{0,8},{4,12},{8,0},{12,4},{1,9},{5,13},{9,1},{13,5},{2,10},{6,14},... | collective-permute-start | bytes 147464 | tf_op jit(solution)/shard_map/ppermute | solution.py:19
  67.9 4.7 %collective-permute-start.17 = (bf16[48,512]{1,0:T(8,128)(2,1)S(1)}, bf16[48,512]{1,0:T(8,128)(2,1)S(1)}, u32[]{:S(2)}, u32[]{:S(2)}) collective-permute-start(bf16[48,512]{1,0:T(8,128)(2,1)S(1)} %get-tuple-element.97), channel_id=1, source_target_pairs={{0,4},{4,0},{8,12},{12,8},{1,5},{5,1},{9,13},{13,9},{2,6},{6,2},{1... | collective-permute-start | bytes 147464 | tf_op jit(solution)/shard_map/ppermute | solution.py:19
  68.5 9.2 %collective-permute-start.21 = (bf16[128,1792]{1,0:T(8,128)(2,1)S(1)}, bf16[128,1792]{1,0:T(8,128)(2,1)S(1)}, u32[]{:S(2)}, u32[]{:S(2)}) collective-permute-start(bf16[128,1792]{1,0:T(8,128)(2,1)S(1)} %get-tuple-element.67.refs_4_), channel_id=1, source_target_pairs={{16,24},{20,28},{24,16},{28,20},{17,25},{21,29},{25,17},{29,21},{1... | collective-permute-start | bytes 1376264 | tf_op jit(solution)/shard_map/ppermute | solution.py:25
  69.8 8.0 %collective-permute-start.22 = (bf16[128,1792]{1,0:T(8,128)(2,1)S(1)}, bf16[128,1792]{1,0:T(8,128)(2,1)S(1)}, u32[]{:S(2)}, u32[]{:S(2)}) collective-permute-start(bf16[128,1792]{1,0:T(8,128)(2,1)S(1)} %get-tuple-element.67.refs_4_), channel_id=1, source_target_pairs={{16,28},{20,24},{24,20},{28,16},{17,29},{21,25},{25,21},{29,17},{1... | collective-permute-start | bytes 1376264 | tf_op jit(solution)/shard_map/ppermute | solution.py:25
  72.8 6.5 %copy-start.7 = (bf16[128,1792]{1,0:T(8,128)(2,1)}, bf16[128,1792]{1,0:T(8,128)(2,1)S(1)}, u32[]{:S(2)}) copy-start(bf16[128,1792]{1,0:T(8,128)(2,1)S(1)} %collective-permute-done.20.refs_5_) | copy-start | bytes 1376260
  72.8 9.1 %collective-permute-start.23 = (bf16[128,512]{1,0:T(8,128)(2,1)S(1)}, bf16[128,512]{1,0:T(8,128)(2,1)S(1)}, u32[]{:S(2)}, u32[]{:S(2)}) collective-permute-start(bf16[128,512]{1,0:T(8,128)(2,1)S(1)} %pad_maximum_fusion.2.refs_0_), channel_id=1, source_target_pairs={{0,1},{1,0},{2,3},{3,2},{4,5},{5,4},{6,7},{7,6},{8,9},{9,8},{10,11... | collective-permute-start | bytes 393224 | tf_op jit(solution)/shard_map/ppermute | solution.py:19
  72.9 9.1 %collective-permute-start.24 = (bf16[128,512]{1,0:T(8,128)(2,1)S(1)}, bf16[128,512]{1,0:T(8,128)(2,1)S(1)}, u32[]{:S(2)}, u32[]{:S(2)}) collective-permute-start(bf16[128,512]{1,0:T(8,128)(2,1)S(1)} %pad_maximum_fusion.2.refs_0_), channel_id=1, source_target_pairs={{0,2},{1,3},{2,0},{3,1},{4,6},{5,7},{6,4},{7,5},{8,10},{9,11},{10,... | collective-permute-start | bytes 393224 | tf_op jit(solution)/shard_map/ppermute | solution.py:19
  75.1 9.4 %collective-permute-start.25 = (bf16[128,512]{1,0:T(8,128)(2,1)S(1)}, bf16[128,512]{1,0:T(8,128)(2,1)S(1)}, u32[]{:S(2)}, u32[]{:S(2)}) collective-permute-start(bf16[128,512]{1,0:T(8,128)(2,1)S(1)} %pad_maximum_fusion.2.refs_0_), channel_id=1, source_target_pairs={{0,3},{1,2},{2,1},{3,0},{4,7},{5,6},{6,5},{7,4},{8,11},{9,10},{10,... | collective-permute-start | bytes 393224 | tf_op jit(solution)/shard_map/ppermute | solution.py:19
  77.7 0.8 copy-start.8
  78.5 0.8 copy-start.9
  85.6 8.6 %collective-permute-start.27 = (f32[8,128]{1,0:T(8,128)S(1)}, f32[8,128]{1,0:T(8,128)S(1)}, u32[]{:S(2)}, u32[]{:S(2)}) collective-permute-start(f32[8,128]{1,0:T(8,128)S(1)} %get-tuple-element.70), channel_id=1, source_target_pairs={{0,2},{1,3},{2,0},{3,1},{4,6},{5,7},{6,4},{7,5},{8,10},{9,11},{10,... | collective-permute-start | bytes 12296 | tf_op jit(solution)/shard_map/ppermute | solution.py:19
  88.8 5.4 %collective-permute-start.28 = (f32[8,128]{1,0:T(8,128)S(1)}, f32[8,128]{1,0:T(8,128)S(1)}, u32[]{:S(2)}, u32[]{:S(2)}) collective-permute-start(f32[8,128]{1,0:T(8,128)S(1)} %get-tuple-element.70), channel_id=1, source_target_pairs={{0,3},{1,2},{2,1},{3,0},{4,7},{5,6},{6,5},{7,4},{8,11},{9,10},{10,... | collective-permute-start | bytes 12296 | tf_op jit(solution)/shard_map/ppermute | solution.py:19
  91.2 3.6 %collective-permute-start.26 = (f32[8,128]{1,0:T(8,128)S(1)}, f32[8,128]{1,0:T(8,128)S(1)}, u32[]{:S(2)}, u32[]{:S(2)}) collective-permute-start(f32[8,128]{1,0:T(8,128)S(1)} %get-tuple-element.70), channel_id=1, source_target_pairs={{0,1},{1,0},{2,3},{3,2},{4,5},{5,4},{6,7},{7,6},{8,9},{9,8},{10,11... | collective-permute-start | bytes 12296 | tf_op jit(solution)/shard_map/ppermute | solution.py:19
  94.8 7.2 %collective-permute-start.30 = (f32[8,128]{1,0:T(8,128)S(1)}, f32[8,128]{1,0:T(8,128)S(1)}, u32[]{:S(2)}, u32[]{:S(2)}) collective-permute-start(f32[8,128]{1,0:T(8,128)S(1)} %add_add_fusion.1), channel_id=1, source_target_pairs={{0,8},{4,12},{8,0},{12,4},{1,9},{5,13},{9,1},{13,5},{2,10},{6,14},... | collective-permute-start | bytes 12296 | tf_op jit(solution)/shard_map/ppermute | solution.py:19
  97.3 4.7 %collective-permute-start.31 = (f32[8,128]{1,0:T(8,128)S(1)}, f32[8,128]{1,0:T(8,128)S(1)}, u32[]{:S(2)}, u32[]{:S(2)}) collective-permute-start(f32[8,128]{1,0:T(8,128)S(1)} %add_add_fusion.1), channel_id=1, source_target_pairs={{0,12},{4,8},{8,4},{12,0},{1,13},{5,9},{9,5},{13,1},{2,14},{6,10},... | collective-permute-start | bytes 12296 | tf_op jit(solution)/shard_map/ppermute | solution.py:19
  97.3 4.7 %collective-permute-start.29 = (f32[8,128]{1,0:T(8,128)S(1)}, f32[8,128]{1,0:T(8,128)S(1)}, u32[]{:S(2)}, u32[]{:S(2)}) collective-permute-start(f32[8,128]{1,0:T(8,128)S(1)} %add_add_fusion.1), channel_id=1, source_target_pairs={{0,4},{4,0},{8,12},{12,8},{1,5},{5,1},{9,13},{13,9},{2,6},{6,2},{1... | collective-permute-start | bytes 12296 | tf_op jit(solution)/shard_map/ppermute | solution.py:19
  102.2 4.1 %copy-start.11 = (f32[3]{0:T(128)S(1)}, f32[3]{0:T(128)}, u32[]{:S(2)}) copy-start(f32[3]{0:T(128)} %constant.50) | copy-start | bytes 40
  102.2 4.0 %collective-permute-start.32 = (f32[8,128]{1,0:T(8,128)S(1)}, f32[8,128]{1,0:T(8,128)S(1)}, u32[]{:S(2)}, u32[]{:S(2)}) collective-permute-start(f32[8,128]{1,0:T(8,128)S(1)} %add_add_fusion), channel_id=1, source_target_pairs={{0,16},{16,0},{1,17},{17,1},{2,18},{18,2},{3,19},{19,3},{4,20},{20... | collective-permute-start | bytes 12296 | tf_op jit(solution)/shard_map/ppermute | solution.py:19

commit v7 on v6

--- a/solution.py
+++ b/solution.py
@@ -52,78 +52,111 @@
         for k in range(lax.axis_size("tensor"))
     ]
     others = []
-    for k in range(1, lax.axis_size("dp")):
-        near = 1 if k == 1 and source == 0 else 0
-        if k == 1 and source == 1:
-            late = None
-            others.append(late)
-            continue
-        late, arrived[near] = lax.optimization_barrier((rows, arrived[near]))
-        others.append(swap_in(late, source, "dp", k))
+    if source == 1:
+        for k in range(2, lax.axis_size("dp")):
+            early, arrived[0] = lax.optimization_barrier((rows, arrived[0]))
+            others.append(swap_in(early, source, "dp", k))
     total = start.astype(jnp.float32)
     for value in arrived:
         total = total + value.astype(jnp.float32)
     total = total.astype(jnp.bfloat16)
-    if others[0] is None:
-        late, total = lax.optimization_barrier((rows, total))
-        others[0] = swap_in(late, source, "dp", 1)
-    return total, [rows] + others
-
-
-def load_kernel(*refs):
-    count = (len(refs) - 1) // 2
-    copies = [
-        pltpu.make_async_copy(refs[i].at[0], refs[count + i], refs[-1].at[i])
-        for i in range(count)
+    late, total = lax.optimization_barrier((rows, total))
+    if source == 0:
+        return total, gather_in(late, source, "dp")
+    return total, [rows, swap_in(late, source, "dp", 1)] + others
+
+
+def load_kernel(gate_in, up_in, down_in, gate, up, down, gate_t, sems):
+    width = gate.shape[0]
+    pieces = [(begin, min(256, width - begin)) for begin in range(0, width, 256)]
+    copies = []
+    for number, (begin, count) in enumerate(pieces):
+        rows = pl.ds(begin, count)
+        copies.append(pltpu.make_async_copy(gate_in.at[0, rows], gate.at[rows], sems.at[2 + number]))
+    rest = [
+        pltpu.make_async_copy(up_in.at[0], up, sems.at[0]),
+        pltpu.make_async_copy(down_in.at[0], down, sems.at[1]),
     ]
-    for copy in copies:
+    for copy in copies + rest:
         copy.start()
-    for copy in copies:
+    for copy, (begin, count) in zip(copies, pieces):
         copy.wait()
-
-
-def load_weights(*weights):
-    total = sum(w.size * 2 for w in weights)
-    weights = [pltpu.with_memory_space_constraint(w, pltpu.HBM) for w in weights]
+        gate_t[:, begin : begin + count] = gate[begin : begin + count, :].T
+    for copy in rest:
+        copy.wait()
+
+
+def load_weights(w_gate, w_up, w_down):
+    _, width, units = w_gate.shape
+    weights = [pltpu.with_memory_space_constraint(w, pltpu.HBM) for w in (w_gate, w_up, w_down)]
+    shapes = [(width, units), (width, units), (units, width), (units, width)]
     return pl.pallas_call(
         load_kernel,
-        in_specs=[pl.BlockSpec(memory_space=pltpu.HBM)] * len(weights),
-        out_specs=[pl.BlockSpec(memory_space=pltpu.VMEM)] * len(weights),
-        out_shape=[pltpu.VMEM(w.shape[1:], w.dtype) for w in weights],
-        scratch_shapes=[pltpu.SemaphoreType.DMA((len(weights),))],
-        compiler_params=pltpu.CompilerParams(vmem_limit_bytes=total + 2**20),
-        cost_estimate=pl.CostEstimate(flops=0, bytes_accessed=total, transcendentals=0),
+        in_specs=[pl.BlockSpec(memory_space=pltpu.HBM)] * 3,
+        out_specs=[pl.BlockSpec(memory_space=pltpu.VMEM)] * 4,
+        out_shape=[pltpu.VMEM(shape, jnp.bfloat16) for shape in shapes],
+        scratch_shapes=[pltpu.SemaphoreType.DMA((2 + -(-width // 256),))],
+        compiler_params=pltpu.CompilerParams(vmem_limit_bytes=4 * 2**20),
+        cost_estimate=pl.CostEstimate(
+            flops=0, bytes_accessed=6 * width * units, transcendentals=0
+        ),
     )(*weights)
 
 
-def gradient_kernel(ids_ref, hidden_ref, y_ref, *rest):
-    out_ref, masked = rest[-2:]
-    piece = y_ref.shape[1]
-
-    @pl.when(pl.program_id(0) == 0)
+def hidden_grad_kernel(flag_ref, rows_ref, down_ref, out_ref):
+    units = down_ref.shape[0]
+
+    @pl.when(flag_ref[0] == 1)
     def _():
-        for e in range(DOMAINS):
-            keep = ids_ref[...] == e
-            masked[:, e * piece : (e + 1) * piece] = jnp.where(
-                keep, y_ref[...].astype(jnp.float32), 0.0
-            ).astype(jnp.bfloat16)
-
+        for begin in range(0, units, TILE):
+            out_ref[:, begin : begin + TILE] = lax.dot_general(
+                rows_ref[...],
+                down_ref[begin : begin + TILE, :],
+                CONTRACT_LAST,
+                preferred_element_type=jnp.float32,
+            )
+
+    @pl.when(flag_ref[0] == 0)
+    def _():
+        out_ref[...] = jnp.zeros_like(out_ref)
+
+
+def hidden_grad(segment, rows, down_w):
+    units, width = down_w.shape
+    return pl.pallas_call(
+        hidden_grad_kernel,
+        in_specs=[pl.BlockSpec(memory_space=pltpu.SMEM)]
+        + [pl.BlockSpec(memory_space=pltpu.VMEM)] * 2,
+        out_specs=pl.BlockSpec(memory_space=pltpu.VMEM),
+        out_shape=jax.ShapeDtypeStruct((rows.shape[0], units), jnp.float32),
+        compiler_params=pltpu.CompilerParams(vmem_limit_bytes=16 * 2**20),
+        cost_estimate=pl.CostEstimate(
+            flops=2 * rows.shape[0] * units * width,
+            bytes_accessed=2 * units * width,
+            transcendentals=0,
+        ),
+    )(segment.reshape(1), rows, down_w)
+
+
+def gradient_kernel(hidden_ref, masked_ref, *rest):
+    out_ref = rest[-1]
+    piece = out_ref.shape[2]
     product = lax.dot_general(
-        hidden_ref[...], masked[...], CONTRACT_FIRST, preferred_element_type=jnp.float32
+        hidden_ref[...], masked_ref[...], CONTRACT_FIRST, preferred_element_type=jnp.float32
     )
     for e in range(DOMAINS):
         out_ref[e] = product[:, e * piece : (e + 1) * piece].astype(jnp.bfloat16)
 
 
-def domain_gradients(row_ids, hidden, y, begin, count, grads=None):
+def domain_gradients(hidden, masked, begin, count, grads=None):
     rows, units = hidden.shape
-    piece = y.shape[1]
+    columns = masked.shape[1]
+    piece = columns // DOMAINS
     in_specs = [
-        pl.BlockSpec((rows, 1), lambda i: (0, 0)),
         pl.BlockSpec((rows, TILE), lambda i: (0, begin + i)),
-        pl.BlockSpec((rows, piece), lambda i: (0, 0)),
+        pl.BlockSpec(memory_space=pltpu.VMEM),
     ]
-    operands = [row_ids, hidden, y]
+    operands = [hidden, masked]
     if grads is not None:
         in_specs.append(pl.BlockSpec(memory_space=pl.ANY))
         operands.append(grads)
@@ -133,12 +166,11 @@
         in_specs=in_specs,
         out_specs=pl.BlockSpec((DOMAINS, TILE, piece), lambda i: (0, begin + i, 0)),
         out_shape=jax.ShapeDtypeStruct((DOMAINS, units, piece), jnp.bfloat16),
-        scratch_shapes=[pltpu.VMEM((rows, DOMAINS * piece), jnp.bfloat16)],
-        input_output_aliases={} if grads is None else {3: 0},
-        compiler_params=pltpu.CompilerParams(vmem_limit_bytes=24 * 2**20),
+        input_output_aliases={} if grads is None else {2: 0},
+        compiler_params=pltpu.CompilerParams(vmem_limit_bytes=16 * 2**20),
         cost_estimate=pl.CostEstimate(
-            flops=2 * rows * count * TILE * DOMAINS * piece,
-            bytes_accessed=2 * count * TILE * (rows + DOMAINS * piece),
+            flops=2 * rows * count * TILE * columns,
+            bytes_accessed=2 * count * TILE * (rows + columns),
             transcendentals=0,
         ),
     )(*operands)
@@ -203,7 +235,8 @@
 
 
 def norms_kernel(replicas, levels, ids_ref, ids_row_ref, gram_ref, *refs):
-    *parts, y_ref, norms_ref, acc = refs
+    *parts, masked_ref, norms_ref, y_ref, acc = refs
+    piece = y_ref.shape[1]
     block = parts[0].shape[0] // replicas
     tok_rows = block * len(parts)
     for t, part in enumerate(parts):
@@ -211,6 +244,10 @@
             y_ref[k * tok_rows + t * block : k * tok_rows + (t + 1) * block, :] = part[
                 k * block : (k + 1) * block, :
             ]
+    for e in range(DOMAINS):
+        masked_ref[:, e * piece : (e + 1) * piece] = jnp.where(
+            ids_ref[...] == e, y_ref[...].astype(jnp.float32), 0.0
+        ).astype(jnp.bfloat16)
     acc[...] = jnp.zeros_like(acc)
     lane = lax.broadcasted_iota(jnp.int32, (1, acc.shape[1]), 1)
     for k in range(replicas):
@@ -239,10 +276,13 @@
         in_specs=[pl.BlockSpec(memory_space=pltpu.VMEM)] * (3 + len(parts)),
         out_specs=[pl.BlockSpec(memory_space=pltpu.VMEM)] * 2,
         out_shape=[
-            jax.ShapeDtypeStruct((total, piece), jnp.bfloat16),
+            pltpu.VMEM((total, DOMAINS * piece), jnp.bfloat16),
             jax.ShapeDtypeStruct((8, 128), jnp.float32),
         ],
-        scratch_shapes=[pltpu.VMEM((total, 128), jnp.float32)],
+        scratch_shapes=[
+            pltpu.VMEM((total, piece), jnp.bfloat16),
+            pltpu.VMEM((total, 128), jnp.float32),
+        ],
         compiler_params=pltpu.CompilerParams(
             vmem_limit_bytes=8 * total * piece + 4 * total * total + 1024 * total * 4 + 8 * 2**20
         ),
@@ -263,7 +303,7 @@
     assert segments == 2
     micro, local_rows, width = layer_input_activations.shape
     gain = norm_gain[0][None, :]
-    gate_w, up_w, down_w = load_weights(w_gate, w_up, w_down)
+    gate_w, up_w, down_w, gate_t = load_weights(w_gate, w_up, w_down)
     units = down_w.shape[0]
     block = micro * local_rows
     tok_rows = block * tensor_size
@@ -285,7 +325,7 @@
     hidden0 = (jax.nn.silu(gate0) * up0).astype(jnp.bfloat16)
     mixed = jnp.dot(hidden0, down_w, preferred_element_type=jnp.float32).astype(jnp.bfloat16)
     cot_rows, hidden0, mixed = lax.optimization_barrier((rows_in, hidden0, mixed))
-    d_hidden = lax.dot_general(cot_rows, down_w, CONTRACT_LAST, preferred_element_type=jnp.float32)
+    d_hidden = hidden_grad(segment, cot_rows, down_w)
     x1_own, pieces0 = scatter_sum(x_own, mixed, 0, block, hidden0)
     x1_own, d_hidden = lax.optimization_barrier((x1_own, d_hidden))
     x1 = jnp.concatenate(gather_in(x1_own, 1, "tensor"), axis=0)
@@ -296,7 +336,7 @@
     d_gate = (d_hidden * up * (sig * (1.0 + gate * (1.0 - sig)))).astype(jnp.bfloat16)
     d_up = (d_hidden * gate * sig).astype(jnp.bfloat16)
     d_gate, d_up = lax.optimization_barrier((d_gate, d_up))
-    d_normed = lax.dot_general(d_gate, gate_w, CONTRACT_LAST, preferred_element_type=jnp.float32)
+    d_normed = jnp.dot(d_gate, gate_t, preferred_element_type=jnp.float32)
     d_normed = d_normed + lax.dot_general(
         d_up, up_w, CONTRACT_LAST, preferred_element_type=jnp.float32
     )
@@ -326,7 +366,7 @@
         ids_all.astype(jnp.int32)[:, None, :, None], (dp_size, tensor_size, micro, local_rows)
     ).reshape(dp_size * tok_rows, 1)
     levels = dp_size.bit_length()
-    y, norms = norm_sums(row_ids, gram_hidden, parts_y, dp_size, levels)
+    masked, norms = norm_sums(row_ids, gram_hidden, parts_y, dp_size, levels)
     rounds = [
         (axis, bit, min(2, bits(axis) - bit))
         for axis in ("tensor", "dp", "section")
@@ -340,12 +380,12 @@
         others = [swap(norms, axis, k << bit) for k in range(1, 1 << count)]
         if part < parts:
             end = tiles * (part + 1) // parts
-            grads = domain_gradients(row_ids, hidden_all, y, begin, end - begin, grads)
+            grads = domain_gradients(hidden_all, masked, begin, end - begin, grads)
             begin = end
         norms = norms + others[0]
         if count == 2:
             norms = norms + (others[1] + others[2])
-        row_ids, norms = lax.optimization_barrier((row_ids, norms))
+        masked, norms = lax.optimization_barrier((masked, norms))
     entries = segments * units * tensor_size * width
     counts = [float((dp_size >> level) * entries) for level in range(levels)]
     return grads[None], norms[:DOMAINS, :levels] / jnp.array(counts, jnp.float32)[None, :]

time: 107 us -> 105 us (0.981)
  matrix products: 13.6 us -> 10.1 us
  waiting for transfers between devices: 15.3 us -> 16.6 us
    dot_general x2 -> x1, matrix products: 4.99 us -> 1.12 us  [shards(): d_normed = jnp.dot(d_gate, gate_t, preferred_element_type=jnp.float32)]
    ppermute x16, waiting for transfers between devices: 8.87 us -> 6.96 us  [swap(): return lax.ppermute(block, axis, [(i, i ^ offset) for i in range(size)])]
    ppermute x8, waiting for transfers between devices: 5.56 us -> 7.34 us  [across(): return lax.ppermute(block, ('section', 'tensor'), route)]
    unnamed x26 -> x24, local copies, waits for them, and re-layouts: 2.37 us -> 0.79 us
    pallas_call x3, Pallas kernels: 9.95 us -> 8.49 us  [domain_gradients(): pl.pallas_call(gradient_kernel, grid=(count,), in_specs=in_specs, out_spe...]
    ppermute x9, waiting for transfers between devices: 0.86 us -> 2.32 us  [swap_in(): return lax.ppermute(block, ('section', axis), route)]
  transfers between devices with their start and end apart: 33 -> 33, of which waited for: 9 -> 11; matrix products, arithmetic and copies ran while one was open for 11% -> 9% of each run, Pallas kernels for 19% -> 18%
where the time goes in v7:
time: 105 us; the launch traced here: 104 us
  starting transfers between devices  49.7 us (47%)
  Pallas kernels  20.3 us (19%)
  waiting for transfers between devices  16.6 us (16%)
  matrix products  10.1 us (10%)
  local copies, waits for them, and re-layouts  3.74 us (4%)
  other arithmetic  2.53 us (2%)
  between operations  1.22 us (1%)
    ppermute x16, starting transfers between devices, swap(): return lax.ppermute(block, axis, [(i, i ^ offset) for i in range(size)])  23.5 us
    ppermute x9, starting transfers between devices, swap_in(): return lax.ppermute(block, ('section', axis), route)  14.2 us
    ppermute x8, starting transfers between devices, across(): return lax.ppermute(block, ('section', 'tensor'), route)  12 us
    pallas_call x3, Pallas kernels, domain_gradients(): pl.pallas_call(gradient_kernel, grid=(count,), in_specs=in_specs, out_spe...  8.49 us
    pallas_call x1, Pallas kernels, load_weights(): pl.pallas_call(load_kernel, in_specs=[pl.BlockSpec(memory_space=pltpu.HBM...  7.46 us
    ppermute x8, waiting for transfers between devices, across(): return lax.ppermute(block, ('section', 'tensor'), route)  7.34 us
    ppermute x16, waiting for transfers between devices, swap(): return lax.ppermute(block, axis, [(i, i ^ offset) for i in range(size)])  6.96 us
    dot_general x2, matrix products, layer_parts(): up = jnp.dot(normed, up_w, preferred_element_type=jnp.float32)  2.88 us
  transfers between devices with their start and end apart: 33, of which 11 were waited for; matrix products, arithmetic and copies ran while one was open for 9% of the time, Pallas kernels for 18%

profile of v7, /device:TPU:0, one launch (start us, length us, event | category | flops | bytes accessed | tf_op | source)
XLA Modules:
  0.0 104.2 jit_solution(18112741772021381394)
XLA Ops:
  0.6 1.0 bitcast_select_fusion.1
  1.6 5.1 %collective-permute-start.2 = (bf16[32,2048]{1,0:T(8,128)(2,1)S(1)}, bf16[32,2048]{1,0:T(8,128)(2,1)S(1)}, u32[]{:S(2)}, u32[]{:S(2)}) collective-permute-start(bf16[32,2048]{1,0:T(8,128)(2,1)S(1)} %bitcast_select_fusion.1), channel_id=1, source_target_pairs={{0,3},{1,2},{2,1},{3,0},{4,7},{5,6},{6,5},{7,4},{8,11},{9,10},{10,... | collective-permute-start | bytes 393224 | tf_op jit(solution)/shard_map/ppermute | solution.py:19
  7.4 7.5 %shard_map.95 = (bf16[2048,1792]{1,0:T(8,128)(2,1)S(1)}, bf16[2048,1792]{1,0:T(8,128)(2,1)S(1)}, bf16[1792,2048]{1,0:T(8,128)(2,1)S(1)}, bf16[1792,2048]{1,0:T(8,128)(2,1)S(1)}) custom-call(bf16[1,2048,1792]{2,1,0:T(8,128)(2,1)} %gate_in.1, bf16[1,2048,1792]{2,1,0:T(8,128)(2,1)} %up_in.1, bf16[1,1792,2048]{2,1,0:T(8,128)(2,1)} %down_in.1), custom_call_target="tpu_custom_call" | custom-call | bytes 22020096 | tf_op jit(solution)/shard_map/pallas_call | solution.py:93
  14.9 3.0 %collective-permute-done.1 = bf16[32,2048]{1,0:T(8,128)(2,1)S(1)} collective-permute-done((bf16[32,2048]{1,0:T(8,128)(2,1)S(1)}, bf16[32,2048]{1,0:T(8,128)(2,1)S(1)}, u32[]{:S(2)}, u32[]{:S(2)}) %collective-permute-start.1) | collective-permute-done | bytes 131104 | tf_op jit(solution)/shard_map/ppermute | solution.py:19
  18.0 1.2 %fusion.16 = f32[128,1792]{1,0:T(8,128)S(1)} fusion(bf16[2048,1792]{1,0:T(8,128)(2,1)S(1)} %get-tuple-element.37, bf16[128,2048]{1,0:T(8,128)(2,1)S(1)} %get-tuple-element.43.rows_ref, f32[2048]{0:T(1024)S(1)} %bitcast.28, f32[128]{0:T(128)S(1)} %add_rsqrt_fusion.1), kind=kOutput, calls=%fused_computation.30 | convolution fusion | flops 940572672 | bytes 8790528 | tf_op jit(solution)/shard_map/dot_general | solution.py:320
  19.2 1.4 %fusion.1.refs_0_ = bf16[128,1792]{1,0:T(8,128)(2,1)S(1)} fusion(bf16[2048,1792]{1,0:T(8,128)(2,1)S(1)} %get-tuple-element.38, f32[128,1792]{1,0:T(8,128)S(1)} %fusion.16, bf16[128,2048]{1,0:T(8,128)(2,1)S(1)} %get-tuple-element.43.rows_ref, f32[2048]{0:T(1024)S(1)} %bitcast.29, f32[128]{0:T(128)S(1)} %add_rsqrt_fusion.1), kind=kOutput, calls=%fused_computation.3 | convolution fusion | flops 941948928 | bytes 9249280 | tf_op jit(solution)/shard_map/dot_general | solution.py:321
  20.6 1.1 %convolution_convert_fusion = bf16[128,2048]{1,0:T(8,128)(2,1)S(1)} fusion(bf16[128,1792]{1,0:T(8,128)(2,1)S(1)} %fusion.1.refs_0_, bf16[1792,2048]{1,0:T(8,128)(2,1)S(1)} %get-tuple-element.39.down_ref), kind=kOutput, calls=%fused_computation.4 | convolution fusion | flops 939786240 | bytes 8323072 | tf_op jit(solution)/shard_map/dot_general | solution.py:326
  21.8 3.0 %collective-permute-start.6 = (bf16[32,2048]{1,0:T(8,128)(2,1)S(1)}, bf16[32,2048]{1,0:T(8,128)(2,1)S(1)}, u32[]{:S(2)}, u32[]{:S(2)}) collective-permute-start(bf16[32,2048]{1,0:T(8,128)(2,1)S(1)} %get-tuple-element.82), channel_id=1, source_target_pairs={{0,19},{1,18},{2,17},{3,16},{4,23},{5,22},{6,21},{7,20},{8,27},{9,... | collective-permute-start | bytes 393224 | tf_op jit(solution)/shard_map/ppermute | solution.py:33
  24.8 1.3 %collective-permute-start.5 = (bf16[32,2048]{1,0:T(8,128)(2,1)S(1)}, bf16[32,2048]{1,0:T(8,128)(2,1)S(1)}, u32[]{:S(2)}, u32[]{:S(2)}) collective-permute-start(bf16[32,2048]{1,0:T(8,128)(2,1)S(1)} %get-tuple-element.83), channel_id=1, source_target_pairs={{0,18},{1,19},{2,16},{3,17},{4,22},{5,23},{6,20},{7,21},{8,26},{9,... | collective-permute-start | bytes 393224 | tf_op jit(solution)/shard_map/ppermute | solution.py:33
  26.1 1.3 %collective-permute-start.4 = (bf16[32,2048]{1,0:T(8,128)(2,1)S(1)}, bf16[32,2048]{1,0:T(8,128)(2,1)S(1)}, u32[]{:S(2)}, u32[]{:S(2)}) collective-permute-start(bf16[32,2048]{1,0:T(8,128)(2,1)S(1)} %get-tuple-element.84), channel_id=1, source_target_pairs={{0,17},{1,16},{2,19},{3,18},{4,21},{5,20},{6,23},{7,22},{8,25},{9,... | collective-permute-start | bytes 393224 | tf_op jit(solution)/shard_map/ppermute | solution.py:33
  27.4 1.3 %collective-permute-start.3 = (bf16[32,2048]{1,0:T(8,128)(2,1)S(1)}, bf16[32,2048]{1,0:T(8,128)(2,1)S(1)}, u32[]{:S(2)}, u32[]{:S(2)}) collective-permute-start(bf16[32,2048]{1,0:T(8,128)(2,1)S(1)} %get-tuple-element.81), channel_id=1, source_target_pairs={{0,16},{1,17},{2,18},{3,19},{4,20},{5,21},{6,22},{7,23},{8,24},{9,... | collective-permute-start | bytes 393224 | tf_op jit(solution)/shard_map/ppermute | solution.py:33
  28.8 1.3 %collective-permute-done.4 = bf16[32,2048]{1,0:T(8,128)(2,1)S(1)} collective-permute-done((bf16[32,2048]{1,0:T(8,128)(2,1)S(1)}, bf16[32,2048]{1,0:T(8,128)(2,1)S(1)}, u32[]{:S(2)}, u32[]{:S(2)}) %collective-permute-start.4) | collective-permute-done | bytes 131104 | tf_op jit(solution)/shard_map/ppermute | solution.py:33
  32.2 3.4 %collective-permute-start.10 = (bf16[128,1792]{1,0:T(8,128)(2,1)S(1)}, bf16[128,1792]{1,0:T(8,128)(2,1)S(1)}, u32[]{:S(2)}, u32[]{:S(2)}) collective-permute-start(bf16[128,1792]{1,0:T(8,128)(2,1)S(1)} %fusion.1.refs_0_), channel_id=1, source_target_pairs={{0,4},{4,0},{8,12},{12,8},{1,5},{5,1},{9,13},{13,9},{2,6},{6,2},{1... | collective-permute-start | bytes 1376264 | tf_op jit(solution)/shard_map/ppermute | solution.py:25
  35.6 3.4 %collective-permute-start.11 = (bf16[128,1792]{1,0:T(8,128)(2,1)S(1)}, bf16[128,1792]{1,0:T(8,128)(2,1)S(1)}, u32[]{:S(2)}, u32[]{:S(2)}) collective-permute-start(bf16[128,1792]{1,0:T(8,128)(2,1)S(1)} %fusion.1.refs_0_), channel_id=1, source_target_pairs={{0,8},{4,12},{8,0},{12,4},{1,9},{5,13},{9,1},{13,5},{2,10},{6,14},... | collective-permute-start | bytes 1376264 | tf_op jit(solution)/shard_map/ppermute | solution.py:25
  39.1 2.6 %collective-permute-start.12 = (bf16[128,1792]{1,0:T(8,128)(2,1)S(1)}, bf16[128,1792]{1,0:T(8,128)(2,1)S(1)}, u32[]{:S(2)}, u32[]{:S(2)}) collective-permute-start(bf16[128,1792]{1,0:T(8,128)(2,1)S(1)} %fusion.1.refs_0_), channel_id=1, source_target_pairs={{0,12},{4,8},{8,4},{12,0},{1,13},{5,9},{9,5},{13,1},{2,14},{6,10},... | collective-permute-start | bytes 1376264 | tf_op jit(solution)/shard_map/ppermute | solution.py:25
  41.9 1.2 %fusion.11 = f32[128,1792]{1,0:T(8,128)S(1)} fusion(bf16[2048,1792]{1,0:T(8,128)(2,1)S(1)} %get-tuple-element.37, f32[128]{0:T(128)S(1)} %add_rsqrt_fusion, f32[2048]{0:T(1024)S(1)} %bitcast.30, bf16[32,2048]{1,0:T(8,128)(2,1)S(1)} %collective-permute-done.9, bf16[32,2048]{1,0:T(8,128)(2,1)S(1)} %collective-permute-done.8, ...), kind=kOutput, calls=%fused_computation.28 | convolution fusion | flops 942407680 | bytes 8790528 | tf_op jit(solution)/shard_map/dot_general | solution.py:320
  43.1 1.5 %multiply_convert_fusion = (bf16[128,1792]{1,0:T(8,128)(2,1)S(1)}, bf16[128,1792]{1,0:T(8,128)(2,1)S(1)}, bf16[128,1792]{1,0:T(8,128)(2,1)S(1)}) fusion(f32[128,1792]{1,0:T(8,128)S(1)} %fusion.11, f32[128,1792]{1,0:T(8,128)S(1)} %shard_map.96, bf16[2048,1792]{1,0:T(8,128)(2,1)S(1)} %get-tuple-element.38, f32[128]{0:T(128)S(1)} %add_rsqrt_fusion, ...), kind=kOutput, calls=%fused_computation.20 | convolution fusion | flops 946077696 | bytes 11084288 | tf_op jit(solution)/shard_map/dot_general | solution.py:321
  44.6 1.1 %fusion.21 = f32[128,2048]{1,0:T(8,128)S(1)} fusion(bf16[128,1792]{1,0:T(8,128)(2,1)S(1)} %get-tuple-element.46, bf16[1792,2048]{1,0:T(8,128)(2,1)S(1)} %get-tuple-element.47), kind=kOutput, calls=%fused_computation.56 | convolution fusion | flops 939524096 | bytes 8847360 | tf_op jit(solution)/shard_map/dot_general | solution.py:339
  45.8 2.6 %fusion.8 = (f32[128]{0:T(128)S(1)}, f32[128,2048]{1,0:T(8,128)S(1)}) fusion(bf16[32,2048]{1,0:T(8,128)(2,1)S(1)} %collective-permute-done.9, bf16[32,2048]{1,0:T(8,128)(2,1)S(1)} %collective-permute-done.8, bf16[32,2048]{1,0:T(8,128)(2,1)S(1)} %collective-permute-done.7, bf16[32,2048]{1,0:T(8,128)(2,1)S(1)} %add_convert_fusion.1, f32[2048]{0:T(1024)S(1)} %bitcast.32, ...), kind=kOutput, calls=%fused_computation.17 | convolution fusion | flops 942669696 | bytes 10428928 | tf_op jit(solution)/shard_map/dot_general | solution.py:340
  48.6 2.3 %collective-permute-done.11.refs_2_ = bf16[128,1792]{1,0:T(8,128)(2,1)S(1)} collective-permute-done((bf16[128,1792]{1,0:T(8,128)(2,1)S(1)}, bf16[128,1792]{1,0:T(8,128)(2,1)S(1)}, u32[]{:S(2)}, u32[]{:S(2)}) %collective-permute-start.11) | collective-permute-done | bytes 458784 | tf_op jit(solution)/shard_map/ppermute | solution.py:25
  51.0 1.3 %collective-permute-start.16 = (bf16[32,2048]{1,0:T(8,128)(2,1)S(1)}, bf16[32,2048]{1,0:T(8,128)(2,1)S(1)}, u32[]{:S(2)}, u32[]{:S(2)}) collective-permute-start(bf16[32,2048]{1,0:T(8,128)(2,1)S(1)} %get-tuple-element.78), channel_id=1, source_target_pairs={{16,3},{17,2},{18,1},{19,0},{20,7},{21,6},{22,5},{23,4},{24,11},{2... | collective-permute-start | bytes 393224 | tf_op jit(solution)/shard_map/ppermute | solution.py:33
  52.3 1.3 %collective-permute-start.15 = (bf16[32,2048]{1,0:T(8,128)(2,1)S(1)}, bf16[32,2048]{1,0:T(8,128)(2,1)S(1)}, u32[]{:S(2)}, u32[]{:S(2)}) collective-permute-start(bf16[32,2048]{1,0:T(8,128)(2,1)S(1)} %get-tuple-element.79), channel_id=1, source_target_pairs={{16,2},{17,3},{18,0},{19,1},{20,6},{21,7},{22,4},{23,5},{24,10},{2... | collective-permute-start | bytes 393224 | tf_op jit(solution)/shard_map/ppermute | solution.py:33
  53.6 1.3 %collective-permute-start.14 = (bf16[32,2048]{1,0:T(8,128)(2,1)S(1)}, bf16[32,2048]{1,0:T(8,128)(2,1)S(1)}, u32[]{:S(2)}, u32[]{:S(2)}) collective-permute-start(bf16[32,2048]{1,0:T(8,128)(2,1)S(1)} %get-tuple-element.80), channel_id=1, source_target_pairs={{16,1},{17,0},{18,3},{19,2},{20,5},{21,4},{22,7},{23,6},{24,9},{25... | collective-permute-start | bytes 393224 | tf_op jit(solution)/shard_map/ppermute | solution.py:33
  54.9 1.3 %collective-permute-start.13 = (bf16[32,2048]{1,0:T(8,128)(2,1)S(1)}, bf16[32,2048]{1,0:T(8,128)(2,1)S(1)}, u32[]{:S(2)}, u32[]{:S(2)}) collective-permute-start(bf16[32,2048]{1,0:T(8,128)(2,1)S(1)} %get-tuple-element.77), channel_id=1, source_target_pairs={{16,0},{17,1},{18,2},{19,3},{20,4},{21,5},{22,6},{23,7},{24,8},{25... | collective-permute-start | bytes 393224 | tf_op jit(solution)/shard_map/ppermute | solution.py:33
  56.3 3.0 %collective-permute-done.13 = bf16[32,2048]{1,0:T(8,128)(2,1)S(1)} collective-permute-done((bf16[32,2048]{1,0:T(8,128)(2,1)S(1)}, bf16[32,2048]{1,0:T(8,128)(2,1)S(1)}, u32[]{:S(2)}, u32[]{:S(2)}) %collective-permute-start.13) | collective-permute-done | bytes 131104 | tf_op jit(solution)/shard_map/ppermute | solution.py:33
  59.3 3.1 %collective-permute-done.15 = bf16[32,2048]{1,0:T(8,128)(2,1)S(1)} collective-permute-done((bf16[32,2048]{1,0:T(8,128)(2,1)S(1)}, bf16[32,2048]{1,0:T(8,128)(2,1)S(1)}, u32[]{:S(2)}, u32[]{:S(2)}) %collective-permute-start.15) | collective-permute-done | bytes 131104 | tf_op jit(solution)/shard_map/ppermute | solution.py:33
  62.6 1.6 %collective-permute-start.19 = (bf16[48,512]{1,0:T(8,128)(2,1)S(1)}, bf16[48,512]{1,0:T(8,128)(2,1)S(1)}, u32[]{:S(2)}, u32[]{:S(2)}) collective-permute-start(bf16[48,512]{1,0:T(8,128)(2,1)S(1)} %get-tuple-element.93), channel_id=1, source_target_pairs={{0,12},{4,8},{8,4},{12,0},{1,13},{5,9},{9,5},{13,1},{2,14},{6,10},... | collective-permute-start | bytes 147464 | tf_op jit(solution)/shard_map/ppermute | solution.py:19
  64.1 0.7 collective-permute-start.20
  65.4 1.5 %collective-permute-start.17 = (bf16[48,512]{1,0:T(8,128)(2,1)S(1)}, bf16[48,512]{1,0:T(8,128)(2,1)S(1)}, u32[]{:S(2)}, u32[]{:S(2)}) collective-permute-start(bf16[48,512]{1,0:T(8,128)(2,1)S(1)} %get-tuple-element.91), channel_id=1, source_target_pairs={{0,4},{4,0},{8,12},{12,8},{1,5},{5,1},{9,13},{13,9},{2,6},{6,2},{1... | collective-permute-start | bytes 147464 | tf_op jit(solution)/shard_map/ppermute | solution.py:19
  66.9 0.7 collective-permute-start.21
  68.2 1.4 %collective-permute-start.22 = (bf16[128,1792]{1,0:T(8,128)(2,1)S(1)}, bf16[128,1792]{1,0:T(8,128)(2,1)}, u32[]{:S(2)}, u32[]{:S(2)}) collective-permute-start(bf16[128,1792]{1,0:T(8,128)(2,1)S(1)} %get-tuple-element.61.refs_4_), channel_id=1, source_target_pairs={{16,28},{20,24},{24,20},{28,16},{17,29},{21,25},{25,21},{29,17},{1... | collective-permute-start | bytes 1376264 | tf_op jit(solution)/shard_map/ppermute | solution.py:25
  70.4 2.1 %collective-permute-start.24 = (bf16[128,512]{1,0:T(8,128)(2,1)S(1)}, bf16[128,512]{1,0:T(8,128)(2,1)S(1)}, u32[]{:S(2)}, u32[]{:S(2)}) collective-permute-start(bf16[128,512]{1,0:T(8,128)(2,1)S(1)} %pad_maximum_fusion.2.refs_0_), channel_id=1, source_target_pairs={{0,2},{1,3},{2,0},{3,1},{4,6},{5,7},{6,4},{7,5},{8,10},{9,11},{10,... | collective-permute-start | bytes 393224 | tf_op jit(solution)/shard_map/ppermute | solution.py:19
  72.5 2.3 %collective-permute-start.25 = (bf16[128,512]{1,0:T(8,128)(2,1)S(1)}, bf16[128,512]{1,0:T(8,128)(2,1)S(1)}, u32[]{:S(2)}, u32[]{:S(2)}) collective-permute-start(bf16[128,512]{1,0:T(8,128)(2,1)S(1)} %pad_maximum_fusion.2.refs_0_), channel_id=1, source_target_pairs={{0,3},{1,2},{2,1},{3,0},{4,7},{5,6},{6,5},{7,4},{8,11},{9,10},{10,... | collective-permute-start | bytes 393224 | tf_op jit(solution)/shard_map/ppermute | solution.py:19
  74.8 0.7 broadcast_in_dim.10
  75.5 0.9 reshape.85.ids_ref
  76.4 0.9 reshape_reshape.3.ids_row_ref
  77.3 0.7 copy-done.8
  78.0 2.6 %shard_map.97 = (bf16[512,1792]{1,0:T(8,128)(2,1)S(1)}, f32[512,512]{1,0:T(8,128)S(1)}) custom-call(s32[1]{0:T(128)} %bitcast.flag_ref, bf16[128,1792]{1,0:T(8,128)(2,1)} %copy-done, bf16[128,1792]{1,0:T(8,128)(2,1)} %copy-done.3, bf16[128,1792]{1,0:T(8,128)(2,1)} %copy-done.4, bf16[128,1792]{1,0:T(8,128)(2,1)} %copy-done.5, bf16[128,1792]{1,0:T(8,128)(2,1)} %copy-done.6, ...), custom_call_target="tpu_custom_call" | custom-call | flops 939524096 | bytes 4718592 | tf_op jit(solution)/shard_map/pallas_call | solution.py:216
  80.7 1.4 %collective-permute-done.25.refs_3_ = bf16[128,512]{1,0:T(8,128)(2,1)S(1)} collective-permute-done((bf16[128,512]{1,0:T(8,128)(2,1)S(1)}, bf16[128,512]{1,0:T(8,128)(2,1)S(1)}, u32[]{:S(2)}, u32[]{:S(2)}) %collective-permute-start.25) | collective-permute-done | bytes 131104 | tf_op jit(solution)/shard_map/ppermute | solution.py:19
  82.1 1.6 %shard_map.98 = (bf16[512,2048]{1,0:T(8,128)(2,1)S(1)}, f32[8,128]{1,0:T(8,128)S(1)}) custom-call(s32[512,1]{1,0:T(8,128)S(1)} %reshape.85.ids_ref, s32[1,512]{1,0:T(1,128)S(1)} %reshape_reshape.3.ids_row_ref, f32[512,512]{1,0:T(8,128)S(1)} %get-tuple-element.63.gram_ref, bf16[128,512]{1,0:T(8,128)(2,1)S(1)} %pad_maximum_fusion.2.refs_0_, ...), custom_call_target="tpu_custom_call" | custom-call | flops 269484032 | bytes 2097152 | tf_op jit(solution)/shard_map/pallas_call | solution.py:274
  83.7 3.1 %collective-permute-start.27 = (f32[8,128]{1,0:T(8,128)S(1)}, f32[8,128]{1,0:T(8,128)S(1)}, u32[]{:S(2)}, u32[]{:S(2)}) collective-permute-start(f32[8,128]{1,0:T(8,128)S(1)} %get-tuple-element.66), channel_id=1, source_target_pairs={{0,2},{1,3},{2,0},{3,1},{4,6},{5,7},{6,4},{7,5},{8,10},{9,11},{10,... | collective-permute-start | bytes 12296 | tf_op jit(solution)/shard_map/ppermute | solution.py:19
  86.7 2.6 %collective-permute-start.28 = (f32[8,128]{1,0:T(8,128)S(1)}, f32[8,128]{1,0:T(8,128)S(1)}, u32[]{:S(2)}, u32[]{:S(2)}) collective-permute-start(f32[8,128]{1,0:T(8,128)S(1)} %get-tuple-element.66), channel_id=1, source_target_pairs={{0,3},{1,2},{2,1},{3,0},{4,7},{5,6},{6,5},{7,4},{8,11},{9,10},{10,... | collective-permute-start | bytes 12296 | tf_op jit(solution)/shard_map/ppermute | solution.py:19
  89.4 2.5 %shard_map.99.rest_0_ = bf16[4,1792,512]{2,1,0:T(8,128)(2,1)} custom-call(bf16[512,1792]{1,0:T(8,128)(2,1)S(1)} %get-tuple-element.62.hidden_ref, bf16[512,2048]{1,0:T(8,128)(2,1)S(1)} %get-tuple-element.69.masked_ref), custom_call_target="tpu_custom_call" | custom-call | flops 1073741824 | bytes 2621440 | tf_op jit(solution)/shard_map/pallas_call | solution.py:163
  92.2 0.8 collective-permute-done.26
  93.0 1.6 %collective-permute-start.30 = (f32[8,128]{1,0:T(8,128)S(1)}, f32[8,128]{1,0:T(8,128)S(1)}, u32[]{:S(2)}, u32[]{:S(2)}) collective-permute-start(f32[8,128]{1,0:T(8,128)S(1)} %add_add_fusion.1), channel_id=1, source_target_pairs={{0,8},{4,12},{8,0},{12,4},{1,9},{5,13},{9,1},{13,5},{2,10},{6,14},... | collective-permute-start | bytes 12296 | tf_op jit(solution)/shard_map/ppermute | solution.py:19
  94.6 1.9 %collective-permute-start.31 = (f32[8,128]{1,0:T(8,128)S(1)}, f32[8,128]{1,0:T(8,128)S(1)}, u32[]{:S(2)}, u32[]{:S(2)}) collective-permute-start(f32[8,128]{1,0:T(8,128)S(1)} %add_add_fusion.1), channel_id=1, source_target_pairs={{0,12},{4,8},{8,4},{12,0},{1,13},{5,9},{9,5},{13,1},{2,14},{6,10},... | collective-permute-start | bytes 12296 | tf_op jit(solution)/shard_map/ppermute | solution.py:19
  97.0 2.5 %shard_map.100.rest_0_ = bf16[4,1792,512]{2,1,0:T(8,128)(2,1)} custom-call(bf16[512,1792]{1,0:T(8,128)(2,1)S(1)} %get-tuple-element.62.hidden_ref, bf16[512,2048]{1,0:T(8,128)(2,1)S(1)} %get-tuple-element.69.masked_ref, bf16[4,1792,512]{2,1,0:T(8,128)(2,1)} %shard_map.99.rest_0_), custom_call_target="tpu_custom_call", output_to_operand_aliasing={{}: (2, {})} | custom-call | flops 1073741824 | bytes 2621440 | tf_op jit(solution)/shard_map/pallas_call | solution.py:163
  100.1 3.5 %shard_map.101 = bf16[4,1792,512]{2,1,0:T(8,128)(2,1)} custom-call(bf16[512,1792]{1,0:T(8,128)(2,1)S(1)} %get-tuple-element.62.hidden_ref, bf16[512,2048]{1,0:T(8,128)(2,1)S(1)} %get-tuple-element.69.masked_ref, bf16[4,1792,512]{2,1,0:T(8,128)(2,1)} %shard_map.100.rest_0_), custom_call_target="tpu_custom_call", output_to_operand_aliasing={{}: (2, {})} | custom-call | flops 1610612736 | bytes 3932160 | tf_op jit(solution)/shard_map/pallas_call | solution.py:163
  (88 shorter events, 7.9 us)
Async XLA Ops:
  1.6 16.4 %copy-start.9 = (f32[1,2048]{1,0:T(1,128)S(1)}, f32[1,2048]{1,0:T(1,128)}, u32[]{:S(2)}) copy-start(f32[1,2048]{1,0:T(1,128)} %param.11) | copy-start | bytes 24580
  1.6 13.2 %collective-permute-start.2 = (bf16[32,2048]{1,0:T(8,128)(2,1)S(1)}, bf16[32,2048]{1,0:T(8,128)(2,1)S(1)}, u32[]{:S(2)}, u32[]{:S(2)}) collective-permute-start(bf16[32,2048]{1,0:T(8,128)(2,1)S(1)} %bitcast_select_fusion.1), channel_id=1, source_target_pairs={{0,3},{1,2},{2,1},{3,0},{4,7},{5,6},{6,5},{7,4},{8,11},{9,10},{10,... | collective-permute-start | bytes 393224 | tf_op jit(solution)/shard_map/ppermute | solution.py:19
  6.8 11.1 %collective-permute-start.1 = (bf16[32,2048]{1,0:T(8,128)(2,1)S(1)}, bf16[32,2048]{1,0:T(8,128)(2,1)S(1)}, u32[]{:S(2)}, u32[]{:S(2)}) collective-permute-start(bf16[32,2048]{1,0:T(8,128)(2,1)S(1)} %bitcast_select_fusion.1), channel_id=1, source_target_pairs={{0,2},{1,3},{2,0},{3,1},{4,6},{5,7},{6,4},{7,5},{8,10},{9,11},{10,... | collective-permute-start | bytes 393224 | tf_op jit(solution)/shard_map/ppermute | solution.py:19
  6.8 11.1 %collective-permute-start = (bf16[32,2048]{1,0:T(8,128)(2,1)S(1)}, bf16[32,2048]{1,0:T(8,128)(2,1)S(1)}, u32[]{:S(2)}, u32[]{:S(2)}) collective-permute-start(bf16[32,2048]{1,0:T(8,128)(2,1)S(1)} %bitcast_select_fusion.1), channel_id=1, source_target_pairs={{0,1},{1,0},{2,3},{3,2},{4,5},{5,4},{6,7},{7,6},{8,9},{9,8},{10,11... | collective-permute-start | bytes 393224 | tf_op jit(solution)/shard_map/ppermute | solution.py:19
  20.6 18.5 %copy-start = (bf16[128,1792]{1,0:T(8,128)(2,1)}, bf16[128,1792]{1,0:T(8,128)(2,1)S(1)}, u32[]{:S(2)}) copy-start(bf16[128,1792]{1,0:T(8,128)(2,1)S(1)} %fusion.1.refs_0_) | copy-start | bytes 1376260
  21.7 8.4 %copy-start.2 = (bf16[4,8,2048]{2,1,0:T(8,128)(2,1)S(1)}, bf16[4,8,2048]{2,1,0:T(8,128)(2,1)}, u32[]{:S(2)}) copy-start(bf16[4,8,2048]{2,1,0:T(8,128)(2,1)} %param.8) | copy-start | bytes 393220
  21.8 7.0 %collective-permute-start.6 = (bf16[32,2048]{1,0:T(8,128)(2,1)S(1)}, bf16[32,2048]{1,0:T(8,128)(2,1)S(1)}, u32[]{:S(2)}, u32[]{:S(2)}) collective-permute-start(bf16[32,2048]{1,0:T(8,128)(2,1)S(1)} %get-tuple-element.82), channel_id=1, source_target_pairs={{0,19},{1,18},{2,17},{3,16},{4,23},{5,22},{6,21},{7,20},{8,27},{9,... | collective-permute-start | bytes 393224 | tf_op jit(solution)/shard_map/ppermute | solution.py:33
  24.8 4.0 %collective-permute-start.5 = (bf16[32,2048]{1,0:T(8,128)(2,1)S(1)}, bf16[32,2048]{1,0:T(8,128)(2,1)S(1)}, u32[]{:S(2)}, u32[]{:S(2)}) collective-permute-start(bf16[32,2048]{1,0:T(8,128)(2,1)S(1)} %get-tuple-element.83), channel_id=1, source_target_pairs={{0,18},{1,19},{2,16},{3,17},{4,22},{5,23},{6,20},{7,21},{8,26},{9,... | collective-permute-start | bytes 393224 | tf_op jit(solution)/shard_map/ppermute | solution.py:33
  26.1 4.0 %collective-permute-start.4 = (bf16[32,2048]{1,0:T(8,128)(2,1)S(1)}, bf16[32,2048]{1,0:T(8,128)(2,1)S(1)}, u32[]{:S(2)}, u32[]{:S(2)}) collective-permute-start(bf16[32,2048]{1,0:T(8,128)(2,1)S(1)} %get-tuple-element.84), channel_id=1, source_target_pairs={{0,17},{1,16},{2,19},{3,18},{4,21},{5,20},{6,23},{7,22},{8,25},{9,... | collective-permute-start | bytes 393224 | tf_op jit(solution)/shard_map/ppermute | solution.py:33
  27.4 2.7 %collective-permute-start.3 = (bf16[32,2048]{1,0:T(8,128)(2,1)S(1)}, bf16[32,2048]{1,0:T(8,128)(2,1)S(1)}, u32[]{:S(2)}, u32[]{:S(2)}) collective-permute-start(bf16[32,2048]{1,0:T(8,128)(2,1)S(1)} %get-tuple-element.81), channel_id=1, source_target_pairs={{0,16},{1,17},{2,18},{3,19},{4,20},{5,21},{6,22},{7,23},{8,24},{9,... | collective-permute-start | bytes 393224 | tf_op jit(solution)/shard_map/ppermute | solution.py:33
  30.2 8.9 %collective-permute-start.9 = (bf16[32,2048]{1,0:T(8,128)(2,1)S(1)}, bf16[32,2048]{1,0:T(8,128)(2,1)S(1)}, u32[]{:S(2)}, u32[]{:S(2)}) collective-permute-start(bf16[32,2048]{1,0:T(8,128)(2,1)S(1)} %add_convert_fusion.1), channel_id=1, source_target_pairs={{16,19},{17,18},{18,17},{19,16},{20,23},{21,22},{22,21},{23,20},{2... | collective-permute-start | bytes 393224 | tf_op jit(solution)/shard_map/ppermute | solution.py:25
  30.9 10.8 %collective-permute-start.8 = (bf16[32,2048]{1,0:T(8,128)(2,1)S(1)}, bf16[32,2048]{1,0:T(8,128)(2,1)S(1)}, u32[]{:S(2)}, u32[]{:S(2)}) collective-permute-start(bf16[32,2048]{1,0:T(8,128)(2,1)S(1)} %add_convert_fusion.1), channel_id=1, source_target_pairs={{16,18},{17,19},{18,16},{19,17},{20,22},{21,23},{22,20},{23,21},{2... | collective-permute-start | bytes 393224 | tf_op jit(solution)/shard_map/ppermute | solution.py:25
  31.6 10.1 %collective-permute-start.7 = (bf16[32,2048]{1,0:T(8,128)(2,1)S(1)}, bf16[32,2048]{1,0:T(8,128)(2,1)S(1)}, u32[]{:S(2)}, u32[]{:S(2)}) collective-permute-start(bf16[32,2048]{1,0:T(8,128)(2,1)S(1)} %add_convert_fusion.1), channel_id=1, source_target_pairs={{16,17},{17,16},{18,19},{19,18},{20,21},{21,20},{22,23},{23,22},{2... | collective-permute-start | bytes 393224 | tf_op jit(solution)/shard_map/ppermute | solution.py:25
  32.2 16.4 %collective-permute-start.10 = (bf16[128,1792]{1,0:T(8,128)(2,1)S(1)}, bf16[128,1792]{1,0:T(8,128)(2,1)S(1)}, u32[]{:S(2)}, u32[]{:S(2)}) collective-permute-start(bf16[128,1792]{1,0:T(8,128)(2,1)S(1)} %fusion.1.refs_0_), channel_id=1, source_target_pairs={{0,4},{4,0},{8,12},{12,8},{1,5},{5,1},{9,13},{13,9},{2,6},{6,2},{1... | collective-permute-start | bytes 1376264 | tf_op jit(solution)/shard_map/ppermute | solution.py:25
  35.6 15.3 %collective-permute-start.11 = (bf16[128,1792]{1,0:T(8,128)(2,1)S(1)}, bf16[128,1792]{1,0:T(8,128)(2,1)S(1)}, u32[]{:S(2)}, u32[]{:S(2)}) collective-permute-start(bf16[128,1792]{1,0:T(8,128)(2,1)S(1)} %fusion.1.refs_0_), channel_id=1, source_target_pairs={{0,8},{4,12},{8,0},{12,4},{1,9},{5,13},{9,1},{13,5},{2,10},{6,14},... | collective-permute-start | bytes 1376264 | tf_op jit(solution)/shard_map/ppermute | solution.py:25
  39.1 11.8 %collective-permute-start.12 = (bf16[128,1792]{1,0:T(8,128)(2,1)S(1)}, bf16[128,1792]{1,0:T(8,128)(2,1)S(1)}, u32[]{:S(2)}, u32[]{:S(2)}) collective-permute-start(bf16[128,1792]{1,0:T(8,128)(2,1)S(1)} %fusion.1.refs_0_), channel_id=1, source_target_pairs={{0,12},{4,8},{8,4},{12,0},{1,13},{5,9},{9,5},{13,1},{2,14},{6,10},... | collective-permute-start | bytes 1376264 | tf_op jit(solution)/shard_map/ppermute | solution.py:25
  44.6 23.6 %copy-start.6 = (bf16[128,1792]{1,0:T(8,128)(2,1)}, bf16[128,1792]{1,0:T(8,128)(2,1)S(1)}, u32[]{:S(2)}) copy-start(bf16[128,1792]{1,0:T(8,128)(2,1)S(1)} %get-tuple-element.61.refs_4_) | copy-start | bytes 1376260
  45.7 10.4 %copy-start.11 = (s32[4,1]{0,1:T(1,128)S(1)}, s32[4,1]{0,1:T(1,128)}, u32[]{:S(2)}) copy-start(s32[4,1]{0,1:T(1,128)} %param.10) | copy-start | bytes 52
  45.8 16.6 %copy-start.1 = (bf16[4,8,2048]{2,1,0:T(8,128)(2,1)S(1)}, bf16[4,8,2048]{2,1,0:T(8,128)(2,1)}, u32[]{:S(2)}) copy-start(bf16[4,8,2048]{2,1,0:T(8,128)(2,1)} %param.9) | copy-start | bytes 393220
  48.6 28.7 %copy-start.3 = (bf16[128,1792]{1,0:T(8,128)(2,1)}, bf16[128,1792]{1,0:T(8,128)(2,1)S(1)}, u32[]{:S(2)}) copy-start(bf16[128,1792]{1,0:T(8,128)(2,1)S(1)} %collective-permute-done.10.refs_1_) | copy-start | bytes 1376260
  50.9 26.4 %copy-start.4 = (bf16[128,1792]{1,0:T(8,128)(2,1)}, bf16[128,1792]{1,0:T(8,128)(2,1)S(1)}, u32[]{:S(2)}) copy-start(bf16[128,1792]{1,0:T(8,128)(2,1)S(1)} %collective-permute-done.11.refs_2_) | copy-start | bytes 1376260
  50.9 26.4 %copy-start.5 = (bf16[128,1792]{1,0:T(8,128)(2,1)}, bf16[128,1792]{1,0:T(8,128)(2,1)S(1)}, u32[]{:S(2)}) copy-start(bf16[128,1792]{1,0:T(8,128)(2,1)S(1)} %collective-permute-done.12.refs_3_) | copy-start | bytes 1376260
  51.0 8.3 %collective-permute-start.16 = (bf16[32,2048]{1,0:T(8,128)(2,1)S(1)}, bf16[32,2048]{1,0:T(8,128)(2,1)S(1)}, u32[]{:S(2)}, u32[]{:S(2)}) collective-permute-start(bf16[32,2048]{1,0:T(8,128)(2,1)S(1)} %get-tuple-element.78), channel_id=1, source_target_pairs={{16,3},{17,2},{18,1},{19,0},{20,7},{21,6},{22,5},{23,4},{24,11},{2... | collective-permute-start | bytes 393224 | tf_op jit(solution)/shard_map/ppermute | solution.py:33
  52.3 10.1 %collective-permute-start.15 = (bf16[32,2048]{1,0:T(8,128)(2,1)S(1)}, bf16[32,2048]{1,0:T(8,128)(2,1)S(1)}, u32[]{:S(2)}, u32[]{:S(2)}) collective-permute-start(bf16[32,2048]{1,0:T(8,128)(2,1)S(1)} %get-tuple-element.79), channel_id=1, source_target_pairs={{16,2},{17,3},{18,0},{19,1},{20,6},{21,7},{22,4},{23,5},{24,10},{2... | collective-permute-start | bytes 393224 | tf_op jit(solution)/shard_map/ppermute | solution.py:33
  53.6 8.8 %collective-permute-start.14 = (bf16[32,2048]{1,0:T(8,128)(2,1)S(1)}, bf16[32,2048]{1,0:T(8,128)(2,1)S(1)}, u32[]{:S(2)}, u32[]{:S(2)}) collective-permute-start(bf16[32,2048]{1,0:T(8,128)(2,1)S(1)} %get-tuple-element.80), channel_id=1, source_target_pairs={{16,1},{17,0},{18,3},{19,2},{20,5},{21,4},{22,7},{23,6},{24,9},{25... | collective-permute-start | bytes 393224 | tf_op jit(solution)/shard_map/ppermute | solution.py:33
  54.9 4.4 %collective-permute-start.13 = (bf16[32,2048]{1,0:T(8,128)(2,1)S(1)}, bf16[32,2048]{1,0:T(8,128)(2,1)S(1)}, u32[]{:S(2)}, u32[]{:S(2)}) collective-permute-start(bf16[32,2048]{1,0:T(8,128)(2,1)S(1)} %get-tuple-element.77), channel_id=1, source_target_pairs={{16,0},{17,1},{18,2},{19,3},{20,4},{21,5},{22,6},{23,7},{24,8},{25... | collective-permute-start | bytes 393224 | tf_op jit(solution)/shard_map/ppermute | solution.py:33
  62.6 5.6 %collective-permute-start.19 = (bf16[48,512]{1,0:T(8,128)(2,1)S(1)}, bf16[48,512]{1,0:T(8,128)(2,1)S(1)}, u32[]{:S(2)}, u32[]{:S(2)}) collective-permute-start(bf16[48,512]{1,0:T(8,128)(2,1)S(1)} %get-tuple-element.93), channel_id=1, source_target_pairs={{0,12},{4,8},{8,4},{12,0},{1,13},{5,9},{9,5},{13,1},{2,14},{6,10},... | collective-permute-start | bytes 147464 | tf_op jit(solution)/shard_map/ppermute | solution.py:19
  64.1 6.2 %collective-permute-start.20 = (bf16[128,1792]{1,0:T(8,128)(2,1)S(1)}, bf16[128,1792]{1,0:T(8,128)(2,1)S(1)}, u32[]{:S(2)}, u32[]{:S(2)}) collective-permute-start(bf16[128,1792]{1,0:T(8,128)(2,1)S(1)} %get-tuple-element.61.refs_4_), channel_id=1, source_target_pairs={{16,20},{20,16},{24,28},{28,24},{17,21},{21,17},{25,29},{29,25},{1... | collective-permute-start | bytes 1376264 | tf_op jit(solution)/shard_map/ppermute | solution.py:25
  64.8 5.0 %collective-permute-start.18 = (bf16[48,512]{1,0:T(8,128)(2,1)S(1)}, bf16[48,512]{1,0:T(8,128)(2,1)S(1)}, u32[]{:S(2)}, u32[]{:S(2)}) collective-permute-start(bf16[48,512]{1,0:T(8,128)(2,1)S(1)} %get-tuple-element.92), channel_id=1, source_target_pairs={{0,8},{4,12},{8,0},{12,4},{1,9},{5,13},{9,1},{13,5},{2,10},{6,14},... | collective-permute-start | bytes 147464 | tf_op jit(solution)/shard_map/ppermute | solution.py:19
  65.4 4.7 %collective-permute-start.17 = (bf16[48,512]{1,0:T(8,128)(2,1)S(1)}, bf16[48,512]{1,0:T(8,128)(2,1)S(1)}, u32[]{:S(2)}, u32[]{:S(2)}) collective-permute-start(bf16[48,512]{1,0:T(8,128)(2,1)S(1)} %get-tuple-element.91), channel_id=1, source_target_pairs={{0,4},{4,0},{8,12},{12,8},{1,5},{5,1},{9,13},{13,9},{2,6},{6,2},{1... | collective-permute-start | bytes 147464 | tf_op jit(solution)/shard_map/ppermute | solution.py:19
  66.9 10.4 %collective-permute-start.21 = (bf16[128,1792]{1,0:T(8,128)(2,1)S(1)}, bf16[128,1792]{1,0:T(8,128)(2,1)S(1)}, u32[]{:S(2)}, u32[]{:S(2)}) collective-permute-start(bf16[128,1792]{1,0:T(8,128)(2,1)S(1)} %get-tuple-element.61.refs_4_), channel_id=1, source_target_pairs={{16,24},{20,28},{24,16},{28,20},{17,25},{21,29},{25,17},{29,21},{1... | collective-permute-start | bytes 1376264 | tf_op jit(solution)/shard_map/ppermute | solution.py:25
  68.2 9.0 %collective-permute-start.22 = (bf16[128,1792]{1,0:T(8,128)(2,1)S(1)}, bf16[128,1792]{1,0:T(8,128)(2,1)}, u32[]{:S(2)}, u32[]{:S(2)}) collective-permute-start(bf16[128,1792]{1,0:T(8,128)(2,1)S(1)} %get-tuple-element.61.refs_4_), channel_id=1, source_target_pairs={{16,28},{20,24},{24,20},{28,16},{17,29},{21,25},{25,21},{29,17},{1... | collective-permute-start | bytes 1376264 | tf_op jit(solution)/shard_map/ppermute | solution.py:25
  70.3 7.0 %copy-start.7 = (bf16[128,1792]{1,0:T(8,128)(2,1)}, bf16[128,1792]{1,0:T(8,128)(2,1)S(1)}, u32[]{:S(2)}) copy-start(bf16[128,1792]{1,0:T(8,128)(2,1)S(1)} %collective-permute-done.20.refs_5_) | copy-start | bytes 1376260
  70.3 10.3 %collective-permute-start.23 = (bf16[128,512]{1,0:T(8,128)(2,1)S(1)}, bf16[128,512]{1,0:T(8,128)(2,1)S(1)}, u32[]{:S(2)}, u32[]{:S(2)}) collective-permute-start(bf16[128,512]{1,0:T(8,128)(2,1)S(1)} %pad_maximum_fusion.2.refs_0_), channel_id=1, source_target_pairs={{0,1},{1,0},{2,3},{3,2},{4,5},{5,4},{6,7},{7,6},{8,9},{9,8},{10,11... | collective-permute-start | bytes 393224 | tf_op jit(solution)/shard_map/ppermute | solution.py:19
  70.4 10.3 %collective-permute-start.24 = (bf16[128,512]{1,0:T(8,128)(2,1)S(1)}, bf16[128,512]{1,0:T(8,128)(2,1)S(1)}, u32[]{:S(2)}, u32[]{:S(2)}) collective-permute-start(bf16[128,512]{1,0:T(8,128)(2,1)S(1)} %pad_maximum_fusion.2.refs_0_), channel_id=1, source_target_pairs={{0,2},{1,3},{2,0},{3,1},{4,6},{5,7},{6,4},{7,5},{8,10},{9,11},{10,... | collective-permute-start | bytes 393224 | tf_op jit(solution)/shard_map/ppermute | solution.py:19
  72.5 9.5 %collective-permute-start.25 = (bf16[128,512]{1,0:T(8,128)(2,1)S(1)}, bf16[128,512]{1,0:T(8,128)(2,1)S(1)}, u32[]{:S(2)}, u32[]{:S(2)}) collective-permute-start(bf16[128,512]{1,0:T(8,128)(2,1)S(1)} %pad_maximum_fusion.2.refs_0_), channel_id=1, source_target_pairs={{0,3},{1,2},{2,1},{3,0},{4,7},{5,6},{6,5},{7,4},{8,11},{9,10},{10,... | collective-permute-start | bytes 393224 | tf_op jit(solution)/shard_map/ppermute | solution.py:19
  77.3 0.8 copy-start.8
  83.7 8.2 %collective-permute-start.27 = (f32[8,128]{1,0:T(8,128)S(1)}, f32[8,128]{1,0:T(8,128)S(1)}, u32[]{:S(2)}, u32[]{:S(2)}) collective-permute-start(f32[8,128]{1,0:T(8,128)S(1)} %get-tuple-element.66), channel_id=1, source_target_pairs={{0,2},{1,3},{2,0},{3,1},{4,6},{5,7},{6,4},{7,5},{8,10},{9,11},{10,... | collective-permute-start | bytes 12296 | tf_op jit(solution)/shard_map/ppermute | solution.py:19
  86.7 5.4 %collective-permute-start.28 = (f32[8,128]{1,0:T(8,128)S(1)}, f32[8,128]{1,0:T(8,128)S(1)}, u32[]{:S(2)}, u32[]{:S(2)}) collective-permute-start(f32[8,128]{1,0:T(8,128)S(1)} %get-tuple-element.66), channel_id=1, source_target_pairs={{0,3},{1,2},{2,1},{3,0},{4,7},{5,6},{6,5},{7,4},{8,11},{9,10},{10,... | collective-permute-start | bytes 12296 | tf_op jit(solution)/shard_map/ppermute | solution.py:19
  89.4 3.6 %collective-permute-start.26 = (f32[8,128]{1,0:T(8,128)S(1)}, f32[8,128]{1,0:T(8,128)S(1)}, u32[]{:S(2)}, u32[]{:S(2)}) collective-permute-start(f32[8,128]{1,0:T(8,128)S(1)} %get-tuple-element.66), channel_id=1, source_target_pairs={{0,1},{1,0},{2,3},{3,2},{4,5},{5,4},{6,7},{7,6},{8,9},{9,8},{10,11... | collective-permute-start | bytes 12296 | tf_op jit(solution)/shard_map/ppermute | solution.py:19
  93.0 6.5 %collective-permute-start.30 = (f32[8,128]{1,0:T(8,128)S(1)}, f32[8,128]{1,0:T(8,128)S(1)}, u32[]{:S(2)}, u32[]{:S(2)}) collective-permute-start(f32[8,128]{1,0:T(8,128)S(1)} %add_add_fusion.1), channel_id=1, source_target_pairs={{0,8},{4,12},{8,0},{12,4},{1,9},{5,13},{9,1},{13,5},{2,10},{6,14},... | collective-permute-start | bytes 12296 | tf_op jit(solution)/shard_map/ppermute | solution.py:19
  94.6 4.9 %collective-permute-start.31 = (f32[8,128]{1,0:T(8,128)S(1)}, f32[8,128]{1,0:T(8,128)S(1)}, u32[]{:S(2)}, u32[]{:S(2)}) collective-permute-start(f32[8,128]{1,0:T(8,128)S(1)} %add_add_fusion.1), channel_id=1, source_target_pairs={{0,12},{4,8},{8,4},{12,0},{1,13},{5,9},{9,5},{13,1},{2,14},{6,10},... | collective-permute-start | bytes 12296 | tf_op jit(solution)/shard_map/ppermute | solution.py:19
  96.5 3.6 %collective-permute-start.29 = (f32[8,128]{1,0:T(8,128)S(1)}, f32[8,128]{1,0:T(8,128)S(1)}, u32[]{:S(2)}, u32[]{:S(2)}) collective-permute-start(f32[8,128]{1,0:T(8,128)S(1)} %add_add_fusion.1), channel_id=1, source_target_pairs={{0,4},{4,0},{8,12},{12,8},{1,5},{5,1},{9,13},{13,9},{2,6},{6,2},{1... | collective-permute-start | bytes 12296 | tf_op jit(solution)/shard_map/ppermute | solution.py:19
  100.1 3.5 %copy-start.10 = (f32[3]{0:T(128)S(1)}, f32[3]{0:T(128)}, u32[]{:S(2)}) copy-start(f32[3]{0:T(128)} %constant.50) | copy-start | bytes 40
  100.1 3.5 %collective-permute-start.32 = (f32[8,128]{1,0:T(8,128)S(1)}, f32[8,128]{1,0:T(8,128)S(1)}, u32[]{:S(2)}, u32[]{:S(2)}) collective-permute-start(f32[8,128]{1,0:T(8,128)S(1)} %add_add_fusion), channel_id=1, source_target_pairs={{0,16},{16,0},{1,17},{17,1},{2,18},{18,2},{3,19},{19,3},{4,20},{20... | collective-permute-start | bytes 12296 | tf_op jit(solution)/shard_map/ppermute | solution.py:19

commit v8 on v7

--- a/solution.py
+++ b/solution.py
@@ -236,6 +236,7 @@
 
 def norms_kernel(replicas, levels, ids_ref, ids_row_ref, gram_ref, *refs):
     *parts, masked_ref, norms_ref, y_ref, acc = refs
+    parts.reverse()
     piece = y_ref.shape[1]
     block = parts[0].shape[0] // replicas
     tok_rows = block * len(parts)
@@ -291,7 +292,7 @@
             bytes_accessed=4 * total * piece + 4 * total * total,
             transcendentals=0,
         ),
-    )(row_ids, row_ids.reshape(1, total), gram_hidden, *parts)
+    )(row_ids, row_ids.reshape(1, total), gram_hidden, *reversed(parts))
 
 
 def shards(layer_input_activations, cotangent, domain_ids, norm_gain, w_gate, w_up, w_down):
@@ -382,9 +383,10 @@
             end = tiles * (part + 1) // parts
             grads = domain_gradients(hidden_all, masked, begin, end - begin, grads)
             begin = end
-        norms = norms + others[0]
         if count == 2:
-            norms = norms + (others[1] + others[2])
+            norms = (others[2] + others[1]) + (others[0] + norms)
+        else:
+            norms = norms + others[0]
         masked, norms = lax.optimization_barrier((masked, norms))
     entries = segments * units * tensor_size * width
     counts = [float((dp_size >> level) * entries) for level in range(levels)]

time: 105 us -> 104 us (level)
  starting transfers between devices: 49.7 us -> 47.1 us
  waiting for transfers between devices: 16.6 us -> 18.3 us
    ppermute x16, starting transfers between devices: 23.5 us -> 20.9 us  [swap(): return lax.ppermute(block, axis, [(i, i ^ offset) for i in range(size)])]
    ppermute x16, waiting for transfers between devices: 6.96 us -> 8.61 us  [swap(): return lax.ppermute(block, axis, [(i, i ^ offset) for i in range(size)])]
  transfers between devices with their start and end apart: 33 -> 33, of which waited for: 11 -> 10; matrix products, arithmetic and copies ran while one was open for 9% -> 9% of each run, Pallas kernels for 18% -> 18%
where the time goes in v8:
time: 104 us; the launch traced here: 103 us
  starting transfers between devices  47.1 us (45%)
  Pallas kernels  20.3 us (20%)
  waiting for transfers between devices  18.3 us (18%)
  matrix products  10.1 us (10%)
  local copies, waits for them, and re-layouts  3.74 us (4%)
  other arithmetic  2.53 us (2%)
  between operations  1.22 us (1%)
    ppermute x16, starting transfers between devices, swap(): return lax.ppermute(block, axis, [(i, i ^ offset) for i in range(size)])  20.9 us
    ppermute x9, starting transfers between devices, swap_in(): return lax.ppermute(block, ('section', axis), route)  14.2 us
    ppermute x8, starting transfers between devices, across(): return lax.ppermute(block, ('section', 'tensor'), route)  12 us
    ppermute x16, waiting for transfers between devices, swap(): return lax.ppermute(block, axis, [(i, i ^ offset) for i in range(size)])  8.61 us
    pallas_call x3, Pallas kernels, domain_gradients(): pl.pallas_call(gradient_kernel, grid=(count,), in_specs=in_specs, out_spe...  8.5 us
    pallas_call x1, Pallas kernels, load_weights(): pl.pallas_call(load_kernel, in_specs=[pl.BlockSpec(memory_space=pltpu.HBM...  7.46 us
    ppermute x8, waiting for transfers between devices, across(): return lax.ppermute(block, ('section', 'tensor'), route)  7.34 us
    dot_general x2, matrix products, layer_parts(): up = jnp.dot(normed, up_w, preferred_element_type=jnp.float32)  2.88 us
  transfers between devices with their start and end apart: 33, of which 10 were waited for; matrix products, arithmetic and copies ran while one was open for 9% of the time, Pallas kernels for 18%

profile of v8, /device:TPU:0, one launch (start us, length us, event | category | flops | bytes accessed | tf_op | source)
XLA Modules:
  0.0 103.2 jit_solution(1730858286756984446)
XLA Ops:
  0.6 1.0 bitcast_select_fusion.1
  1.6 5.1 %collective-permute-start.2 = (bf16[32,2048]{1,0:T(8,128)(2,1)S(1)}, bf16[32,2048]{1,0:T(8,128)(2,1)S(1)}, u32[]{:S(2)}, u32[]{:S(2)}) collective-permute-start(bf16[32,2048]{1,0:T(8,128)(2,1)S(1)} %bitcast_select_fusion.1), channel_id=1, source_target_pairs={{0,3},{1,2},{2,1},{3,0},{4,7},{5,6},{6,5},{7,4},{8,11},{9,10},{10,... | collective-permute-start | bytes 393224 | tf_op jit(solution)/shard_map/ppermute | solution.py:19
  7.4 7.5 %shard_map.95 = (bf16[2048,1792]{1,0:T(8,128)(2,1)S(1)}, bf16[2048,1792]{1,0:T(8,128)(2,1)S(1)}, bf16[1792,2048]{1,0:T(8,128)(2,1)S(1)}, bf16[1792,2048]{1,0:T(8,128)(2,1)S(1)}) custom-call(bf16[1,2048,1792]{2,1,0:T(8,128)(2,1)} %gate_in.1, bf16[1,2048,1792]{2,1,0:T(8,128)(2,1)} %up_in.1, bf16[1,1792,2048]{2,1,0:T(8,128)(2,1)} %down_in.1), custom_call_target="tpu_custom_call" | custom-call | bytes 22020096 | tf_op jit(solution)/shard_map/pallas_call | solution.py:93
  14.9 3.0 %collective-permute-done.1 = bf16[32,2048]{1,0:T(8,128)(2,1)S(1)} collective-permute-done((bf16[32,2048]{1,0:T(8,128)(2,1)S(1)}, bf16[32,2048]{1,0:T(8,128)(2,1)S(1)}, u32[]{:S(2)}, u32[]{:S(2)}) %collective-permute-start.1) | collective-permute-done | bytes 131104 | tf_op jit(solution)/shard_map/ppermute | solution.py:19
  18.0 1.2 %fusion.16 = f32[128,1792]{1,0:T(8,128)S(1)} fusion(bf16[2048,1792]{1,0:T(8,128)(2,1)S(1)} %get-tuple-element.37, bf16[128,2048]{1,0:T(8,128)(2,1)S(1)} %get-tuple-element.43.rows_ref, f32[2048]{0:T(1024)S(1)} %bitcast.28, f32[128]{0:T(128)S(1)} %add_rsqrt_fusion.1), kind=kOutput, calls=%fused_computation.30 | convolution fusion | flops 940572672 | bytes 8790528 | tf_op jit(solution)/shard_map/dot_general | solution.py:321
  19.2 1.4 %fusion.1.refs_0_ = bf16[128,1792]{1,0:T(8,128)(2,1)S(1)} fusion(bf16[2048,1792]{1,0:T(8,128)(2,1)S(1)} %get-tuple-element.38, f32[128,1792]{1,0:T(8,128)S(1)} %fusion.16, bf16[128,2048]{1,0:T(8,128)(2,1)S(1)} %get-tuple-element.43.rows_ref, f32[2048]{0:T(1024)S(1)} %bitcast.29, f32[128]{0:T(128)S(1)} %add_rsqrt_fusion.1), kind=kOutput, calls=%fused_computation.3 | convolution fusion | flops 941948928 | bytes 9249280 | tf_op jit(solution)/shard_map/dot_general | solution.py:322
  20.6 1.1 %convolution_convert_fusion = bf16[128,2048]{1,0:T(8,128)(2,1)S(1)} fusion(bf16[128,1792]{1,0:T(8,128)(2,1)S(1)} %fusion.1.refs_0_, bf16[1792,2048]{1,0:T(8,128)(2,1)S(1)} %get-tuple-element.39.down_ref), kind=kOutput, calls=%fused_computation.4 | convolution fusion | flops 939786240 | bytes 8323072 | tf_op jit(solution)/shard_map/dot_general | solution.py:327
  21.8 3.0 %collective-permute-start.6 = (bf16[32,2048]{1,0:T(8,128)(2,1)S(1)}, bf16[32,2048]{1,0:T(8,128)(2,1)S(1)}, u32[]{:S(2)}, u32[]{:S(2)}) collective-permute-start(bf16[32,2048]{1,0:T(8,128)(2,1)S(1)} %get-tuple-element.82), channel_id=1, source_target_pairs={{0,19},{1,18},{2,17},{3,16},{4,23},{5,22},{6,21},{7,20},{8,27},{9,... | collective-permute-start | bytes 393224 | tf_op jit(solution)/shard_map/ppermute | solution.py:33
  24.8 1.3 %collective-permute-start.5 = (bf16[32,2048]{1,0:T(8,128)(2,1)S(1)}, bf16[32,2048]{1,0:T(8,128)(2,1)S(1)}, u32[]{:S(2)}, u32[]{:S(2)}) collective-permute-start(bf16[32,2048]{1,0:T(8,128)(2,1)S(1)} %get-tuple-element.83), channel_id=1, source_target_pairs={{0,18},{1,19},{2,16},{3,17},{4,22},{5,23},{6,20},{7,21},{8,26},{9,... | collective-permute-start | bytes 393224 | tf_op jit(solution)/shard_map/ppermute | solution.py:33
  26.1 1.3 %collective-permute-start.4 = (bf16[32,2048]{1,0:T(8,128)(2,1)S(1)}, bf16[32,2048]{1,0:T(8,128)(2,1)S(1)}, u32[]{:S(2)}, u32[]{:S(2)}) collective-permute-start(bf16[32,2048]{1,0:T(8,128)(2,1)S(1)} %get-tuple-element.84), channel_id=1, source_target_pairs={{0,17},{1,16},{2,19},{3,18},{4,21},{5,20},{6,23},{7,22},{8,25},{9,... | collective-permute-start | bytes 393224 | tf_op jit(solution)/shard_map/ppermute | solution.py:33
  27.4 1.3 %collective-permute-start.3 = (bf16[32,2048]{1,0:T(8,128)(2,1)S(1)}, bf16[32,2048]{1,0:T(8,128)(2,1)S(1)}, u32[]{:S(2)}, u32[]{:S(2)}) collective-permute-start(bf16[32,2048]{1,0:T(8,128)(2,1)S(1)} %get-tuple-element.81), channel_id=1, source_target_pairs={{0,16},{1,17},{2,18},{3,19},{4,20},{5,21},{6,22},{7,23},{8,24},{9,... | collective-permute-start | bytes 393224 | tf_op jit(solution)/shard_map/ppermute | solution.py:33
  28.8 1.3 %collective-permute-done.4 = bf16[32,2048]{1,0:T(8,128)(2,1)S(1)} collective-permute-done((bf16[32,2048]{1,0:T(8,128)(2,1)S(1)}, bf16[32,2048]{1,0:T(8,128)(2,1)S(1)}, u32[]{:S(2)}, u32[]{:S(2)}) %collective-permute-start.4) | collective-permute-done | bytes 131104 | tf_op jit(solution)/shard_map/ppermute | solution.py:33
  32.2 3.4 %collective-permute-start.10 = (bf16[128,1792]{1,0:T(8,128)(2,1)S(1)}, bf16[128,1792]{1,0:T(8,128)(2,1)S(1)}, u32[]{:S(2)}, u32[]{:S(2)}) collective-permute-start(bf16[128,1792]{1,0:T(8,128)(2,1)S(1)} %fusion.1.refs_0_), channel_id=1, source_target_pairs={{0,4},{4,0},{8,12},{12,8},{1,5},{5,1},{9,13},{13,9},{2,6},{6,2},{1... | collective-permute-start | bytes 1376264 | tf_op jit(solution)/shard_map/ppermute | solution.py:25
  35.6 3.4 %collective-permute-start.11 = (bf16[128,1792]{1,0:T(8,128)(2,1)S(1)}, bf16[128,1792]{1,0:T(8,128)(2,1)S(1)}, u32[]{:S(2)}, u32[]{:S(2)}) collective-permute-start(bf16[128,1792]{1,0:T(8,128)(2,1)S(1)} %fusion.1.refs_0_), channel_id=1, source_target_pairs={{0,8},{4,12},{8,0},{12,4},{1,9},{5,13},{9,1},{13,5},{2,10},{6,14},... | collective-permute-start | bytes 1376264 | tf_op jit(solution)/shard_map/ppermute | solution.py:25
  39.1 2.6 %collective-permute-start.12 = (bf16[128,1792]{1,0:T(8,128)(2,1)S(1)}, bf16[128,1792]{1,0:T(8,128)(2,1)S(1)}, u32[]{:S(2)}, u32[]{:S(2)}) collective-permute-start(bf16[128,1792]{1,0:T(8,128)(2,1)S(1)} %fusion.1.refs_0_), channel_id=1, source_target_pairs={{0,12},{4,8},{8,4},{12,0},{1,13},{5,9},{9,5},{13,1},{2,14},{6,10},... | collective-permute-start | bytes 1376264 | tf_op jit(solution)/shard_map/ppermute | solution.py:25
  41.9 1.2 %fusion.11 = f32[128,1792]{1,0:T(8,128)S(1)} fusion(bf16[2048,1792]{1,0:T(8,128)(2,1)S(1)} %get-tuple-element.37, f32[128]{0:T(128)S(1)} %add_rsqrt_fusion, f32[2048]{0:T(1024)S(1)} %bitcast.30, bf16[32,2048]{1,0:T(8,128)(2,1)S(1)} %collective-permute-done.9, bf16[32,2048]{1,0:T(8,128)(2,1)S(1)} %collective-permute-done.8, ...), kind=kOutput, calls=%fused_computation.28 | convolution fusion | flops 942407680 | bytes 8790528 | tf_op jit(solution)/shard_map/dot_general | solution.py:321
  43.1 1.5 %multiply_convert_fusion = (bf16[128,1792]{1,0:T(8,128)(2,1)S(1)}, bf16[128,1792]{1,0:T(8,128)(2,1)S(1)}, bf16[128,1792]{1,0:T(8,128)(2,1)S(1)}) fusion(f32[128,1792]{1,0:T(8,128)S(1)} %fusion.11, f32[128,1792]{1,0:T(8,128)S(1)} %shard_map.96, bf16[2048,1792]{1,0:T(8,128)(2,1)S(1)} %get-tuple-element.38, f32[128]{0:T(128)S(1)} %add_rsqrt_fusion, ...), kind=kOutput, calls=%fused_computation.20 | convolution fusion | flops 946077696 | bytes 11084288 | tf_op jit(solution)/shard_map/dot_general | solution.py:322
  44.6 1.1 %fusion.21 = f32[128,2048]{1,0:T(8,128)S(1)} fusion(bf16[128,1792]{1,0:T(8,128)(2,1)S(1)} %get-tuple-element.46, bf16[1792,2048]{1,0:T(8,128)(2,1)S(1)} %get-tuple-element.47), kind=kOutput, calls=%fused_computation.56 | convolution fusion | flops 939524096 | bytes 8847360 | tf_op jit(solution)/shard_map/dot_general | solution.py:340
  45.8 2.6 %fusion.8 = (f32[128]{0:T(128)S(1)}, f32[128,2048]{1,0:T(8,128)S(1)}) fusion(bf16[32,2048]{1,0:T(8,128)(2,1)S(1)} %collective-permute-done.9, bf16[32,2048]{1,0:T(8,128)(2,1)S(1)} %collective-permute-done.8, bf16[32,2048]{1,0:T(8,128)(2,1)S(1)} %collective-permute-done.7, bf16[32,2048]{1,0:T(8,128)(2,1)S(1)} %add_convert_fusion.1, f32[2048]{0:T(1024)S(1)} %bitcast.32, ...), kind=kOutput, calls=%fused_computation.17 | convolution fusion | flops 942669696 | bytes 10428928 | tf_op jit(solution)/shard_map/dot_general | solution.py:341
  48.6 2.3 %collective-permute-done.11.refs_2_ = bf16[128,1792]{1,0:T(8,128)(2,1)S(1)} collective-permute-done((bf16[128,1792]{1,0:T(8,128)(2,1)S(1)}, bf16[128,1792]{1,0:T(8,128)(2,1)S(1)}, u32[]{:S(2)}, u32[]{:S(2)}) %collective-permute-start.11) | collective-permute-done | bytes 458784 | tf_op jit(solution)/shard_map/ppermute | solution.py:25
  51.0 1.3 %collective-permute-start.16 = (bf16[32,2048]{1,0:T(8,128)(2,1)S(1)}, bf16[32,2048]{1,0:T(8,128)(2,1)S(1)}, u32[]{:S(2)}, u32[]{:S(2)}) collective-permute-start(bf16[32,2048]{1,0:T(8,128)(2,1)S(1)} %get-tuple-element.78), channel_id=1, source_target_pairs={{16,3},{17,2},{18,1},{19,0},{20,7},{21,6},{22,5},{23,4},{24,11},{2... | collective-permute-start | bytes 393224 | tf_op jit(solution)/shard_map/ppermute | solution.py:33
  52.3 1.3 %collective-permute-start.15 = (bf16[32,2048]{1,0:T(8,128)(2,1)S(1)}, bf16[32,2048]{1,0:T(8,128)(2,1)S(1)}, u32[]{:S(2)}, u32[]{:S(2)}) collective-permute-start(bf16[32,2048]{1,0:T(8,128)(2,1)S(1)} %get-tuple-element.79), channel_id=1, source_target_pairs={{16,2},{17,3},{18,0},{19,1},{20,6},{21,7},{22,4},{23,5},{24,10},{2... | collective-permute-start | bytes 393224 | tf_op jit(solution)/shard_map/ppermute | solution.py:33
  53.6 1.3 %collective-permute-start.14 = (bf16[32,2048]{1,0:T(8,128)(2,1)S(1)}, bf16[32,2048]{1,0:T(8,128)(2,1)S(1)}, u32[]{:S(2)}, u32[]{:S(2)}) collective-permute-start(bf16[32,2048]{1,0:T(8,128)(2,1)S(1)} %get-tuple-element.80), channel_id=1, source_target_pairs={{16,1},{17,0},{18,3},{19,2},{20,5},{21,4},{22,7},{23,6},{24,9},{25... | collective-permute-start | bytes 393224 | tf_op jit(solution)/shard_map/ppermute | solution.py:33
  54.9 1.3 %collective-permute-start.13 = (bf16[32,2048]{1,0:T(8,128)(2,1)S(1)}, bf16[32,2048]{1,0:T(8,128)(2,1)S(1)}, u32[]{:S(2)}, u32[]{:S(2)}) collective-permute-start(bf16[32,2048]{1,0:T(8,128)(2,1)S(1)} %get-tuple-element.77), channel_id=1, source_target_pairs={{16,0},{17,1},{18,2},{19,3},{20,4},{21,5},{22,6},{23,7},{24,8},{25... | collective-permute-start | bytes 393224 | tf_op jit(solution)/shard_map/ppermute | solution.py:33
  56.3 3.0 %collective-permute-done.13 = bf16[32,2048]{1,0:T(8,128)(2,1)S(1)} collective-permute-done((bf16[32,2048]{1,0:T(8,128)(2,1)S(1)}, bf16[32,2048]{1,0:T(8,128)(2,1)S(1)}, u32[]{:S(2)}, u32[]{:S(2)}) %collective-permute-start.13) | collective-permute-done | bytes 131104 | tf_op jit(solution)/shard_map/ppermute | solution.py:33
  59.3 3.1 %collective-permute-done.15 = bf16[32,2048]{1,0:T(8,128)(2,1)S(1)} collective-permute-done((bf16[32,2048]{1,0:T(8,128)(2,1)S(1)}, bf16[32,2048]{1,0:T(8,128)(2,1)S(1)}, u32[]{:S(2)}, u32[]{:S(2)}) %collective-permute-start.15) | collective-permute-done | bytes 131104 | tf_op jit(solution)/shard_map/ppermute | solution.py:33
  62.6 1.6 %collective-permute-start.19 = (bf16[48,512]{1,0:T(8,128)(2,1)S(1)}, bf16[48,512]{1,0:T(8,128)(2,1)S(1)}, u32[]{:S(2)}, u32[]{:S(2)}) collective-permute-start(bf16[48,512]{1,0:T(8,128)(2,1)S(1)} %get-tuple-element.93), channel_id=1, source_target_pairs={{0,12},{4,8},{8,4},{12,0},{1,13},{5,9},{9,5},{13,1},{2,14},{6,10},... | collective-permute-start | bytes 147464 | tf_op jit(solution)/shard_map/ppermute | solution.py:19
  64.1 0.7 collective-permute-start.20
  65.4 1.5 %collective-permute-start.17 = (bf16[48,512]{1,0:T(8,128)(2,1)S(1)}, bf16[48,512]{1,0:T(8,128)(2,1)S(1)}, u32[]{:S(2)}, u32[]{:S(2)}) collective-permute-start(bf16[48,512]{1,0:T(8,128)(2,1)S(1)} %get-tuple-element.91), channel_id=1, source_target_pairs={{0,4},{4,0},{8,12},{12,8},{1,5},{5,1},{9,13},{13,9},{2,6},{6,2},{1... | collective-permute-start | bytes 147464 | tf_op jit(solution)/shard_map/ppermute | solution.py:19
  66.9 0.7 collective-permute-start.21
  68.2 1.4 %collective-permute-start.22 = (bf16[128,1792]{1,0:T(8,128)(2,1)S(1)}, bf16[128,1792]{1,0:T(8,128)(2,1)}, u32[]{:S(2)}, u32[]{:S(2)}) collective-permute-start(bf16[128,1792]{1,0:T(8,128)(2,1)S(1)} %get-tuple-element.61.refs_4_), channel_id=1, source_target_pairs={{16,28},{20,24},{24,20},{28,16},{17,29},{21,25},{25,21},{29,17},{1... | collective-permute-start | bytes 1376264 | tf_op jit(solution)/shard_map/ppermute | solution.py:25
  70.3 1.6 %collective-permute-start.23 = (bf16[128,512]{1,0:T(8,128)(2,1)S(1)}, bf16[128,512]{1,0:T(8,128)(2,1)S(1)}, u32[]{:S(2)}, u32[]{:S(2)}) collective-permute-start(bf16[128,512]{1,0:T(8,128)(2,1)S(1)} %pad_maximum_fusion.2.refs_3_), channel_id=1, source_target_pairs={{0,3},{1,2},{2,1},{3,0},{4,7},{5,6},{6,5},{7,4},{8,11},{9,10},{10,... | collective-permute-start | bytes 393224 | tf_op jit(solution)/shard_map/ppermute | solution.py:19
  72.0 2.8 %collective-permute-start.25 = (bf16[128,512]{1,0:T(8,128)(2,1)S(1)}, bf16[128,512]{1,0:T(8,128)(2,1)S(1)}, u32[]{:S(2)}, u32[]{:S(2)}) collective-permute-start(bf16[128,512]{1,0:T(8,128)(2,1)S(1)} %pad_maximum_fusion.2.refs_3_), channel_id=1, source_target_pairs={{0,1},{1,0},{2,3},{3,2},{4,5},{5,4},{6,7},{7,6},{8,9},{9,8},{10,11... | collective-permute-start | bytes 393224 | tf_op jit(solution)/shard_map/ppermute | solution.py:19
  74.8 0.7 broadcast_in_dim.10
  75.5 0.9 reshape.85.ids_ref
  76.4 0.9 reshape_reshape.3.ids_row_ref
  77.3 0.7 copy-done.8
  78.0 2.6 %shard_map.97 = (bf16[512,1792]{1,0:T(8,128)(2,1)S(1)}, f32[512,512]{1,0:T(8,128)S(1)}) custom-call(s32[1]{0:T(128)} %bitcast.flag_ref, bf16[128,1792]{1,0:T(8,128)(2,1)} %copy-done, bf16[128,1792]{1,0:T(8,128)(2,1)} %copy-done.3, bf16[128,1792]{1,0:T(8,128)(2,1)} %copy-done.4, bf16[128,1792]{1,0:T(8,128)(2,1)} %copy-done.5, bf16[128,1792]{1,0:T(8,128)(2,1)} %copy-done.6, ...), custom_call_target="tpu_custom_call" | custom-call | flops 939524096 | bytes 4718592 | tf_op jit(solution)/shard_map/pallas_call | solution.py:216
  80.7 3.6 %collective-permute-done.24.refs_1_ = bf16[128,512]{1,0:T(8,128)(2,1)S(1)} collective-permute-done((bf16[128,512]{1,0:T(8,128)(2,1)S(1)}, bf16[128,512]{1,0:T(8,128)(2,1)S(1)}, u32[]{:S(2)}, u32[]{:S(2)}) %collective-permute-start.24) | collective-permute-done | bytes 131104 | tf_op jit(solution)/shard_map/ppermute | solution.py:19
  84.3 1.6 %shard_map.98 = (bf16[512,2048]{1,0:T(8,128)(2,1)S(1)}, f32[8,128]{1,0:T(8,128)S(1)}) custom-call(s32[512,1]{1,0:T(8,128)S(1)} %reshape.85.ids_ref, s32[1,512]{1,0:T(1,128)S(1)} %reshape_reshape.3.ids_row_ref, f32[512,512]{1,0:T(8,128)S(1)} %get-tuple-element.63.gram_ref, bf16[128,512]{1,0:T(8,128)(2,1)S(1)} %collective-permute-done.23.refs_0_, ...), custom_call_target="tpu_custom_call" | custom-call | flops 269484032 | bytes 2097152 | tf_op jit(solution)/shard_map/pallas_call | solution.py:275
  86.0 1.6 %collective-permute-start.26 = (f32[8,128]{1,0:T(8,128)S(1)}, f32[8,128]{1,0:T(8,128)S(1)}, u32[]{:S(2)}, u32[]{:S(2)}) collective-permute-start(f32[8,128]{1,0:T(8,128)S(1)} %get-tuple-element.66), channel_id=1, source_target_pairs={{0,3},{1,2},{2,1},{3,0},{4,7},{5,6},{6,5},{7,4},{8,11},{9,10},{10,... | collective-permute-start | bytes 12296 | tf_op jit(solution)/shard_map/ppermute | solution.py:19
  87.6 1.9 %collective-permute-start.27 = (f32[8,128]{1,0:T(8,128)S(1)}, f32[8,128]{1,0:T(8,128)S(1)}, u32[]{:S(2)}, u32[]{:S(2)}) collective-permute-start(f32[8,128]{1,0:T(8,128)S(1)} %get-tuple-element.66), channel_id=1, source_target_pairs={{0,2},{1,3},{2,0},{3,1},{4,6},{5,7},{6,4},{7,5},{8,10},{9,11},{10,... | collective-permute-start | bytes 12296 | tf_op jit(solution)/shard_map/ppermute | solution.py:19
  89.5 2.5 %shard_map.99.rest_0_ = bf16[4,1792,512]{2,1,0:T(8,128)(2,1)} custom-call(bf16[512,1792]{1,0:T(8,128)(2,1)S(1)} %get-tuple-element.62.hidden_ref, bf16[512,2048]{1,0:T(8,128)(2,1)S(1)} %get-tuple-element.69.masked_ref), custom_call_target="tpu_custom_call" | custom-call | flops 1073741824 | bytes 2621440 | tf_op jit(solution)/shard_map/pallas_call | solution.py:163
  92.2 1.5 %collective-permute-start.31 = (f32[8,128]{1,0:T(8,128)S(1)}, f32[8,128]{1,0:T(8,128)S(1)}, u32[]{:S(2)}, u32[]{:S(2)}) collective-permute-start(f32[8,128]{1,0:T(8,128)S(1)} %add_add_fusion.1), channel_id=1, source_target_pairs={{0,4},{4,0},{8,12},{12,8},{1,5},{5,1},{9,13},{13,9},{2,6},{6,2},{1... | collective-permute-start | bytes 12296 | tf_op jit(solution)/shard_map/ppermute | solution.py:19
  93.6 1.8 %collective-permute-start.29 = (f32[8,128]{1,0:T(8,128)S(1)}, f32[8,128]{1,0:T(8,128)S(1)}, u32[]{:S(2)}, u32[]{:S(2)}) collective-permute-start(f32[8,128]{1,0:T(8,128)S(1)} %add_add_fusion.1), channel_id=1, source_target_pairs={{0,12},{4,8},{8,4},{12,0},{1,13},{5,9},{9,5},{13,1},{2,14},{6,10},... | collective-permute-start | bytes 12296 | tf_op jit(solution)/shard_map/ppermute | solution.py:19
  95.6 2.5 %shard_map.100.rest_0_ = bf16[4,1792,512]{2,1,0:T(8,128)(2,1)} custom-call(bf16[512,1792]{1,0:T(8,128)(2,1)S(1)} %get-tuple-element.62.hidden_ref, bf16[512,2048]{1,0:T(8,128)(2,1)S(1)} %get-tuple-element.69.masked_ref, bf16[4,1792,512]{2,1,0:T(8,128)(2,1)} %shard_map.99.rest_0_), custom_call_target="tpu_custom_call", output_to_operand_aliasing={{}: (2, {})} | custom-call | flops 1073741824 | bytes 2621440 | tf_op jit(solution)/shard_map/pallas_call | solution.py:163
  98.2 0.9 collective-permute-done.30
  99.1 3.5 %shard_map.101 = bf16[4,1792,512]{2,1,0:T(8,128)(2,1)} custom-call(bf16[512,1792]{1,0:T(8,128)(2,1)S(1)} %get-tuple-element.62.hidden_ref, bf16[512,2048]{1,0:T(8,128)(2,1)S(1)} %get-tuple-element.69.masked_ref, bf16[4,1792,512]{2,1,0:T(8,128)(2,1)} %shard_map.100.rest_0_), custom_call_target="tpu_custom_call", output_to_operand_aliasing={{}: (2, {})} | custom-call | flops 1610612736 | bytes 3932160 | tf_op jit(solution)/shard_map/pallas_call | solution.py:163
  (88 shorter events, 6.8 us)
Async XLA Ops:
  1.6 16.4 %copy-start.9 = (f32[1,2048]{1,0:T(1,128)S(1)}, f32[1,2048]{1,0:T(1,128)}, u32[]{:S(2)}) copy-start(f32[1,2048]{1,0:T(1,128)} %param.11) | copy-start | bytes 24580
  1.6 13.2 %collective-permute-start.2 = (bf16[32,2048]{1,0:T(8,128)(2,1)S(1)}, bf16[32,2048]{1,0:T(8,128)(2,1)S(1)}, u32[]{:S(2)}, u32[]{:S(2)}) collective-permute-start(bf16[32,2048]{1,0:T(8,128)(2,1)S(1)} %bitcast_select_fusion.1), channel_id=1, source_target_pairs={{0,3},{1,2},{2,1},{3,0},{4,7},{5,6},{6,5},{7,4},{8,11},{9,10},{10,... | collective-permute-start | bytes 393224 | tf_op jit(solution)/shard_map/ppermute | solution.py:19
  6.8 11.1 %collective-permute-start.1 = (bf16[32,2048]{1,0:T(8,128)(2,1)S(1)}, bf16[32,2048]{1,0:T(8,128)(2,1)S(1)}, u32[]{:S(2)}, u32[]{:S(2)}) collective-permute-start(bf16[32,2048]{1,0:T(8,128)(2,1)S(1)} %bitcast_select_fusion.1), channel_id=1, source_target_pairs={{0,2},{1,3},{2,0},{3,1},{4,6},{5,7},{6,4},{7,5},{8,10},{9,11},{10,... | collective-permute-start | bytes 393224 | tf_op jit(solution)/shard_map/ppermute | solution.py:19
  6.8 11.1 %collective-permute-start = (bf16[32,2048]{1,0:T(8,128)(2,1)S(1)}, bf16[32,2048]{1,0:T(8,128)(2,1)S(1)}, u32[]{:S(2)}, u32[]{:S(2)}) collective-permute-start(bf16[32,2048]{1,0:T(8,128)(2,1)S(1)} %bitcast_select_fusion.1), channel_id=1, source_target_pairs={{0,1},{1,0},{2,3},{3,2},{4,5},{5,4},{6,7},{7,6},{8,9},{9,8},{10,11... | collective-permute-start | bytes 393224 | tf_op jit(solution)/shard_map/ppermute | solution.py:19
  20.6 18.5 %copy-start = (bf16[128,1792]{1,0:T(8,128)(2,1)}, bf16[128,1792]{1,0:T(8,128)(2,1)S(1)}, u32[]{:S(2)}) copy-start(bf16[128,1792]{1,0:T(8,128)(2,1)S(1)} %fusion.1.refs_0_) | copy-start | bytes 1376260
  21.7 8.4 %copy-start.2 = (bf16[4,8,2048]{2,1,0:T(8,128)(2,1)S(1)}, bf16[4,8,2048]{2,1,0:T(8,128)(2,1)}, u32[]{:S(2)}) copy-start(bf16[4,8,2048]{2,1,0:T(8,128)(2,1)} %param.8) | copy-start | bytes 393220
  21.8 7.0 %collective-permute-start.6 = (bf16[32,2048]{1,0:T(8,128)(2,1)S(1)}, bf16[32,2048]{1,0:T(8,128)(2,1)S(1)}, u32[]{:S(2)}, u32[]{:S(2)}) collective-permute-start(bf16[32,2048]{1,0:T(8,128)(2,1)S(1)} %get-tuple-element.82), channel_id=1, source_target_pairs={{0,19},{1,18},{2,17},{3,16},{4,23},{5,22},{6,21},{7,20},{8,27},{9,... | collective-permute-start | bytes 393224 | tf_op jit(solution)/shard_map/ppermute | solution.py:33
  24.8 4.0 %collective-permute-start.5 = (bf16[32,2048]{1,0:T(8,128)(2,1)S(1)}, bf16[32,2048]{1,0:T(8,128)(2,1)S(1)}, u32[]{:S(2)}, u32[]{:S(2)}) collective-permute-start(bf16[32,2048]{1,0:T(8,128)(2,1)S(1)} %get-tuple-element.83), channel_id=1, source_target_pairs={{0,18},{1,19},{2,16},{3,17},{4,22},{5,23},{6,20},{7,21},{8,26},{9,... | collective-permute-start | bytes 393224 | tf_op jit(solution)/shard_map/ppermute | solution.py:33
  26.1 4.0 %collective-permute-start.4 = (bf16[32,2048]{1,0:T(8,128)(2,1)S(1)}, bf16[32,2048]{1,0:T(8,128)(2,1)S(1)}, u32[]{:S(2)}, u32[]{:S(2)}) collective-permute-start(bf16[32,2048]{1,0:T(8,128)(2,1)S(1)} %get-tuple-element.84), channel_id=1, source_target_pairs={{0,17},{1,16},{2,19},{3,18},{4,21},{5,20},{6,23},{7,22},{8,25},{9,... | collective-permute-start | bytes 393224 | tf_op jit(solution)/shard_map/ppermute | solution.py:33
  27.4 2.7 %collective-permute-start.3 = (bf16[32,2048]{1,0:T(8,128)(2,1)S(1)}, bf16[32,2048]{1,0:T(8,128)(2,1)S(1)}, u32[]{:S(2)}, u32[]{:S(2)}) collective-permute-start(bf16[32,2048]{1,0:T(8,128)(2,1)S(1)} %get-tuple-element.81), channel_id=1, source_target_pairs={{0,16},{1,17},{2,18},{3,19},{4,20},{5,21},{6,22},{7,23},{8,24},{9,... | collective-permute-start | bytes 393224 | tf_op jit(solution)/shard_map/ppermute | solution.py:33
  30.2 8.9 %collective-permute-start.9 = (bf16[32,2048]{1,0:T(8,128)(2,1)S(1)}, bf16[32,2048]{1,0:T(8,128)(2,1)S(1)}, u32[]{:S(2)}, u32[]{:S(2)}) collective-permute-start(bf16[32,2048]{1,0:T(8,128)(2,1)S(1)} %add_convert_fusion.1), channel_id=1, source_target_pairs={{16,19},{17,18},{18,17},{19,16},{20,23},{21,22},{22,21},{23,20},{2... | collective-permute-start | bytes 393224 | tf_op jit(solution)/shard_map/ppermute | solution.py:25
  30.9 10.8 %collective-permute-start.8 = (bf16[32,2048]{1,0:T(8,128)(2,1)S(1)}, bf16[32,2048]{1,0:T(8,128)(2,1)S(1)}, u32[]{:S(2)}, u32[]{:S(2)}) collective-permute-start(bf16[32,2048]{1,0:T(8,128)(2,1)S(1)} %add_convert_fusion.1), channel_id=1, source_target_pairs={{16,18},{17,19},{18,16},{19,17},{20,22},{21,23},{22,20},{23,21},{2... | collective-permute-start | bytes 393224 | tf_op jit(solution)/shard_map/ppermute | solution.py:25
  31.6 10.1 %collective-permute-start.7 = (bf16[32,2048]{1,0:T(8,128)(2,1)S(1)}, bf16[32,2048]{1,0:T(8,128)(2,1)S(1)}, u32[]{:S(2)}, u32[]{:S(2)}) collective-permute-start(bf16[32,2048]{1,0:T(8,128)(2,1)S(1)} %add_convert_fusion.1), channel_id=1, source_target_pairs={{16,17},{17,16},{18,19},{19,18},{20,21},{21,20},{22,23},{23,22},{2... | collective-permute-start | bytes 393224 | tf_op jit(solution)/shard_map/ppermute | solution.py:25
  32.2 16.4 %collective-permute-start.10 = (bf16[128,1792]{1,0:T(8,128)(2,1)S(1)}, bf16[128,1792]{1,0:T(8,128)(2,1)S(1)}, u32[]{:S(2)}, u32[]{:S(2)}) collective-permute-start(bf16[128,1792]{1,0:T(8,128)(2,1)S(1)} %fusion.1.refs_0_), channel_id=1, source_target_pairs={{0,4},{4,0},{8,12},{12,8},{1,5},{5,1},{9,13},{13,9},{2,6},{6,2},{1... | collective-permute-start | bytes 1376264 | tf_op jit(solution)/shard_map/ppermute | solution.py:25
  35.6 15.3 %collective-permute-start.11 = (bf16[128,1792]{1,0:T(8,128)(2,1)S(1)}, bf16[128,1792]{1,0:T(8,128)(2,1)S(1)}, u32[]{:S(2)}, u32[]{:S(2)}) collective-permute-start(bf16[128,1792]{1,0:T(8,128)(2,1)S(1)} %fusion.1.refs_0_), channel_id=1, source_target_pairs={{0,8},{4,12},{8,0},{12,4},{1,9},{5,13},{9,1},{13,5},{2,10},{6,14},... | collective-permute-start | bytes 1376264 | tf_op jit(solution)/shard_map/ppermute | solution.py:25
  39.1 11.8 %collective-permute-start.12 = (bf16[128,1792]{1,0:T(8,128)(2,1)S(1)}, bf16[128,1792]{1,0:T(8,128)(2,1)S(1)}, u32[]{:S(2)}, u32[]{:S(2)}) collective-permute-start(bf16[128,1792]{1,0:T(8,128)(2,1)S(1)} %fusion.1.refs_0_), channel_id=1, source_target_pairs={{0,12},{4,8},{8,4},{12,0},{1,13},{5,9},{9,5},{13,1},{2,14},{6,10},... | collective-permute-start | bytes 1376264 | tf_op jit(solution)/shard_map/ppermute | solution.py:25
  44.6 23.6 %copy-start.6 = (bf16[128,1792]{1,0:T(8,128)(2,1)}, bf16[128,1792]{1,0:T(8,128)(2,1)S(1)}, u32[]{:S(2)}) copy-start(bf16[128,1792]{1,0:T(8,128)(2,1)S(1)} %get-tuple-element.61.refs_4_) | copy-start | bytes 1376260
  45.7 10.4 %copy-start.11 = (s32[4,1]{0,1:T(1,128)S(1)}, s32[4,1]{0,1:T(1,128)}, u32[]{:S(2)}) copy-start(s32[4,1]{0,1:T(1,128)} %param.10) | copy-start | bytes 52
  45.8 16.6 %copy-start.1 = (bf16[4,8,2048]{2,1,0:T(8,128)(2,1)S(1)}, bf16[4,8,2048]{2,1,0:T(8,128)(2,1)}, u32[]{:S(2)}) copy-start(bf16[4,8,2048]{2,1,0:T(8,128)(2,1)} %param.9) | copy-start | bytes 393220
  48.6 28.7 %copy-start.3 = (bf16[128,1792]{1,0:T(8,128)(2,1)}, bf16[128,1792]{1,0:T(8,128)(2,1)S(1)}, u32[]{:S(2)}) copy-start(bf16[128,1792]{1,0:T(8,128)(2,1)S(1)} %collective-permute-done.10.refs_1_) | copy-start | bytes 1376260
  50.9 26.4 %copy-start.4 = (bf16[128,1792]{1,0:T(8,128)(2,1)}, bf16[128,1792]{1,0:T(8,128)(2,1)S(1)}, u32[]{:S(2)}) copy-start(bf16[128,1792]{1,0:T(8,128)(2,1)S(1)} %collective-permute-done.11.refs_2_) | copy-start | bytes 1376260
  50.9 26.4 %copy-start.5 = (bf16[128,1792]{1,0:T(8,128)(2,1)}, bf16[128,1792]{1,0:T(8,128)(2,1)S(1)}, u32[]{:S(2)}) copy-start(bf16[128,1792]{1,0:T(8,128)(2,1)S(1)} %collective-permute-done.12.refs_3_) | copy-start | bytes 1376260
  51.0 8.3 %collective-permute-start.16 = (bf16[32,2048]{1,0:T(8,128)(2,1)S(1)}, bf16[32,2048]{1,0:T(8,128)(2,1)S(1)}, u32[]{:S(2)}, u32[]{:S(2)}) collective-permute-start(bf16[32,2048]{1,0:T(8,128)(2,1)S(1)} %get-tuple-element.78), channel_id=1, source_target_pairs={{16,3},{17,2},{18,1},{19,0},{20,7},{21,6},{22,5},{23,4},{24,11},{2... | collective-permute-start | bytes 393224 | tf_op jit(solution)/shard_map/ppermute | solution.py:33
  52.3 10.1 %collective-permute-start.15 = (bf16[32,2048]{1,0:T(8,128)(2,1)S(1)}, bf16[32,2048]{1,0:T(8,128)(2,1)S(1)}, u32[]{:S(2)}, u32[]{:S(2)}) collective-permute-start(bf16[32,2048]{1,0:T(8,128)(2,1)S(1)} %get-tuple-element.79), channel_id=1, source_target_pairs={{16,2},{17,3},{18,0},{19,1},{20,6},{21,7},{22,4},{23,5},{24,10},{2... | collective-permute-start | bytes 393224 | tf_op jit(solution)/shard_map/ppermute | solution.py:33
  53.6 8.8 %collective-permute-start.14 = (bf16[32,2048]{1,0:T(8,128)(2,1)S(1)}, bf16[32,2048]{1,0:T(8,128)(2,1)S(1)}, u32[]{:S(2)}, u32[]{:S(2)}) collective-permute-start(bf16[32,2048]{1,0:T(8,128)(2,1)S(1)} %get-tuple-element.80), channel_id=1, source_target_pairs={{16,1},{17,0},{18,3},{19,2},{20,5},{21,4},{22,7},{23,6},{24,9},{25... | collective-permute-start | bytes 393224 | tf_op jit(solution)/shard_map/ppermute | solution.py:33
  54.9 4.4 %collective-permute-start.13 = (bf16[32,2048]{1,0:T(8,128)(2,1)S(1)}, bf16[32,2048]{1,0:T(8,128)(2,1)S(1)}, u32[]{:S(2)}, u32[]{:S(2)}) collective-permute-start(bf16[32,2048]{1,0:T(8,128)(2,1)S(1)} %get-tuple-element.77), channel_id=1, source_target_pairs={{16,0},{17,1},{18,2},{19,3},{20,4},{21,5},{22,6},{23,7},{24,8},{25... | collective-permute-start | bytes 393224 | tf_op jit(solution)/shard_map/ppermute | solution.py:33
  62.6 5.6 %collective-permute-start.19 = (bf16[48,512]{1,0:T(8,128)(2,1)S(1)}, bf16[48,512]{1,0:T(8,128)(2,1)S(1)}, u32[]{:S(2)}, u32[]{:S(2)}) collective-permute-start(bf16[48,512]{1,0:T(8,128)(2,1)S(1)} %get-tuple-element.93), channel_id=1, source_target_pairs={{0,12},{4,8},{8,4},{12,0},{1,13},{5,9},{9,5},{13,1},{2,14},{6,10},... | collective-permute-start | bytes 147464 | tf_op jit(solution)/shard_map/ppermute | solution.py:19
  64.1 6.2 %collective-permute-start.20 = (bf16[128,1792]{1,0:T(8,128)(2,1)S(1)}, bf16[128,1792]{1,0:T(8,128)(2,1)S(1)}, u32[]{:S(2)}, u32[]{:S(2)}) collective-permute-start(bf16[128,1792]{1,0:T(8,128)(2,1)S(1)} %get-tuple-element.61.refs_4_), channel_id=1, source_target_pairs={{16,20},{20,16},{24,28},{28,24},{17,21},{21,17},{25,29},{29,25},{1... | collective-permute-start | bytes 1376264 | tf_op jit(solution)/shard_map/ppermute | solution.py:25
  64.8 5.0 %collective-permute-start.18 = (bf16[48,512]{1,0:T(8,128)(2,1)S(1)}, bf16[48,512]{1,0:T(8,128)(2,1)S(1)}, u32[]{:S(2)}, u32[]{:S(2)}) collective-permute-start(bf16[48,512]{1,0:T(8,128)(2,1)S(1)} %get-tuple-element.92), channel_id=1, source_target_pairs={{0,8},{4,12},{8,0},{12,4},{1,9},{5,13},{9,1},{13,5},{2,10},{6,14},... | collective-permute-start | bytes 147464 | tf_op jit(solution)/shard_map/ppermute | solution.py:19
  65.4 4.7 %collective-permute-start.17 = (bf16[48,512]{1,0:T(8,128)(2,1)S(1)}, bf16[48,512]{1,0:T(8,128)(2,1)S(1)}, u32[]{:S(2)}, u32[]{:S(2)}) collective-permute-start(bf16[48,512]{1,0:T(8,128)(2,1)S(1)} %get-tuple-element.91), channel_id=1, source_target_pairs={{0,4},{4,0},{8,12},{12,8},{1,5},{5,1},{9,13},{13,9},{2,6},{6,2},{1... | collective-permute-start | bytes 147464 | tf_op jit(solution)/shard_map/ppermute | solution.py:19
  66.9 10.4 %collective-permute-start.21 = (bf16[128,1792]{1,0:T(8,128)(2,1)S(1)}, bf16[128,1792]{1,0:T(8,128)(2,1)S(1)}, u32[]{:S(2)}, u32[]{:S(2)}) collective-permute-start(bf16[128,1792]{1,0:T(8,128)(2,1)S(1)} %get-tuple-element.61.refs_4_), channel_id=1, source_target_pairs={{16,24},{20,28},{24,16},{28,20},{17,25},{21,29},{25,17},{29,21},{1... | collective-permute-start | bytes 1376264 | tf_op jit(solution)/shard_map/ppermute | solution.py:25
  68.2 9.0 %collective-permute-start.22 = (bf16[128,1792]{1,0:T(8,128)(2,1)S(1)}, bf16[128,1792]{1,0:T(8,128)(2,1)}, u32[]{:S(2)}, u32[]{:S(2)}) collective-permute-start(bf16[128,1792]{1,0:T(8,128)(2,1)S(1)} %get-tuple-element.61.refs_4_), channel_id=1, source_target_pairs={{16,28},{20,24},{24,20},{28,16},{17,29},{21,25},{25,21},{29,17},{1... | collective-permute-start | bytes 1376264 | tf_op jit(solution)/shard_map/ppermute | solution.py:25
  70.3 7.0 %copy-start.7 = (bf16[128,1792]{1,0:T(8,128)(2,1)}, bf16[128,1792]{1,0:T(8,128)(2,1)S(1)}, u32[]{:S(2)}) copy-start(bf16[128,1792]{1,0:T(8,128)(2,1)S(1)} %collective-permute-done.20.refs_5_) | copy-start | bytes 1376260
  70.3 10.3 %collective-permute-start.23 = (bf16[128,512]{1,0:T(8,128)(2,1)S(1)}, bf16[128,512]{1,0:T(8,128)(2,1)S(1)}, u32[]{:S(2)}, u32[]{:S(2)}) collective-permute-start(bf16[128,512]{1,0:T(8,128)(2,1)S(1)} %pad_maximum_fusion.2.refs_3_), channel_id=1, source_target_pairs={{0,3},{1,2},{2,1},{3,0},{4,7},{5,6},{6,5},{7,4},{8,11},{9,10},{10,... | collective-permute-start | bytes 393224 | tf_op jit(solution)/shard_map/ppermute | solution.py:19
  72.0 12.3 %collective-permute-start.24 = (bf16[128,512]{1,0:T(8,128)(2,1)S(1)}, bf16[128,512]{1,0:T(8,128)(2,1)S(1)}, u32[]{:S(2)}, u32[]{:S(2)}) collective-permute-start(bf16[128,512]{1,0:T(8,128)(2,1)S(1)} %pad_maximum_fusion.2.refs_3_), channel_id=1, source_target_pairs={{0,2},{1,3},{2,0},{3,1},{4,6},{5,7},{6,4},{7,5},{8,10},{9,11},{10,... | collective-permute-start | bytes 393224 | tf_op jit(solution)/shard_map/ppermute | solution.py:19
  72.0 12.3 %collective-permute-start.25 = (bf16[128,512]{1,0:T(8,128)(2,1)S(1)}, bf16[128,512]{1,0:T(8,128)(2,1)S(1)}, u32[]{:S(2)}, u32[]{:S(2)}) collective-permute-start(bf16[128,512]{1,0:T(8,128)(2,1)S(1)} %pad_maximum_fusion.2.refs_3_), channel_id=1, source_target_pairs={{0,1},{1,0},{2,3},{3,2},{4,5},{5,4},{6,7},{7,6},{8,9},{9,8},{10,11... | collective-permute-start | bytes 393224 | tf_op jit(solution)/shard_map/ppermute | solution.py:19
  77.3 0.8 copy-start.8
  86.0 6.1 %collective-permute-start.28 = (f32[8,128]{1,0:T(8,128)S(1)}, f32[8,128]{1,0:T(8,128)S(1)}, u32[]{:S(2)}, u32[]{:S(2)}) collective-permute-start(f32[8,128]{1,0:T(8,128)S(1)} %get-tuple-element.66), channel_id=1, source_target_pairs={{0,1},{1,0},{2,3},{3,2},{4,5},{5,4},{6,7},{7,6},{8,9},{9,8},{10,11... | collective-permute-start | bytes 12296 | tf_op jit(solution)/shard_map/ppermute | solution.py:19
  86.0 6.0 %collective-permute-start.26 = (f32[8,128]{1,0:T(8,128)S(1)}, f32[8,128]{1,0:T(8,128)S(1)}, u32[]{:S(2)}, u32[]{:S(2)}) collective-permute-start(f32[8,128]{1,0:T(8,128)S(1)} %get-tuple-element.66), channel_id=1, source_target_pairs={{0,3},{1,2},{2,1},{3,0},{4,7},{5,6},{6,5},{7,4},{8,11},{9,10},{10,... | collective-permute-start | bytes 12296 | tf_op jit(solution)/shard_map/ppermute | solution.py:19
  87.6 4.5 %collective-permute-start.27 = (f32[8,128]{1,0:T(8,128)S(1)}, f32[8,128]{1,0:T(8,128)S(1)}, u32[]{:S(2)}, u32[]{:S(2)}) collective-permute-start(f32[8,128]{1,0:T(8,128)S(1)} %get-tuple-element.66), channel_id=1, source_target_pairs={{0,2},{1,3},{2,0},{3,1},{4,6},{5,7},{6,4},{7,5},{8,10},{9,11},{10,... | collective-permute-start | bytes 12296 | tf_op jit(solution)/shard_map/ppermute | solution.py:19
  92.2 6.0 %collective-permute-start.31 = (f32[8,128]{1,0:T(8,128)S(1)}, f32[8,128]{1,0:T(8,128)S(1)}, u32[]{:S(2)}, u32[]{:S(2)}) collective-permute-start(f32[8,128]{1,0:T(8,128)S(1)} %add_add_fusion.1), channel_id=1, source_target_pairs={{0,4},{4,0},{8,12},{12,8},{1,5},{5,1},{9,13},{13,9},{2,6},{6,2},{1... | collective-permute-start | bytes 12296 | tf_op jit(solution)/shard_map/ppermute | solution.py:19
  93.6 4.5 %collective-permute-start.29 = (f32[8,128]{1,0:T(8,128)S(1)}, f32[8,128]{1,0:T(8,128)S(1)}, u32[]{:S(2)}, u32[]{:S(2)}) collective-permute-start(f32[8,128]{1,0:T(8,128)S(1)} %add_add_fusion.1), channel_id=1, source_target_pairs={{0,12},{4,8},{8,4},{12,0},{1,13},{5,9},{9,5},{13,1},{2,14},{6,10},... | collective-permute-start | bytes 12296 | tf_op jit(solution)/shard_map/ppermute | solution.py:19
  95.5 3.6 %collective-permute-start.30 = (f32[8,128]{1,0:T(8,128)S(1)}, f32[8,128]{1,0:T(8,128)S(1)}, u32[]{:S(2)}, u32[]{:S(2)}) collective-permute-start(f32[8,128]{1,0:T(8,128)S(1)} %add_add_fusion.1), channel_id=1, source_target_pairs={{0,8},{4,12},{8,0},{12,4},{1,9},{5,13},{9,1},{13,5},{2,10},{6,14},... | collective-permute-start | bytes 12296 | tf_op jit(solution)/shard_map/ppermute | solution.py:19
  99.1 3.5 %copy-start.10 = (f32[3]{0:T(128)S(1)}, f32[3]{0:T(128)}, u32[]{:S(2)}) copy-start(f32[3]{0:T(128)} %constant.50) | copy-start | bytes 40
  99.1 3.5 %collective-permute-start.32 = (f32[8,128]{1,0:T(8,128)S(1)}, f32[8,128]{1,0:T(8,128)S(1)}, u32[]{:S(2)}, u32[]{:S(2)}) collective-permute-start(f32[8,128]{1,0:T(8,128)S(1)} %add_add_fusion), channel_id=1, source_target_pairs={{0,16},{16,0},{1,17},{17,1},{2,18},{18,2},{3,19},{19,3},{4,20},{20... | collective-permute-start | bytes 12296 | tf_op jit(solution)/shard_map/ppermute | solution.py:19

commit v9 on v8

--- a/solution.py
+++ b/solution.py
@@ -37,9 +37,20 @@
     return lax.axis_size(axis).bit_length() - 1
 
 
-def gather_in(rows, section, axis):
-    size = lax.axis_size(axis)
-    return [rows] + [swap_in(rows, section, axis, k) for k in range(1, size)]
+def gather_beside(rows):
+    dp_size, tensor_size = lax.axis_size("dp"), lax.axis_size("tensor")
+
+    def route(k):
+        beside = (k - 1) % (dp_size - 1) + 1
+        pairs = []
+        for d in range(dp_size):
+            for t in range(tensor_size):
+                pairs.append((d * tensor_size + t, (d ^ beside) * tensor_size + t))
+                pairs.append(((dp_size + d) * tensor_size + t, (dp_size + d) * tensor_size + (t ^ k)))
+        return pairs
+
+    axes = ("section", "dp", "tensor")
+    return [rows] + [lax.ppermute(rows, axes, route(k)) for k in range(1, tensor_size)]
 
 
 def gather(rows, axis):
@@ -62,7 +73,11 @@
     total = total.astype(jnp.bfloat16)
     late, total = lax.optimization_barrier((rows, total))
     if source == 0:
-        return total, gather_in(late, source, "dp")
+        short = min(lax.axis_size("dp"), lax.axis_size("tensor"))
+        return total, [rows] + [
+            swap_in(late[block:] if k < short else late, source, "dp", k)
+            for k in range(1, lax.axis_size("dp"))
+        ]
     return total, [rows, swap_in(late, source, "dp", 1)] + others
 
 
@@ -138,6 +153,42 @@
     )(segment.reshape(1), rows, down_w)
 
 
+def normed_grad_kernel(flag_ref, d_gate_ref, d_up_ref, gate_t_ref, up_ref, out_ref):
+    width = out_ref.shape[1]
+
+    @pl.when(flag_ref[0] == 1)
+    def _():
+        for begin in range(0, width, TILE):
+            columns = slice(begin, begin + TILE)
+            out_ref[:, columns] = jnp.dot(
+                d_gate_ref[...], gate_t_ref[:, columns], preferred_element_type=jnp.float32
+            ) + lax.dot_general(
+                d_up_ref[...], up_ref[columns, :], CONTRACT_LAST, preferred_element_type=jnp.float32
+            )
+
+    @pl.when(flag_ref[0] == 0)
+    def _():
+        out_ref[...] = jnp.zeros_like(out_ref)
+
+
+def normed_grad(segment, d_gate, d_up, gate_t, up_w):
+    rows, units = d_gate.shape
+    width = up_w.shape[0]
+    return pl.pallas_call(
+        normed_grad_kernel,
+        in_specs=[pl.BlockSpec(memory_space=pltpu.SMEM)]
+        + [pl.BlockSpec(memory_space=pltpu.VMEM)] * 4,
+        out_specs=pl.BlockSpec(memory_space=pltpu.VMEM),
+        out_shape=jax.ShapeDtypeStruct((rows, width), jnp.float32),
+        compiler_params=pltpu.CompilerParams(vmem_limit_bytes=24 * 2**20),
+        cost_estimate=pl.CostEstimate(
+            flops=4 * rows * units * width,
+            bytes_accessed=4 * units * width,
+            transcendentals=0,
+        ),
+    )(segment.reshape(1), d_gate, d_up, gate_t, up_w)
+
+
 def gradient_kernel(hidden_ref, masked_ref, *rest):
     out_ref = rest[-1]
     piece = out_ref.shape[2]
@@ -177,21 +228,36 @@
 
 
 def assemble_kernel(count, flag_ref, *refs):
-    pieces = refs[: 2 * count]
-    hidden_ref, gram_ref, sems = refs[2 * count :]
-    rows = pieces[0].shape[0]
+    heads = len(refs) - 3 - 2 * count
+    pieces = (refs[:count][::-1], refs[count : 2 * count])
+    firsts = refs[2 * count : 2 * count + heads]
+    hidden_ref, gram_ref, sems = refs[2 * count + heads :]
+    rows, units = pieces[1][0].shape
     for section in range(2):
 
         @pl.when(flag_ref[0] == section)
         def _(section=section):
-            copies = [
-                pltpu.make_async_copy(
-                    pieces[section * count + k],
-                    hidden_ref.at[pl.ds(k * rows, rows)],
-                    sems.at[k],
+            copies = []
+            for k in range(count):
+                begin = k * rows
+                if section == 0 and 1 <= k <= heads:
+                    head = firsts[k - 1]
+                    size = head.shape[0]
+                    copies.append(
+                        pltpu.make_async_copy(
+                            head.at[:, pl.ds(0, units)],
+                            hidden_ref.at[pl.ds(begin, size)],
+                            sems.at[count + k],
+                        )
+                    )
+                    begin += size
+                copies.append(
+                    pltpu.make_async_copy(
+                        pieces[section][k],
+                        hidden_ref.at[pl.ds(begin, pieces[section][k].shape[0])],
+                        sems.at[k],
+                    )
                 )
-                for k in range(count)
-            ]
             for copy in copies:
                 copy.start()
             for copy in copies:
@@ -208,21 +274,21 @@
         )
 
 
-def assemble(segment, pieces0, pieces1):
+def assemble(segment, pieces0, pieces1, heads):
     count = len(pieces0)
     rows, units = pieces0[0].shape
     total = rows * count
-    pieces = [pltpu.with_memory_space_constraint(p, pltpu.HBM) for p in pieces0 + pieces1]
+    pieces = [pltpu.with_memory_space_constraint(p, pltpu.HBM) for p in pieces0[::-1] + pieces1 + heads]
     return pl.pallas_call(
         functools.partial(assemble_kernel, count),
         in_specs=[pl.BlockSpec(memory_space=pltpu.SMEM)]
-        + [pl.BlockSpec(memory_space=pl.ANY)] * (2 * count),
+        + [pl.BlockSpec(memory_space=pl.ANY)] * len(pieces),
         out_specs=[pl.BlockSpec(memory_space=pltpu.VMEM)] * 2,
         out_shape=[
             jax.ShapeDtypeStruct((total, units), jnp.bfloat16),
             jax.ShapeDtypeStruct((total, total), jnp.float32),
         ],
-        scratch_shapes=[pltpu.SemaphoreType.DMA((count,))],
+        scratch_shapes=[pltpu.SemaphoreType.DMA((2 * count,))],
         compiler_params=pltpu.CompilerParams(
             vmem_limit_bytes=2 * total * units + 4 * total * total + 4 * 2**20
         ),
@@ -329,22 +395,23 @@
     d_hidden = hidden_grad(segment, cot_rows, down_w)
     x1_own, pieces0 = scatter_sum(x_own, mixed, 0, block, hidden0)
     x1_own, d_hidden = lax.optimization_barrier((x1_own, d_hidden))
-    x1 = jnp.concatenate(gather_in(x1_own, 1, "tensor"), axis=0)
+    head = jnp.pad(hidden0[:block], ((0, 0), (0, width - units)))
+    blocks = gather_beside(jnp.where(first, head, x1_own))
+    x1 = jnp.concatenate(blocks, axis=0)
+    heads = blocks[1 : min(dp_size, tensor_size)]
 
     widened, scale, gate, up = layer_parts(x1)
     sig = jax.nn.sigmoid(gate)
     hidden1 = (gate * sig * up).astype(jnp.bfloat16)
     d_gate = (d_hidden * up * (sig * (1.0 + gate * (1.0 - sig)))).astype(jnp.bfloat16)
     d_up = (d_hidden * gate * sig).astype(jnp.bfloat16)
-    d_gate, d_up = lax.optimization_barrier((d_gate, d_up))
-    d_normed = jnp.dot(d_gate, gate_t, preferred_element_type=jnp.float32)
-    d_normed = d_normed + lax.dot_general(
-        d_up, up_w, CONTRACT_LAST, preferred_element_type=jnp.float32
-    )
+    d_normed = normed_grad(segment, d_gate, d_up, gate_t, up_w)
     pulled = d_normed * gain
     along = jnp.sum(pulled * widened, axis=-1, keepdims=True) / width
     term = (pulled * scale - widened * (scale * scale * scale * along)).astype(jnp.bfloat16)
+    pieces0 = pieces0[::-1]
     term, pieces0 = lax.optimization_barrier((term, pieces0))
+    pieces0 = pieces0[::-1]
     dy_own, pieces1 = scatter_sum(cot_own, term, 1, block, hidden1)
     dy_own = jnp.where(first, dy_own, cot_own)
 
@@ -361,7 +428,7 @@
     columns = jnp.concatenate([message[:block] for message in messages], axis=0)
     columns, pieces1[1] = lax.optimization_barrier((columns, pieces1[1]))
     parts_y = gather(columns, "tensor")
-    hidden_all, gram_hidden = assemble(segment, pieces0, pieces1)
+    hidden_all, gram_hidden = assemble(segment, pieces0, pieces1, heads)
     ids_all = jnp.stack([message[block : block + micro, 0] for message in messages])
     row_ids = jnp.broadcast_to(
         ids_all.astype(jnp.int32)[:, None, :, None], (dp_size, tensor_size, micro, local_rows)

time: 104 us -> 103 us (level)
  matrix products: 10.1 us -> 6.42 us
  waiting for transfers between devices: 18.3 us -> 20.9 us
  local copies, waits for them, and re-layouts: 3.74 us -> 2.44 us
    dot_general x2 -> x0, matrix products: 3.69 us -> none  [the longest x1 2.58 us: shards(): lax.dot_general(d_up, up_w, CONTRACT_LAST, preferred_element_type=jnp.flo...]
    ppermute x0 -> x3, starting transfers between devices: none -> 3.55 us  [gather_beside(): lax.ppermute(rows, axes, route(k))]
    ppermute x9 -> x6, starting transfers between devices: 14.2 us -> 11.2 us  [swap_in(): return lax.ppermute(block, ('section', axis), route)]
    ppermute x16, waiting for transfers between devices: 8.61 us -> 10.7 us  [swap(): return lax.ppermute(block, axis, [(i, i ^ offset) for i in range(size)])]
    ppermute x9 -> x6, waiting for transfers between devices: 2.32 us -> 2.91 us  [swap_in(): return lax.ppermute(block, ('section', axis), route)]
  transfers between devices with their start and end apart: 33 -> 33, of which waited for: 10 -> 11; matrix products, arithmetic and copies ran while one was open for 9% -> 4% of each run, Pallas kernels for 18% -> 19%
where the time goes in v9:
time: 103 us; the launch traced here: 102 us
  starting transfers between devices  47.7 us (46%)
  waiting for transfers between devices  20.9 us (20%)
  Pallas kernels  20.6 us (20%)
  matrix products  6.42 us (6%)
  other arithmetic  2.8 us (3%)
  local copies, waits for them, and re-layouts  2.44 us (2%)
  between operations  1.27 us (1%)
    ppermute x16, starting transfers between devices, swap(): return lax.ppermute(block, axis, [(i, i ^ offset) for i in range(size)])  20.9 us
    ppermute x8, starting transfers between devices, across(): return lax.ppermute(block, ('section', 'tensor'), route)  12 us
    ppermute x6, starting transfers between devices, swap_in(): return lax.ppermute(block, ('section', axis), route)  11.2 us
    ppermute x16, waiting for transfers between devices, swap(): return lax.ppermute(block, axis, [(i, i ^ offset) for i in range(size)])  10.7 us
    pallas_call x3, Pallas kernels, domain_gradients(): pl.pallas_call(gradient_kernel, grid=(count,), in_specs=in_specs, out_spe...  8.49 us
    pallas_call x1, Pallas kernels, load_weights(): pl.pallas_call(load_kernel, in_specs=[pl.BlockSpec(memory_space=pltpu.HBM...  7.46 us
    ppermute x8, waiting for transfers between devices, across(): return lax.ppermute(block, ('section', 'tensor'), route)  7.31 us
    ppermute x3, starting transfers between devices, gather_beside(): lax.ppermute(rows, axes, route(k))  3.55 us
  transfers between devices with their start and end apart: 33, of which 11 were waited for; matrix products, arithmetic and copies ran while one was open for 4% of the time, Pallas kernels for 19%

profile of v9, /device:TPU:0, one launch (start us, length us, event | category | flops | bytes accessed | tf_op | source)
XLA Modules:
  0.0 102.1 jit_solution(9226767717803634312)
XLA Ops:
  0.6 1.0 bitcast_select_fusion.1
  1.6 5.1 %collective-permute-start.2 = (bf16[32,2048]{1,0:T(8,128)(2,1)S(1)}, bf16[32,2048]{1,0:T(8,128)(2,1)S(1)}, u32[]{:S(2)}, u32[]{:S(2)}) collective-permute-start(bf16[32,2048]{1,0:T(8,128)(2,1)S(1)} %bitcast_select_fusion.1), channel_id=1, source_target_pairs={{0,3},{1,2},{2,1},{3,0},{4,7},{5,6},{6,5},{7,4},{8,11},{9,10},{10,... | collective-permute-start | bytes 393224 | tf_op jit(solution)/shard_map/ppermute | solution.py:19
  7.4 7.5 %shard_map.95 = (bf16[2048,1792]{1,0:T(8,128)(2,1)S(1)}, bf16[2048,1792]{1,0:T(8,128)(2,1)S(1)}, bf16[1792,2048]{1,0:T(8,128)(2,1)S(1)}, bf16[1792,2048]{1,0:T(8,128)(2,1)S(1)}) custom-call(bf16[1,2048,1792]{2,1,0:T(8,128)(2,1)} %gate_in.1, bf16[1,2048,1792]{2,1,0:T(8,128)(2,1)} %up_in.1, bf16[1,1792,2048]{2,1,0:T(8,128)(2,1)} %down_in.1), custom_call_target="tpu_custom_call" | custom-call | bytes 22020096 | tf_op jit(solution)/shard_map/pallas_call | solution.py:108
  14.9 3.0 %collective-permute-done.1 = bf16[32,2048]{1,0:T(8,128)(2,1)S(1)} collective-permute-done((bf16[32,2048]{1,0:T(8,128)(2,1)S(1)}, bf16[32,2048]{1,0:T(8,128)(2,1)S(1)}, u32[]{:S(2)}, u32[]{:S(2)}) %collective-permute-start.1) | collective-permute-done | bytes 131104 | tf_op jit(solution)/shard_map/ppermute | solution.py:19
  18.0 1.2 %fusion.15 = f32[128,1792]{1,0:T(8,128)S(1)} fusion(bf16[2048,1792]{1,0:T(8,128)(2,1)S(1)} %get-tuple-element.35, bf16[128,2048]{1,0:T(8,128)(2,1)S(1)} %get-tuple-element.41.rows_ref, f32[2048]{0:T(1024)S(1)} %bitcast.24, f32[128]{0:T(128)S(1)} %add_rsqrt_fusion.1), kind=kOutput, calls=%fused_computation.28 | convolution fusion | flops 940572672 | bytes 8790528 | tf_op jit(solution)/shard_map/dot_general | solution.py:387
  19.2 1.4 %fusion.refs_3_ = bf16[128,1792]{1,0:T(8,128)(2,1)S(1)} fusion(bf16[2048,1792]{1,0:T(8,128)(2,1)S(1)} %get-tuple-element.36.up_ref, f32[128,1792]{1,0:T(8,128)S(1)} %fusion.15, bf16[128,2048]{1,0:T(8,128)(2,1)S(1)} %get-tuple-element.41.rows_ref, f32[2048]{0:T(1024)S(1)} %bitcast.25, f32[128]{0:T(128)S(1)} %add_rsqrt_fusion.1), kind=kOutput, calls=%fused_computation.1 | convolution fusion | flops 941948928 | bytes 9249280 | tf_op jit(solution)/shard_map/dot_general | solution.py:388
  20.6 1.2 %convolution_convert_fusion = bf16[128,2048]{1,0:T(8,128)(2,1)S(1)} fusion(bf16[128,1792]{1,0:T(8,128)(2,1)S(1)} %fusion.refs_3_, bf16[1792,2048]{1,0:T(8,128)(2,1)S(1)} %get-tuple-element.37.down_ref), kind=kOutput, calls=%fused_computation.2 | convolution fusion | flops 939786240 | bytes 8323072 | tf_op jit(solution)/shard_map/dot_general | solution.py:393
  21.9 3.0 %collective-permute-start.6 = (bf16[32,2048]{1,0:T(8,128)(2,1)S(1)}, bf16[32,2048]{1,0:T(8,128)(2,1)S(1)}, u32[]{:S(2)}, u32[]{:S(2)}) collective-permute-start(bf16[32,2048]{1,0:T(8,128)(2,1)S(1)} %get-tuple-element.78), channel_id=1, source_target_pairs={{0,19},{1,18},{2,17},{3,16},{4,23},{5,22},{6,21},{7,20},{8,27},{9,... | collective-permute-start | bytes 393224 | tf_op jit(solution)/shard_map/ppermute | solution.py:33
  24.8 1.3 %collective-permute-start.5 = (bf16[32,2048]{1,0:T(8,128)(2,1)S(1)}, bf16[32,2048]{1,0:T(8,128)(2,1)S(1)}, u32[]{:S(2)}, u32[]{:S(2)}) collective-permute-start(bf16[32,2048]{1,0:T(8,128)(2,1)S(1)} %get-tuple-element.79), channel_id=1, source_target_pairs={{0,18},{1,19},{2,16},{3,17},{4,22},{5,23},{6,20},{7,21},{8,26},{9,... | collective-permute-start | bytes 393224 | tf_op jit(solution)/shard_map/ppermute | solution.py:33
  26.1 1.3 %collective-permute-start.4 = (bf16[32,2048]{1,0:T(8,128)(2,1)S(1)}, bf16[32,2048]{1,0:T(8,128)(2,1)S(1)}, u32[]{:S(2)}, u32[]{:S(2)}) collective-permute-start(bf16[32,2048]{1,0:T(8,128)(2,1)S(1)} %get-tuple-element.80), channel_id=1, source_target_pairs={{0,17},{1,16},{2,19},{3,18},{4,21},{5,20},{6,23},{7,22},{8,25},{9,... | collective-permute-start | bytes 393224 | tf_op jit(solution)/shard_map/ppermute | solution.py:33
  27.4 1.3 %collective-permute-start.3 = (bf16[32,2048]{1,0:T(8,128)(2,1)S(1)}, bf16[32,2048]{1,0:T(8,128)(2,1)S(1)}, u32[]{:S(2)}, u32[]{:S(2)}) collective-permute-start(bf16[32,2048]{1,0:T(8,128)(2,1)S(1)} %get-tuple-element.77), channel_id=1, source_target_pairs={{0,16},{1,17},{2,18},{3,19},{4,20},{5,21},{6,22},{7,23},{8,24},{9,... | collective-permute-start | bytes 393224 | tf_op jit(solution)/shard_map/ppermute | solution.py:33
  28.9 1.3 %collective-permute-done.4 = bf16[32,2048]{1,0:T(8,128)(2,1)S(1)} collective-permute-done((bf16[32,2048]{1,0:T(8,128)(2,1)S(1)}, bf16[32,2048]{1,0:T(8,128)(2,1)S(1)}, u32[]{:S(2)}, u32[]{:S(2)}) %collective-permute-start.4) | collective-permute-done | bytes 131104 | tf_op jit(solution)/shard_map/ppermute | solution.py:33
  30.3 2.5 %collective-permute-start.9 = (bf16[32,2048]{1,0:T(8,128)(2,1)S(1)}, bf16[32,2048]{1,0:T(8,128)(2,1)S(1)}, u32[]{:S(2)}, u32[]{:S(2)}) collective-permute-start(bf16[32,2048]{1,0:T(8,128)(2,1)S(1)} %pad_select_fusion), channel_id=1, source_target_pairs={{0,12},{16,19},{1,13},{17,18},{2,14},{18,17},{3,15},{19,16},{4,8},... | collective-permute-start | bytes 393224 | tf_op jit(solution)/shard_map/ppermute | solution.py:53
  33.9 4.4 %collective-permute-start.10 = (bf16[96,1792]{1,0:T(8,128)(2,1)S(1)}, bf16[96,1792]{1,0:T(8,128)(2,1)S(1)}, u32[]{:S(2)}, u32[]{:S(2)}) collective-permute-start(bf16[96,1792]{1,0:T(8,128)(2,1)S(1)} %slice.61), channel_id=1, source_target_pairs={{0,12},{4,8},{8,4},{12,0},{1,13},{5,9},{9,5},{13,1},{2,14},{6,10},... | collective-permute-start | bytes 1032200 | tf_op jit(solution)/shard_map/ppermute | solution.py:25
  38.2 2.4 %collective-permute-start.11 = (bf16[96,1792]{1,0:T(8,128)(2,1)S(1)}, bf16[96,1792]{1,0:T(8,128)(2,1)S(1)}, u32[]{:S(2)}, u32[]{:S(2)}) collective-permute-start(bf16[96,1792]{1,0:T(8,128)(2,1)S(1)} %slice.61), channel_id=1, source_target_pairs={{0,8},{4,12},{8,0},{12,4},{1,9},{5,13},{9,1},{13,5},{2,10},{6,14},... | collective-permute-start | bytes 1032200 | tf_op jit(solution)/shard_map/ppermute | solution.py:25
  40.7 2.4 %collective-permute-start.12 = (bf16[96,1792]{1,0:T(8,128)(2,1)S(1)}, bf16[96,1792]{1,0:T(8,128)(2,1)S(1)}, u32[]{:S(2)}, u32[]{:S(2)}) collective-permute-start(bf16[96,1792]{1,0:T(8,128)(2,1)S(1)} %slice.61), channel_id=1, source_target_pairs={{0,4},{4,0},{8,12},{12,8},{1,5},{5,1},{9,13},{13,9},{2,6},{6,2},{1... | collective-permute-start | bytes 1032200 | tf_op jit(solution)/shard_map/ppermute | solution.py:25
  43.4 1.2 %fusion.10 = f32[128,1792]{1,0:T(8,128)S(1)} fusion(bf16[2048,1792]{1,0:T(8,128)(2,1)S(1)} %get-tuple-element.35, f32[128]{0:T(128)S(1)} %add_rsqrt_fusion, f32[2048]{0:T(1024)S(1)} %bitcast.26, bf16[32,2048]{1,0:T(8,128)(2,1)S(1)} %collective-permute-done.9.refs_10_, bf16[32,2048]{1,0:T(8,128)(2,1)S(1)} %collective-permute-done.8.refs_9_, ...), kind=kOutput, calls=%fused_computation.26 | convolution fusion | flops 942407680 | bytes 8790528 | tf_op jit(solution)/shard_map/dot_general | solution.py:387
  44.6 1.5 %multiply_convert_fusion = (bf16[128,1792]{1,0:T(8,128)(2,1)S(1)}, bf16[128,1792]{1,0:T(8,128)(2,1)S(1)}, bf16[128,1792]{1,0:T(8,128)(2,1)S(1)}) fusion(f32[128,1792]{1,0:T(8,128)S(1)} %fusion.10, f32[128,1792]{1,0:T(8,128)S(1)} %shard_map.96, bf16[2048,1792]{1,0:T(8,128)(2,1)S(1)} %get-tuple-element.36.up_ref, f32[128]{0:T(128)S(1)} %add_rsqrt_fusion, ...), kind=kOutput, calls=%fused_computation.18 | convolution fusion | flops 946077696 | bytes 11084288 | tf_op jit(solution)/shard_map/dot_general | solution.py:388
  46.9 0.7 collective-permute-done.11.refs_1_
  47.6 2.2 %collective-permute-done.12.refs_2_ = bf16[96,1792]{1,0:T(8,128)(2,1)S(1)} collective-permute-done((bf16[96,1792]{1,0:T(8,128)(2,1)S(1)}, bf16[96,1792]{1,0:T(8,128)(2,1)S(1)}, u32[]{:S(2)}, u32[]{:S(2)}) %collective-permute-start.12) | collective-permute-done | bytes 344096 | tf_op jit(solution)/shard_map/ppermute | solution.py:25
  49.9 1.3 %collective-permute-start.16 = (bf16[32,2048]{1,0:T(8,128)(2,1)S(1)}, bf16[32,2048]{1,0:T(8,128)(2,1)S(1)}, u32[]{:S(2)}, u32[]{:S(2)}) collective-permute-start(bf16[32,2048]{1,0:T(8,128)(2,1)S(1)} %get-tuple-element.74), channel_id=1, source_target_pairs={{16,3},{17,2},{18,1},{19,0},{20,7},{21,6},{22,5},{23,4},{24,11},{2... | collective-permute-start | bytes 393224 | tf_op jit(solution)/shard_map/ppermute | solution.py:33
  51.2 1.3 %collective-permute-start.15 = (bf16[32,2048]{1,0:T(8,128)(2,1)S(1)}, bf16[32,2048]{1,0:T(8,128)(2,1)S(1)}, u32[]{:S(2)}, u32[]{:S(2)}) collective-permute-start(bf16[32,2048]{1,0:T(8,128)(2,1)S(1)} %get-tuple-element.75), channel_id=1, source_target_pairs={{16,2},{17,3},{18,0},{19,1},{20,6},{21,7},{22,4},{23,5},{24,10},{2... | collective-permute-start | bytes 393224 | tf_op jit(solution)/shard_map/ppermute | solution.py:33
  52.5 1.3 %collective-permute-start.14 = (bf16[32,2048]{1,0:T(8,128)(2,1)S(1)}, bf16[32,2048]{1,0:T(8,128)(2,1)S(1)}, u32[]{:S(2)}, u32[]{:S(2)}) collective-permute-start(bf16[32,2048]{1,0:T(8,128)(2,1)S(1)} %get-tuple-element.76), channel_id=1, source_target_pairs={{16,1},{17,0},{18,3},{19,2},{20,5},{21,4},{22,7},{23,6},{24,9},{25... | collective-permute-start | bytes 393224 | tf_op jit(solution)/shard_map/ppermute | solution.py:33
  53.8 1.3 %collective-permute-start.13 = (bf16[32,2048]{1,0:T(8,128)(2,1)S(1)}, bf16[32,2048]{1,0:T(8,128)(2,1)S(1)}, u32[]{:S(2)}, u32[]{:S(2)}) collective-permute-start(bf16[32,2048]{1,0:T(8,128)(2,1)S(1)} %get-tuple-element.73), channel_id=1, source_target_pairs={{16,0},{17,1},{18,2},{19,3},{20,4},{21,5},{22,6},{23,7},{24,8},{25... | collective-permute-start | bytes 393224 | tf_op jit(solution)/shard_map/ppermute | solution.py:33
  55.2 3.0 %collective-permute-done.13 = bf16[32,2048]{1,0:T(8,128)(2,1)S(1)} collective-permute-done((bf16[32,2048]{1,0:T(8,128)(2,1)S(1)}, bf16[32,2048]{1,0:T(8,128)(2,1)S(1)}, u32[]{:S(2)}, u32[]{:S(2)}) %collective-permute-start.13) | collective-permute-done | bytes 131104 | tf_op jit(solution)/shard_map/ppermute | solution.py:33
  58.2 3.1 %collective-permute-done.15 = bf16[32,2048]{1,0:T(8,128)(2,1)S(1)} collective-permute-done((bf16[32,2048]{1,0:T(8,128)(2,1)S(1)}, bf16[32,2048]{1,0:T(8,128)(2,1)S(1)}, u32[]{:S(2)}, u32[]{:S(2)}) %collective-permute-start.15) | collective-permute-done | bytes 131104 | tf_op jit(solution)/shard_map/ppermute | solution.py:33
  61.5 1.5 %collective-permute-start.19 = (bf16[48,512]{1,0:T(8,128)(2,1)S(1)}, bf16[48,512]{1,0:T(8,128)(2,1)S(1)}, u32[]{:S(2)}, u32[]{:S(2)}) collective-permute-start(bf16[48,512]{1,0:T(8,128)(2,1)S(1)} %get-tuple-element.89), channel_id=1, source_target_pairs={{0,12},{4,8},{8,4},{12,0},{1,13},{5,9},{9,5},{13,1},{2,14},{6,10},... | collective-permute-start | bytes 147464 | tf_op jit(solution)/shard_map/ppermute | solution.py:19
  63.0 0.7 collective-permute-start.20
  64.3 1.5 %collective-permute-start.17 = (bf16[48,512]{1,0:T(8,128)(2,1)S(1)}, bf16[48,512]{1,0:T(8,128)(2,1)S(1)}, u32[]{:S(2)}, u32[]{:S(2)}) collective-permute-start(bf16[48,512]{1,0:T(8,128)(2,1)S(1)} %get-tuple-element.87), channel_id=1, source_target_pairs={{0,4},{4,0},{8,12},{12,8},{1,5},{5,1},{9,13},{13,9},{2,6},{6,2},{1... | collective-permute-start | bytes 147464 | tf_op jit(solution)/shard_map/ppermute | solution.py:19
  65.8 0.7 collective-permute-start.21
  66.5 0.6 collective-permute-done.19
  67.1 0.7 collective-permute-start.22
  68.0 1.0 %collective-permute-done.17 = bf16[48,512]{1,0:T(8,128)(2,1)S(1)} collective-permute-done((bf16[48,512]{1,0:T(8,128)(2,1)S(1)}, bf16[48,512]{1,0:T(8,128)(2,1)S(1)}, u32[]{:S(2)}, u32[]{:S(2)}) %collective-permute-start.17) | collective-permute-done | bytes 49184 | tf_op jit(solution)/shard_map/ppermute | solution.py:19
  69.3 1.6 %collective-permute-start.23 = (bf16[128,512]{1,0:T(8,128)(2,1)S(1)}, bf16[128,512]{1,0:T(8,128)(2,1)S(1)}, u32[]{:S(2)}, u32[]{:S(2)}) collective-permute-start(bf16[128,512]{1,0:T(8,128)(2,1)S(1)} %pad_maximum_fusion.2.refs_3_), channel_id=1, source_target_pairs={{0,3},{1,2},{2,1},{3,0},{4,7},{5,6},{6,5},{7,4},{8,11},{9,10},{10,... | collective-permute-start | bytes 393224 | tf_op jit(solution)/shard_map/ppermute | solution.py:19
  70.9 2.8 %collective-permute-start.25 = (bf16[128,512]{1,0:T(8,128)(2,1)S(1)}, bf16[128,512]{1,0:T(8,128)(2,1)S(1)}, u32[]{:S(2)}, u32[]{:S(2)}) collective-permute-start(bf16[128,512]{1,0:T(8,128)(2,1)S(1)} %pad_maximum_fusion.2.refs_3_), channel_id=1, source_target_pairs={{0,1},{1,0},{2,3},{3,2},{4,5},{5,4},{6,7},{7,6},{8,9},{9,8},{10,11... | collective-permute-start | bytes 393224 | tf_op jit(solution)/shard_map/ppermute | solution.py:19
  74.1 0.7 copy-done.9
  74.8 0.8 copy-done.10
  75.6 2.7 %shard_map.98 = (bf16[512,1792]{1,0:T(8,128)(2,1)S(1)}, f32[512,512]{1,0:T(8,128)S(1)}) custom-call(s32[1]{0:T(128)} %bitcast.flag_ref, bf16[96,1792]{1,0:T(8,128)(2,1)} %copy-done.11, bf16[96,1792]{1,0:T(8,128)(2,1)} %copy-done.12, bf16[96,1792]{1,0:T(8,128)(2,1)} %copy-done.13, bf16[128,1792]{1,0:T(8,128)(2,1)} %copy-done, bf16[128,1792]{1,0:T(8,128)(2,1)} %copy-done.7, ...), custom_call_target="tpu_custom_call" | custom-call | flops 939524096 | bytes 4718592 | tf_op jit(solution)/shard_map/pallas_call | solution.py:282
  78.3 5.0 %collective-permute-done.24.refs_1_ = bf16[128,512]{1,0:T(8,128)(2,1)S(1)} collective-permute-done((bf16[128,512]{1,0:T(8,128)(2,1)S(1)}, bf16[128,512]{1,0:T(8,128)(2,1)S(1)}, u32[]{:S(2)}, u32[]{:S(2)}) %collective-permute-start.24) | collective-permute-done | bytes 131104 | tf_op jit(solution)/shard_map/ppermute | solution.py:19
  83.2 1.6 %shard_map.99 = (bf16[512,2048]{1,0:T(8,128)(2,1)S(1)}, f32[8,128]{1,0:T(8,128)S(1)}) custom-call(s32[512,1]{1,0:T(8,128)S(1)} %reshape.86.ids_ref, s32[1,512]{1,0:T(1,128)S(1)} %reshape_reshape.3.ids_row_ref, f32[512,512]{1,0:T(8,128)S(1)} %get-tuple-element.59.gram_ref, bf16[128,512]{1,0:T(8,128)(2,1)S(1)} %collective-permute-done.23.refs_0_, ...), custom_call_target="tpu_custom_call" | custom-call | flops 269484032 | bytes 2097152 | tf_op jit(solution)/shard_map/pallas_call | solution.py:341
  84.9 1.6 %collective-permute-start.26 = (f32[8,128]{1,0:T(8,128)S(1)}, f32[8,128]{1,0:T(8,128)S(1)}, u32[]{:S(2)}, u32[]{:S(2)}) collective-permute-start(f32[8,128]{1,0:T(8,128)S(1)} %get-tuple-element.62), channel_id=1, source_target_pairs={{0,3},{1,2},{2,1},{3,0},{4,7},{5,6},{6,5},{7,4},{8,11},{9,10},{10,... | collective-permute-start | bytes 12296 | tf_op jit(solution)/shard_map/ppermute | solution.py:19
  86.6 1.9 %collective-permute-start.27 = (f32[8,128]{1,0:T(8,128)S(1)}, f32[8,128]{1,0:T(8,128)S(1)}, u32[]{:S(2)}, u32[]{:S(2)}) collective-permute-start(f32[8,128]{1,0:T(8,128)S(1)} %get-tuple-element.62), channel_id=1, source_target_pairs={{0,2},{1,3},{2,0},{3,1},{4,6},{5,7},{6,4},{7,5},{8,10},{9,11},{10,... | collective-permute-start | bytes 12296 | tf_op jit(solution)/shard_map/ppermute | solution.py:19
  88.4 2.5 %shard_map.100.rest_0_ = bf16[4,1792,512]{2,1,0:T(8,128)(2,1)} custom-call(bf16[512,1792]{1,0:T(8,128)(2,1)S(1)} %get-tuple-element.58.hidden_ref, bf16[512,2048]{1,0:T(8,128)(2,1)S(1)} %get-tuple-element.65.masked_ref), custom_call_target="tpu_custom_call" | custom-call | flops 1073741824 | bytes 2621440 | tf_op jit(solution)/shard_map/pallas_call | solution.py:214
  91.1 1.5 %collective-permute-start.31 = (f32[8,128]{1,0:T(8,128)S(1)}, f32[8,128]{1,0:T(8,128)S(1)}, u32[]{:S(2)}, u32[]{:S(2)}) collective-permute-start(f32[8,128]{1,0:T(8,128)S(1)} %add_add_fusion.1), channel_id=1, source_target_pairs={{0,4},{4,0},{8,12},{12,8},{1,5},{5,1},{9,13},{13,9},{2,6},{6,2},{1... | collective-permute-start | bytes 12296 | tf_op jit(solution)/shard_map/ppermute | solution.py:19
  92.6 1.8 %collective-permute-start.29 = (f32[8,128]{1,0:T(8,128)S(1)}, f32[8,128]{1,0:T(8,128)S(1)}, u32[]{:S(2)}, u32[]{:S(2)}) collective-permute-start(f32[8,128]{1,0:T(8,128)S(1)} %add_add_fusion.1), channel_id=1, source_target_pairs={{0,12},{4,8},{8,4},{12,0},{1,13},{5,9},{9,5},{13,1},{2,14},{6,10},... | collective-permute-start | bytes 12296 | tf_op jit(solution)/shard_map/ppermute | solution.py:19
  94.6 2.5 %shard_map.101.rest_0_ = bf16[4,1792,512]{2,1,0:T(8,128)(2,1)} custom-call(bf16[512,1792]{1,0:T(8,128)(2,1)S(1)} %get-tuple-element.58.hidden_ref, bf16[512,2048]{1,0:T(8,128)(2,1)S(1)} %get-tuple-element.65.masked_ref, bf16[4,1792,512]{2,1,0:T(8,128)(2,1)} %shard_map.100.rest_0_), custom_call_target="tpu_custom_call", output_to_operand_aliasing={{}: (2, {})} | custom-call | flops 1073741824 | bytes 2621440 | tf_op jit(solution)/shard_map/pallas_call | solution.py:214
  97.1 0.9 collective-permute-done.30
  98.0 3.5 %shard_map.102 = bf16[4,1792,512]{2,1,0:T(8,128)(2,1)} custom-call(bf16[512,1792]{1,0:T(8,128)(2,1)S(1)} %get-tuple-element.58.hidden_ref, bf16[512,2048]{1,0:T(8,128)(2,1)S(1)} %get-tuple-element.65.masked_ref, bf16[4,1792,512]{2,1,0:T(8,128)(2,1)} %shard_map.101.rest_0_), custom_call_target="tpu_custom_call", output_to_operand_aliasing={{}: (2, {})} | custom-call | flops 1610612736 | bytes 3932160 | tf_op jit(solution)/shard_map/pallas_call | solution.py:214
  (102 shorter events, 5.8 us)
Async XLA Ops:
  1.6 16.4 %copy-start.14 = (f32[1,2048]{1,0:T(1,128)S(1)}, f32[1,2048]{1,0:T(1,128)}, u32[]{:S(2)}) copy-start(f32[1,2048]{1,0:T(1,128)} %param.11) | copy-start | bytes 24580
  1.6 13.2 %collective-permute-start.2 = (bf16[32,2048]{1,0:T(8,128)(2,1)S(1)}, bf16[32,2048]{1,0:T(8,128)(2,1)S(1)}, u32[]{:S(2)}, u32[]{:S(2)}) collective-permute-start(bf16[32,2048]{1,0:T(8,128)(2,1)S(1)} %bitcast_select_fusion.1), channel_id=1, source_target_pairs={{0,3},{1,2},{2,1},{3,0},{4,7},{5,6},{6,5},{7,4},{8,11},{9,10},{10,... | collective-permute-start | bytes 393224 | tf_op jit(solution)/shard_map/ppermute | solution.py:19
  6.8 11.1 %collective-permute-start.1 = (bf16[32,2048]{1,0:T(8,128)(2,1)S(1)}, bf16[32,2048]{1,0:T(8,128)(2,1)S(1)}, u32[]{:S(2)}, u32[]{:S(2)}) collective-permute-start(bf16[32,2048]{1,0:T(8,128)(2,1)S(1)} %bitcast_select_fusion.1), channel_id=1, source_target_pairs={{0,2},{1,3},{2,0},{3,1},{4,6},{5,7},{6,4},{7,5},{8,10},{9,11},{10,... | collective-permute-start | bytes 393224 | tf_op jit(solution)/shard_map/ppermute | solution.py:19
  6.8 11.1 %collective-permute-start = (bf16[32,2048]{1,0:T(8,128)(2,1)S(1)}, bf16[32,2048]{1,0:T(8,128)(2,1)S(1)}, u32[]{:S(2)}, u32[]{:S(2)}) collective-permute-start(bf16[32,2048]{1,0:T(8,128)(2,1)S(1)} %bitcast_select_fusion.1), channel_id=1, source_target_pairs={{0,1},{1,0},{2,3},{3,2},{4,5},{5,4},{6,7},{7,6},{8,9},{9,8},{10,11... | collective-permute-start | bytes 393224 | tf_op jit(solution)/shard_map/ppermute | solution.py:19
  20.6 8.2 %copy-start = (bf16[128,1792]{1,0:T(8,128)(2,1)}, bf16[128,1792]{1,0:T(8,128)(2,1)S(1)}, u32[]{:S(2)}) copy-start(bf16[128,1792]{1,0:T(8,128)(2,1)S(1)} %fusion.refs_3_) | copy-start | bytes 1376260
  21.8 8.4 %copy-start.6 = (bf16[4,8,2048]{2,1,0:T(8,128)(2,1)S(1)}, bf16[4,8,2048]{2,1,0:T(8,128)(2,1)}, u32[]{:S(2)}) copy-start(bf16[4,8,2048]{2,1,0:T(8,128)(2,1)} %param.8) | copy-start | bytes 393220
  21.9 7.0 %collective-permute-start.6 = (bf16[32,2048]{1,0:T(8,128)(2,1)S(1)}, bf16[32,2048]{1,0:T(8,128)(2,1)S(1)}, u32[]{:S(2)}, u32[]{:S(2)}) collective-permute-start(bf16[32,2048]{1,0:T(8,128)(2,1)S(1)} %get-tuple-element.78), channel_id=1, source_target_pairs={{0,19},{1,18},{2,17},{3,16},{4,23},{5,22},{6,21},{7,20},{8,27},{9,... | collective-permute-start | bytes 393224 | tf_op jit(solution)/shard_map/ppermute | solution.py:33
  24.8 4.0 %collective-permute-start.5 = (bf16[32,2048]{1,0:T(8,128)(2,1)S(1)}, bf16[32,2048]{1,0:T(8,128)(2,1)S(1)}, u32[]{:S(2)}, u32[]{:S(2)}) collective-permute-start(bf16[32,2048]{1,0:T(8,128)(2,1)S(1)} %get-tuple-element.79), channel_id=1, source_target_pairs={{0,18},{1,19},{2,16},{3,17},{4,22},{5,23},{6,20},{7,21},{8,26},{9,... | collective-permute-start | bytes 393224 | tf_op jit(solution)/shard_map/ppermute | solution.py:33
  26.1 4.0 %collective-permute-start.4 = (bf16[32,2048]{1,0:T(8,128)(2,1)S(1)}, bf16[32,2048]{1,0:T(8,128)(2,1)S(1)}, u32[]{:S(2)}, u32[]{:S(2)}) collective-permute-start(bf16[32,2048]{1,0:T(8,128)(2,1)S(1)} %get-tuple-element.80), channel_id=1, source_target_pairs={{0,17},{1,16},{2,19},{3,18},{4,21},{5,20},{6,23},{7,22},{8,25},{9,... | collective-permute-start | bytes 393224 | tf_op jit(solution)/shard_map/ppermute | solution.py:33
  27.4 2.7 %collective-permute-start.3 = (bf16[32,2048]{1,0:T(8,128)(2,1)S(1)}, bf16[32,2048]{1,0:T(8,128)(2,1)S(1)}, u32[]{:S(2)}, u32[]{:S(2)}) collective-permute-start(bf16[32,2048]{1,0:T(8,128)(2,1)S(1)} %get-tuple-element.77), channel_id=1, source_target_pairs={{0,16},{1,17},{2,18},{3,19},{4,20},{5,21},{6,22},{7,23},{8,24},{9,... | collective-permute-start | bytes 393224 | tf_op jit(solution)/shard_map/ppermute | solution.py:33
  28.8 5.1 %copy-start.1 = (bf16[128,1792]{1,0:T(8,128)(2,1)S(1)}, bf16[128,1792]{1,0:T(8,128)(2,1)}, u32[]{:S(2)}) copy-start(bf16[128,1792]{1,0:T(8,128)(2,1)} %copy-done) | copy-start | bytes 1376260
  30.3 10.4 %collective-permute-start.9 = (bf16[32,2048]{1,0:T(8,128)(2,1)S(1)}, bf16[32,2048]{1,0:T(8,128)(2,1)S(1)}, u32[]{:S(2)}, u32[]{:S(2)}) collective-permute-start(bf16[32,2048]{1,0:T(8,128)(2,1)S(1)} %pad_select_fusion), channel_id=1, source_target_pairs={{0,12},{16,19},{1,13},{17,18},{2,14},{18,17},{3,15},{19,16},{4,8},... | collective-permute-start | bytes 393224 | tf_op jit(solution)/shard_map/ppermute | solution.py:53
  32.8 10.3 %collective-permute-start.8 = (bf16[32,2048]{1,0:T(8,128)(2,1)S(1)}, bf16[32,2048]{1,0:T(8,128)(2,1)S(1)}, u32[]{:S(2)}, u32[]{:S(2)}) collective-permute-start(bf16[32,2048]{1,0:T(8,128)(2,1)S(1)} %pad_select_fusion), channel_id=1, source_target_pairs={{0,8},{16,18},{1,9},{17,19},{2,10},{18,16},{3,11},{19,17},{4,12},{... | collective-permute-start | bytes 393224 | tf_op jit(solution)/shard_map/ppermute | solution.py:53
  33.3 9.8 %collective-permute-start.7 = (bf16[32,2048]{1,0:T(8,128)(2,1)S(1)}, bf16[32,2048]{1,0:T(8,128)(2,1)S(1)}, u32[]{:S(2)}, u32[]{:S(2)}) collective-permute-start(bf16[32,2048]{1,0:T(8,128)(2,1)S(1)} %pad_select_fusion), channel_id=1, source_target_pairs={{0,4},{16,17},{1,5},{17,16},{2,6},{18,19},{3,7},{19,18},{4,0},{20,... | collective-permute-start | bytes 393224 | tf_op jit(solution)/shard_map/ppermute | solution.py:53
  33.9 13.0 %collective-permute-start.10 = (bf16[96,1792]{1,0:T(8,128)(2,1)S(1)}, bf16[96,1792]{1,0:T(8,128)(2,1)S(1)}, u32[]{:S(2)}, u32[]{:S(2)}) collective-permute-start(bf16[96,1792]{1,0:T(8,128)(2,1)S(1)} %slice.61), channel_id=1, source_target_pairs={{0,12},{4,8},{8,4},{12,0},{1,13},{5,9},{9,5},{13,1},{2,14},{6,10},... | collective-permute-start | bytes 1032200 | tf_op jit(solution)/shard_map/ppermute | solution.py:25
  38.2 9.4 %collective-permute-start.11 = (bf16[96,1792]{1,0:T(8,128)(2,1)S(1)}, bf16[96,1792]{1,0:T(8,128)(2,1)S(1)}, u32[]{:S(2)}, u32[]{:S(2)}) collective-permute-start(bf16[96,1792]{1,0:T(8,128)(2,1)S(1)} %slice.61), channel_id=1, source_target_pairs={{0,8},{4,12},{8,0},{12,4},{1,9},{5,13},{9,1},{13,5},{2,10},{6,14},... | collective-permute-start | bytes 1032200 | tf_op jit(solution)/shard_map/ppermute | solution.py:25
  40.7 6.0 %copy-start.2 = (bf16[32,2048]{1,0:T(8,128)(2,1)}, bf16[32,2048]{1,0:T(8,128)(2,1)S(1)}, u32[]{:S(2)}) copy-start(bf16[32,2048]{1,0:T(8,128)(2,1)S(1)} %collective-permute-done.9.refs_10_) | copy-start | bytes 393220
  40.7 9.1 %collective-permute-start.12 = (bf16[96,1792]{1,0:T(8,128)(2,1)S(1)}, bf16[96,1792]{1,0:T(8,128)(2,1)S(1)}, u32[]{:S(2)}, u32[]{:S(2)}) collective-permute-start(bf16[96,1792]{1,0:T(8,128)(2,1)S(1)} %slice.61), channel_id=1, source_target_pairs={{0,4},{4,0},{8,12},{12,8},{1,5},{5,1},{9,13},{13,9},{2,6},{6,2},{1... | collective-permute-start | bytes 1032200 | tf_op jit(solution)/shard_map/ppermute | solution.py:25
  43.1 3.5 %copy-start.3 = (bf16[32,2048]{1,0:T(8,128)(2,1)}, bf16[32,2048]{1,0:T(8,128)(2,1)S(1)}, u32[]{:S(2)}) copy-start(bf16[32,2048]{1,0:T(8,128)(2,1)S(1)} %collective-permute-done.8.refs_9_) | copy-start | bytes 393220
  43.2 3.5 %copy-start.4 = (bf16[32,2048]{1,0:T(8,128)(2,1)}, bf16[32,2048]{1,0:T(8,128)(2,1)S(1)}, u32[]{:S(2)}) copy-start(bf16[32,2048]{1,0:T(8,128)(2,1)S(1)} %collective-permute-done.7.refs_8_) | copy-start | bytes 393220
  46.1 21.0 %copy-start.7 = (bf16[128,1792]{1,0:T(8,128)(2,1)}, bf16[128,1792]{1,0:T(8,128)(2,1)S(1)}, u32[]{:S(2)}) copy-start(bf16[128,1792]{1,0:T(8,128)(2,1)S(1)} %get-tuple-element.57.refs_4_) | copy-start | bytes 1376260
  46.1 9.0 %copy-start.16 = (s32[4,1]{0,1:T(1,128)S(1)}, s32[4,1]{0,1:T(1,128)}, u32[]{:S(2)}) copy-start(s32[4,1]{0,1:T(1,128)} %param.10) | copy-start | bytes 52
  46.1 15.1 %copy-start.5 = (bf16[4,8,2048]{2,1,0:T(8,128)(2,1)S(1)}, bf16[4,8,2048]{2,1,0:T(8,128)(2,1)}, u32[]{:S(2)}) copy-start(bf16[4,8,2048]{2,1,0:T(8,128)(2,1)} %param.9) | copy-start | bytes 393220
  46.9 27.2 %copy-start.11 = (bf16[96,1792]{1,0:T(8,128)(2,1)}, bf16[96,1792]{1,0:T(8,128)(2,1)S(1)}, u32[]{:S(2)}) copy-start(bf16[96,1792]{1,0:T(8,128)(2,1)S(1)} %collective-permute-done.10.refs_0_) | copy-start | bytes 1032196
  47.6 26.5 %copy-start.12 = (bf16[96,1792]{1,0:T(8,128)(2,1)}, bf16[96,1792]{1,0:T(8,128)(2,1)S(1)}, u32[]{:S(2)}) copy-start(bf16[96,1792]{1,0:T(8,128)(2,1)S(1)} %collective-permute-done.11.refs_1_) | copy-start | bytes 1032196
  49.8 14.5 %copy-start.13 = (bf16[96,1792]{1,0:T(8,128)(2,1)}, bf16[96,1792]{1,0:T(8,128)(2,1)S(1)}, u32[]{:S(2)}) copy-start(bf16[96,1792]{1,0:T(8,128)(2,1)S(1)} %collective-permute-done.12.refs_2_) | copy-start | bytes 1032196
  49.9 8.3 %collective-permute-start.16 = (bf16[32,2048]{1,0:T(8,128)(2,1)S(1)}, bf16[32,2048]{1,0:T(8,128)(2,1)S(1)}, u32[]{:S(2)}, u32[]{:S(2)}) collective-permute-start(bf16[32,2048]{1,0:T(8,128)(2,1)S(1)} %get-tuple-element.74), channel_id=1, source_target_pairs={{16,3},{17,2},{18,1},{19,0},{20,7},{21,6},{22,5},{23,4},{24,11},{2... | collective-permute-start | bytes 393224 | tf_op jit(solution)/shard_map/ppermute | solution.py:33
  51.2 10.1 %collective-permute-start.15 = (bf16[32,2048]{1,0:T(8,128)(2,1)S(1)}, bf16[32,2048]{1,0:T(8,128)(2,1)S(1)}, u32[]{:S(2)}, u32[]{:S(2)}) collective-permute-start(bf16[32,2048]{1,0:T(8,128)(2,1)S(1)} %get-tuple-element.75), channel_id=1, source_target_pairs={{16,2},{17,3},{18,0},{19,1},{20,6},{21,7},{22,4},{23,5},{24,10},{2... | collective-permute-start | bytes 393224 | tf_op jit(solution)/shard_map/ppermute | solution.py:33
  52.5 8.8 %collective-permute-start.14 = (bf16[32,2048]{1,0:T(8,128)(2,1)S(1)}, bf16[32,2048]{1,0:T(8,128)(2,1)S(1)}, u32[]{:S(2)}, u32[]{:S(2)}) collective-permute-start(bf16[32,2048]{1,0:T(8,128)(2,1)S(1)} %get-tuple-element.76), channel_id=1, source_target_pairs={{16,1},{17,0},{18,3},{19,2},{20,5},{21,4},{22,7},{23,6},{24,9},{25... | collective-permute-start | bytes 393224 | tf_op jit(solution)/shard_map/ppermute | solution.py:33
  53.8 4.4 %collective-permute-start.13 = (bf16[32,2048]{1,0:T(8,128)(2,1)S(1)}, bf16[32,2048]{1,0:T(8,128)(2,1)S(1)}, u32[]{:S(2)}, u32[]{:S(2)}) collective-permute-start(bf16[32,2048]{1,0:T(8,128)(2,1)S(1)} %get-tuple-element.73), channel_id=1, source_target_pairs={{16,0},{17,1},{18,2},{19,3},{20,4},{21,5},{22,6},{23,7},{24,8},{25... | collective-permute-start | bytes 393224 | tf_op jit(solution)/shard_map/ppermute | solution.py:33
  61.5 5.6 %collective-permute-start.19 = (bf16[48,512]{1,0:T(8,128)(2,1)S(1)}, bf16[48,512]{1,0:T(8,128)(2,1)S(1)}, u32[]{:S(2)}, u32[]{:S(2)}) collective-permute-start(bf16[48,512]{1,0:T(8,128)(2,1)S(1)} %get-tuple-element.89), channel_id=1, source_target_pairs={{0,12},{4,8},{8,4},{12,0},{1,13},{5,9},{9,5},{13,1},{2,14},{6,10},... | collective-permute-start | bytes 147464 | tf_op jit(solution)/shard_map/ppermute | solution.py:19
  63.0 6.2 %collective-permute-start.20 = (bf16[128,1792]{1,0:T(8,128)(2,1)S(1)}, bf16[128,1792]{1,0:T(8,128)(2,1)S(1)}, u32[]{:S(2)}, u32[]{:S(2)}) collective-permute-start(bf16[128,1792]{1,0:T(8,128)(2,1)S(1)} %get-tuple-element.57.refs_4_), channel_id=1, source_target_pairs={{16,20},{20,16},{24,28},{28,24},{17,21},{21,17},{25,29},{29,25},{1... | collective-permute-start | bytes 1376264 | tf_op jit(solution)/shard_map/ppermute | solution.py:25
  63.7 4.2 %collective-permute-start.18 = (bf16[48,512]{1,0:T(8,128)(2,1)S(1)}, bf16[48,512]{1,0:T(8,128)(2,1)S(1)}, u32[]{:S(2)}, u32[]{:S(2)}) collective-permute-start(bf16[48,512]{1,0:T(8,128)(2,1)S(1)} %get-tuple-element.88), channel_id=1, source_target_pairs={{0,8},{4,12},{8,0},{12,4},{1,9},{5,13},{9,1},{13,5},{2,10},{6,14},... | collective-permute-start | bytes 147464 | tf_op jit(solution)/shard_map/ppermute | solution.py:19
  64.3 4.7 %collective-permute-start.17 = (bf16[48,512]{1,0:T(8,128)(2,1)S(1)}, bf16[48,512]{1,0:T(8,128)(2,1)S(1)}, u32[]{:S(2)}, u32[]{:S(2)}) collective-permute-start(bf16[48,512]{1,0:T(8,128)(2,1)S(1)} %get-tuple-element.87), channel_id=1, source_target_pairs={{0,4},{4,0},{8,12},{12,8},{1,5},{5,1},{9,13},{13,9},{2,6},{6,2},{1... | collective-permute-start | bytes 147464 | tf_op jit(solution)/shard_map/ppermute | solution.py:19
  65.8 8.3 %collective-permute-start.21 = (bf16[128,1792]{1,0:T(8,128)(2,1)S(1)}, bf16[128,1792]{1,0:T(8,128)(2,1)S(1)}, u32[]{:S(2)}, u32[]{:S(2)}) collective-permute-start(bf16[128,1792]{1,0:T(8,128)(2,1)S(1)} %get-tuple-element.57.refs_4_), channel_id=1, source_target_pairs={{16,24},{20,28},{24,16},{28,20},{17,25},{21,29},{25,17},{29,21},{1... | collective-permute-start | bytes 1376264 | tf_op jit(solution)/shard_map/ppermute | solution.py:25
  67.1 6.9 %collective-permute-start.22 = (bf16[128,1792]{1,0:T(8,128)(2,1)S(1)}, bf16[128,1792]{1,0:T(8,128)(2,1)S(1)}, u32[]{:S(2)}, u32[]{:S(2)}) collective-permute-start(bf16[128,1792]{1,0:T(8,128)(2,1)S(1)} %get-tuple-element.57.refs_4_), channel_id=1, source_target_pairs={{16,28},{20,24},{24,20},{28,16},{17,29},{21,25},{25,21},{29,17},{1... | collective-permute-start | bytes 1376264 | tf_op jit(solution)/shard_map/ppermute | solution.py:25
  69.2 4.8 %copy-start.8 = (bf16[128,1792]{1,0:T(8,128)(2,1)}, bf16[128,1792]{1,0:T(8,128)(2,1)S(1)}, u32[]{:S(2)}) copy-start(bf16[128,1792]{1,0:T(8,128)(2,1)S(1)} %collective-permute-done.20.refs_5_) | copy-start | bytes 1376260
  69.3 9.0 %collective-permute-start.23 = (bf16[128,512]{1,0:T(8,128)(2,1)S(1)}, bf16[128,512]{1,0:T(8,128)(2,1)S(1)}, u32[]{:S(2)}, u32[]{:S(2)}) collective-permute-start(bf16[128,512]{1,0:T(8,128)(2,1)S(1)} %pad_maximum_fusion.2.refs_3_), channel_id=1, source_target_pairs={{0,3},{1,2},{2,1},{3,0},{4,7},{5,6},{6,5},{7,4},{8,11},{9,10},{10,... | collective-permute-start | bytes 393224 | tf_op jit(solution)/shard_map/ppermute | solution.py:19
  70.9 12.3 %collective-permute-start.24 = (bf16[128,512]{1,0:T(8,128)(2,1)S(1)}, bf16[128,512]{1,0:T(8,128)(2,1)S(1)}, u32[]{:S(2)}, u32[]{:S(2)}) collective-permute-start(bf16[128,512]{1,0:T(8,128)(2,1)S(1)} %pad_maximum_fusion.2.refs_3_), channel_id=1, source_target_pairs={{0,2},{1,3},{2,0},{3,1},{4,6},{5,7},{6,4},{7,5},{8,10},{9,11},{10,... | collective-permute-start | bytes 393224 | tf_op jit(solution)/shard_map/ppermute | solution.py:19
  70.9 12.3 %collective-permute-start.25 = (bf16[128,512]{1,0:T(8,128)(2,1)S(1)}, bf16[128,512]{1,0:T(8,128)(2,1)S(1)}, u32[]{:S(2)}, u32[]{:S(2)}) collective-permute-start(bf16[128,512]{1,0:T(8,128)(2,1)S(1)} %pad_maximum_fusion.2.refs_3_), channel_id=1, source_target_pairs={{0,1},{1,0},{2,3},{3,2},{4,5},{5,4},{6,7},{7,6},{8,9},{9,8},{10,11... | collective-permute-start | bytes 393224 | tf_op jit(solution)/shard_map/ppermute | solution.py:19
  84.9 6.1 %collective-permute-start.28 = (f32[8,128]{1,0:T(8,128)S(1)}, f32[8,128]{1,0:T(8,128)S(1)}, u32[]{:S(2)}, u32[]{:S(2)}) collective-permute-start(f32[8,128]{1,0:T(8,128)S(1)} %get-tuple-element.62), channel_id=1, source_target_pairs={{0,1},{1,0},{2,3},{3,2},{4,5},{5,4},{6,7},{7,6},{8,9},{9,8},{10,11... | collective-permute-start | bytes 12296 | tf_op jit(solution)/shard_map/ppermute | solution.py:19
  84.9 6.0 %collective-permute-start.26 = (f32[8,128]{1,0:T(8,128)S(1)}, f32[8,128]{1,0:T(8,128)S(1)}, u32[]{:S(2)}, u32[]{:S(2)}) collective-permute-start(f32[8,128]{1,0:T(8,128)S(1)} %get-tuple-element.62), channel_id=1, source_target_pairs={{0,3},{1,2},{2,1},{3,0},{4,7},{5,6},{6,5},{7,4},{8,11},{9,10},{10,... | collective-permute-start | bytes 12296 | tf_op jit(solution)/shard_map/ppermute | solution.py:19
  86.6 4.5 %collective-permute-start.27 = (f32[8,128]{1,0:T(8,128)S(1)}, f32[8,128]{1,0:T(8,128)S(1)}, u32[]{:S(2)}, u32[]{:S(2)}) collective-permute-start(f32[8,128]{1,0:T(8,128)S(1)} %get-tuple-element.62), channel_id=1, source_target_pairs={{0,2},{1,3},{2,0},{3,1},{4,6},{5,7},{6,4},{7,5},{8,10},{9,11},{10,... | collective-permute-start | bytes 12296 | tf_op jit(solution)/shard_map/ppermute | solution.py:19
  91.1 6.0 %collective-permute-start.31 = (f32[8,128]{1,0:T(8,128)S(1)}, f32[8,128]{1,0:T(8,128)S(1)}, u32[]{:S(2)}, u32[]{:S(2)}) collective-permute-start(f32[8,128]{1,0:T(8,128)S(1)} %add_add_fusion.1), channel_id=1, source_target_pairs={{0,4},{4,0},{8,12},{12,8},{1,5},{5,1},{9,13},{13,9},{2,6},{6,2},{1... | collective-permute-start | bytes 12296 | tf_op jit(solution)/shard_map/ppermute | solution.py:19
  92.6 4.5 %collective-permute-start.29 = (f32[8,128]{1,0:T(8,128)S(1)}, f32[8,128]{1,0:T(8,128)S(1)}, u32[]{:S(2)}, u32[]{:S(2)}) collective-permute-start(f32[8,128]{1,0:T(8,128)S(1)} %add_add_fusion.1), channel_id=1, source_target_pairs={{0,12},{4,8},{8,4},{12,0},{1,13},{5,9},{9,5},{13,1},{2,14},{6,10},... | collective-permute-start | bytes 12296 | tf_op jit(solution)/shard_map/ppermute | solution.py:19
  94.4 3.6 %collective-permute-start.30 = (f32[8,128]{1,0:T(8,128)S(1)}, f32[8,128]{1,0:T(8,128)S(1)}, u32[]{:S(2)}, u32[]{:S(2)}) collective-permute-start(f32[8,128]{1,0:T(8,128)S(1)} %add_add_fusion.1), channel_id=1, source_target_pairs={{0,8},{4,12},{8,0},{12,4},{1,9},{5,13},{9,1},{13,5},{2,10},{6,14},... | collective-permute-start | bytes 12296 | tf_op jit(solution)/shard_map/ppermute | solution.py:19
  98.0 3.5 %copy-start.15 = (f32[3]{0:T(128)S(1)}, f32[3]{0:T(128)}, u32[]{:S(2)}) copy-start(f32[3]{0:T(128)} %constant.52) | copy-start | bytes 40
  98.0 3.5 %collective-permute-start.32 = (f32[8,128]{1,0:T(8,128)S(1)}, f32[8,128]{1,0:T(8,128)S(1)}, u32[]{:S(2)}, u32[]{:S(2)}) collective-permute-start(f32[8,128]{1,0:T(8,128)S(1)} %add_add_fusion), channel_id=1, source_target_pairs={{0,16},{16,0},{1,17},{17,1},{2,18},{18,2},{3,19},{19,3},{4,20},{20... | collective-permute-start | bytes 12296 | tf_op jit(solution)/shard_map/ppermute | solution.py:19
  (3 other events, 3.0 us)

commit v10 on v9

--- a/solution.py
+++ b/solution.py
@@ -51,6 +51,16 @@
 
     axes = ("section", "dp", "tensor")
     return [rows] + [lax.ppermute(rows, axes, route(k)) for k in range(1, tensor_size)]
+
+
+def exchange(block, k):
+    dp_size, tensor_size = lax.axis_size("dp"), lax.axis_size("tensor")
+    pairs = []
+    for d in range(dp_size):
+        for t in range(tensor_size):
+            pairs.append((d * tensor_size + t, d * tensor_size + (t ^ k)))
+            pairs.append(((dp_size + d) * tensor_size + t, (dp_size + (d ^ k)) * tensor_size + t))
+    return lax.ppermute(block, ("section", "dp", "tensor"), pairs)
 
 
 def gather(rows, axis):
@@ -300,17 +310,28 @@
     )(segment.reshape(1), *pieces)
 
 
-def norms_kernel(replicas, levels, ids_ref, ids_row_ref, gram_ref, *refs):
+def norms_kernel(replicas, levels, flag_ref, ids_ref, ids_row_ref, gram_ref, *refs):
     *parts, masked_ref, norms_ref, y_ref, acc = refs
     parts.reverse()
     piece = y_ref.shape[1]
     block = parts[0].shape[0] // replicas
     tok_rows = block * len(parts)
-    for t, part in enumerate(parts):
-        for k in range(replicas):
-            y_ref[k * tok_rows + t * block : k * tok_rows + (t + 1) * block, :] = part[
-                k * block : (k + 1) * block, :
-            ]
+
+    @pl.when(flag_ref[0] == 0)
+    def _():
+        for t, part in enumerate(parts):
+            for k in range(replicas):
+                y_ref[k * tok_rows + t * block : k * tok_rows + (t + 1) * block, :] = part[
+                    k * block : (k + 1) * block, :
+                ]
+
+    if len(parts) == replicas:
+
+        @pl.when(flag_ref[0] == 1)
+        def _():
+            for k, part in enumerate(parts):
+                y_ref[k * tok_rows : (k + 1) * tok_rows, :] = part[...]
+
     for e in range(DOMAINS):
         masked_ref[:, e * piece : (e + 1) * piece] = jnp.where(
             ids_ref[...] == e, y_ref[...].astype(jnp.float32), 0.0
@@ -335,12 +356,13 @@
     norms_ref[DOMAINS:, :] = jnp.zeros_like(norms_ref[DOMAINS:, :])
 
 
-def norm_sums(row_ids, gram_hidden, parts, replicas, levels):
+def norm_sums(by_dp, row_ids, gram_hidden, parts, replicas, levels):
     total = gram_hidden.shape[0]
     piece = parts[0].shape[1]
     return pl.pallas_call(
         functools.partial(norms_kernel, replicas, levels),
-        in_specs=[pl.BlockSpec(memory_space=pltpu.VMEM)] * (3 + len(parts)),
+        in_specs=[pl.BlockSpec(memory_space=pltpu.SMEM)]
+        + [pl.BlockSpec(memory_space=pltpu.VMEM)] * (3 + len(parts)),
         out_specs=[pl.BlockSpec(memory_space=pltpu.VMEM)] * 2,
         out_shape=[
             pltpu.VMEM((total, DOMAINS * piece), jnp.bfloat16),
@@ -358,7 +380,7 @@
             bytes_accessed=4 * total * piece + 4 * total * total,
             transcendentals=0,
         ),
-    )(row_ids, row_ids.reshape(1, total), gram_hidden, *reversed(parts))
+    )(by_dp.reshape(1), row_ids, row_ids.reshape(1, total), gram_hidden, *reversed(parts))
 
 
 def shards(layer_input_activations, cotangent, domain_ids, norm_gain, w_gate, w_up, w_down):
@@ -427,14 +449,23 @@
         messages.append(part if k == 0 else swap(part, "dp", k))
     columns = jnp.concatenate([message[:block] for message in messages], axis=0)
     columns, pieces1[1] = lax.optimization_barrier((columns, pieces1[1]))
-    parts_y = gather(columns, "tensor")
+    if dp_size == tensor_size:
+        by_dp = segment
+        parts_y = []
+        for k in range(dp_size):
+            part = lax.dynamic_slice_in_dim(cot_rows, (dp_index ^ k) * piece, piece, axis=1)
+            part = jnp.where(first, columns, part)
+            parts_y.append(part if k == 0 else exchange(part, k))
+    else:
+        by_dp = jnp.zeros_like(segment)
+        parts_y = gather(columns, "tensor")
     hidden_all, gram_hidden = assemble(segment, pieces0, pieces1, heads)
     ids_all = jnp.stack([message[block : block + micro, 0] for message in messages])
     row_ids = jnp.broadcast_to(
         ids_all.astype(jnp.int32)[:, None, :, None], (dp_size, tensor_size, micro, local_rows)
     ).reshape(dp_size * tok_rows, 1)
     levels = dp_size.bit_length()
-    masked, norms = norm_sums(row_ids, gram_hidden, parts_y, dp_size, levels)
+    masked, norms = norm_sums(by_dp, row_ids, gram_hidden, parts_y, dp_size, levels)
     rounds = [
         (axis, bit, min(2, bits(axis) - bit))
         for axis in ("tensor", "dp", "section")

time: 103 us -> 102 us (level)
  waiting for transfers between devices: 20.9 us -> 16.3 us
  starting transfers between devices: 47.7 us -> 50.5 us
    ppermute x16 -> x13, waiting for transfers between devices: 10.7 us -> 5.2 us  [swap(): return lax.ppermute(block, axis, [(i, i ^ offset) for i in range(size)])]
    ppermute x0 -> x3, starting transfers between devices: none -> 4.39 us  [exchange(): return lax.ppermute(block, ('section', 'dp', 'tensor'), pairs)]
    ppermute x16 -> x13, starting transfers between devices: 20.9 us -> 19.3 us  [swap(): return lax.ppermute(block, axis, [(i, i ^ offset) for i in range(size)])]
  transfers between devices with their start and end apart: 33 -> 33, of which waited for: 11 -> 11; matrix products, arithmetic and copies ran while one was open for 4% -> 5% of each run, Pallas kernels for 19% -> 19%
where the time goes in v10:
time: 102 us; the launch traced here: 101 us
  starting transfers between devices  50.5 us (50%)
  Pallas kernels  20.7 us (20%)
  waiting for transfers between devices  16.3 us (16%)
  matrix products  6.38 us (6%)
  other arithmetic  3.67 us (4%)
  local copies, waits for them, and re-layouts  2.44 us (2%)
  between operations  1.26 us (1%)
    ppermute x13, starting transfers between devices, swap(): return lax.ppermute(block, axis, [(i, i ^ offset) for i in range(size)])  19.3 us
    ppermute x8, starting transfers between devices, across(): return lax.ppermute(block, ('section', 'tensor'), route)  12 us
    ppermute x6, starting transfers between devices, swap_in(): return lax.ppermute(block, ('section', axis), route)  11.3 us
    pallas_call x3, Pallas kernels, domain_gradients(): pl.pallas_call(gradient_kernel, grid=(count,), in_specs=in_specs, out_spe...  8.48 us
    pallas_call x1, Pallas kernels, load_weights(): pl.pallas_call(load_kernel, in_specs=[pl.BlockSpec(memory_space=pltpu.HBM...  7.46 us
    ppermute x8, waiting for transfers between devices, across(): return lax.ppermute(block, ('section', 'tensor'), route)  7.31 us
    ppermute x13, waiting for transfers between devices, swap(): return lax.ppermute(block, axis, [(i, i ^ offset) for i in range(size)])  5.2 us
    ppermute x3, starting transfers between devices, exchange(): return lax.ppermute(block, ('section', 'dp', 'tensor'), pairs)  4.39 us
  transfers between devices with their start and end apart: 33, of which 11 were waited for; matrix products, arithmetic and copies ran while one was open for 5% of the time, Pallas kernels for 19%

profile of v10, /device:TPU:0, one launch (start us, length us, event | category | flops | bytes accessed | tf_op | source)
XLA Modules:
  0.0 101.1 jit_solution(6922464852035364754)
XLA Ops:
  0.6 1.0 bitcast_select_fusion.1
  1.6 5.1 %collective-permute-start.2 = (bf16[32,2048]{1,0:T(8,128)(2,1)S(1)}, bf16[32,2048]{1,0:T(8,128)(2,1)S(1)}, u32[]{:S(2)}, u32[]{:S(2)}) collective-permute-start(bf16[32,2048]{1,0:T(8,128)(2,1)S(1)} %bitcast_select_fusion.1), channel_id=1, source_target_pairs={{0,3},{1,2},{2,1},{3,0},{4,7},{5,6},{6,5},{7,4},{8,11},{9,10},{10,... | collective-permute-start | bytes 393224 | tf_op jit(solution)/shard_map/ppermute | solution.py:19
  7.4 7.5 %shard_map.95 = (bf16[2048,1792]{1,0:T(8,128)(2,1)S(1)}, bf16[2048,1792]{1,0:T(8,128)(2,1)S(1)}, bf16[1792,2048]{1,0:T(8,128)(2,1)S(1)}, bf16[1792,2048]{1,0:T(8,128)(2,1)S(1)}) custom-call(bf16[1,2048,1792]{2,1,0:T(8,128)(2,1)} %gate_in.1, bf16[1,2048,1792]{2,1,0:T(8,128)(2,1)} %up_in.1, bf16[1,1792,2048]{2,1,0:T(8,128)(2,1)} %down_in.1), custom_call_target="tpu_custom_call" | custom-call | bytes 22020096 | tf_op jit(solution)/shard_map/pallas_call | solution.py:118
  14.9 3.0 %collective-permute-done.1 = bf16[32,2048]{1,0:T(8,128)(2,1)S(1)} collective-permute-done((bf16[32,2048]{1,0:T(8,128)(2,1)S(1)}, bf16[32,2048]{1,0:T(8,128)(2,1)S(1)}, u32[]{:S(2)}, u32[]{:S(2)}) %collective-permute-start.1) | collective-permute-done | bytes 131104 | tf_op jit(solution)/shard_map/ppermute | solution.py:19
  18.0 1.2 %fusion.15 = f32[128,1792]{1,0:T(8,128)S(1)} fusion(bf16[2048,1792]{1,0:T(8,128)(2,1)S(1)} %get-tuple-element.35, bf16[128,2048]{1,0:T(8,128)(2,1)S(1)} %get-tuple-element.41.rows_ref, f32[2048]{0:T(1024)S(1)} %bitcast.24, f32[128]{0:T(128)S(1)} %add_rsqrt_fusion.1), kind=kOutput, calls=%fused_computation.28 | convolution fusion | flops 940572672 | bytes 8790528 | tf_op jit(solution)/shard_map/dot_general | solution.py:409
  19.2 1.3 %fusion.refs_3_ = bf16[128,1792]{1,0:T(8,128)(2,1)S(1)} fusion(bf16[2048,1792]{1,0:T(8,128)(2,1)S(1)} %get-tuple-element.36.up_ref, f32[128,1792]{1,0:T(8,128)S(1)} %fusion.15, bf16[128,2048]{1,0:T(8,128)(2,1)S(1)} %get-tuple-element.41.rows_ref, f32[2048]{0:T(1024)S(1)} %bitcast.25, f32[128]{0:T(128)S(1)} %add_rsqrt_fusion.1), kind=kOutput, calls=%fused_computation.1 | convolution fusion | flops 941948928 | bytes 9249280 | tf_op jit(solution)/shard_map/dot_general | solution.py:410
  20.6 1.2 %convolution_convert_fusion = bf16[128,2048]{1,0:T(8,128)(2,1)S(1)} fusion(bf16[128,1792]{1,0:T(8,128)(2,1)S(1)} %fusion.refs_3_, bf16[1792,2048]{1,0:T(8,128)(2,1)S(1)} %get-tuple-element.37.down_ref), kind=kOutput, calls=%fused_computation.2 | convolution fusion | flops 939786240 | bytes 8323072 | tf_op jit(solution)/shard_map/dot_general | solution.py:415
  21.8 3.0 %collective-permute-start.6 = (bf16[32,2048]{1,0:T(8,128)(2,1)S(1)}, bf16[32,2048]{1,0:T(8,128)(2,1)S(1)}, u32[]{:S(2)}, u32[]{:S(2)}) collective-permute-start(bf16[32,2048]{1,0:T(8,128)(2,1)S(1)} %get-tuple-element.82), channel_id=1, source_target_pairs={{0,19},{1,18},{2,17},{3,16},{4,23},{5,22},{6,21},{7,20},{8,27},{9,... | collective-permute-start | bytes 393224 | tf_op jit(solution)/shard_map/ppermute | solution.py:33
  24.8 1.3 %collective-permute-start.5 = (bf16[32,2048]{1,0:T(8,128)(2,1)S(1)}, bf16[32,2048]{1,0:T(8,128)(2,1)S(1)}, u32[]{:S(2)}, u32[]{:S(2)}) collective-permute-start(bf16[32,2048]{1,0:T(8,128)(2,1)S(1)} %get-tuple-element.83), channel_id=1, source_target_pairs={{0,18},{1,19},{2,16},{3,17},{4,22},{5,23},{6,20},{7,21},{8,26},{9,... | collective-permute-start | bytes 393224 | tf_op jit(solution)/shard_map/ppermute | solution.py:33
  26.1 1.3 %collective-permute-start.4 = (bf16[32,2048]{1,0:T(8,128)(2,1)S(1)}, bf16[32,2048]{1,0:T(8,128)(2,1)S(1)}, u32[]{:S(2)}, u32[]{:S(2)}) collective-permute-start(bf16[32,2048]{1,0:T(8,128)(2,1)S(1)} %get-tuple-element.84), channel_id=1, source_target_pairs={{0,17},{1,16},{2,19},{3,18},{4,21},{5,20},{6,23},{7,22},{8,25},{9,... | collective-permute-start | bytes 393224 | tf_op jit(solution)/shard_map/ppermute | solution.py:33
  27.4 1.3 %collective-permute-start.3 = (bf16[32,2048]{1,0:T(8,128)(2,1)S(1)}, bf16[32,2048]{1,0:T(8,128)(2,1)S(1)}, u32[]{:S(2)}, u32[]{:S(2)}) collective-permute-start(bf16[32,2048]{1,0:T(8,128)(2,1)S(1)} %get-tuple-element.81), channel_id=1, source_target_pairs={{0,16},{1,17},{2,18},{3,19},{4,20},{5,21},{6,22},{7,23},{8,24},{9,... | collective-permute-start | bytes 393224 | tf_op jit(solution)/shard_map/ppermute | solution.py:33
  28.8 1.3 %collective-permute-done.4 = bf16[32,2048]{1,0:T(8,128)(2,1)S(1)} collective-permute-done((bf16[32,2048]{1,0:T(8,128)(2,1)S(1)}, bf16[32,2048]{1,0:T(8,128)(2,1)S(1)}, u32[]{:S(2)}, u32[]{:S(2)}) %collective-permute-start.4) | collective-permute-done | bytes 131104 | tf_op jit(solution)/shard_map/ppermute | solution.py:33
  30.3 2.5 %collective-permute-start.9 = (bf16[32,2048]{1,0:T(8,128)(2,1)S(1)}, bf16[32,2048]{1,0:T(8,128)(2,1)S(1)}, u32[]{:S(2)}, u32[]{:S(2)}) collective-permute-start(bf16[32,2048]{1,0:T(8,128)(2,1)S(1)} %pad_select_fusion), channel_id=1, source_target_pairs={{0,12},{16,19},{1,13},{17,18},{2,14},{18,17},{3,15},{19,16},{4,8},... | collective-permute-start | bytes 393224 | tf_op jit(solution)/shard_map/ppermute | solution.py:53
  33.8 4.4 %collective-permute-start.10 = (bf16[96,1792]{1,0:T(8,128)(2,1)S(1)}, bf16[96,1792]{1,0:T(8,128)(2,1)S(1)}, u32[]{:S(2)}, u32[]{:S(2)}) collective-permute-start(bf16[96,1792]{1,0:T(8,128)(2,1)S(1)} %slice.61), channel_id=1, source_target_pairs={{0,12},{4,8},{8,4},{12,0},{1,13},{5,9},{9,5},{13,1},{2,14},{6,10},... | collective-permute-start | bytes 1032200 | tf_op jit(solution)/shard_map/ppermute | solution.py:25
  38.2 2.4 %collective-permute-start.11 = (bf16[96,1792]{1,0:T(8,128)(2,1)S(1)}, bf16[96,1792]{1,0:T(8,128)(2,1)S(1)}, u32[]{:S(2)}, u32[]{:S(2)}) collective-permute-start(bf16[96,1792]{1,0:T(8,128)(2,1)S(1)} %slice.61), channel_id=1, source_target_pairs={{0,8},{4,12},{8,0},{12,4},{1,9},{5,13},{9,1},{13,5},{2,10},{6,14},... | collective-permute-start | bytes 1032200 | tf_op jit(solution)/shard_map/ppermute | solution.py:25
  40.6 2.4 %collective-permute-start.12 = (bf16[96,1792]{1,0:T(8,128)(2,1)S(1)}, bf16[96,1792]{1,0:T(8,128)(2,1)S(1)}, u32[]{:S(2)}, u32[]{:S(2)}) collective-permute-start(bf16[96,1792]{1,0:T(8,128)(2,1)S(1)} %slice.61), channel_id=1, source_target_pairs={{0,4},{4,0},{8,12},{12,8},{1,5},{5,1},{9,13},{13,9},{2,6},{6,2},{1... | collective-permute-start | bytes 1032200 | tf_op jit(solution)/shard_map/ppermute | solution.py:25
  43.3 1.2 %fusion.10 = f32[128,1792]{1,0:T(8,128)S(1)} fusion(bf16[2048,1792]{1,0:T(8,128)(2,1)S(1)} %get-tuple-element.35, f32[128]{0:T(128)S(1)} %add_rsqrt_fusion, f32[2048]{0:T(1024)S(1)} %bitcast.26, bf16[32,2048]{1,0:T(8,128)(2,1)S(1)} %collective-permute-done.9.refs_10_, bf16[32,2048]{1,0:T(8,128)(2,1)S(1)} %collective-permute-done.8.refs_9_, ...), kind=kOutput, calls=%fused_computation.26 | convolution fusion | flops 942407680 | bytes 8790528 | tf_op jit(solution)/shard_map/dot_general | solution.py:409
  44.5 1.5 %multiply_convert_fusion = (bf16[128,1792]{1,0:T(8,128)(2,1)S(1)}, bf16[128,1792]{1,0:T(8,128)(2,1)S(1)}, bf16[128,1792]{1,0:T(8,128)(2,1)S(1)}) fusion(f32[128,1792]{1,0:T(8,128)S(1)} %fusion.10, f32[128,1792]{1,0:T(8,128)S(1)} %shard_map.96, bf16[2048,1792]{1,0:T(8,128)(2,1)S(1)} %get-tuple-element.36.up_ref, f32[128]{0:T(128)S(1)} %add_rsqrt_fusion, ...), kind=kOutput, calls=%fused_computation.18 | convolution fusion | flops 946077696 | bytes 11084288 | tf_op jit(solution)/shard_map/dot_general | solution.py:410
  46.9 0.7 collective-permute-done.11.refs_1_
  47.6 2.2 %collective-permute-done.12.refs_2_ = bf16[96,1792]{1,0:T(8,128)(2,1)S(1)} collective-permute-done((bf16[96,1792]{1,0:T(8,128)(2,1)S(1)}, bf16[96,1792]{1,0:T(8,128)(2,1)S(1)}, u32[]{:S(2)}, u32[]{:S(2)}) %collective-permute-start.12) | collective-permute-done | bytes 344096 | tf_op jit(solution)/shard_map/ppermute | solution.py:25
  49.8 1.3 %collective-permute-start.16 = (bf16[32,2048]{1,0:T(8,128)(2,1)S(1)}, bf16[32,2048]{1,0:T(8,128)(2,1)S(1)}, u32[]{:S(2)}, u32[]{:S(2)}) collective-permute-start(bf16[32,2048]{1,0:T(8,128)(2,1)S(1)} %get-tuple-element.78), channel_id=1, source_target_pairs={{16,3},{17,2},{18,1},{19,0},{20,7},{21,6},{22,5},{23,4},{24,11},{2... | collective-permute-start | bytes 393224 | tf_op jit(solution)/shard_map/ppermute | solution.py:33
  51.1 1.3 %collective-permute-start.15 = (bf16[32,2048]{1,0:T(8,128)(2,1)S(1)}, bf16[32,2048]{1,0:T(8,128)(2,1)S(1)}, u32[]{:S(2)}, u32[]{:S(2)}) collective-permute-start(bf16[32,2048]{1,0:T(8,128)(2,1)S(1)} %get-tuple-element.79), channel_id=1, source_target_pairs={{16,2},{17,3},{18,0},{19,1},{20,6},{21,7},{22,4},{23,5},{24,10},{2... | collective-permute-start | bytes 393224 | tf_op jit(solution)/shard_map/ppermute | solution.py:33
  52.4 1.3 %collective-permute-start.14 = (bf16[32,2048]{1,0:T(8,128)(2,1)S(1)}, bf16[32,2048]{1,0:T(8,128)(2,1)S(1)}, u32[]{:S(2)}, u32[]{:S(2)}) collective-permute-start(bf16[32,2048]{1,0:T(8,128)(2,1)S(1)} %get-tuple-element.80), channel_id=1, source_target_pairs={{16,1},{17,0},{18,3},{19,2},{20,5},{21,4},{22,7},{23,6},{24,9},{25... | collective-permute-start | bytes 393224 | tf_op jit(solution)/shard_map/ppermute | solution.py:33
  53.7 1.3 %collective-permute-start.13 = (bf16[32,2048]{1,0:T(8,128)(2,1)S(1)}, bf16[32,2048]{1,0:T(8,128)(2,1)S(1)}, u32[]{:S(2)}, u32[]{:S(2)}) collective-permute-start(bf16[32,2048]{1,0:T(8,128)(2,1)S(1)} %get-tuple-element.77), channel_id=1, source_target_pairs={{16,0},{17,1},{18,2},{19,3},{20,4},{21,5},{22,6},{23,7},{24,8},{25... | collective-permute-start | bytes 393224 | tf_op jit(solution)/shard_map/ppermute | solution.py:33
  55.2 3.0 %collective-permute-done.13 = bf16[32,2048]{1,0:T(8,128)(2,1)S(1)} collective-permute-done((bf16[32,2048]{1,0:T(8,128)(2,1)S(1)}, bf16[32,2048]{1,0:T(8,128)(2,1)S(1)}, u32[]{:S(2)}, u32[]{:S(2)}) %collective-permute-start.13) | collective-permute-done | bytes 131104 | tf_op jit(solution)/shard_map/ppermute | solution.py:33
  58.1 3.1 %collective-permute-done.15 = bf16[32,2048]{1,0:T(8,128)(2,1)S(1)} collective-permute-done((bf16[32,2048]{1,0:T(8,128)(2,1)S(1)}, bf16[32,2048]{1,0:T(8,128)(2,1)S(1)}, u32[]{:S(2)}, u32[]{:S(2)}) %collective-permute-start.15) | collective-permute-done | bytes 131104 | tf_op jit(solution)/shard_map/ppermute | solution.py:33
  61.4 1.5 %collective-permute-start.19 = (bf16[48,512]{1,0:T(8,128)(2,1)S(1)}, bf16[48,512]{1,0:T(8,128)(2,1)S(1)}, u32[]{:S(2)}, u32[]{:S(2)}) collective-permute-start(bf16[48,512]{1,0:T(8,128)(2,1)S(1)} %get-tuple-element.93), channel_id=1, source_target_pairs={{0,12},{4,8},{8,4},{12,0},{1,13},{5,9},{9,5},{13,1},{2,14},{6,10},... | collective-permute-start | bytes 147464 | tf_op jit(solution)/shard_map/ppermute | solution.py:19
  63.5 1.5 %collective-permute-start.17 = (bf16[48,512]{1,0:T(8,128)(2,1)S(1)}, bf16[48,512]{1,0:T(8,128)(2,1)S(1)}, u32[]{:S(2)}, u32[]{:S(2)}) collective-permute-start(bf16[48,512]{1,0:T(8,128)(2,1)S(1)} %get-tuple-element.91), channel_id=1, source_target_pairs={{0,4},{4,0},{8,12},{12,8},{1,5},{5,1},{9,13},{13,9},{2,6},{6,2},{1... | collective-permute-start | bytes 147464 | tf_op jit(solution)/shard_map/ppermute | solution.py:19
  65.0 0.7 collective-permute-start.20
  65.7 0.7 collective-permute-start.21
  66.5 0.7 collective-permute-start.22
  67.2 0.9 collective-permute-done.17
  68.5 0.9 dynamic-slice_select_fusion
  69.4 1.5 %collective-permute-start.23 = (bf16[128,512]{1,0:T(8,128)(2,1)}, bf16[128,512]{1,0:T(8,128)(2,1)S(1)}, u32[]{:S(2)}, u32[]{:S(2)}) collective-permute-start(bf16[128,512]{1,0:T(8,128)(2,1)} %get-tuple-element.76), channel_id=1, source_target_pairs={{0,3},{16,28},{1,2},{17,29},{2,1},{18,30},{3,0},{19,31},{4,7},{20,... | collective-permute-start | bytes 393224 | tf_op jit(solution)/shard_map/ppermute | solution.py:63
  70.9 2.9 %collective-permute-start.25 = (bf16[128,512]{1,0:T(8,128)(2,1)S(1)}, bf16[128,512]{1,0:T(8,128)(2,1)S(1)}, u32[]{:S(2)}, u32[]{:S(2)}) collective-permute-start(bf16[128,512]{1,0:T(8,128)(2,1)S(1)} %get-tuple-element.74), channel_id=1, source_target_pairs={{0,1},{16,20},{1,0},{17,21},{2,3},{18,22},{3,2},{19,23},{4,5},{20,... | collective-permute-start | bytes 393224 | tf_op jit(solution)/shard_map/ppermute | solution.py:63
  74.1 0.7 copy-done.9
  74.9 0.8 copy-done.10
  75.6 2.7 %shard_map.98 = (bf16[512,1792]{1,0:T(8,128)(2,1)S(1)}, f32[512,512]{1,0:T(8,128)S(1)}) custom-call(s32[1]{0:T(128)} %bitcast.flag_ref, bf16[96,1792]{1,0:T(8,128)(2,1)} %copy-done.11, bf16[96,1792]{1,0:T(8,128)(2,1)} %copy-done.12, bf16[96,1792]{1,0:T(8,128)(2,1)} %copy-done.13, bf16[128,1792]{1,0:T(8,128)(2,1)} %copy-done, bf16[128,1792]{1,0:T(8,128)(2,1)} %copy-done.7, ...), custom_call_target="tpu_custom_call" | custom-call | flops 939524096 | bytes 4718592 | tf_op jit(solution)/shard_map/pallas_call | solution.py:292
  78.3 0.8 collective-permute-done.24.refs_1_
  79.2 1.7 %shard_map.99 = (bf16[512,2048]{1,0:T(8,128)(2,1)S(1)}, f32[8,128]{1,0:T(8,128)S(1)}) custom-call(s32[1]{0:T(128)} %bitcast.flag_ref, s32[512,1]{1,0:T(8,128)S(1)} %reshape.87.ids_ref, s32[1,512]{1,0:T(1,128)S(1)} %reshape_reshape.3.ids_row_ref, f32[512,512]{1,0:T(8,128)S(1)} %get-tuple-element.59.gram_ref, ...), custom_call_target="tpu_custom_call" | custom-call | flops 269484032 | bytes 2097152 | tf_op jit(solution)/shard_map/pallas_call | solution.py:362
  81.0 2.0 %collective-permute-start.26 = (f32[8,128]{1,0:T(8,128)S(1)}, f32[8,128]{1,0:T(8,128)S(1)}, u32[]{:S(2)}, u32[]{:S(2)}) collective-permute-start(f32[8,128]{1,0:T(8,128)S(1)} %get-tuple-element.62), channel_id=1, source_target_pairs={{0,3},{1,2},{2,1},{3,0},{4,7},{5,6},{6,5},{7,4},{8,11},{9,10},{10,... | collective-permute-start | bytes 12296 | tf_op jit(solution)/shard_map/ppermute | solution.py:19
  83.0 1.4 %collective-permute-start.27 = (f32[8,128]{1,0:T(8,128)S(1)}, f32[8,128]{1,0:T(8,128)S(1)}, u32[]{:S(2)}, u32[]{:S(2)}) collective-permute-start(f32[8,128]{1,0:T(8,128)S(1)} %get-tuple-element.62), channel_id=1, source_target_pairs={{0,2},{1,3},{2,0},{3,1},{4,6},{5,7},{6,4},{7,5},{8,10},{9,11},{10,... | collective-permute-start | bytes 12296 | tf_op jit(solution)/shard_map/ppermute | solution.py:19
  84.5 2.5 %shard_map.100.rest_0_ = bf16[4,1792,512]{2,1,0:T(8,128)(2,1)} custom-call(bf16[512,1792]{1,0:T(8,128)(2,1)S(1)} %get-tuple-element.58.hidden_ref, bf16[512,2048]{1,0:T(8,128)(2,1)S(1)} %get-tuple-element.65.masked_ref), custom_call_target="tpu_custom_call" | custom-call | flops 1073741824 | bytes 2621440 | tf_op jit(solution)/shard_map/pallas_call | solution.py:224
  87.6 1.5 %collective-permute-start.31 = (f32[8,128]{1,0:T(8,128)S(1)}, f32[8,128]{1,0:T(8,128)S(1)}, u32[]{:S(2)}, u32[]{:S(2)}) collective-permute-start(f32[8,128]{1,0:T(8,128)S(1)} %add_add_fusion.1), channel_id=1, source_target_pairs={{0,4},{4,0},{8,12},{12,8},{1,5},{5,1},{9,13},{13,9},{2,6},{6,2},{1... | collective-permute-start | bytes 12296 | tf_op jit(solution)/shard_map/ppermute | solution.py:19
  89.1 1.5 %collective-permute-start.29 = (f32[8,128]{1,0:T(8,128)S(1)}, f32[8,128]{1,0:T(8,128)S(1)}, u32[]{:S(2)}, u32[]{:S(2)}) collective-permute-start(f32[8,128]{1,0:T(8,128)S(1)} %add_add_fusion.1), channel_id=1, source_target_pairs={{0,12},{4,8},{8,4},{12,0},{1,13},{5,9},{9,5},{13,1},{2,14},{6,10},... | collective-permute-start | bytes 12296 | tf_op jit(solution)/shard_map/ppermute | solution.py:19
  91.0 2.5 %shard_map.101.rest_0_ = bf16[4,1792,512]{2,1,0:T(8,128)(2,1)} custom-call(bf16[512,1792]{1,0:T(8,128)(2,1)S(1)} %get-tuple-element.58.hidden_ref, bf16[512,2048]{1,0:T(8,128)(2,1)S(1)} %get-tuple-element.65.masked_ref, bf16[4,1792,512]{2,1,0:T(8,128)(2,1)} %shard_map.100.rest_0_), custom_call_target="tpu_custom_call", output_to_operand_aliasing={{}: (2, {})} | custom-call | flops 1073741824 | bytes 2621440 | tf_op jit(solution)/shard_map/pallas_call | solution.py:224
  94.2 2.9 %collective-permute-start.32 = (f32[8,128]{1,0:T(8,128)S(1)}, f32[8,128]{1,0:T(8,128)S(1)}, u32[]{:S(2)}, u32[]{:S(2)}) collective-permute-start(f32[8,128]{1,0:T(8,128)S(1)} %add_add_fusion), channel_id=1, source_target_pairs={{0,16},{16,0},{1,17},{17,1},{2,18},{18,2},{3,19},{19,3},{4,20},{20... | collective-permute-start | bytes 12296 | tf_op jit(solution)/shard_map/ppermute | solution.py:19
  97.1 3.5 %shard_map.102 = bf16[4,1792,512]{2,1,0:T(8,128)(2,1)} custom-call(bf16[512,1792]{1,0:T(8,128)(2,1)S(1)} %get-tuple-element.58.hidden_ref, bf16[512,2048]{1,0:T(8,128)(2,1)S(1)} %get-tuple-element.65.masked_ref, bf16[4,1792,512]{2,1,0:T(8,128)(2,1)} %shard_map.101.rest_0_), custom_call_target="tpu_custom_call", output_to_operand_aliasing={{}: (2, {})} | custom-call | flops 1610612736 | bytes 3932160 | tf_op jit(solution)/shard_map/pallas_call | solution.py:224
  (103 shorter events, 7.2 us)
Async XLA Ops:
  1.6 16.4 %copy-start.14 = (f32[1,2048]{1,0:T(1,128)S(1)}, f32[1,2048]{1,0:T(1,128)}, u32[]{:S(2)}) copy-start(f32[1,2048]{1,0:T(1,128)} %param.11) | copy-start | bytes 24580
  1.6 13.2 %collective-permute-start.2 = (bf16[32,2048]{1,0:T(8,128)(2,1)S(1)}, bf16[32,2048]{1,0:T(8,128)(2,1)S(1)}, u32[]{:S(2)}, u32[]{:S(2)}) collective-permute-start(bf16[32,2048]{1,0:T(8,128)(2,1)S(1)} %bitcast_select_fusion.1), channel_id=1, source_target_pairs={{0,3},{1,2},{2,1},{3,0},{4,7},{5,6},{6,5},{7,4},{8,11},{9,10},{10,... | collective-permute-start | bytes 393224 | tf_op jit(solution)/shard_map/ppermute | solution.py:19
  6.8 11.1 %collective-permute-start.1 = (bf16[32,2048]{1,0:T(8,128)(2,1)S(1)}, bf16[32,2048]{1,0:T(8,128)(2,1)S(1)}, u32[]{:S(2)}, u32[]{:S(2)}) collective-permute-start(bf16[32,2048]{1,0:T(8,128)(2,1)S(1)} %bitcast_select_fusion.1), channel_id=1, source_target_pairs={{0,2},{1,3},{2,0},{3,1},{4,6},{5,7},{6,4},{7,5},{8,10},{9,11},{10,... | collective-permute-start | bytes 393224 | tf_op jit(solution)/shard_map/ppermute | solution.py:19
  6.8 11.1 %collective-permute-start = (bf16[32,2048]{1,0:T(8,128)(2,1)S(1)}, bf16[32,2048]{1,0:T(8,128)(2,1)S(1)}, u32[]{:S(2)}, u32[]{:S(2)}) collective-permute-start(bf16[32,2048]{1,0:T(8,128)(2,1)S(1)} %bitcast_select_fusion.1), channel_id=1, source_target_pairs={{0,1},{1,0},{2,3},{3,2},{4,5},{5,4},{6,7},{7,6},{8,9},{9,8},{10,11... | collective-permute-start | bytes 393224 | tf_op jit(solution)/shard_map/ppermute | solution.py:19
  20.6 8.2 %copy-start = (bf16[128,1792]{1,0:T(8,128)(2,1)}, bf16[128,1792]{1,0:T(8,128)(2,1)S(1)}, u32[]{:S(2)}) copy-start(bf16[128,1792]{1,0:T(8,128)(2,1)S(1)} %fusion.refs_3_) | copy-start | bytes 1376260
  21.8 8.3 %copy-start.6 = (bf16[4,8,2048]{2,1,0:T(8,128)(2,1)S(1)}, bf16[4,8,2048]{2,1,0:T(8,128)(2,1)}, u32[]{:S(2)}) copy-start(bf16[4,8,2048]{2,1,0:T(8,128)(2,1)} %param.8) | copy-start | bytes 393220
  21.8 7.0 %collective-permute-start.6 = (bf16[32,2048]{1,0:T(8,128)(2,1)S(1)}, bf16[32,2048]{1,0:T(8,128)(2,1)S(1)}, u32[]{:S(2)}, u32[]{:S(2)}) collective-permute-start(bf16[32,2048]{1,0:T(8,128)(2,1)S(1)} %get-tuple-element.82), channel_id=1, source_target_pairs={{0,19},{1,18},{2,17},{3,16},{4,23},{5,22},{6,21},{7,20},{8,27},{9,... | collective-permute-start | bytes 393224 | tf_op jit(solution)/shard_map/ppermute | solution.py:33
  24.8 4.0 %collective-permute-start.5 = (bf16[32,2048]{1,0:T(8,128)(2,1)S(1)}, bf16[32,2048]{1,0:T(8,128)(2,1)S(1)}, u32[]{:S(2)}, u32[]{:S(2)}) collective-permute-start(bf16[32,2048]{1,0:T(8,128)(2,1)S(1)} %get-tuple-element.83), channel_id=1, source_target_pairs={{0,18},{1,19},{2,16},{3,17},{4,22},{5,23},{6,20},{7,21},{8,26},{9,... | collective-permute-start | bytes 393224 | tf_op jit(solution)/shard_map/ppermute | solution.py:33
  26.1 4.0 %collective-permute-start.4 = (bf16[32,2048]{1,0:T(8,128)(2,1)S(1)}, bf16[32,2048]{1,0:T(8,128)(2,1)S(1)}, u32[]{:S(2)}, u32[]{:S(2)}) collective-permute-start(bf16[32,2048]{1,0:T(8,128)(2,1)S(1)} %get-tuple-element.84), channel_id=1, source_target_pairs={{0,17},{1,16},{2,19},{3,18},{4,21},{5,20},{6,23},{7,22},{8,25},{9,... | collective-permute-start | bytes 393224 | tf_op jit(solution)/shard_map/ppermute | solution.py:33
  27.4 2.7 %collective-permute-start.3 = (bf16[32,2048]{1,0:T(8,128)(2,1)S(1)}, bf16[32,2048]{1,0:T(8,128)(2,1)S(1)}, u32[]{:S(2)}, u32[]{:S(2)}) collective-permute-start(bf16[32,2048]{1,0:T(8,128)(2,1)S(1)} %get-tuple-element.81), channel_id=1, source_target_pairs={{0,16},{1,17},{2,18},{3,19},{4,20},{5,21},{6,22},{7,23},{8,24},{9,... | collective-permute-start | bytes 393224 | tf_op jit(solution)/shard_map/ppermute | solution.py:33
  28.7 5.1 %copy-start.1 = (bf16[128,1792]{1,0:T(8,128)(2,1)S(1)}, bf16[128,1792]{1,0:T(8,128)(2,1)}, u32[]{:S(2)}) copy-start(bf16[128,1792]{1,0:T(8,128)(2,1)} %copy-done) | copy-start | bytes 1376260
  30.3 10.4 %collective-permute-start.9 = (bf16[32,2048]{1,0:T(8,128)(2,1)S(1)}, bf16[32,2048]{1,0:T(8,128)(2,1)S(1)}, u32[]{:S(2)}, u32[]{:S(2)}) collective-permute-start(bf16[32,2048]{1,0:T(8,128)(2,1)S(1)} %pad_select_fusion), channel_id=1, source_target_pairs={{0,12},{16,19},{1,13},{17,18},{2,14},{18,17},{3,15},{19,16},{4,8},... | collective-permute-start | bytes 393224 | tf_op jit(solution)/shard_map/ppermute | solution.py:53
  32.8 10.3 %collective-permute-start.8 = (bf16[32,2048]{1,0:T(8,128)(2,1)S(1)}, bf16[32,2048]{1,0:T(8,128)(2,1)S(1)}, u32[]{:S(2)}, u32[]{:S(2)}) collective-permute-start(bf16[32,2048]{1,0:T(8,128)(2,1)S(1)} %pad_select_fusion), channel_id=1, source_target_pairs={{0,8},{16,18},{1,9},{17,19},{2,10},{18,16},{3,11},{19,17},{4,12},{... | collective-permute-start | bytes 393224 | tf_op jit(solution)/shard_map/ppermute | solution.py:53
  33.3 9.8 %collective-permute-start.7 = (bf16[32,2048]{1,0:T(8,128)(2,1)S(1)}, bf16[32,2048]{1,0:T(8,128)(2,1)S(1)}, u32[]{:S(2)}, u32[]{:S(2)}) collective-permute-start(bf16[32,2048]{1,0:T(8,128)(2,1)S(1)} %pad_select_fusion), channel_id=1, source_target_pairs={{0,4},{16,17},{1,5},{17,16},{2,6},{18,19},{3,7},{19,18},{4,0},{20,... | collective-permute-start | bytes 393224 | tf_op jit(solution)/shard_map/ppermute | solution.py:53
  33.8 13.0 %collective-permute-start.10 = (bf16[96,1792]{1,0:T(8,128)(2,1)S(1)}, bf16[96,1792]{1,0:T(8,128)(2,1)S(1)}, u32[]{:S(2)}, u32[]{:S(2)}) collective-permute-start(bf16[96,1792]{1,0:T(8,128)(2,1)S(1)} %slice.61), channel_id=1, source_target_pairs={{0,12},{4,8},{8,4},{12,0},{1,13},{5,9},{9,5},{13,1},{2,14},{6,10},... | collective-permute-start | bytes 1032200 | tf_op jit(solution)/shard_map/ppermute | solution.py:25
  38.2 9.4 %collective-permute-start.11 = (bf16[96,1792]{1,0:T(8,128)(2,1)S(1)}, bf16[96,1792]{1,0:T(8,128)(2,1)S(1)}, u32[]{:S(2)}, u32[]{:S(2)}) collective-permute-start(bf16[96,1792]{1,0:T(8,128)(2,1)S(1)} %slice.61), channel_id=1, source_target_pairs={{0,8},{4,12},{8,0},{12,4},{1,9},{5,13},{9,1},{13,5},{2,10},{6,14},... | collective-permute-start | bytes 1032200 | tf_op jit(solution)/shard_map/ppermute | solution.py:25
  40.6 6.0 %copy-start.2 = (bf16[32,2048]{1,0:T(8,128)(2,1)}, bf16[32,2048]{1,0:T(8,128)(2,1)S(1)}, u32[]{:S(2)}) copy-start(bf16[32,2048]{1,0:T(8,128)(2,1)S(1)} %collective-permute-done.9.refs_10_) | copy-start | bytes 393220
  40.6 9.1 %collective-permute-start.12 = (bf16[96,1792]{1,0:T(8,128)(2,1)S(1)}, bf16[96,1792]{1,0:T(8,128)(2,1)S(1)}, u32[]{:S(2)}, u32[]{:S(2)}) collective-permute-start(bf16[96,1792]{1,0:T(8,128)(2,1)S(1)} %slice.61), channel_id=1, source_target_pairs={{0,4},{4,0},{8,12},{12,8},{1,5},{5,1},{9,13},{13,9},{2,6},{6,2},{1... | collective-permute-start | bytes 1032200 | tf_op jit(solution)/shard_map/ppermute | solution.py:25
  43.1 3.5 %copy-start.3 = (bf16[32,2048]{1,0:T(8,128)(2,1)}, bf16[32,2048]{1,0:T(8,128)(2,1)S(1)}, u32[]{:S(2)}) copy-start(bf16[32,2048]{1,0:T(8,128)(2,1)S(1)} %collective-permute-done.8.refs_9_) | copy-start | bytes 393220
  43.1 3.5 %copy-start.4 = (bf16[32,2048]{1,0:T(8,128)(2,1)}, bf16[32,2048]{1,0:T(8,128)(2,1)S(1)}, u32[]{:S(2)}) copy-start(bf16[32,2048]{1,0:T(8,128)(2,1)S(1)} %collective-permute-done.7.refs_8_) | copy-start | bytes 393220
  46.0 20.5 %copy-start.7 = (bf16[128,1792]{1,0:T(8,128)(2,1)}, bf16[128,1792]{1,0:T(8,128)(2,1)S(1)}, u32[]{:S(2)}) copy-start(bf16[128,1792]{1,0:T(8,128)(2,1)S(1)} %get-tuple-element.57.refs_4_) | copy-start | bytes 1376260
  46.1 9.0 %copy-start.16 = (s32[4,1]{0,1:T(1,128)S(1)}, s32[4,1]{0,1:T(1,128)}, u32[]{:S(2)}) copy-start(s32[4,1]{0,1:T(1,128)} %param.10) | copy-start | bytes 52
  46.1 15.1 %copy-start.5 = (bf16[4,8,2048]{2,1,0:T(8,128)(2,1)S(1)}, bf16[4,8,2048]{2,1,0:T(8,128)(2,1)}, u32[]{:S(2)}) copy-start(bf16[4,8,2048]{2,1,0:T(8,128)(2,1)} %param.9) | copy-start | bytes 393220
  46.9 27.2 %copy-start.11 = (bf16[96,1792]{1,0:T(8,128)(2,1)}, bf16[96,1792]{1,0:T(8,128)(2,1)S(1)}, u32[]{:S(2)}) copy-start(bf16[96,1792]{1,0:T(8,128)(2,1)S(1)} %collective-permute-done.10.refs_0_) | copy-start | bytes 1032196
  47.6 26.6 %copy-start.12 = (bf16[96,1792]{1,0:T(8,128)(2,1)}, bf16[96,1792]{1,0:T(8,128)(2,1)S(1)}, u32[]{:S(2)}) copy-start(bf16[96,1792]{1,0:T(8,128)(2,1)S(1)} %collective-permute-done.11.refs_1_) | copy-start | bytes 1032196
  49.8 15.2 %copy-start.13 = (bf16[96,1792]{1,0:T(8,128)(2,1)}, bf16[96,1792]{1,0:T(8,128)(2,1)S(1)}, u32[]{:S(2)}) copy-start(bf16[96,1792]{1,0:T(8,128)(2,1)S(1)} %collective-permute-done.12.refs_2_) | copy-start | bytes 1032196
  49.8 8.3 %collective-permute-start.16 = (bf16[32,2048]{1,0:T(8,128)(2,1)S(1)}, bf16[32,2048]{1,0:T(8,128)(2,1)S(1)}, u32[]{:S(2)}, u32[]{:S(2)}) collective-permute-start(bf16[32,2048]{1,0:T(8,128)(2,1)S(1)} %get-tuple-element.78), channel_id=1, source_target_pairs={{16,3},{17,2},{18,1},{19,0},{20,7},{21,6},{22,5},{23,4},{24,11},{2... | collective-permute-start | bytes 393224 | tf_op jit(solution)/shard_map/ppermute | solution.py:33
  51.1 10.1 %collective-permute-start.15 = (bf16[32,2048]{1,0:T(8,128)(2,1)S(1)}, bf16[32,2048]{1,0:T(8,128)(2,1)S(1)}, u32[]{:S(2)}, u32[]{:S(2)}) collective-permute-start(bf16[32,2048]{1,0:T(8,128)(2,1)S(1)} %get-tuple-element.79), channel_id=1, source_target_pairs={{16,2},{17,3},{18,0},{19,1},{20,6},{21,7},{22,4},{23,5},{24,10},{2... | collective-permute-start | bytes 393224 | tf_op jit(solution)/shard_map/ppermute | solution.py:33
  52.4 8.8 %collective-permute-start.14 = (bf16[32,2048]{1,0:T(8,128)(2,1)S(1)}, bf16[32,2048]{1,0:T(8,128)(2,1)S(1)}, u32[]{:S(2)}, u32[]{:S(2)}) collective-permute-start(bf16[32,2048]{1,0:T(8,128)(2,1)S(1)} %get-tuple-element.80), channel_id=1, source_target_pairs={{16,1},{17,0},{18,3},{19,2},{20,5},{21,4},{22,7},{23,6},{24,9},{25... | collective-permute-start | bytes 393224 | tf_op jit(solution)/shard_map/ppermute | solution.py:33
  53.7 4.4 %collective-permute-start.13 = (bf16[32,2048]{1,0:T(8,128)(2,1)S(1)}, bf16[32,2048]{1,0:T(8,128)(2,1)S(1)}, u32[]{:S(2)}, u32[]{:S(2)}) collective-permute-start(bf16[32,2048]{1,0:T(8,128)(2,1)S(1)} %get-tuple-element.77), channel_id=1, source_target_pairs={{16,0},{17,1},{18,2},{19,3},{20,4},{21,5},{22,6},{23,7},{24,8},{25... | collective-permute-start | bytes 393224 | tf_op jit(solution)/shard_map/ppermute | solution.py:33
  61.4 5.1 %collective-permute-start.19 = (bf16[48,512]{1,0:T(8,128)(2,1)S(1)}, bf16[48,512]{1,0:T(8,128)(2,1)S(1)}, u32[]{:S(2)}, u32[]{:S(2)}) collective-permute-start(bf16[48,512]{1,0:T(8,128)(2,1)S(1)} %get-tuple-element.93), channel_id=1, source_target_pairs={{0,12},{4,8},{8,4},{12,0},{1,13},{5,9},{9,5},{13,1},{2,14},{6,10},... | collective-permute-start | bytes 147464 | tf_op jit(solution)/shard_map/ppermute | solution.py:19
  63.0 4.2 %collective-permute-start.18 = (bf16[48,512]{1,0:T(8,128)(2,1)S(1)}, bf16[48,512]{1,0:T(8,128)(2,1)S(1)}, u32[]{:S(2)}, u32[]{:S(2)}) collective-permute-start(bf16[48,512]{1,0:T(8,128)(2,1)S(1)} %get-tuple-element.92), channel_id=1, source_target_pairs={{0,8},{4,12},{8,0},{12,4},{1,9},{5,13},{9,1},{13,5},{2,10},{6,14},... | collective-permute-start | bytes 147464 | tf_op jit(solution)/shard_map/ppermute | solution.py:19
  63.5 4.6 %collective-permute-start.17 = (bf16[48,512]{1,0:T(8,128)(2,1)S(1)}, bf16[48,512]{1,0:T(8,128)(2,1)S(1)}, u32[]{:S(2)}, u32[]{:S(2)}) collective-permute-start(bf16[48,512]{1,0:T(8,128)(2,1)S(1)} %get-tuple-element.91), channel_id=1, source_target_pairs={{0,4},{4,0},{8,12},{12,8},{1,5},{5,1},{9,13},{13,9},{2,6},{6,2},{1... | collective-permute-start | bytes 147464 | tf_op jit(solution)/shard_map/ppermute | solution.py:19
  65.0 3.5 %collective-permute-start.20 = (bf16[128,1792]{1,0:T(8,128)(2,1)S(1)}, bf16[128,1792]{1,0:T(8,128)(2,1)S(1)}, u32[]{:S(2)}, u32[]{:S(2)}) collective-permute-start(bf16[128,1792]{1,0:T(8,128)(2,1)S(1)} %get-tuple-element.57.refs_4_), channel_id=1, source_target_pairs={{16,20},{20,16},{24,28},{28,24},{17,21},{21,17},{25,29},{29,25},{1... | collective-permute-start | bytes 1376264 | tf_op jit(solution)/shard_map/ppermute | solution.py:25
  65.7 8.4 %collective-permute-start.21 = (bf16[128,1792]{1,0:T(8,128)(2,1)S(1)}, bf16[128,1792]{1,0:T(8,128)(2,1)S(1)}, u32[]{:S(2)}, u32[]{:S(2)}) collective-permute-start(bf16[128,1792]{1,0:T(8,128)(2,1)S(1)} %get-tuple-element.57.refs_4_), channel_id=1, source_target_pairs={{16,24},{20,28},{24,16},{28,20},{17,25},{21,29},{25,17},{29,21},{1... | collective-permute-start | bytes 1376264 | tf_op jit(solution)/shard_map/ppermute | solution.py:25
  66.5 7.6 %collective-permute-start.22 = (bf16[128,1792]{1,0:T(8,128)(2,1)S(1)}, bf16[128,1792]{1,0:T(8,128)(2,1)S(1)}, u32[]{:S(2)}, u32[]{:S(2)}) collective-permute-start(bf16[128,1792]{1,0:T(8,128)(2,1)S(1)} %get-tuple-element.57.refs_4_), channel_id=1, source_target_pairs={{16,28},{20,24},{24,20},{28,16},{17,29},{21,25},{25,21},{29,17},{1... | collective-permute-start | bytes 1376264 | tf_op jit(solution)/shard_map/ppermute | solution.py:25
  68.5 5.6 %copy-start.8 = (bf16[128,1792]{1,0:T(8,128)(2,1)}, bf16[128,1792]{1,0:T(8,128)(2,1)S(1)}, u32[]{:S(2)}) copy-start(bf16[128,1792]{1,0:T(8,128)(2,1)S(1)} %collective-permute-done.20.refs_5_) | copy-start | bytes 1376260
  69.4 8.9 %collective-permute-start.23 = (bf16[128,512]{1,0:T(8,128)(2,1)}, bf16[128,512]{1,0:T(8,128)(2,1)S(1)}, u32[]{:S(2)}, u32[]{:S(2)}) collective-permute-start(bf16[128,512]{1,0:T(8,128)(2,1)} %get-tuple-element.76), channel_id=1, source_target_pairs={{0,3},{16,28},{1,2},{17,29},{2,1},{18,30},{3,0},{19,31},{4,7},{20,... | collective-permute-start | bytes 393224 | tf_op jit(solution)/shard_map/ppermute | solution.py:63
  70.9 8.3 %collective-permute-start.24 = (bf16[128,512]{1,0:T(8,128)(2,1)}, bf16[128,512]{1,0:T(8,128)(2,1)S(1)}, u32[]{:S(2)}, u32[]{:S(2)}) collective-permute-start(bf16[128,512]{1,0:T(8,128)(2,1)} %get-tuple-element.75), channel_id=1, source_target_pairs={{0,2},{16,24},{1,3},{17,25},{2,0},{18,26},{3,1},{19,27},{4,6},{20,... | collective-permute-start | bytes 393224 | tf_op jit(solution)/shard_map/ppermute | solution.py:63
  70.9 8.3 %collective-permute-start.25 = (bf16[128,512]{1,0:T(8,128)(2,1)S(1)}, bf16[128,512]{1,0:T(8,128)(2,1)S(1)}, u32[]{:S(2)}, u32[]{:S(2)}) collective-permute-start(bf16[128,512]{1,0:T(8,128)(2,1)S(1)} %get-tuple-element.74), channel_id=1, source_target_pairs={{0,1},{16,20},{1,0},{17,21},{2,3},{18,22},{3,2},{19,23},{4,5},{20,... | collective-permute-start | bytes 393224 | tf_op jit(solution)/shard_map/ppermute | solution.py:63
  80.9 6.1 %collective-permute-start.28 = (f32[8,128]{1,0:T(8,128)S(1)}, f32[8,128]{1,0:T(8,128)S(1)}, u32[]{:S(2)}, u32[]{:S(2)}) collective-permute-start(f32[8,128]{1,0:T(8,128)S(1)} %get-tuple-element.62), channel_id=1, source_target_pairs={{0,1},{1,0},{2,3},{3,2},{4,5},{5,4},{6,7},{7,6},{8,9},{9,8},{10,11... | collective-permute-start | bytes 12296 | tf_op jit(solution)/shard_map/ppermute | solution.py:19
  81.0 6.0 %collective-permute-start.26 = (f32[8,128]{1,0:T(8,128)S(1)}, f32[8,128]{1,0:T(8,128)S(1)}, u32[]{:S(2)}, u32[]{:S(2)}) collective-permute-start(f32[8,128]{1,0:T(8,128)S(1)} %get-tuple-element.62), channel_id=1, source_target_pairs={{0,3},{1,2},{2,1},{3,0},{4,7},{5,6},{6,5},{7,4},{8,11},{9,10},{10,... | collective-permute-start | bytes 12296 | tf_op jit(solution)/shard_map/ppermute | solution.py:19
  83.0 4.5 %collective-permute-start.27 = (f32[8,128]{1,0:T(8,128)S(1)}, f32[8,128]{1,0:T(8,128)S(1)}, u32[]{:S(2)}, u32[]{:S(2)}) collective-permute-start(f32[8,128]{1,0:T(8,128)S(1)} %get-tuple-element.62), channel_id=1, source_target_pairs={{0,2},{1,3},{2,0},{3,1},{4,6},{5,7},{6,4},{7,5},{8,10},{9,11},{10,... | collective-permute-start | bytes 12296 | tf_op jit(solution)/shard_map/ppermute | solution.py:19
  87.6 6.0 %collective-permute-start.31 = (f32[8,128]{1,0:T(8,128)S(1)}, f32[8,128]{1,0:T(8,128)S(1)}, u32[]{:S(2)}, u32[]{:S(2)}) collective-permute-start(f32[8,128]{1,0:T(8,128)S(1)} %add_add_fusion.1), channel_id=1, source_target_pairs={{0,4},{4,0},{8,12},{12,8},{1,5},{5,1},{9,13},{13,9},{2,6},{6,2},{1... | collective-permute-start | bytes 12296 | tf_op jit(solution)/shard_map/ppermute | solution.py:19
  89.1 4.5 %collective-permute-start.29 = (f32[8,128]{1,0:T(8,128)S(1)}, f32[8,128]{1,0:T(8,128)S(1)}, u32[]{:S(2)}, u32[]{:S(2)}) collective-permute-start(f32[8,128]{1,0:T(8,128)S(1)} %add_add_fusion.1), channel_id=1, source_target_pairs={{0,12},{4,8},{8,4},{12,0},{1,13},{5,9},{9,5},{13,1},{2,14},{6,10},... | collective-permute-start | bytes 12296 | tf_op jit(solution)/shard_map/ppermute | solution.py:19
  90.6 3.6 %collective-permute-start.30 = (f32[8,128]{1,0:T(8,128)S(1)}, f32[8,128]{1,0:T(8,128)S(1)}, u32[]{:S(2)}, u32[]{:S(2)}) collective-permute-start(f32[8,128]{1,0:T(8,128)S(1)} %add_add_fusion.1), channel_id=1, source_target_pairs={{0,8},{4,12},{8,0},{12,4},{1,9},{5,13},{9,1},{13,5},{2,10},{6,14},... | collective-permute-start | bytes 12296 | tf_op jit(solution)/shard_map/ppermute | solution.py:19
  94.2 6.4 %copy-start.15 = (f32[3]{0:T(128)S(1)}, f32[3]{0:T(128)}, u32[]{:S(2)}) copy-start(f32[3]{0:T(128)} %constant.52) | copy-start | bytes 40
  94.2 6.4 %collective-permute-start.32 = (f32[8,128]{1,0:T(8,128)S(1)}, f32[8,128]{1,0:T(8,128)S(1)}, u32[]{:S(2)}, u32[]{:S(2)}) collective-permute-start(f32[8,128]{1,0:T(8,128)S(1)} %add_add_fusion), channel_id=1, source_target_pairs={{0,16},{16,0},{1,17},{17,1},{2,18},{18,2},{3,19},{19,3},{4,20},{20... | collective-permute-start | bytes 12296 | tf_op jit(solution)/shard_map/ppermute | solution.py:19
  (3 other events, 3.0 us)

commit v11 on v10

--- a/solution.py
+++ b/solution.py
@@ -448,7 +448,7 @@
         part = jnp.concatenate([part, id_block], axis=0)
         messages.append(part if k == 0 else swap(part, "dp", k))
     columns = jnp.concatenate([message[:block] for message in messages], axis=0)
-    columns, pieces1[1] = lax.optimization_barrier((columns, pieces1[1]))
+    columns, pieces1[-1] = lax.optimization_barrier((columns, pieces1[-1]))
     if dp_size == tensor_size:
         by_dp = segment
         parts_y = []

time: 102 us -> 100 us (0.980)
  starting transfers between devices: 50.5 us -> 48.5 us
    ppermute x13, starting transfers between devices: 19.3 us -> 17.3 us  [swap(): return lax.ppermute(block, axis, [(i, i ^ offset) for i in range(size)])]
where the time goes in v11:
time: 100 us; the launch traced here: 99.6 us
  starting transfers between devices  48.5 us (48%)
  Pallas kernels  20.7 us (21%)
  waiting for transfers between devices  16.6 us (17%)
  matrix products  6.38 us (6%)
  other arithmetic  3.67 us (4%)
  local copies, waits for them, and re-layouts  2.44 us (2%)
  between operations  1.26 us (1%)
    ppermute x13, starting transfers between devices, swap(): return lax.ppermute(block, axis, [(i, i ^ offset) for i in range(size)])  17.3 us
    ppermute x8, starting transfers between devices, across(): return lax.ppermute(block, ('section', 'tensor'), route)  12 us
    ppermute x6, starting transfers between devices, swap_in(): return lax.ppermute(block, ('section', axis), route)  11.3 us
    pallas_call x3, Pallas kernels, domain_gradients(): pl.pallas_call(gradient_kernel, grid=(count,), in_specs=in_specs, out_spe...  8.48 us
    pallas_call x1, Pallas kernels, load_weights(): pl.pallas_call(load_kernel, in_specs=[pl.BlockSpec(memory_space=pltpu.HBM...  7.46 us
    ppermute x8, waiting for transfers between devices, across(): return lax.ppermute(block, ('section', 'tensor'), route)  7.31 us
    ppermute x13, waiting for transfers between devices, swap(): return lax.ppermute(block, axis, [(i, i ^ offset) for i in range(size)])  6.01 us
    ppermute x3, starting transfers between devices, exchange(): return lax.ppermute(block, ('section', 'dp', 'tensor'), pairs)  4.39 us
  transfers between devices with their start and end apart: 33, of which 11 were waited for; matrix products, arithmetic and copies ran while one was open for 5% of the time, Pallas kernels for 19%

profile of v11, /device:TPU:0, one launch (start us, length us, event | category | flops | bytes accessed | tf_op | source)
XLA Modules:
  0.0 99.6 jit_solution(264488131525625430)
XLA Ops:
  0.6 1.0 bitcast_select_fusion.1
  1.6 5.1 %collective-permute-start.2 = (bf16[32,2048]{1,0:T(8,128)(2,1)S(1)}, bf16[32,2048]{1,0:T(8,128)(2,1)S(1)}, u32[]{:S(2)}, u32[]{:S(2)}) collective-permute-start(bf16[32,2048]{1,0:T(8,128)(2,1)S(1)} %bitcast_select_fusion.1), channel_id=1, source_target_pairs={{0,3},{1,2},{2,1},{3,0},{4,7},{5,6},{6,5},{7,4},{8,11},{9,10},{10,... | collective-permute-start | bytes 393224 | tf_op jit(solution)/shard_map/ppermute | solution.py:19
  6.8 0.6 collective-permute-start
  7.4 7.5 %shard_map.95 = (bf16[2048,1792]{1,0:T(8,128)(2,1)S(1)}, bf16[2048,1792]{1,0:T(8,128)(2,1)S(1)}, bf16[1792,2048]{1,0:T(8,128)(2,1)S(1)}, bf16[1792,2048]{1,0:T(8,128)(2,1)S(1)}) custom-call(bf16[1,2048,1792]{2,1,0:T(8,128)(2,1)} %gate_in.1, bf16[1,2048,1792]{2,1,0:T(8,128)(2,1)} %up_in.1, bf16[1,1792,2048]{2,1,0:T(8,128)(2,1)} %down_in.1), custom_call_target="tpu_custom_call" | custom-call | bytes 22020096 | tf_op jit(solution)/shard_map/pallas_call | solution.py:118
  14.9 3.0 %collective-permute-done.1 = bf16[32,2048]{1,0:T(8,128)(2,1)S(1)} collective-permute-done((bf16[32,2048]{1,0:T(8,128)(2,1)S(1)}, bf16[32,2048]{1,0:T(8,128)(2,1)S(1)}, u32[]{:S(2)}, u32[]{:S(2)}) %collective-permute-start.1) | collective-permute-done | bytes 131104 | tf_op jit(solution)/shard_map/ppermute | solution.py:19
  18.0 1.2 %fusion.15 = f32[128,1792]{1,0:T(8,128)S(1)} fusion(bf16[2048,1792]{1,0:T(8,128)(2,1)S(1)} %get-tuple-element.35, bf16[128,2048]{1,0:T(8,128)(2,1)S(1)} %get-tuple-element.41.rows_ref, f32[2048]{0:T(1024)S(1)} %bitcast.24, f32[128]{0:T(128)S(1)} %add_rsqrt_fusion.1), kind=kOutput, calls=%fused_computation.28 | convolution fusion | flops 940572672 | bytes 8790528 | tf_op jit(solution)/shard_map/dot_general | solution.py:409
  19.2 1.3 %fusion.refs_3_ = bf16[128,1792]{1,0:T(8,128)(2,1)S(1)} fusion(bf16[2048,1792]{1,0:T(8,128)(2,1)S(1)} %get-tuple-element.36.up_ref, f32[128,1792]{1,0:T(8,128)S(1)} %fusion.15, bf16[128,2048]{1,0:T(8,128)(2,1)S(1)} %get-tuple-element.41.rows_ref, f32[2048]{0:T(1024)S(1)} %bitcast.25, f32[128]{0:T(128)S(1)} %add_rsqrt_fusion.1), kind=kOutput, calls=%fused_computation.1 | convolution fusion | flops 941948928 | bytes 9249280 | tf_op jit(solution)/shard_map/dot_general | solution.py:410
  20.6 1.2 %convolution_convert_fusion = bf16[128,2048]{1,0:T(8,128)(2,1)S(1)} fusion(bf16[128,1792]{1,0:T(8,128)(2,1)S(1)} %fusion.refs_3_, bf16[1792,2048]{1,0:T(8,128)(2,1)S(1)} %get-tuple-element.37.down_ref), kind=kOutput, calls=%fused_computation.2 | convolution fusion | flops 939786240 | bytes 8323072 | tf_op jit(solution)/shard_map/dot_general | solution.py:415
  21.8 3.0 %collective-permute-start.6 = (bf16[32,2048]{1,0:T(8,128)(2,1)S(1)}, bf16[32,2048]{1,0:T(8,128)(2,1)S(1)}, u32[]{:S(2)}, u32[]{:S(2)}) collective-permute-start(bf16[32,2048]{1,0:T(8,128)(2,1)S(1)} %get-tuple-element.82), channel_id=1, source_target_pairs={{0,19},{1,18},{2,17},{3,16},{4,23},{5,22},{6,21},{7,20},{8,27},{9,... | collective-permute-start | bytes 393224 | tf_op jit(solution)/shard_map/ppermute | solution.py:33
  24.8 1.3 %collective-permute-start.5 = (bf16[32,2048]{1,0:T(8,128)(2,1)S(1)}, bf16[32,2048]{1,0:T(8,128)(2,1)S(1)}, u32[]{:S(2)}, u32[]{:S(2)}) collective-permute-start(bf16[32,2048]{1,0:T(8,128)(2,1)S(1)} %get-tuple-element.83), channel_id=1, source_target_pairs={{0,18},{1,19},{2,16},{3,17},{4,22},{5,23},{6,20},{7,21},{8,26},{9,... | collective-permute-start | bytes 393224 | tf_op jit(solution)/shard_map/ppermute | solution.py:33
  26.1 1.3 %collective-permute-start.4 = (bf16[32,2048]{1,0:T(8,128)(2,1)S(1)}, bf16[32,2048]{1,0:T(8,128)(2,1)S(1)}, u32[]{:S(2)}, u32[]{:S(2)}) collective-permute-start(bf16[32,2048]{1,0:T(8,128)(2,1)S(1)} %get-tuple-element.84), channel_id=1, source_target_pairs={{0,17},{1,16},{2,19},{3,18},{4,21},{5,20},{6,23},{7,22},{8,25},{9,... | collective-permute-start | bytes 393224 | tf_op jit(solution)/shard_map/ppermute | solution.py:33
  27.4 1.3 %collective-permute-start.3 = (bf16[32,2048]{1,0:T(8,128)(2,1)S(1)}, bf16[32,2048]{1,0:T(8,128)(2,1)S(1)}, u32[]{:S(2)}, u32[]{:S(2)}) collective-permute-start(bf16[32,2048]{1,0:T(8,128)(2,1)S(1)} %get-tuple-element.81), channel_id=1, source_target_pairs={{0,16},{1,17},{2,18},{3,19},{4,20},{5,21},{6,22},{7,23},{8,24},{9,... | collective-permute-start | bytes 393224 | tf_op jit(solution)/shard_map/ppermute | solution.py:33
  28.8 1.3 %collective-permute-done.4 = bf16[32,2048]{1,0:T(8,128)(2,1)S(1)} collective-permute-done((bf16[32,2048]{1,0:T(8,128)(2,1)S(1)}, bf16[32,2048]{1,0:T(8,128)(2,1)S(1)}, u32[]{:S(2)}, u32[]{:S(2)}) %collective-permute-start.4) | collective-permute-done | bytes 131104 | tf_op jit(solution)/shard_map/ppermute | solution.py:33
  30.3 2.5 %collective-permute-start.9 = (bf16[32,2048]{1,0:T(8,128)(2,1)S(1)}, bf16[32,2048]{1,0:T(8,128)(2,1)S(1)}, u32[]{:S(2)}, u32[]{:S(2)}) collective-permute-start(bf16[32,2048]{1,0:T(8,128)(2,1)S(1)} %pad_select_fusion), channel_id=1, source_target_pairs={{0,12},{16,19},{1,13},{17,18},{2,14},{18,17},{3,15},{19,16},{4,8},... | collective-permute-start | bytes 393224 | tf_op jit(solution)/shard_map/ppermute | solution.py:53
  33.8 4.4 %collective-permute-start.10 = (bf16[96,1792]{1,0:T(8,128)(2,1)S(1)}, bf16[96,1792]{1,0:T(8,128)(2,1)S(1)}, u32[]{:S(2)}, u32[]{:S(2)}) collective-permute-start(bf16[96,1792]{1,0:T(8,128)(2,1)S(1)} %slice.61), channel_id=1, source_target_pairs={{0,12},{4,8},{8,4},{12,0},{1,13},{5,9},{9,5},{13,1},{2,14},{6,10},... | collective-permute-start | bytes 1032200 | tf_op jit(solution)/shard_map/ppermute | solution.py:25
  38.2 2.4 %collective-permute-start.11 = (bf16[96,1792]{1,0:T(8,128)(2,1)S(1)}, bf16[96,1792]{1,0:T(8,128)(2,1)S(1)}, u32[]{:S(2)}, u32[]{:S(2)}) collective-permute-start(bf16[96,1792]{1,0:T(8,128)(2,1)S(1)} %slice.61), channel_id=1, source_target_pairs={{0,8},{4,12},{8,0},{12,4},{1,9},{5,13},{9,1},{13,5},{2,10},{6,14},... | collective-permute-start | bytes 1032200 | tf_op jit(solution)/shard_map/ppermute | solution.py:25
  40.6 2.4 %collective-permute-start.12 = (bf16[96,1792]{1,0:T(8,128)(2,1)S(1)}, bf16[96,1792]{1,0:T(8,128)(2,1)S(1)}, u32[]{:S(2)}, u32[]{:S(2)}) collective-permute-start(bf16[96,1792]{1,0:T(8,128)(2,1)S(1)} %slice.61), channel_id=1, source_target_pairs={{0,4},{4,0},{8,12},{12,8},{1,5},{5,1},{9,13},{13,9},{2,6},{6,2},{1... | collective-permute-start | bytes 1032200 | tf_op jit(solution)/shard_map/ppermute | solution.py:25
  43.3 1.2 %fusion.10 = f32[128,1792]{1,0:T(8,128)S(1)} fusion(bf16[2048,1792]{1,0:T(8,128)(2,1)S(1)} %get-tuple-element.35, f32[128]{0:T(128)S(1)} %add_rsqrt_fusion, f32[2048]{0:T(1024)S(1)} %bitcast.26, bf16[32,2048]{1,0:T(8,128)(2,1)S(1)} %collective-permute-done.9.refs_10_, bf16[32,2048]{1,0:T(8,128)(2,1)S(1)} %collective-permute-done.8.refs_9_, ...), kind=kOutput, calls=%fused_computation.26 | convolution fusion | flops 942407680 | bytes 8790528 | tf_op jit(solution)/shard_map/dot_general | solution.py:409
  44.5 1.5 %multiply_convert_fusion = (bf16[128,1792]{1,0:T(8,128)(2,1)S(1)}, bf16[128,1792]{1,0:T(8,128)(2,1)S(1)}, bf16[128,1792]{1,0:T(8,128)(2,1)S(1)}) fusion(f32[128,1792]{1,0:T(8,128)S(1)} %fusion.10, f32[128,1792]{1,0:T(8,128)S(1)} %shard_map.96, bf16[2048,1792]{1,0:T(8,128)(2,1)S(1)} %get-tuple-element.36.up_ref, f32[128]{0:T(128)S(1)} %add_rsqrt_fusion, ...), kind=kOutput, calls=%fused_computation.18 | convolution fusion | flops 946077696 | bytes 11084288 | tf_op jit(solution)/shard_map/dot_general | solution.py:410
  46.9 0.7 collective-permute-done.11.refs_1_
  47.6 2.2 %collective-permute-done.12.refs_2_ = bf16[96,1792]{1,0:T(8,128)(2,1)S(1)} collective-permute-done((bf16[96,1792]{1,0:T(8,128)(2,1)S(1)}, bf16[96,1792]{1,0:T(8,128)(2,1)S(1)}, u32[]{:S(2)}, u32[]{:S(2)}) %collective-permute-start.12) | collective-permute-done | bytes 344096 | tf_op jit(solution)/shard_map/ppermute | solution.py:25
  49.8 1.3 %collective-permute-start.16 = (bf16[32,2048]{1,0:T(8,128)(2,1)S(1)}, bf16[32,2048]{1,0:T(8,128)(2,1)S(1)}, u32[]{:S(2)}, u32[]{:S(2)}) collective-permute-start(bf16[32,2048]{1,0:T(8,128)(2,1)S(1)} %get-tuple-element.78), channel_id=1, source_target_pairs={{16,3},{17,2},{18,1},{19,0},{20,7},{21,6},{22,5},{23,4},{24,11},{2... | collective-permute-start | bytes 393224 | tf_op jit(solution)/shard_map/ppermute | solution.py:33
  51.1 1.3 %collective-permute-start.15 = (bf16[32,2048]{1,0:T(8,128)(2,1)S(1)}, bf16[32,2048]{1,0:T(8,128)(2,1)S(1)}, u32[]{:S(2)}, u32[]{:S(2)}) collective-permute-start(bf16[32,2048]{1,0:T(8,128)(2,1)S(1)} %get-tuple-element.79), channel_id=1, source_target_pairs={{16,2},{17,3},{18,0},{19,1},{20,6},{21,7},{22,4},{23,5},{24,10},{2... | collective-permute-start | bytes 393224 | tf_op jit(solution)/shard_map/ppermute | solution.py:33
  52.4 1.3 %collective-permute-start.14 = (bf16[32,2048]{1,0:T(8,128)(2,1)S(1)}, bf16[32,2048]{1,0:T(8,128)(2,1)S(1)}, u32[]{:S(2)}, u32[]{:S(2)}) collective-permute-start(bf16[32,2048]{1,0:T(8,128)(2,1)S(1)} %get-tuple-element.80), channel_id=1, source_target_pairs={{16,1},{17,0},{18,3},{19,2},{20,5},{21,4},{22,7},{23,6},{24,9},{25... | collective-permute-start | bytes 393224 | tf_op jit(solution)/shard_map/ppermute | solution.py:33
  53.7 1.3 %collective-permute-start.13 = (bf16[32,2048]{1,0:T(8,128)(2,1)S(1)}, bf16[32,2048]{1,0:T(8,128)(2,1)S(1)}, u32[]{:S(2)}, u32[]{:S(2)}) collective-permute-start(bf16[32,2048]{1,0:T(8,128)(2,1)S(1)} %get-tuple-element.77), channel_id=1, source_target_pairs={{16,0},{17,1},{18,2},{19,3},{20,4},{21,5},{22,6},{23,7},{24,8},{25... | collective-permute-start | bytes 393224 | tf_op jit(solution)/shard_map/ppermute | solution.py:33
  55.2 3.0 %collective-permute-done.13 = bf16[32,2048]{1,0:T(8,128)(2,1)S(1)} collective-permute-done((bf16[32,2048]{1,0:T(8,128)(2,1)S(1)}, bf16[32,2048]{1,0:T(8,128)(2,1)S(1)}, u32[]{:S(2)}, u32[]{:S(2)}) %collective-permute-start.13) | collective-permute-done | bytes 131104 | tf_op jit(solution)/shard_map/ppermute | solution.py:33
  58.1 3.1 %collective-permute-done.15 = bf16[32,2048]{1,0:T(8,128)(2,1)S(1)} collective-permute-done((bf16[32,2048]{1,0:T(8,128)(2,1)S(1)}, bf16[32,2048]{1,0:T(8,128)(2,1)S(1)}, u32[]{:S(2)}, u32[]{:S(2)}) %collective-permute-start.15) | collective-permute-done | bytes 131104 | tf_op jit(solution)/shard_map/ppermute | solution.py:33
  61.4 1.5 %collective-permute-start.21 = (bf16[48,512]{1,0:T(8,128)(2,1)S(1)}, bf16[48,512]{1,0:T(8,128)(2,1)S(1)}, u32[]{:S(2)}, u32[]{:S(2)}) collective-permute-start(bf16[48,512]{1,0:T(8,128)(2,1)S(1)} %get-tuple-element.93), channel_id=1, source_target_pairs={{0,12},{4,8},{8,4},{12,0},{1,13},{5,9},{9,5},{13,1},{2,14},{6,10},... | collective-permute-start | bytes 147464 | tf_op jit(solution)/shard_map/ppermute | solution.py:19
  63.5 1.5 %collective-permute-start.19 = (bf16[48,512]{1,0:T(8,128)(2,1)S(1)}, bf16[48,512]{1,0:T(8,128)(2,1)S(1)}, u32[]{:S(2)}, u32[]{:S(2)}) collective-permute-start(bf16[48,512]{1,0:T(8,128)(2,1)S(1)} %get-tuple-element.91), channel_id=1, source_target_pairs={{0,4},{4,0},{8,12},{12,8},{1,5},{5,1},{9,13},{13,9},{2,6},{6,2},{1... | collective-permute-start | bytes 147464 | tf_op jit(solution)/shard_map/ppermute | solution.py:19
  65.0 0.7 collective-permute-start.22
  65.7 0.7 collective-permute-start.17
  66.5 0.7 collective-permute-start.18
  67.2 1.7 %collective-permute-done.20 = bf16[48,512]{1,0:T(8,128)(2,1)S(1)} collective-permute-done((bf16[48,512]{1,0:T(8,128)(2,1)S(1)}, bf16[48,512]{1,0:T(8,128)(2,1)S(1)}, u32[]{:S(2)}, u32[]{:S(2)}) %collective-permute-start.20) | collective-permute-done | bytes 49184 | tf_op jit(solution)/shard_map/ppermute | solution.py:19
  69.3 0.9 dynamic-slice_select_fusion
  70.6 3.9 %collective-permute-start.25 = (bf16[128,512]{1,0:T(8,128)(2,1)S(1)}, bf16[128,512]{1,0:T(8,128)(2,1)S(1)}, u32[]{:S(2)}, u32[]{:S(2)}) collective-permute-start(bf16[128,512]{1,0:T(8,128)(2,1)S(1)} %get-tuple-element.74), channel_id=1, source_target_pairs={{0,1},{16,20},{1,0},{17,21},{2,3},{18,22},{3,2},{19,23},{4,5},{20,... | collective-permute-start | bytes 393224 | tf_op jit(solution)/shard_map/ppermute | solution.py:63
  74.9 0.7 copy-done.9
  75.6 0.8 copy-done.10
  76.4 2.7 %shard_map.98 = (bf16[512,1792]{1,0:T(8,128)(2,1)S(1)}, f32[512,512]{1,0:T(8,128)S(1)}) custom-call(s32[1]{0:T(128)} %bitcast.flag_ref, bf16[96,1792]{1,0:T(8,128)(2,1)} %copy-done.11, bf16[96,1792]{1,0:T(8,128)(2,1)} %copy-done.12, bf16[96,1792]{1,0:T(8,128)(2,1)} %copy-done.13, bf16[128,1792]{1,0:T(8,128)(2,1)} %copy-done, bf16[128,1792]{1,0:T(8,128)(2,1)} %copy-done.7, ...), custom_call_target="tpu_custom_call" | custom-call | flops 939524096 | bytes 4718592 | tf_op jit(solution)/shard_map/pallas_call | solution.py:292
  79.5 1.7 %shard_map.99 = (bf16[512,2048]{1,0:T(8,128)(2,1)S(1)}, f32[8,128]{1,0:T(8,128)S(1)}) custom-call(s32[1]{0:T(128)} %bitcast.flag_ref, s32[512,1]{1,0:T(8,128)S(1)} %reshape.87.ids_ref, s32[1,512]{1,0:T(1,128)S(1)} %reshape_reshape.3.ids_row_ref, f32[512,512]{1,0:T(8,128)S(1)} %get-tuple-element.59.gram_ref, ...), custom_call_target="tpu_custom_call" | custom-call | flops 269484032 | bytes 2097152 | tf_op jit(solution)/shard_map/pallas_call | solution.py:362
  81.3 2.5 %collective-permute-start.26 = (f32[8,128]{1,0:T(8,128)S(1)}, f32[8,128]{1,0:T(8,128)S(1)}, u32[]{:S(2)}, u32[]{:S(2)}) collective-permute-start(f32[8,128]{1,0:T(8,128)S(1)} %get-tuple-element.62), channel_id=1, source_target_pairs={{0,3},{1,2},{2,1},{3,0},{4,7},{5,6},{6,5},{7,4},{8,11},{9,10},{10,... | collective-permute-start | bytes 12296 | tf_op jit(solution)/shard_map/ppermute | solution.py:19
  83.8 1.0 %collective-permute-start.27 = (f32[8,128]{1,0:T(8,128)S(1)}, f32[8,128]{1,0:T(8,128)S(1)}, u32[]{:S(2)}, u32[]{:S(2)}) collective-permute-start(f32[8,128]{1,0:T(8,128)S(1)} %get-tuple-element.62), channel_id=1, source_target_pairs={{0,2},{1,3},{2,0},{3,1},{4,6},{5,7},{6,4},{7,5},{8,10},{9,11},{10,... | collective-permute-start | bytes 12296 | tf_op jit(solution)/shard_map/ppermute | solution.py:19
  84.8 2.5 %shard_map.100.rest_0_ = bf16[4,1792,512]{2,1,0:T(8,128)(2,1)} custom-call(bf16[512,1792]{1,0:T(8,128)(2,1)S(1)} %get-tuple-element.58.hidden_ref, bf16[512,2048]{1,0:T(8,128)(2,1)S(1)} %get-tuple-element.65.masked_ref), custom_call_target="tpu_custom_call" | custom-call | flops 1073741824 | bytes 2621440 | tf_op jit(solution)/shard_map/pallas_call | solution.py:224
  87.3 1.0 collective-permute-done.27
  88.3 1.8 %collective-permute-start.31 = (f32[8,128]{1,0:T(8,128)S(1)}, f32[8,128]{1,0:T(8,128)S(1)}, u32[]{:S(2)}, u32[]{:S(2)}) collective-permute-start(f32[8,128]{1,0:T(8,128)S(1)} %add_add_fusion.1), channel_id=1, source_target_pairs={{0,4},{4,0},{8,12},{12,8},{1,5},{5,1},{9,13},{13,9},{2,6},{6,2},{1... | collective-permute-start | bytes 12296 | tf_op jit(solution)/shard_map/ppermute | solution.py:19
  90.6 1.2 %collective-permute-start.30 = (f32[8,128]{1,0:T(8,128)S(1)}, f32[8,128]{1,0:T(8,128)S(1)}, u32[]{:S(2)}, u32[]{:S(2)}) collective-permute-start(f32[8,128]{1,0:T(8,128)S(1)} %add_add_fusion.1), channel_id=1, source_target_pairs={{0,8},{4,12},{8,0},{12,4},{1,9},{5,13},{9,1},{13,5},{2,10},{6,14},... | collective-permute-start | bytes 12296 | tf_op jit(solution)/shard_map/ppermute | solution.py:19
  91.8 2.5 %shard_map.101.rest_0_ = bf16[4,1792,512]{2,1,0:T(8,128)(2,1)} custom-call(bf16[512,1792]{1,0:T(8,128)(2,1)S(1)} %get-tuple-element.58.hidden_ref, bf16[512,2048]{1,0:T(8,128)(2,1)S(1)} %get-tuple-element.65.masked_ref, bf16[4,1792,512]{2,1,0:T(8,128)(2,1)} %shard_map.100.rest_0_), custom_call_target="tpu_custom_call", output_to_operand_aliasing={{}: (2, {})} | custom-call | flops 1073741824 | bytes 2621440 | tf_op jit(solution)/shard_map/pallas_call | solution.py:224
  94.6 1.0 collective-permute-start.32
  95.5 3.5 %shard_map.102 = bf16[4,1792,512]{2,1,0:T(8,128)(2,1)} custom-call(bf16[512,1792]{1,0:T(8,128)(2,1)S(1)} %get-tuple-element.58.hidden_ref, bf16[512,2048]{1,0:T(8,128)(2,1)S(1)} %get-tuple-element.65.masked_ref, bf16[4,1792,512]{2,1,0:T(8,128)(2,1)} %shard_map.101.rest_0_), custom_call_target="tpu_custom_call", output_to_operand_aliasing={{}: (2, {})} | custom-call | flops 1610612736 | bytes 3932160 | tf_op jit(solution)/shard_map/pallas_call | solution.py:224
  (103 shorter events, 6.6 us)
Async XLA Ops:
  1.6 16.4 %copy-start.14 = (f32[1,2048]{1,0:T(1,128)S(1)}, f32[1,2048]{1,0:T(1,128)}, u32[]{:S(2)}) copy-start(f32[1,2048]{1,0:T(1,128)} %param.11) | copy-start | bytes 24580
  1.6 13.2 %collective-permute-start.2 = (bf16[32,2048]{1,0:T(8,128)(2,1)S(1)}, bf16[32,2048]{1,0:T(8,128)(2,1)S(1)}, u32[]{:S(2)}, u32[]{:S(2)}) collective-permute-start(bf16[32,2048]{1,0:T(8,128)(2,1)S(1)} %bitcast_select_fusion.1), channel_id=1, source_target_pairs={{0,3},{1,2},{2,1},{3,0},{4,7},{5,6},{6,5},{7,4},{8,11},{9,10},{10,... | collective-permute-start | bytes 393224 | tf_op jit(solution)/shard_map/ppermute | solution.py:19
  6.8 11.1 %collective-permute-start.1 = (bf16[32,2048]{1,0:T(8,128)(2,1)S(1)}, bf16[32,2048]{1,0:T(8,128)(2,1)S(1)}, u32[]{:S(2)}, u32[]{:S(2)}) collective-permute-start(bf16[32,2048]{1,0:T(8,128)(2,1)S(1)} %bitcast_select_fusion.1), channel_id=1, source_target_pairs={{0,2},{1,3},{2,0},{3,1},{4,6},{5,7},{6,4},{7,5},{8,10},{9,11},{10,... | collective-permute-start | bytes 393224 | tf_op jit(solution)/shard_map/ppermute | solution.py:19
  6.8 11.1 %collective-permute-start = (bf16[32,2048]{1,0:T(8,128)(2,1)S(1)}, bf16[32,2048]{1,0:T(8,128)(2,1)S(1)}, u32[]{:S(2)}, u32[]{:S(2)}) collective-permute-start(bf16[32,2048]{1,0:T(8,128)(2,1)S(1)} %bitcast_select_fusion.1), channel_id=1, source_target_pairs={{0,1},{1,0},{2,3},{3,2},{4,5},{5,4},{6,7},{7,6},{8,9},{9,8},{10,11... | collective-permute-start | bytes 393224 | tf_op jit(solution)/shard_map/ppermute | solution.py:19
  20.6 8.2 %copy-start = (bf16[128,1792]{1,0:T(8,128)(2,1)}, bf16[128,1792]{1,0:T(8,128)(2,1)S(1)}, u32[]{:S(2)}) copy-start(bf16[128,1792]{1,0:T(8,128)(2,1)S(1)} %fusion.refs_3_) | copy-start | bytes 1376260
  21.8 8.3 %copy-start.6 = (bf16[4,8,2048]{2,1,0:T(8,128)(2,1)S(1)}, bf16[4,8,2048]{2,1,0:T(8,128)(2,1)}, u32[]{:S(2)}) copy-start(bf16[4,8,2048]{2,1,0:T(8,128)(2,1)} %param.8) | copy-start | bytes 393220
  21.8 7.0 %collective-permute-start.6 = (bf16[32,2048]{1,0:T(8,128)(2,1)S(1)}, bf16[32,2048]{1,0:T(8,128)(2,1)S(1)}, u32[]{:S(2)}, u32[]{:S(2)}) collective-permute-start(bf16[32,2048]{1,0:T(8,128)(2,1)S(1)} %get-tuple-element.82), channel_id=1, source_target_pairs={{0,19},{1,18},{2,17},{3,16},{4,23},{5,22},{6,21},{7,20},{8,27},{9,... | collective-permute-start | bytes 393224 | tf_op jit(solution)/shard_map/ppermute | solution.py:33
  24.8 4.0 %collective-permute-start.5 = (bf16[32,2048]{1,0:T(8,128)(2,1)S(1)}, bf16[32,2048]{1,0:T(8,128)(2,1)S(1)}, u32[]{:S(2)}, u32[]{:S(2)}) collective-permute-start(bf16[32,2048]{1,0:T(8,128)(2,1)S(1)} %get-tuple-element.83), channel_id=1, source_target_pairs={{0,18},{1,19},{2,16},{3,17},{4,22},{5,23},{6,20},{7,21},{8,26},{9,... | collective-permute-start | bytes 393224 | tf_op jit(solution)/shard_map/ppermute | solution.py:33
  26.1 4.0 %collective-permute-start.4 = (bf16[32,2048]{1,0:T(8,128)(2,1)S(1)}, bf16[32,2048]{1,0:T(8,128)(2,1)S(1)}, u32[]{:S(2)}, u32[]{:S(2)}) collective-permute-start(bf16[32,2048]{1,0:T(8,128)(2,1)S(1)} %get-tuple-element.84), channel_id=1, source_target_pairs={{0,17},{1,16},{2,19},{3,18},{4,21},{5,20},{6,23},{7,22},{8,25},{9,... | collective-permute-start | bytes 393224 | tf_op jit(solution)/shard_map/ppermute | solution.py:33
  27.4 2.7 %collective-permute-start.3 = (bf16[32,2048]{1,0:T(8,128)(2,1)S(1)}, bf16[32,2048]{1,0:T(8,128)(2,1)S(1)}, u32[]{:S(2)}, u32[]{:S(2)}) collective-permute-start(bf16[32,2048]{1,0:T(8,128)(2,1)S(1)} %get-tuple-element.81), channel_id=1, source_target_pairs={{0,16},{1,17},{2,18},{3,19},{4,20},{5,21},{6,22},{7,23},{8,24},{9,... | collective-permute-start | bytes 393224 | tf_op jit(solution)/shard_map/ppermute | solution.py:33
  28.7 5.1 %copy-start.1 = (bf16[128,1792]{1,0:T(8,128)(2,1)S(1)}, bf16[128,1792]{1,0:T(8,128)(2,1)}, u32[]{:S(2)}) copy-start(bf16[128,1792]{1,0:T(8,128)(2,1)} %copy-done) | copy-start | bytes 1376260
  30.3 10.4 %collective-permute-start.9 = (bf16[32,2048]{1,0:T(8,128)(2,1)S(1)}, bf16[32,2048]{1,0:T(8,128)(2,1)S(1)}, u32[]{:S(2)}, u32[]{:S(2)}) collective-permute-start(bf16[32,2048]{1,0:T(8,128)(2,1)S(1)} %pad_select_fusion), channel_id=1, source_target_pairs={{0,12},{16,19},{1,13},{17,18},{2,14},{18,17},{3,15},{19,16},{4,8},... | collective-permute-start | bytes 393224 | tf_op jit(solution)/shard_map/ppermute | solution.py:53
  32.8 10.3 %collective-permute-start.8 = (bf16[32,2048]{1,0:T(8,128)(2,1)S(1)}, bf16[32,2048]{1,0:T(8,128)(2,1)S(1)}, u32[]{:S(2)}, u32[]{:S(2)}) collective-permute-start(bf16[32,2048]{1,0:T(8,128)(2,1)S(1)} %pad_select_fusion), channel_id=1, source_target_pairs={{0,8},{16,18},{1,9},{17,19},{2,10},{18,16},{3,11},{19,17},{4,12},{... | collective-permute-start | bytes 393224 | tf_op jit(solution)/shard_map/ppermute | solution.py:53
  33.3 9.8 %collective-permute-start.7 = (bf16[32,2048]{1,0:T(8,128)(2,1)S(1)}, bf16[32,2048]{1,0:T(8,128)(2,1)S(1)}, u32[]{:S(2)}, u32[]{:S(2)}) collective-permute-start(bf16[32,2048]{1,0:T(8,128)(2,1)S(1)} %pad_select_fusion), channel_id=1, source_target_pairs={{0,4},{16,17},{1,5},{17,16},{2,6},{18,19},{3,7},{19,18},{4,0},{20,... | collective-permute-start | bytes 393224 | tf_op jit(solution)/shard_map/ppermute | solution.py:53
  33.8 13.0 %collective-permute-start.10 = (bf16[96,1792]{1,0:T(8,128)(2,1)S(1)}, bf16[96,1792]{1,0:T(8,128)(2,1)S(1)}, u32[]{:S(2)}, u32[]{:S(2)}) collective-permute-start(bf16[96,1792]{1,0:T(8,128)(2,1)S(1)} %slice.61), channel_id=1, source_target_pairs={{0,12},{4,8},{8,4},{12,0},{1,13},{5,9},{9,5},{13,1},{2,14},{6,10},... | collective-permute-start | bytes 1032200 | tf_op jit(solution)/shard_map/ppermute | solution.py:25
  38.2 9.4 %collective-permute-start.11 = (bf16[96,1792]{1,0:T(8,128)(2,1)S(1)}, bf16[96,1792]{1,0:T(8,128)(2,1)S(1)}, u32[]{:S(2)}, u32[]{:S(2)}) collective-permute-start(bf16[96,1792]{1,0:T(8,128)(2,1)S(1)} %slice.61), channel_id=1, source_target_pairs={{0,8},{4,12},{8,0},{12,4},{1,9},{5,13},{9,1},{13,5},{2,10},{6,14},... | collective-permute-start | bytes 1032200 | tf_op jit(solution)/shard_map/ppermute | solution.py:25
  40.6 6.0 %copy-start.2 = (bf16[32,2048]{1,0:T(8,128)(2,1)}, bf16[32,2048]{1,0:T(8,128)(2,1)S(1)}, u32[]{:S(2)}) copy-start(bf16[32,2048]{1,0:T(8,128)(2,1)S(1)} %collective-permute-done.9.refs_10_) | copy-start | bytes 393220
  40.6 9.1 %collective-permute-start.12 = (bf16[96,1792]{1,0:T(8,128)(2,1)S(1)}, bf16[96,1792]{1,0:T(8,128)(2,1)S(1)}, u32[]{:S(2)}, u32[]{:S(2)}) collective-permute-start(bf16[96,1792]{1,0:T(8,128)(2,1)S(1)} %slice.61), channel_id=1, source_target_pairs={{0,4},{4,0},{8,12},{12,8},{1,5},{5,1},{9,13},{13,9},{2,6},{6,2},{1... | collective-permute-start | bytes 1032200 | tf_op jit(solution)/shard_map/ppermute | solution.py:25
  43.1 3.5 %copy-start.3 = (bf16[32,2048]{1,0:T(8,128)(2,1)}, bf16[32,2048]{1,0:T(8,128)(2,1)S(1)}, u32[]{:S(2)}) copy-start(bf16[32,2048]{1,0:T(8,128)(2,1)S(1)} %collective-permute-done.8.refs_9_) | copy-start | bytes 393220
  43.1 3.5 %copy-start.4 = (bf16[32,2048]{1,0:T(8,128)(2,1)}, bf16[32,2048]{1,0:T(8,128)(2,1)S(1)}, u32[]{:S(2)}) copy-start(bf16[32,2048]{1,0:T(8,128)(2,1)S(1)} %collective-permute-done.7.refs_8_) | copy-start | bytes 393220
  46.0 20.5 %copy-start.7 = (bf16[128,1792]{1,0:T(8,128)(2,1)}, bf16[128,1792]{1,0:T(8,128)(2,1)S(1)}, u32[]{:S(2)}) copy-start(bf16[128,1792]{1,0:T(8,128)(2,1)S(1)} %get-tuple-element.56.refs_4_) | copy-start | bytes 1376260
  46.1 9.0 %copy-start.16 = (s32[4,1]{0,1:T(1,128)S(1)}, s32[4,1]{0,1:T(1,128)}, u32[]{:S(2)}) copy-start(s32[4,1]{0,1:T(1,128)} %param.10) | copy-start | bytes 52
  46.1 15.1 %copy-start.5 = (bf16[4,8,2048]{2,1,0:T(8,128)(2,1)S(1)}, bf16[4,8,2048]{2,1,0:T(8,128)(2,1)}, u32[]{:S(2)}) copy-start(bf16[4,8,2048]{2,1,0:T(8,128)(2,1)} %param.9) | copy-start | bytes 393220
  46.9 28.0 %copy-start.11 = (bf16[96,1792]{1,0:T(8,128)(2,1)}, bf16[96,1792]{1,0:T(8,128)(2,1)S(1)}, u32[]{:S(2)}) copy-start(bf16[96,1792]{1,0:T(8,128)(2,1)S(1)} %collective-permute-done.10.refs_0_) | copy-start | bytes 1032196
  47.6 27.3 %copy-start.12 = (bf16[96,1792]{1,0:T(8,128)(2,1)}, bf16[96,1792]{1,0:T(8,128)(2,1)S(1)}, u32[]{:S(2)}) copy-start(bf16[96,1792]{1,0:T(8,128)(2,1)S(1)} %collective-permute-done.11.refs_1_) | copy-start | bytes 1032196
  49.8 15.2 %copy-start.13 = (bf16[96,1792]{1,0:T(8,128)(2,1)}, bf16[96,1792]{1,0:T(8,128)(2,1)S(1)}, u32[]{:S(2)}) copy-start(bf16[96,1792]{1,0:T(8,128)(2,1)S(1)} %collective-permute-done.12.refs_2_) | copy-start | bytes 1032196
  49.8 8.3 %collective-permute-start.16 = (bf16[32,2048]{1,0:T(8,128)(2,1)S(1)}, bf16[32,2048]{1,0:T(8,128)(2,1)S(1)}, u32[]{:S(2)}, u32[]{:S(2)}) collective-permute-start(bf16[32,2048]{1,0:T(8,128)(2,1)S(1)} %get-tuple-element.78), channel_id=1, source_target_pairs={{16,3},{17,2},{18,1},{19,0},{20,7},{21,6},{22,5},{23,4},{24,11},{2... | collective-permute-start | bytes 393224 | tf_op jit(solution)/shard_map/ppermute | solution.py:33
  51.1 10.1 %collective-permute-start.15 = (bf16[32,2048]{1,0:T(8,128)(2,1)S(1)}, bf16[32,2048]{1,0:T(8,128)(2,1)S(1)}, u32[]{:S(2)}, u32[]{:S(2)}) collective-permute-start(bf16[32,2048]{1,0:T(8,128)(2,1)S(1)} %get-tuple-element.79), channel_id=1, source_target_pairs={{16,2},{17,3},{18,0},{19,1},{20,6},{21,7},{22,4},{23,5},{24,10},{2... | collective-permute-start | bytes 393224 | tf_op jit(solution)/shard_map/ppermute | solution.py:33
  52.4 8.8 %collective-permute-start.14 = (bf16[32,2048]{1,0:T(8,128)(2,1)S(1)}, bf16[32,2048]{1,0:T(8,128)(2,1)S(1)}, u32[]{:S(2)}, u32[]{:S(2)}) collective-permute-start(bf16[32,2048]{1,0:T(8,128)(2,1)S(1)} %get-tuple-element.80), channel_id=1, source_target_pairs={{16,1},{17,0},{18,3},{19,2},{20,5},{21,4},{22,7},{23,6},{24,9},{25... | collective-permute-start | bytes 393224 | tf_op jit(solution)/shard_map/ppermute | solution.py:33
  53.7 4.4 %collective-permute-start.13 = (bf16[32,2048]{1,0:T(8,128)(2,1)S(1)}, bf16[32,2048]{1,0:T(8,128)(2,1)S(1)}, u32[]{:S(2)}, u32[]{:S(2)}) collective-permute-start(bf16[32,2048]{1,0:T(8,128)(2,1)S(1)} %get-tuple-element.77), channel_id=1, source_target_pairs={{16,0},{17,1},{18,2},{19,3},{20,4},{21,5},{22,6},{23,7},{24,8},{25... | collective-permute-start | bytes 393224 | tf_op jit(solution)/shard_map/ppermute | solution.py:33
  61.4 5.1 %collective-permute-start.21 = (bf16[48,512]{1,0:T(8,128)(2,1)S(1)}, bf16[48,512]{1,0:T(8,128)(2,1)S(1)}, u32[]{:S(2)}, u32[]{:S(2)}) collective-permute-start(bf16[48,512]{1,0:T(8,128)(2,1)S(1)} %get-tuple-element.93), channel_id=1, source_target_pairs={{0,12},{4,8},{8,4},{12,0},{1,13},{5,9},{9,5},{13,1},{2,14},{6,10},... | collective-permute-start | bytes 147464 | tf_op jit(solution)/shard_map/ppermute | solution.py:19
  63.0 5.9 %collective-permute-start.20 = (bf16[48,512]{1,0:T(8,128)(2,1)S(1)}, bf16[48,512]{1,0:T(8,128)(2,1)S(1)}, u32[]{:S(2)}, u32[]{:S(2)}) collective-permute-start(bf16[48,512]{1,0:T(8,128)(2,1)S(1)} %get-tuple-element.92), channel_id=1, source_target_pairs={{0,8},{4,12},{8,0},{12,4},{1,9},{5,13},{9,1},{13,5},{2,10},{6,14},... | collective-permute-start | bytes 147464 | tf_op jit(solution)/shard_map/ppermute | solution.py:19
  63.5 5.4 %collective-permute-start.19 = (bf16[48,512]{1,0:T(8,128)(2,1)S(1)}, bf16[48,512]{1,0:T(8,128)(2,1)S(1)}, u32[]{:S(2)}, u32[]{:S(2)}) collective-permute-start(bf16[48,512]{1,0:T(8,128)(2,1)S(1)} %get-tuple-element.91), channel_id=1, source_target_pairs={{0,4},{4,0},{8,12},{12,8},{1,5},{5,1},{9,13},{13,9},{2,6},{6,2},{1... | collective-permute-start | bytes 147464 | tf_op jit(solution)/shard_map/ppermute | solution.py:19
  65.0 4.2 %collective-permute-start.22 = (bf16[128,1792]{1,0:T(8,128)(2,1)S(1)}, bf16[128,1792]{1,0:T(8,128)(2,1)S(1)}, u32[]{:S(2)}, u32[]{:S(2)}) collective-permute-start(bf16[128,1792]{1,0:T(8,128)(2,1)S(1)} %get-tuple-element.56.refs_4_), channel_id=1, source_target_pairs={{16,28},{20,24},{24,20},{28,16},{17,29},{21,25},{25,21},{29,17},{1... | collective-permute-start | bytes 1376264 | tf_op jit(solution)/shard_map/ppermute | solution.py:25
  65.7 9.1 %collective-permute-start.17 = (bf16[128,1792]{1,0:T(8,128)(2,1)S(1)}, bf16[128,1792]{1,0:T(8,128)(2,1)S(1)}, u32[]{:S(2)}, u32[]{:S(2)}) collective-permute-start(bf16[128,1792]{1,0:T(8,128)(2,1)S(1)} %get-tuple-element.56.refs_4_), channel_id=1, source_target_pairs={{16,20},{20,16},{24,28},{28,24},{17,21},{21,17},{25,29},{29,25},{1... | collective-permute-start | bytes 1376264 | tf_op jit(solution)/shard_map/ppermute | solution.py:25
  66.5 8.4 %collective-permute-start.18 = (bf16[128,1792]{1,0:T(8,128)(2,1)S(1)}, bf16[128,1792]{1,0:T(8,128)(2,1)S(1)}, u32[]{:S(2)}, u32[]{:S(2)}) collective-permute-start(bf16[128,1792]{1,0:T(8,128)(2,1)S(1)} %get-tuple-element.56.refs_4_), channel_id=1, source_target_pairs={{16,24},{20,28},{24,16},{28,20},{17,25},{21,29},{25,17},{29,21},{1... | collective-permute-start | bytes 1376264 | tf_op jit(solution)/shard_map/ppermute | solution.py:25
  69.2 5.6 %copy-start.8 = (bf16[128,1792]{1,0:T(8,128)(2,1)}, bf16[128,1792]{1,0:T(8,128)(2,1)S(1)}, u32[]{:S(2)}) copy-start(bf16[128,1792]{1,0:T(8,128)(2,1)S(1)} %collective-permute-done.22.refs_7_) | copy-start | bytes 1376260
  70.1 8.9 %collective-permute-start.23 = (bf16[128,512]{1,0:T(8,128)(2,1)}, bf16[128,512]{1,0:T(8,128)(2,1)S(1)}, u32[]{:S(2)}, u32[]{:S(2)}) collective-permute-start(bf16[128,512]{1,0:T(8,128)(2,1)} %get-tuple-element.76), channel_id=1, source_target_pairs={{0,3},{16,28},{1,2},{17,29},{2,1},{18,30},{3,0},{19,31},{4,7},{20,... | collective-permute-start | bytes 393224 | tf_op jit(solution)/shard_map/ppermute | solution.py:63
  70.6 8.9 %collective-permute-start.24 = (bf16[128,512]{1,0:T(8,128)(2,1)}, bf16[128,512]{1,0:T(8,128)(2,1)S(1)}, u32[]{:S(2)}, u32[]{:S(2)}) collective-permute-start(bf16[128,512]{1,0:T(8,128)(2,1)} %get-tuple-element.75), channel_id=1, source_target_pairs={{0,2},{16,24},{1,3},{17,25},{2,0},{18,26},{3,1},{19,27},{4,6},{20,... | collective-permute-start | bytes 393224 | tf_op jit(solution)/shard_map/ppermute | solution.py:63
  70.6 8.9 %collective-permute-start.25 = (bf16[128,512]{1,0:T(8,128)(2,1)S(1)}, bf16[128,512]{1,0:T(8,128)(2,1)S(1)}, u32[]{:S(2)}, u32[]{:S(2)}) collective-permute-start(bf16[128,512]{1,0:T(8,128)(2,1)S(1)} %get-tuple-element.74), channel_id=1, source_target_pairs={{0,1},{16,20},{1,0},{17,21},{2,3},{18,22},{3,2},{19,23},{4,5},{20,... | collective-permute-start | bytes 393224 | tf_op jit(solution)/shard_map/ppermute | solution.py:63
  81.2 6.1 %collective-permute-start.28 = (f32[8,128]{1,0:T(8,128)S(1)}, f32[8,128]{1,0:T(8,128)S(1)}, u32[]{:S(2)}, u32[]{:S(2)}) collective-permute-start(f32[8,128]{1,0:T(8,128)S(1)} %get-tuple-element.62), channel_id=1, source_target_pairs={{0,1},{1,0},{2,3},{3,2},{4,5},{5,4},{6,7},{7,6},{8,9},{9,8},{10,11... | collective-permute-start | bytes 12296 | tf_op jit(solution)/shard_map/ppermute | solution.py:19
  81.3 6.0 %collective-permute-start.26 = (f32[8,128]{1,0:T(8,128)S(1)}, f32[8,128]{1,0:T(8,128)S(1)}, u32[]{:S(2)}, u32[]{:S(2)}) collective-permute-start(f32[8,128]{1,0:T(8,128)S(1)} %get-tuple-element.62), channel_id=1, source_target_pairs={{0,3},{1,2},{2,1},{3,0},{4,7},{5,6},{6,5},{7,4},{8,11},{9,10},{10,... | collective-permute-start | bytes 12296 | tf_op jit(solution)/shard_map/ppermute | solution.py:19
  83.8 4.5 %collective-permute-start.27 = (f32[8,128]{1,0:T(8,128)S(1)}, f32[8,128]{1,0:T(8,128)S(1)}, u32[]{:S(2)}, u32[]{:S(2)}) collective-permute-start(f32[8,128]{1,0:T(8,128)S(1)} %get-tuple-element.62), channel_id=1, source_target_pairs={{0,2},{1,3},{2,0},{3,1},{4,6},{5,7},{6,4},{7,5},{8,10},{9,11},{10,... | collective-permute-start | bytes 12296 | tf_op jit(solution)/shard_map/ppermute | solution.py:19
  88.3 6.0 %collective-permute-start.31 = (f32[8,128]{1,0:T(8,128)S(1)}, f32[8,128]{1,0:T(8,128)S(1)}, u32[]{:S(2)}, u32[]{:S(2)}) collective-permute-start(f32[8,128]{1,0:T(8,128)S(1)} %add_add_fusion.1), channel_id=1, source_target_pairs={{0,4},{4,0},{8,12},{12,8},{1,5},{5,1},{9,13},{13,9},{2,6},{6,2},{1... | collective-permute-start | bytes 12296 | tf_op jit(solution)/shard_map/ppermute | solution.py:19
  90.0 4.5 %collective-permute-start.29 = (f32[8,128]{1,0:T(8,128)S(1)}, f32[8,128]{1,0:T(8,128)S(1)}, u32[]{:S(2)}, u32[]{:S(2)}) collective-permute-start(f32[8,128]{1,0:T(8,128)S(1)} %add_add_fusion.1), channel_id=1, source_target_pairs={{0,12},{4,8},{8,4},{12,0},{1,13},{5,9},{9,5},{13,1},{2,14},{6,10},... | collective-permute-start | bytes 12296 | tf_op jit(solution)/shard_map/ppermute | solution.py:19
  90.6 4.0 %collective-permute-start.30 = (f32[8,128]{1,0:T(8,128)S(1)}, f32[8,128]{1,0:T(8,128)S(1)}, u32[]{:S(2)}, u32[]{:S(2)}) collective-permute-start(f32[8,128]{1,0:T(8,128)S(1)} %add_add_fusion.1), channel_id=1, source_target_pairs={{0,8},{4,12},{8,0},{12,4},{1,9},{5,13},{9,1},{13,5},{2,10},{6,14},... | collective-permute-start | bytes 12296 | tf_op jit(solution)/shard_map/ppermute | solution.py:19
  94.6 4.4 %copy-start.15 = (f32[3]{0:T(128)S(1)}, f32[3]{0:T(128)}, u32[]{:S(2)}) copy-start(f32[3]{0:T(128)} %constant.52) | copy-start | bytes 40
  94.6 4.4 %collective-permute-start.32 = (f32[8,128]{1,0:T(8,128)S(1)}, f32[8,128]{1,0:T(8,128)S(1)}, u32[]{:S(2)}, u32[]{:S(2)}) collective-permute-start(f32[8,128]{1,0:T(8,128)S(1)} %add_add_fusion), channel_id=1, source_target_pairs={{0,16},{16,0},{1,17},{17,1},{2,18},{18,2},{3,19},{19,3},{4,20},{20... | collective-permute-start | bytes 12296 | tf_op jit(solution)/shard_map/ppermute | solution.py:19
  (3 other events, 3.0 us)

commit v12 on v11

--- a/solution.py
+++ b/solution.py
@@ -312,7 +312,6 @@
 
 def norms_kernel(replicas, levels, flag_ref, ids_ref, ids_row_ref, gram_ref, *refs):
     *parts, masked_ref, norms_ref, y_ref, acc = refs
-    parts.reverse()
     piece = y_ref.shape[1]
     block = parts[0].shape[0] // replicas
     tok_rows = block * len(parts)
@@ -380,7 +379,7 @@
             bytes_accessed=4 * total * piece + 4 * total * total,
             transcendentals=0,
         ),
-    )(by_dp.reshape(1), row_ids, row_ids.reshape(1, total), gram_hidden, *reversed(parts))
+    )(by_dp.reshape(1), row_ids, row_ids.reshape(1, total), gram_hidden, *parts)
 
 
 def shards(layer_input_activations, cotangent, domain_ids, norm_gain, w_gate, w_up, w_down):

time: 100 us -> 99.8 us (level)
  transfers between devices with their start and end apart: 33 -> 33, of which waited for: 11 -> 12; matrix products, arithmetic and copies ran while one was open for 5% -> 5% of each run, Pallas kernels for 19% -> 19%
where the time goes in v12:
time: 99.8 us; the launch traced here: 99.4 us
  starting transfers between devices  47.6 us (48%)
  Pallas kernels  20.7 us (21%)
  waiting for transfers between devices  17.3 us (17%)
  matrix products  6.38 us (6%)
  other arithmetic  3.67 us (4%)
  local copies, waits for them, and re-layouts  2.44 us (2%)
  between operations  1.27 us (1%)
    ppermute x13, starting transfers between devices, swap(): return lax.ppermute(block, axis, [(i, i ^ offset) for i in range(size)])  16.4 us
    ppermute x8, starting transfers between devices, across(): return lax.ppermute(block, ('section', 'tensor'), route)  12 us
    ppermute x6, starting transfers between devices, swap_in(): return lax.ppermute(block, ('section', axis), route)  11.3 us
    pallas_call x3, Pallas kernels, domain_gradients(): pl.pallas_call(gradient_kernel, grid=(count,), in_specs=in_specs, out_spe...  8.49 us
    pallas_call x1, Pallas kernels, load_weights(): pl.pallas_call(load_kernel, in_specs=[pl.BlockSpec(memory_space=pltpu.HBM...  7.46 us
    ppermute x8, waiting for transfers between devices, across(): return lax.ppermute(block, ('section', 'tensor'), route)  7.31 us
    ppermute x13, waiting for transfers between devices, swap(): return lax.ppermute(block, axis, [(i, i ^ offset) for i in range(size)])  6.95 us
    ppermute x3, starting transfers between devices, exchange(): return lax.ppermute(block, ('section', 'dp', 'tensor'), pairs)  4.39 us
  transfers between devices with their start and end apart: 33, of which 12 were waited for; matrix products, arithmetic and copies ran while one was open for 5% of the time, Pallas kernels for 19%

profile of v12, /device:TPU:0, one launch (start us, length us, event | category | flops | bytes accessed | tf_op | source)
XLA Modules:
  0.0 99.4 jit_solution(6332360325243874449)
XLA Ops:
  0.6 1.0 bitcast_select_fusion.1
  1.6 5.1 %collective-permute-start.2 = (bf16[32,2048]{1,0:T(8,128)(2,1)S(1)}, bf16[32,2048]{1,0:T(8,128)(2,1)S(1)}, u32[]{:S(2)}, u32[]{:S(2)}) collective-permute-start(bf16[32,2048]{1,0:T(8,128)(2,1)S(1)} %bitcast_select_fusion.1), channel_id=1, source_target_pairs={{0,3},{1,2},{2,1},{3,0},{4,7},{5,6},{6,5},{7,4},{8,11},{9,10},{10,... | collective-permute-start | bytes 393224 | tf_op jit(solution)/shard_map/ppermute | solution.py:19
  6.8 0.6 collective-permute-start
  7.4 7.5 %shard_map.95 = (bf16[2048,1792]{1,0:T(8,128)(2,1)S(1)}, bf16[2048,1792]{1,0:T(8,128)(2,1)S(1)}, bf16[1792,2048]{1,0:T(8,128)(2,1)S(1)}, bf16[1792,2048]{1,0:T(8,128)(2,1)S(1)}) custom-call(bf16[1,2048,1792]{2,1,0:T(8,128)(2,1)} %gate_in.1, bf16[1,2048,1792]{2,1,0:T(8,128)(2,1)} %up_in.1, bf16[1,1792,2048]{2,1,0:T(8,128)(2,1)} %down_in.1), custom_call_target="tpu_custom_call" | custom-call | bytes 22020096 | tf_op jit(solution)/shard_map/pallas_call | solution.py:118
  14.9 3.0 %collective-permute-done.1 = bf16[32,2048]{1,0:T(8,128)(2,1)S(1)} collective-permute-done((bf16[32,2048]{1,0:T(8,128)(2,1)S(1)}, bf16[32,2048]{1,0:T(8,128)(2,1)S(1)}, u32[]{:S(2)}, u32[]{:S(2)}) %collective-permute-start.1) | collective-permute-done | bytes 131104 | tf_op jit(solution)/shard_map/ppermute | solution.py:19
  18.0 1.2 %fusion.15 = f32[128,1792]{1,0:T(8,128)S(1)} fusion(bf16[2048,1792]{1,0:T(8,128)(2,1)S(1)} %get-tuple-element.35, bf16[128,2048]{1,0:T(8,128)(2,1)S(1)} %get-tuple-element.41.rows_ref, f32[2048]{0:T(1024)S(1)} %bitcast.24, f32[128]{0:T(128)S(1)} %add_rsqrt_fusion.1), kind=kOutput, calls=%fused_computation.28 | convolution fusion | flops 940572672 | bytes 8790528 | tf_op jit(solution)/shard_map/dot_general | solution.py:408
  19.2 1.3 %fusion.refs_3_ = bf16[128,1792]{1,0:T(8,128)(2,1)S(1)} fusion(bf16[2048,1792]{1,0:T(8,128)(2,1)S(1)} %get-tuple-element.36.up_ref, f32[128,1792]{1,0:T(8,128)S(1)} %fusion.15, bf16[128,2048]{1,0:T(8,128)(2,1)S(1)} %get-tuple-element.41.rows_ref, f32[2048]{0:T(1024)S(1)} %bitcast.25, f32[128]{0:T(128)S(1)} %add_rsqrt_fusion.1), kind=kOutput, calls=%fused_computation.1 | convolution fusion | flops 941948928 | bytes 9249280 | tf_op jit(solution)/shard_map/dot_general | solution.py:409
  20.6 1.2 %convolution_convert_fusion = bf16[128,2048]{1,0:T(8,128)(2,1)S(1)} fusion(bf16[128,1792]{1,0:T(8,128)(2,1)S(1)} %fusion.refs_3_, bf16[1792,2048]{1,0:T(8,128)(2,1)S(1)} %get-tuple-element.37.down_ref), kind=kOutput, calls=%fused_computation.2 | convolution fusion | flops 939786240 | bytes 8323072 | tf_op jit(solution)/shard_map/dot_general | solution.py:414
  21.8 3.0 %collective-permute-start.6 = (bf16[32,2048]{1,0:T(8,128)(2,1)S(1)}, bf16[32,2048]{1,0:T(8,128)(2,1)S(1)}, u32[]{:S(2)}, u32[]{:S(2)}) collective-permute-start(bf16[32,2048]{1,0:T(8,128)(2,1)S(1)} %get-tuple-element.82), channel_id=1, source_target_pairs={{0,19},{1,18},{2,17},{3,16},{4,23},{5,22},{6,21},{7,20},{8,27},{9,... | collective-permute-start | bytes 393224 | tf_op jit(solution)/shard_map/ppermute | solution.py:33
  24.8 1.3 %collective-permute-start.5 = (bf16[32,2048]{1,0:T(8,128)(2,1)S(1)}, bf16[32,2048]{1,0:T(8,128)(2,1)S(1)}, u32[]{:S(2)}, u32[]{:S(2)}) collective-permute-start(bf16[32,2048]{1,0:T(8,128)(2,1)S(1)} %get-tuple-element.83), channel_id=1, source_target_pairs={{0,18},{1,19},{2,16},{3,17},{4,22},{5,23},{6,20},{7,21},{8,26},{9,... | collective-permute-start | bytes 393224 | tf_op jit(solution)/shard_map/ppermute | solution.py:33
  26.1 1.3 %collective-permute-start.4 = (bf16[32,2048]{1,0:T(8,128)(2,1)S(1)}, bf16[32,2048]{1,0:T(8,128)(2,1)S(1)}, u32[]{:S(2)}, u32[]{:S(2)}) collective-permute-start(bf16[32,2048]{1,0:T(8,128)(2,1)S(1)} %get-tuple-element.84), channel_id=1, source_target_pairs={{0,17},{1,16},{2,19},{3,18},{4,21},{5,20},{6,23},{7,22},{8,25},{9,... | collective-permute-start | bytes 393224 | tf_op jit(solution)/shard_map/ppermute | solution.py:33
  27.4 1.3 %collective-permute-start.3 = (bf16[32,2048]{1,0:T(8,128)(2,1)S(1)}, bf16[32,2048]{1,0:T(8,128)(2,1)S(1)}, u32[]{:S(2)}, u32[]{:S(2)}) collective-permute-start(bf16[32,2048]{1,0:T(8,128)(2,1)S(1)} %get-tuple-element.81), channel_id=1, source_target_pairs={{0,16},{1,17},{2,18},{3,19},{4,20},{5,21},{6,22},{7,23},{8,24},{9,... | collective-permute-start | bytes 393224 | tf_op jit(solution)/shard_map/ppermute | solution.py:33
  28.8 1.3 %collective-permute-done.4 = bf16[32,2048]{1,0:T(8,128)(2,1)S(1)} collective-permute-done((bf16[32,2048]{1,0:T(8,128)(2,1)S(1)}, bf16[32,2048]{1,0:T(8,128)(2,1)S(1)}, u32[]{:S(2)}, u32[]{:S(2)}) %collective-permute-start.4) | collective-permute-done | bytes 131104 | tf_op jit(solution)/shard_map/ppermute | solution.py:33
  30.3 2.5 %collective-permute-start.9 = (bf16[32,2048]{1,0:T(8,128)(2,1)S(1)}, bf16[32,2048]{1,0:T(8,128)(2,1)S(1)}, u32[]{:S(2)}, u32[]{:S(2)}) collective-permute-start(bf16[32,2048]{1,0:T(8,128)(2,1)S(1)} %pad_select_fusion), channel_id=1, source_target_pairs={{0,12},{16,19},{1,13},{17,18},{2,14},{18,17},{3,15},{19,16},{4,8},... | collective-permute-start | bytes 393224 | tf_op jit(solution)/shard_map/ppermute | solution.py:53
  33.8 4.4 %collective-permute-start.10 = (bf16[96,1792]{1,0:T(8,128)(2,1)S(1)}, bf16[96,1792]{1,0:T(8,128)(2,1)S(1)}, u32[]{:S(2)}, u32[]{:S(2)}) collective-permute-start(bf16[96,1792]{1,0:T(8,128)(2,1)S(1)} %slice.61), channel_id=1, source_target_pairs={{0,12},{4,8},{8,4},{12,0},{1,13},{5,9},{9,5},{13,1},{2,14},{6,10},... | collective-permute-start | bytes 1032200 | tf_op jit(solution)/shard_map/ppermute | solution.py:25
  38.2 2.4 %collective-permute-start.11 = (bf16[96,1792]{1,0:T(8,128)(2,1)S(1)}, bf16[96,1792]{1,0:T(8,128)(2,1)S(1)}, u32[]{:S(2)}, u32[]{:S(2)}) collective-permute-start(bf16[96,1792]{1,0:T(8,128)(2,1)S(1)} %slice.61), channel_id=1, source_target_pairs={{0,8},{4,12},{8,0},{12,4},{1,9},{5,13},{9,1},{13,5},{2,10},{6,14},... | collective-permute-start | bytes 1032200 | tf_op jit(solution)/shard_map/ppermute | solution.py:25
  40.6 2.4 %collective-permute-start.12 = (bf16[96,1792]{1,0:T(8,128)(2,1)S(1)}, bf16[96,1792]{1,0:T(8,128)(2,1)S(1)}, u32[]{:S(2)}, u32[]{:S(2)}) collective-permute-start(bf16[96,1792]{1,0:T(8,128)(2,1)S(1)} %slice.61), channel_id=1, source_target_pairs={{0,4},{4,0},{8,12},{12,8},{1,5},{5,1},{9,13},{13,9},{2,6},{6,2},{1... | collective-permute-start | bytes 1032200 | tf_op jit(solution)/shard_map/ppermute | solution.py:25
  43.3 1.2 %fusion.10 = f32[128,1792]{1,0:T(8,128)S(1)} fusion(bf16[2048,1792]{1,0:T(8,128)(2,1)S(1)} %get-tuple-element.35, f32[128]{0:T(128)S(1)} %add_rsqrt_fusion, f32[2048]{0:T(1024)S(1)} %bitcast.26, bf16[32,2048]{1,0:T(8,128)(2,1)S(1)} %collective-permute-done.9.refs_10_, bf16[32,2048]{1,0:T(8,128)(2,1)S(1)} %collective-permute-done.8.refs_9_, ...), kind=kOutput, calls=%fused_computation.26 | convolution fusion | flops 942407680 | bytes 8790528 | tf_op jit(solution)/shard_map/dot_general | solution.py:408
  44.5 1.5 %multiply_convert_fusion = (bf16[128,1792]{1,0:T(8,128)(2,1)S(1)}, bf16[128,1792]{1,0:T(8,128)(2,1)S(1)}, bf16[128,1792]{1,0:T(8,128)(2,1)S(1)}) fusion(f32[128,1792]{1,0:T(8,128)S(1)} %fusion.10, f32[128,1792]{1,0:T(8,128)S(1)} %shard_map.96, bf16[2048,1792]{1,0:T(8,128)(2,1)S(1)} %get-tuple-element.36.up_ref, f32[128]{0:T(128)S(1)} %add_rsqrt_fusion, ...), kind=kOutput, calls=%fused_computation.18 | convolution fusion | flops 946077696 | bytes 11084288 | tf_op jit(solution)/shard_map/dot_general | solution.py:409
  46.9 0.7 collective-permute-done.11.refs_1_
  47.6 2.2 %collective-permute-done.12.refs_2_ = bf16[96,1792]{1,0:T(8,128)(2,1)S(1)} collective-permute-done((bf16[96,1792]{1,0:T(8,128)(2,1)S(1)}, bf16[96,1792]{1,0:T(8,128)(2,1)S(1)}, u32[]{:S(2)}, u32[]{:S(2)}) %collective-permute-start.12) | collective-permute-done | bytes 344096 | tf_op jit(solution)/shard_map/ppermute | solution.py:25
  49.8 1.3 %collective-permute-start.16 = (bf16[32,2048]{1,0:T(8,128)(2,1)S(1)}, bf16[32,2048]{1,0:T(8,128)(2,1)S(1)}, u32[]{:S(2)}, u32[]{:S(2)}) collective-permute-start(bf16[32,2048]{1,0:T(8,128)(2,1)S(1)} %get-tuple-element.78), channel_id=1, source_target_pairs={{16,3},{17,2},{18,1},{19,0},{20,7},{21,6},{22,5},{23,4},{24,11},{2... | collective-permute-start | bytes 393224 | tf_op jit(solution)/shard_map/ppermute | solution.py:33
  51.1 1.3 %collective-permute-start.15 = (bf16[32,2048]{1,0:T(8,128)(2,1)S(1)}, bf16[32,2048]{1,0:T(8,128)(2,1)S(1)}, u32[]{:S(2)}, u32[]{:S(2)}) collective-permute-start(bf16[32,2048]{1,0:T(8,128)(2,1)S(1)} %get-tuple-element.79), channel_id=1, source_target_pairs={{16,2},{17,3},{18,0},{19,1},{20,6},{21,7},{22,4},{23,5},{24,10},{2... | collective-permute-start | bytes 393224 | tf_op jit(solution)/shard_map/ppermute | solution.py:33
  52.4 1.3 %collective-permute-start.14 = (bf16[32,2048]{1,0:T(8,128)(2,1)S(1)}, bf16[32,2048]{1,0:T(8,128)(2,1)S(1)}, u32[]{:S(2)}, u32[]{:S(2)}) collective-permute-start(bf16[32,2048]{1,0:T(8,128)(2,1)S(1)} %get-tuple-element.80), channel_id=1, source_target_pairs={{16,1},{17,0},{18,3},{19,2},{20,5},{21,4},{22,7},{23,6},{24,9},{25... | collective-permute-start | bytes 393224 | tf_op jit(solution)/shard_map/ppermute | solution.py:33
  53.7 1.3 %collective-permute-start.13 = (bf16[32,2048]{1,0:T(8,128)(2,1)S(1)}, bf16[32,2048]{1,0:T(8,128)(2,1)S(1)}, u32[]{:S(2)}, u32[]{:S(2)}) collective-permute-start(bf16[32,2048]{1,0:T(8,128)(2,1)S(1)} %get-tuple-element.77), channel_id=1, source_target_pairs={{16,0},{17,1},{18,2},{19,3},{20,4},{21,5},{22,6},{23,7},{24,8},{25... | collective-permute-start | bytes 393224 | tf_op jit(solution)/shard_map/ppermute | solution.py:33
  55.2 3.0 %collective-permute-done.13 = bf16[32,2048]{1,0:T(8,128)(2,1)S(1)} collective-permute-done((bf16[32,2048]{1,0:T(8,128)(2,1)S(1)}, bf16[32,2048]{1,0:T(8,128)(2,1)S(1)}, u32[]{:S(2)}, u32[]{:S(2)}) %collective-permute-start.13) | collective-permute-done | bytes 131104 | tf_op jit(solution)/shard_map/ppermute | solution.py:33
  58.1 3.1 %collective-permute-done.15 = bf16[32,2048]{1,0:T(8,128)(2,1)S(1)} collective-permute-done((bf16[32,2048]{1,0:T(8,128)(2,1)S(1)}, bf16[32,2048]{1,0:T(8,128)(2,1)S(1)}, u32[]{:S(2)}, u32[]{:S(2)}) %collective-permute-start.15) | collective-permute-done | bytes 131104 | tf_op jit(solution)/shard_map/ppermute | solution.py:33
  61.4 1.5 %collective-permute-start.21 = (bf16[48,512]{1,0:T(8,128)(2,1)S(1)}, bf16[48,512]{1,0:T(8,128)(2,1)S(1)}, u32[]{:S(2)}, u32[]{:S(2)}) collective-permute-start(bf16[48,512]{1,0:T(8,128)(2,1)S(1)} %get-tuple-element.93), channel_id=1, source_target_pairs={{0,12},{4,8},{8,4},{12,0},{1,13},{5,9},{9,5},{13,1},{2,14},{6,10},... | collective-permute-start | bytes 147464 | tf_op jit(solution)/shard_map/ppermute | solution.py:19
  63.5 1.5 %collective-permute-start.19 = (bf16[48,512]{1,0:T(8,128)(2,1)S(1)}, bf16[48,512]{1,0:T(8,128)(2,1)S(1)}, u32[]{:S(2)}, u32[]{:S(2)}) collective-permute-start(bf16[48,512]{1,0:T(8,128)(2,1)S(1)} %get-tuple-element.91), channel_id=1, source_target_pairs={{0,4},{4,0},{8,12},{12,8},{1,5},{5,1},{9,13},{13,9},{2,6},{6,2},{1... | collective-permute-start | bytes 147464 | tf_op jit(solution)/shard_map/ppermute | solution.py:19
  65.0 0.7 collective-permute-start.22
  65.7 0.7 collective-permute-start.17
  66.5 0.7 collective-permute-start.18
  67.2 1.7 %collective-permute-done.20 = bf16[48,512]{1,0:T(8,128)(2,1)S(1)} collective-permute-done((bf16[48,512]{1,0:T(8,128)(2,1)S(1)}, bf16[48,512]{1,0:T(8,128)(2,1)S(1)}, u32[]{:S(2)}, u32[]{:S(2)}) %collective-permute-start.20) | collective-permute-done | bytes 49184 | tf_op jit(solution)/shard_map/ppermute | solution.py:19
  69.3 0.9 dynamic-slice_select_fusion
  70.1 1.0 %collective-permute-start.24 = (bf16[128,512]{1,0:T(8,128)(2,1)}, bf16[128,512]{1,0:T(8,128)(2,1)S(1)}, u32[]{:S(2)}, u32[]{:S(2)}) collective-permute-start(bf16[128,512]{1,0:T(8,128)(2,1)} %get-tuple-element.74), channel_id=1, source_target_pairs={{0,2},{16,24},{1,3},{17,25},{2,0},{18,26},{3,1},{19,27},{4,6},{20,... | collective-permute-start | bytes 393224 | tf_op jit(solution)/shard_map/ppermute | solution.py:63
  71.2 3.3 %collective-permute-start.25 = (bf16[128,512]{1,0:T(8,128)(2,1)S(1)}, bf16[128,512]{1,0:T(8,128)(2,1)S(1)}, u32[]{:S(2)}, u32[]{:S(2)}) collective-permute-start(bf16[128,512]{1,0:T(8,128)(2,1)S(1)} %get-tuple-element.73), channel_id=1, source_target_pairs={{0,3},{16,28},{1,2},{17,29},{2,1},{18,30},{3,0},{19,31},{4,7},{20,... | collective-permute-start | bytes 393224 | tf_op jit(solution)/shard_map/ppermute | solution.py:63
  74.9 0.7 copy-done.9
  75.6 0.8 copy-done.10
  76.4 2.7 %shard_map.98 = (bf16[512,1792]{1,0:T(8,128)(2,1)S(1)}, f32[512,512]{1,0:T(8,128)S(1)}) custom-call(s32[1]{0:T(128)} %bitcast.flag_ref, bf16[96,1792]{1,0:T(8,128)(2,1)} %copy-done.11, bf16[96,1792]{1,0:T(8,128)(2,1)} %copy-done.12, bf16[96,1792]{1,0:T(8,128)(2,1)} %copy-done.13, bf16[128,1792]{1,0:T(8,128)(2,1)} %copy-done, bf16[128,1792]{1,0:T(8,128)(2,1)} %copy-done.7, ...), custom_call_target="tpu_custom_call" | custom-call | flops 939524096 | bytes 4718592 | tf_op jit(solution)/shard_map/pallas_call | solution.py:292
  79.2 1.7 %shard_map.99 = (bf16[512,2048]{1,0:T(8,128)(2,1)S(1)}, f32[8,128]{1,0:T(8,128)S(1)}) custom-call(s32[1]{0:T(128)} %bitcast.flag_ref, s32[512,1]{1,0:T(8,128)S(1)} %reshape.87.ids_ref, s32[1,512]{1,0:T(1,128)S(1)} %reshape_reshape.3.ids_row_ref, f32[512,512]{1,0:T(8,128)S(1)} %get-tuple-element.59.gram_ref, bf16[128,512]{1,0:T(8,128)(2,1)S(1)} %get-tuple-element.76.refs_0_, ...), custom_call_target="tpu_custom_call" | custom-call | flops 269484032 | bytes 2097152 | tf_op jit(solution)/shard_map/pallas_call | solution.py:361
  80.9 1.9 %collective-permute-start.28 = (f32[8,128]{1,0:T(8,128)S(1)}, f32[8,128]{1,0:T(8,128)S(1)}, u32[]{:S(2)}, u32[]{:S(2)}) collective-permute-start(f32[8,128]{1,0:T(8,128)S(1)} %get-tuple-element.62), channel_id=1, source_target_pairs={{0,1},{1,0},{2,3},{3,2},{4,5},{5,4},{6,7},{7,6},{8,9},{9,8},{10,11... | collective-permute-start | bytes 12296 | tf_op jit(solution)/shard_map/ppermute | solution.py:19
  82.8 1.4 %collective-permute-start.26 = (f32[8,128]{1,0:T(8,128)S(1)}, f32[8,128]{1,0:T(8,128)S(1)}, u32[]{:S(2)}, u32[]{:S(2)}) collective-permute-start(f32[8,128]{1,0:T(8,128)S(1)} %get-tuple-element.62), channel_id=1, source_target_pairs={{0,3},{1,2},{2,1},{3,0},{4,7},{5,6},{6,5},{7,4},{8,11},{9,10},{10,... | collective-permute-start | bytes 12296 | tf_op jit(solution)/shard_map/ppermute | solution.py:19
  84.5 2.5 %shard_map.100.rest_0_ = bf16[4,1792,512]{2,1,0:T(8,128)(2,1)} custom-call(bf16[512,1792]{1,0:T(8,128)(2,1)S(1)} %get-tuple-element.58.hidden_ref, bf16[512,2048]{1,0:T(8,128)(2,1)S(1)} %get-tuple-element.65.masked_ref), custom_call_target="tpu_custom_call" | custom-call | flops 1073741824 | bytes 2621440 | tf_op jit(solution)/shard_map/pallas_call | solution.py:224
  87.0 1.3 %collective-permute-done.26 = f32[8,128]{1,0:T(8,128)S(1)} collective-permute-done((f32[8,128]{1,0:T(8,128)S(1)}, f32[8,128]{1,0:T(8,128)S(1)}, u32[]{:S(2)}, u32[]{:S(2)}) %collective-permute-start.26) | collective-permute-done | bytes 4128 | tf_op jit(solution)/shard_map/ppermute | solution.py:19
  88.8 1.9 %collective-permute-start.31 = (f32[8,128]{1,0:T(8,128)S(1)}, f32[8,128]{1,0:T(8,128)S(1)}, u32[]{:S(2)}, u32[]{:S(2)}) collective-permute-start(f32[8,128]{1,0:T(8,128)S(1)} %add_add_fusion.1), channel_id=1, source_target_pairs={{0,4},{4,0},{8,12},{12,8},{1,5},{5,1},{9,13},{13,9},{2,6},{6,2},{1... | collective-permute-start | bytes 12296 | tf_op jit(solution)/shard_map/ppermute | solution.py:19
  91.1 1.2 %collective-permute-start.30 = (f32[8,128]{1,0:T(8,128)S(1)}, f32[8,128]{1,0:T(8,128)S(1)}, u32[]{:S(2)}, u32[]{:S(2)}) collective-permute-start(f32[8,128]{1,0:T(8,128)S(1)} %add_add_fusion.1), channel_id=1, source_target_pairs={{0,8},{4,12},{8,0},{12,4},{1,9},{5,13},{9,1},{13,5},{2,10},{6,14},... | collective-permute-start | bytes 12296 | tf_op jit(solution)/shard_map/ppermute | solution.py:19
  92.2 2.5 %shard_map.101.rest_0_ = bf16[4,1792,512]{2,1,0:T(8,128)(2,1)} custom-call(bf16[512,1792]{1,0:T(8,128)(2,1)S(1)} %get-tuple-element.58.hidden_ref, bf16[512,2048]{1,0:T(8,128)(2,1)S(1)} %get-tuple-element.65.masked_ref, bf16[4,1792,512]{2,1,0:T(8,128)(2,1)} %shard_map.100.rest_0_), custom_call_target="tpu_custom_call", output_to_operand_aliasing={{}: (2, {})} | custom-call | flops 1073741824 | bytes 2621440 | tf_op jit(solution)/shard_map/pallas_call | solution.py:224
  95.3 3.5 %shard_map.102 = bf16[4,1792,512]{2,1,0:T(8,128)(2,1)} custom-call(bf16[512,1792]{1,0:T(8,128)(2,1)S(1)} %get-tuple-element.58.hidden_ref, bf16[512,2048]{1,0:T(8,128)(2,1)S(1)} %get-tuple-element.65.masked_ref, bf16[4,1792,512]{2,1,0:T(8,128)(2,1)} %shard_map.101.rest_0_), custom_call_target="tpu_custom_call", output_to_operand_aliasing={{}: (2, {})} | custom-call | flops 1610612736 | bytes 3932160 | tf_op jit(solution)/shard_map/pallas_call | solution.py:224
  (103 shorter events, 6.6 us)
Async XLA Ops:
  1.6 16.4 %copy-start.14 = (f32[1,2048]{1,0:T(1,128)S(1)}, f32[1,2048]{1,0:T(1,128)}, u32[]{:S(2)}) copy-start(f32[1,2048]{1,0:T(1,128)} %param.11) | copy-start | bytes 24580
  1.6 13.2 %collective-permute-start.2 = (bf16[32,2048]{1,0:T(8,128)(2,1)S(1)}, bf16[32,2048]{1,0:T(8,128)(2,1)S(1)}, u32[]{:S(2)}, u32[]{:S(2)}) collective-permute-start(bf16[32,2048]{1,0:T(8,128)(2,1)S(1)} %bitcast_select_fusion.1), channel_id=1, source_target_pairs={{0,3},{1,2},{2,1},{3,0},{4,7},{5,6},{6,5},{7,4},{8,11},{9,10},{10,... | collective-permute-start | bytes 393224 | tf_op jit(solution)/shard_map/ppermute | solution.py:19
  6.8 11.1 %collective-permute-start.1 = (bf16[32,2048]{1,0:T(8,128)(2,1)S(1)}, bf16[32,2048]{1,0:T(8,128)(2,1)S(1)}, u32[]{:S(2)}, u32[]{:S(2)}) collective-permute-start(bf16[32,2048]{1,0:T(8,128)(2,1)S(1)} %bitcast_select_fusion.1), channel_id=1, source_target_pairs={{0,2},{1,3},{2,0},{3,1},{4,6},{5,7},{6,4},{7,5},{8,10},{9,11},{10,... | collective-permute-start | bytes 393224 | tf_op jit(solution)/shard_map/ppermute | solution.py:19
  6.8 11.1 %collective-permute-start = (bf16[32,2048]{1,0:T(8,128)(2,1)S(1)}, bf16[32,2048]{1,0:T(8,128)(2,1)S(1)}, u32[]{:S(2)}, u32[]{:S(2)}) collective-permute-start(bf16[32,2048]{1,0:T(8,128)(2,1)S(1)} %bitcast_select_fusion.1), channel_id=1, source_target_pairs={{0,1},{1,0},{2,3},{3,2},{4,5},{5,4},{6,7},{7,6},{8,9},{9,8},{10,11... | collective-permute-start | bytes 393224 | tf_op jit(solution)/shard_map/ppermute | solution.py:19
  20.6 8.2 %copy-start = (bf16[128,1792]{1,0:T(8,128)(2,1)}, bf16[128,1792]{1,0:T(8,128)(2,1)S(1)}, u32[]{:S(2)}) copy-start(bf16[128,1792]{1,0:T(8,128)(2,1)S(1)} %fusion.refs_3_) | copy-start | bytes 1376260
  21.8 8.3 %copy-start.6 = (bf16[4,8,2048]{2,1,0:T(8,128)(2,1)S(1)}, bf16[4,8,2048]{2,1,0:T(8,128)(2,1)}, u32[]{:S(2)}) copy-start(bf16[4,8,2048]{2,1,0:T(8,128)(2,1)} %param.8) | copy-start | bytes 393220
  21.8 7.0 %collective-permute-start.6 = (bf16[32,2048]{1,0:T(8,128)(2,1)S(1)}, bf16[32,2048]{1,0:T(8,128)(2,1)S(1)}, u32[]{:S(2)}, u32[]{:S(2)}) collective-permute-start(bf16[32,2048]{1,0:T(8,128)(2,1)S(1)} %get-tuple-element.82), channel_id=1, source_target_pairs={{0,19},{1,18},{2,17},{3,16},{4,23},{5,22},{6,21},{7,20},{8,27},{9,... | collective-permute-start | bytes 393224 | tf_op jit(solution)/shard_map/ppermute | solution.py:33
  24.8 4.0 %collective-permute-start.5 = (bf16[32,2048]{1,0:T(8,128)(2,1)S(1)}, bf16[32,2048]{1,0:T(8,128)(2,1)S(1)}, u32[]{:S(2)}, u32[]{:S(2)}) collective-permute-start(bf16[32,2048]{1,0:T(8,128)(2,1)S(1)} %get-tuple-element.83), channel_id=1, source_target_pairs={{0,18},{1,19},{2,16},{3,17},{4,22},{5,23},{6,20},{7,21},{8,26},{9,... | collective-permute-start | bytes 393224 | tf_op jit(solution)/shard_map/ppermute | solution.py:33
  26.1 4.0 %collective-permute-start.4 = (bf16[32,2048]{1,0:T(8,128)(2,1)S(1)}, bf16[32,2048]{1,0:T(8,128)(2,1)S(1)}, u32[]{:S(2)}, u32[]{:S(2)}) collective-permute-start(bf16[32,2048]{1,0:T(8,128)(2,1)S(1)} %get-tuple-element.84), channel_id=1, source_target_pairs={{0,17},{1,16},{2,19},{3,18},{4,21},{5,20},{6,23},{7,22},{8,25},{9,... | collective-permute-start | bytes 393224 | tf_op jit(solution)/shard_map/ppermute | solution.py:33
  27.4 2.7 %collective-permute-start.3 = (bf16[32,2048]{1,0:T(8,128)(2,1)S(1)}, bf16[32,2048]{1,0:T(8,128)(2,1)S(1)}, u32[]{:S(2)}, u32[]{:S(2)}) collective-permute-start(bf16[32,2048]{1,0:T(8,128)(2,1)S(1)} %get-tuple-element.81), channel_id=1, source_target_pairs={{0,16},{1,17},{2,18},{3,19},{4,20},{5,21},{6,22},{7,23},{8,24},{9,... | collective-permute-start | bytes 393224 | tf_op jit(solution)/shard_map/ppermute | solution.py:33
  28.7 5.1 %copy-start.1 = (bf16[128,1792]{1,0:T(8,128)(2,1)S(1)}, bf16[128,1792]{1,0:T(8,128)(2,1)}, u32[]{:S(2)}) copy-start(bf16[128,1792]{1,0:T(8,128)(2,1)} %copy-done) | copy-start | bytes 1376260
  30.3 10.4 %collective-permute-start.9 = (bf16[32,2048]{1,0:T(8,128)(2,1)S(1)}, bf16[32,2048]{1,0:T(8,128)(2,1)S(1)}, u32[]{:S(2)}, u32[]{:S(2)}) collective-permute-start(bf16[32,2048]{1,0:T(8,128)(2,1)S(1)} %pad_select_fusion), channel_id=1, source_target_pairs={{0,12},{16,19},{1,13},{17,18},{2,14},{18,17},{3,15},{19,16},{4,8},... | collective-permute-start | bytes 393224 | tf_op jit(solution)/shard_map/ppermute | solution.py:53
  32.8 10.3 %collective-permute-start.8 = (bf16[32,2048]{1,0:T(8,128)(2,1)S(1)}, bf16[32,2048]{1,0:T(8,128)(2,1)S(1)}, u32[]{:S(2)}, u32[]{:S(2)}) collective-permute-start(bf16[32,2048]{1,0:T(8,128)(2,1)S(1)} %pad_select_fusion), channel_id=1, source_target_pairs={{0,8},{16,18},{1,9},{17,19},{2,10},{18,16},{3,11},{19,17},{4,12},{... | collective-permute-start | bytes 393224 | tf_op jit(solution)/shard_map/ppermute | solution.py:53
  33.3 9.8 %collective-permute-start.7 = (bf16[32,2048]{1,0:T(8,128)(2,1)S(1)}, bf16[32,2048]{1,0:T(8,128)(2,1)S(1)}, u32[]{:S(2)}, u32[]{:S(2)}) collective-permute-start(bf16[32,2048]{1,0:T(8,128)(2,1)S(1)} %pad_select_fusion), channel_id=1, source_target_pairs={{0,4},{16,17},{1,5},{17,16},{2,6},{18,19},{3,7},{19,18},{4,0},{20,... | collective-permute-start | bytes 393224 | tf_op jit(solution)/shard_map/ppermute | solution.py:53
  33.8 13.0 %collective-permute-start.10 = (bf16[96,1792]{1,0:T(8,128)(2,1)S(1)}, bf16[96,1792]{1,0:T(8,128)(2,1)S(1)}, u32[]{:S(2)}, u32[]{:S(2)}) collective-permute-start(bf16[96,1792]{1,0:T(8,128)(2,1)S(1)} %slice.61), channel_id=1, source_target_pairs={{0,12},{4,8},{8,4},{12,0},{1,13},{5,9},{9,5},{13,1},{2,14},{6,10},... | collective-permute-start | bytes 1032200 | tf_op jit(solution)/shard_map/ppermute | solution.py:25
  38.2 9.4 %collective-permute-start.11 = (bf16[96,1792]{1,0:T(8,128)(2,1)S(1)}, bf16[96,1792]{1,0:T(8,128)(2,1)S(1)}, u32[]{:S(2)}, u32[]{:S(2)}) collective-permute-start(bf16[96,1792]{1,0:T(8,128)(2,1)S(1)} %slice.61), channel_id=1, source_target_pairs={{0,8},{4,12},{8,0},{12,4},{1,9},{5,13},{9,1},{13,5},{2,10},{6,14},... | collective-permute-start | bytes 1032200 | tf_op jit(solution)/shard_map/ppermute | solution.py:25
  40.6 6.0 %copy-start.2 = (bf16[32,2048]{1,0:T(8,128)(2,1)}, bf16[32,2048]{1,0:T(8,128)(2,1)S(1)}, u32[]{:S(2)}) copy-start(bf16[32,2048]{1,0:T(8,128)(2,1)S(1)} %collective-permute-done.9.refs_10_) | copy-start | bytes 393220
  40.6 9.1 %collective-permute-start.12 = (bf16[96,1792]{1,0:T(8,128)(2,1)S(1)}, bf16[96,1792]{1,0:T(8,128)(2,1)S(1)}, u32[]{:S(2)}, u32[]{:S(2)}) collective-permute-start(bf16[96,1792]{1,0:T(8,128)(2,1)S(1)} %slice.61), channel_id=1, source_target_pairs={{0,4},{4,0},{8,12},{12,8},{1,5},{5,1},{9,13},{13,9},{2,6},{6,2},{1... | collective-permute-start | bytes 1032200 | tf_op jit(solution)/shard_map/ppermute | solution.py:25
  43.1 3.5 %copy-start.3 = (bf16[32,2048]{1,0:T(8,128)(2,1)}, bf16[32,2048]{1,0:T(8,128)(2,1)S(1)}, u32[]{:S(2)}) copy-start(bf16[32,2048]{1,0:T(8,128)(2,1)S(1)} %collective-permute-done.8.refs_9_) | copy-start | bytes 393220
  43.1 3.5 %copy-start.4 = (bf16[32,2048]{1,0:T(8,128)(2,1)}, bf16[32,2048]{1,0:T(8,128)(2,1)S(1)}, u32[]{:S(2)}) copy-start(bf16[32,2048]{1,0:T(8,128)(2,1)S(1)} %collective-permute-done.7.refs_8_) | copy-start | bytes 393220
  46.0 20.5 %copy-start.7 = (bf16[128,1792]{1,0:T(8,128)(2,1)}, bf16[128,1792]{1,0:T(8,128)(2,1)S(1)}, u32[]{:S(2)}) copy-start(bf16[128,1792]{1,0:T(8,128)(2,1)S(1)} %get-tuple-element.56.refs_4_) | copy-start | bytes 1376260
  46.1 9.0 %copy-start.16 = (s32[4,1]{0,1:T(1,128)S(1)}, s32[4,1]{0,1:T(1,128)}, u32[]{:S(2)}) copy-start(s32[4,1]{0,1:T(1,128)} %param.10) | copy-start | bytes 52
  46.1 15.1 %copy-start.5 = (bf16[4,8,2048]{2,1,0:T(8,128)(2,1)S(1)}, bf16[4,8,2048]{2,1,0:T(8,128)(2,1)}, u32[]{:S(2)}) copy-start(bf16[4,8,2048]{2,1,0:T(8,128)(2,1)} %param.9) | copy-start | bytes 393220
  46.9 28.0 %copy-start.11 = (bf16[96,1792]{1,0:T(8,128)(2,1)}, bf16[96,1792]{1,0:T(8,128)(2,1)S(1)}, u32[]{:S(2)}) copy-start(bf16[96,1792]{1,0:T(8,128)(2,1)S(1)} %collective-permute-done.10.refs_0_) | copy-start | bytes 1032196
  47.6 27.3 %copy-start.12 = (bf16[96,1792]{1,0:T(8,128)(2,1)}, bf16[96,1792]{1,0:T(8,128)(2,1)S(1)}, u32[]{:S(2)}) copy-start(bf16[96,1792]{1,0:T(8,128)(2,1)S(1)} %collective-permute-done.11.refs_1_) | copy-start | bytes 1032196
  49.8 15.2 %copy-start.13 = (bf16[96,1792]{1,0:T(8,128)(2,1)}, bf16[96,1792]{1,0:T(8,128)(2,1)S(1)}, u32[]{:S(2)}) copy-start(bf16[96,1792]{1,0:T(8,128)(2,1)S(1)} %collective-permute-done.12.refs_2_) | copy-start | bytes 1032196
  49.8 8.3 %collective-permute-start.16 = (bf16[32,2048]{1,0:T(8,128)(2,1)S(1)}, bf16[32,2048]{1,0:T(8,128)(2,1)S(1)}, u32[]{:S(2)}, u32[]{:S(2)}) collective-permute-start(bf16[32,2048]{1,0:T(8,128)(2,1)S(1)} %get-tuple-element.78), channel_id=1, source_target_pairs={{16,3},{17,2},{18,1},{19,0},{20,7},{21,6},{22,5},{23,4},{24,11},{2... | collective-permute-start | bytes 393224 | tf_op jit(solution)/shard_map/ppermute | solution.py:33
  51.1 10.1 %collective-permute-start.15 = (bf16[32,2048]{1,0:T(8,128)(2,1)S(1)}, bf16[32,2048]{1,0:T(8,128)(2,1)S(1)}, u32[]{:S(2)}, u32[]{:S(2)}) collective-permute-start(bf16[32,2048]{1,0:T(8,128)(2,1)S(1)} %get-tuple-element.79), channel_id=1, source_target_pairs={{16,2},{17,3},{18,0},{19,1},{20,6},{21,7},{22,4},{23,5},{24,10},{2... | collective-permute-start | bytes 393224 | tf_op jit(solution)/shard_map/ppermute | solution.py:33
  52.4 8.8 %collective-permute-start.14 = (bf16[32,2048]{1,0:T(8,128)(2,1)S(1)}, bf16[32,2048]{1,0:T(8,128)(2,1)S(1)}, u32[]{:S(2)}, u32[]{:S(2)}) collective-permute-start(bf16[32,2048]{1,0:T(8,128)(2,1)S(1)} %get-tuple-element.80), channel_id=1, source_target_pairs={{16,1},{17,0},{18,3},{19,2},{20,5},{21,4},{22,7},{23,6},{24,9},{25... | collective-permute-start | bytes 393224 | tf_op jit(solution)/shard_map/ppermute | solution.py:33
  53.7 4.4 %collective-permute-start.13 = (bf16[32,2048]{1,0:T(8,128)(2,1)S(1)}, bf16[32,2048]{1,0:T(8,128)(2,1)S(1)}, u32[]{:S(2)}, u32[]{:S(2)}) collective-permute-start(bf16[32,2048]{1,0:T(8,128)(2,1)S(1)} %get-tuple-element.77), channel_id=1, source_target_pairs={{16,0},{17,1},{18,2},{19,3},{20,4},{21,5},{22,6},{23,7},{24,8},{25... | collective-permute-start | bytes 393224 | tf_op jit(solution)/shard_map/ppermute | solution.py:33
  61.4 5.1 %collective-permute-start.21 = (bf16[48,512]{1,0:T(8,128)(2,1)S(1)}, bf16[48,512]{1,0:T(8,128)(2,1)S(1)}, u32[]{:S(2)}, u32[]{:S(2)}) collective-permute-start(bf16[48,512]{1,0:T(8,128)(2,1)S(1)} %get-tuple-element.93), channel_id=1, source_target_pairs={{0,12},{4,8},{8,4},{12,0},{1,13},{5,9},{9,5},{13,1},{2,14},{6,10},... | collective-permute-start | bytes 147464 | tf_op jit(solution)/shard_map/ppermute | solution.py:19
  63.0 5.9 %collective-permute-start.20 = (bf16[48,512]{1,0:T(8,128)(2,1)S(1)}, bf16[48,512]{1,0:T(8,128)(2,1)S(1)}, u32[]{:S(2)}, u32[]{:S(2)}) collective-permute-start(bf16[48,512]{1,0:T(8,128)(2,1)S(1)} %get-tuple-element.92), channel_id=1, source_target_pairs={{0,8},{4,12},{8,0},{12,4},{1,9},{5,13},{9,1},{13,5},{2,10},{6,14},... | collective-permute-start | bytes 147464 | tf_op jit(solution)/shard_map/ppermute | solution.py:19
  63.5 5.4 %collective-permute-start.19 = (bf16[48,512]{1,0:T(8,128)(2,1)S(1)}, bf16[48,512]{1,0:T(8,128)(2,1)S(1)}, u32[]{:S(2)}, u32[]{:S(2)}) collective-permute-start(bf16[48,512]{1,0:T(8,128)(2,1)S(1)} %get-tuple-element.91), channel_id=1, source_target_pairs={{0,4},{4,0},{8,12},{12,8},{1,5},{5,1},{9,13},{13,9},{2,6},{6,2},{1... | collective-permute-start | bytes 147464 | tf_op jit(solution)/shard_map/ppermute | solution.py:19
  65.0 4.2 %collective-permute-start.22 = (bf16[128,1792]{1,0:T(8,128)(2,1)S(1)}, bf16[128,1792]{1,0:T(8,128)(2,1)S(1)}, u32[]{:S(2)}, u32[]{:S(2)}) collective-permute-start(bf16[128,1792]{1,0:T(8,128)(2,1)S(1)} %get-tuple-element.56.refs_4_), channel_id=1, source_target_pairs={{16,28},{20,24},{24,20},{28,16},{17,29},{21,25},{25,21},{29,17},{1... | collective-permute-start | bytes 1376264 | tf_op jit(solution)/shard_map/ppermute | solution.py:25
  65.7 9.1 %collective-permute-start.17 = (bf16[128,1792]{1,0:T(8,128)(2,1)S(1)}, bf16[128,1792]{1,0:T(8,128)(2,1)S(1)}, u32[]{:S(2)}, u32[]{:S(2)}) collective-permute-start(bf16[128,1792]{1,0:T(8,128)(2,1)S(1)} %get-tuple-element.56.refs_4_), channel_id=1, source_target_pairs={{16,20},{20,16},{24,28},{28,24},{17,21},{21,17},{25,29},{29,25},{1... | collective-permute-start | bytes 1376264 | tf_op jit(solution)/shard_map/ppermute | solution.py:25
  66.5 8.4 %collective-permute-start.18 = (bf16[128,1792]{1,0:T(8,128)(2,1)S(1)}, bf16[128,1792]{1,0:T(8,128)(2,1)S(1)}, u32[]{:S(2)}, u32[]{:S(2)}) collective-permute-start(bf16[128,1792]{1,0:T(8,128)(2,1)S(1)} %get-tuple-element.56.refs_4_), channel_id=1, source_target_pairs={{16,24},{20,28},{24,16},{28,20},{17,25},{21,29},{25,17},{29,21},{1... | collective-permute-start | bytes 1376264 | tf_op jit(solution)/shard_map/ppermute | solution.py:25
  69.2 5.6 %copy-start.8 = (bf16[128,1792]{1,0:T(8,128)(2,1)}, bf16[128,1792]{1,0:T(8,128)(2,1)S(1)}, u32[]{:S(2)}) copy-start(bf16[128,1792]{1,0:T(8,128)(2,1)S(1)} %collective-permute-done.22.refs_7_) | copy-start | bytes 1376260
  70.1 8.9 %collective-permute-start.23 = (bf16[128,512]{1,0:T(8,128)(2,1)}, bf16[128,512]{1,0:T(8,128)(2,1)S(1)}, u32[]{:S(2)}, u32[]{:S(2)}) collective-permute-start(bf16[128,512]{1,0:T(8,128)(2,1)} %get-tuple-element.75), channel_id=1, source_target_pairs={{0,1},{16,20},{1,0},{17,21},{2,3},{18,22},{3,2},{19,23},{4,5},{20,... | collective-permute-start | bytes 393224 | tf_op jit(solution)/shard_map/ppermute | solution.py:63
  70.1 8.9 %collective-permute-start.24 = (bf16[128,512]{1,0:T(8,128)(2,1)}, bf16[128,512]{1,0:T(8,128)(2,1)S(1)}, u32[]{:S(2)}, u32[]{:S(2)}) collective-permute-start(bf16[128,512]{1,0:T(8,128)(2,1)} %get-tuple-element.74), channel_id=1, source_target_pairs={{0,2},{16,24},{1,3},{17,25},{2,0},{18,26},{3,1},{19,27},{4,6},{20,... | collective-permute-start | bytes 393224 | tf_op jit(solution)/shard_map/ppermute | solution.py:63
  71.2 8.0 %collective-permute-start.25 = (bf16[128,512]{1,0:T(8,128)(2,1)S(1)}, bf16[128,512]{1,0:T(8,128)(2,1)S(1)}, u32[]{:S(2)}, u32[]{:S(2)}) collective-permute-start(bf16[128,512]{1,0:T(8,128)(2,1)S(1)} %get-tuple-element.73), channel_id=1, source_target_pairs={{0,3},{16,28},{1,2},{17,29},{2,1},{18,30},{3,0},{19,31},{4,7},{20,... | collective-permute-start | bytes 393224 | tf_op jit(solution)/shard_map/ppermute | solution.py:63
  80.9 6.1 %collective-permute-start.28 = (f32[8,128]{1,0:T(8,128)S(1)}, f32[8,128]{1,0:T(8,128)S(1)}, u32[]{:S(2)}, u32[]{:S(2)}) collective-permute-start(f32[8,128]{1,0:T(8,128)S(1)} %get-tuple-element.62), channel_id=1, source_target_pairs={{0,1},{1,0},{2,3},{3,2},{4,5},{5,4},{6,7},{7,6},{8,9},{9,8},{10,11... | collective-permute-start | bytes 12296 | tf_op jit(solution)/shard_map/ppermute | solution.py:19
  82.8 5.4 %collective-permute-start.26 = (f32[8,128]{1,0:T(8,128)S(1)}, f32[8,128]{1,0:T(8,128)S(1)}, u32[]{:S(2)}, u32[]{:S(2)}) collective-permute-start(f32[8,128]{1,0:T(8,128)S(1)} %get-tuple-element.62), channel_id=1, source_target_pairs={{0,3},{1,2},{2,1},{3,0},{4,7},{5,6},{6,5},{7,4},{8,11},{9,10},{10,... | collective-permute-start | bytes 12296 | tf_op jit(solution)/shard_map/ppermute | solution.py:19
  84.2 4.5 %collective-permute-start.27 = (f32[8,128]{1,0:T(8,128)S(1)}, f32[8,128]{1,0:T(8,128)S(1)}, u32[]{:S(2)}, u32[]{:S(2)}) collective-permute-start(f32[8,128]{1,0:T(8,128)S(1)} %get-tuple-element.62), channel_id=1, source_target_pairs={{0,2},{1,3},{2,0},{3,1},{4,6},{5,7},{6,4},{7,5},{8,10},{9,11},{10,... | collective-permute-start | bytes 12296 | tf_op jit(solution)/shard_map/ppermute | solution.py:19
  88.8 6.0 %collective-permute-start.31 = (f32[8,128]{1,0:T(8,128)S(1)}, f32[8,128]{1,0:T(8,128)S(1)}, u32[]{:S(2)}, u32[]{:S(2)}) collective-permute-start(f32[8,128]{1,0:T(8,128)S(1)} %add_add_fusion.1), channel_id=1, source_target_pairs={{0,4},{4,0},{8,12},{12,8},{1,5},{5,1},{9,13},{13,9},{2,6},{6,2},{1... | collective-permute-start | bytes 12296 | tf_op jit(solution)/shard_map/ppermute | solution.py:19
  90.7 4.5 %collective-permute-start.29 = (f32[8,128]{1,0:T(8,128)S(1)}, f32[8,128]{1,0:T(8,128)S(1)}, u32[]{:S(2)}, u32[]{:S(2)}) collective-permute-start(f32[8,128]{1,0:T(8,128)S(1)} %add_add_fusion.1), channel_id=1, source_target_pairs={{0,12},{4,8},{8,4},{12,0},{1,13},{5,9},{9,5},{13,1},{2,14},{6,10},... | collective-permute-start | bytes 12296 | tf_op jit(solution)/shard_map/ppermute | solution.py:19
  91.1 4.1 %collective-permute-start.30 = (f32[8,128]{1,0:T(8,128)S(1)}, f32[8,128]{1,0:T(8,128)S(1)}, u32[]{:S(2)}, u32[]{:S(2)}) collective-permute-start(f32[8,128]{1,0:T(8,128)S(1)} %add_add_fusion.1), channel_id=1, source_target_pairs={{0,8},{4,12},{8,0},{12,4},{1,9},{5,13},{9,1},{13,5},{2,10},{6,14},... | collective-permute-start | bytes 12296 | tf_op jit(solution)/shard_map/ppermute | solution.py:19
  95.2 3.6 %copy-start.15 = (f32[3]{0:T(128)S(1)}, f32[3]{0:T(128)}, u32[]{:S(2)}) copy-start(f32[3]{0:T(128)} %constant.52) | copy-start | bytes 40
  95.2 3.6 %collective-permute-start.32 = (f32[8,128]{1,0:T(8,128)S(1)}, f32[8,128]{1,0:T(8,128)S(1)}, u32[]{:S(2)}, u32[]{:S(2)}) collective-permute-start(f32[8,128]{1,0:T(8,128)S(1)} %add_add_fusion), channel_id=1, source_target_pairs={{0,16},{16,0},{1,17},{17,1},{2,18},{18,2},{3,19},{19,3},{4,20},{20... | collective-permute-start | bytes 12296 | tf_op jit(solution)/shard_map/ppermute | solution.py:19
  (3 other events, 3.0 us)
